TPU v7x, 32 devices: a whole 2x2x4 slice. The times are simulated.
32 devices in a mesh: dp: 8 (over y, x, core), seq: 4 (over z).
Axes of the slice: x: 2, y: 2, z: 4, core: 2. Of those that a mesh axis runs over, the one named last changes fastest.
Arguments:
- latents: bfloat16 [8, 1024, 1536], P('dp', 'seq'), may hold values from -6 to 6
- context: bfloat16 [8, 384, 768], P('dp'), may hold values from -6 to 6
- clip_bounds: int32 [8, 2], P('dp'), may hold values from 1 to 1023, as said below
- timesteps: int32 [8, 3], P('dp'), may hold values from 0 to 999
- self_inward: bfloat16 [1536, 4608], P(('dp', 'seq')), may hold values from -0.1875 to 0.1875
- self_outward: bfloat16 [1536, 1536], P(('dp', 'seq')), may hold values from -2.5 to 2.5
- cross_query: bfloat16 [1536, 1536], P(('dp', 'seq')), may hold values from -0.15625 to 0.15625
- cross_keyval: bfloat16 [768, 3072], P(('dp', 'seq')), may hold values from -0.25 to 0.25
- cross_return: bfloat16 [1536, 1536], P(('dp', 'seq')), may hold values from -0.875 to 0.875
- time_weight: bfloat16 [256, 1536], P(('dp', 'seq')), may hold values from -1.5 to 1.5
- expand_weight: bfloat16 [1536, 12288], P(('dp', 'seq')), may hold values from -0.15625 to 0.15625
- shrink_weight: bfloat16 [6144, 1536], P(('dp', 'seq')), may hold values from -0.15625 to 0.15625
- gain_attend: bfloat16 [1536], P(('dp', 'seq')), may hold values from 0.25 to 1.75
- gain_cross: bfloat16 [1536], P(('dp', 'seq')), may hold values from 0.25 to 1.75
- gain_feed: bfloat16 [1536], P(('dp', 'seq')), may hold values from 0.25 to 1.75
- cotangent: bfloat16 [8, 1024, 1536], P('dp', 'seq'), may hold values from -6 to 6
Outputs:
- block_output: bfloat16 [8, 1024, 1536], P('dp', 'seq')
- grad_latents: float32 [8, 1024, 1536], P('dp', 'seq')
- grad_inward: float32 [1536, 4608], P(('dp', 'seq'))
- grad_outward: float32 [1536, 1536], P(('dp', 'seq'))
- grad_query: float32 [1536, 1536], P(('dp', 'seq'))
- grad_keyval: float32 [768, 3072], P(('dp', 'seq'))
- grad_return: float32 [1536, 1536], P(('dp', 'seq'))
- grad_time: float32 [256, 1536], P(('dp', 'seq'))
- grad_expand: float32 [1536, 12288], P(('dp', 'seq'))
- grad_shrink: float32 [6144, 1536], P(('dp', 'seq'))
- grad_attend: float32 [1536], P(('dp', 'seq'))
- grad_cross: float32 [1536], P(('dp', 'seq'))
- grad_feed: float32 [1536], P(('dp', 'seq'))
Inputs may be any that keep to these rules, and one draw needn't show every extreme that they name: `clip_bounds`: in each row the first entry lies in 1 to 255 and the second in 769 to 1023, so every clip is non-empty and the second clip runs from the first index of seq to the last.
All inputs are finite; a program needn't handle non-finite values.
Results may differ from a plain program's by a relative error of at most 0.025.
Values may be sent and summed in bfloat16 or wider, within the bound.
No kernel may reach another device: no remote copies, remote signals or barrier semaphores. Data moves between devices by JAX's collectives and lax.ppermute only.
A program may use at most 320 MiB of HBM per device.

v0:
```python
import math

import jax
import jax.numpy as jnp
from jax import lax
from jax.sharding import PartitionSpec as P

D = 1536
HEADS = 24
HEAD_DIM = 64
FF = 6144
CTX_LEN = 128
TFEAT = 256
CLIPS = 3


EPSILON = 1e-05
SCORE_SCALE = 0.125
MASKED = -1e30
PRECISE = lax.Precision.HIGHEST


def dense(activations, weight):
    return jnp.einsum("rfd,dn->rfn", activations, weight, preferred_element_type=jnp.float32)


def dense_back(gradients, weight):
    return jnp.einsum("rfn,dn->rfd", gradients, weight, preferred_element_type=jnp.float32)


def norm_forward(hidden):
    centre = jnp.mean(hidden, axis=-1, keepdims=True)
    centred = hidden - centre
    spread = jnp.mean(centred * centred, axis=-1, keepdims=True)
    scale_inv = lax.rsqrt(spread + EPSILON)
    return (centred * scale_inv, scale_inv)


def norm_backward(grad_norm, normalized, scale_inv, gain_vector):
    scaled = grad_norm * gain_vector
    gain_grad = jnp.sum(grad_norm * normalized, axis=(0, 1))
    inner = (
        scaled
        - jnp.mean(scaled, axis=-1, keepdims=True)
        - normalized * jnp.mean(scaled * normalized, axis=-1, keepdims=True)
    )
    return (scale_inv * inner, gain_grad)


def rotate(head_values, cosine_table, sine_table):
    half_width = head_values.shape[-1] // 2
    first_half = head_values[..., :half_width]
    second_half = head_values[..., half_width:]
    return jnp.concatenate(
        [
            first_half * cosine_table - second_half * sine_table,
            first_half * sine_table + second_half * cosine_table,
        ],
        axis=-1,
    )


def rotary_tables(positions):
    half_width = HEAD_DIM // 2
    frequencies = jnp.exp(
        -math.log(10000.0) * jnp.arange(half_width, dtype=jnp.float32) / half_width
    )
    angles = positions[..., None] * frequencies
    return (jnp.cos(angles)[..., None, :], jnp.sin(angles)[..., None, :])


def time_features(step_values):
    half_width = TFEAT // 2
    frequencies = jnp.exp(
        -math.log(10000.0) * jnp.arange(half_width, dtype=jnp.float32) / half_width
    )
    angles = step_values.astype(jnp.float32)[..., None] * frequencies
    return jnp.concatenate([jnp.cos(angles), jnp.sin(angles)], axis=-1)


def score_block(query_low, key_block, query_clip, key_clip):
    raw_scores = jnp.einsum(
        "rqhd,rkhd->rhqk", query_low, key_block, preferred_element_type=jnp.float32
    )
    allowed = (query_clip[:, :, None] == key_clip[:, None, :])[:, None]
    return (jnp.where(allowed, raw_scores * SCORE_SCALE, MASKED), allowed)


def attend_forward(query_low, keys_low, values_low, query_clip, key_clip):
    key_count = keys_low.shape[1]
    key_width = min(512, key_count)
    stat_shape = (query_low.shape[0], query_low.shape[2], query_low.shape[1], 1)
    row_top = jnp.full(stat_shape, MASKED, jnp.float32)
    norm_sum = jnp.zeros(stat_shape, jnp.float32)
    for offset in range(0, key_count, key_width):
        scores, allowed = score_block(
            query_low,
            keys_low[:, offset : offset + key_width],
            query_clip,
            key_clip[:, offset : offset + key_width],
        )
        next_top = jnp.maximum(row_top, jnp.max(scores, axis=-1, keepdims=True))
        norm_sum = norm_sum * jnp.exp(row_top - next_top) + jnp.sum(
            jnp.where(allowed, jnp.exp(scores - next_top), 0.0), axis=-1, keepdims=True
        )
        row_top = next_top
    mixture = jnp.zeros(query_low.shape, jnp.float32)
    for offset in range(0, key_count, key_width):
        scores, allowed = score_block(
            query_low,
            keys_low[:, offset : offset + key_width],
            query_clip,
            key_clip[:, offset : offset + key_width],
        )
        weights = jnp.where(allowed, jnp.exp(scores - row_top) / norm_sum, 0.0)
        mixture = mixture + jnp.einsum(
            "rhqk,rkhd->rqhd",
            weights.astype(jnp.bfloat16),
            values_low[:, offset : offset + key_width],
            preferred_element_type=jnp.float32,
        )
    return (mixture, row_top, norm_sum)


def attend_backward(
    query_low, keys_low, values_low, query_clip, key_clip, row_top, norm_sum, grad_low
):
    key_count = keys_low.shape[1]
    key_width = min(512, key_count)
    diagonal = jnp.zeros_like(row_top)
    for offset in range(0, key_count, key_width):
        scores, allowed = score_block(
            query_low,
            keys_low[:, offset : offset + key_width],
            query_clip,
            key_clip[:, offset : offset + key_width],
        )
        weights = jnp.where(allowed, jnp.exp(scores - row_top) / norm_sum, 0.0)
        grad_weights = jnp.einsum(
            "rqhd,rkhd->rhqk",
            grad_low,
            values_low[:, offset : offset + key_width],
            preferred_element_type=jnp.float32,
        )
        diagonal = diagonal + jnp.sum(weights * grad_weights, axis=-1, keepdims=True)
    query_grad = jnp.zeros(query_low.shape, jnp.float32)
    key_parts = []
    value_parts = []
    for offset in range(0, key_count, key_width):
        key_block = keys_low[:, offset : offset + key_width]
        scores, allowed = score_block(
            query_low, key_block, query_clip, key_clip[:, offset : offset + key_width]
        )
        weights = jnp.where(allowed, jnp.exp(scores - row_top) / norm_sum, 0.0)
        grad_weights = jnp.einsum(
            "rqhd,rkhd->rhqk",
            grad_low,
            values_low[:, offset : offset + key_width],
            preferred_element_type=jnp.float32,
        )
        score_grad = (weights * (grad_weights - diagonal) * SCORE_SCALE).astype(jnp.bfloat16)
        query_grad = query_grad + jnp.einsum(
            "rhqk,rkhd->rqhd", score_grad, key_block, preferred_element_type=jnp.float32
        )
        key_parts.append(
            jnp.einsum("rhqk,rqhd->rkhd", score_grad, query_low, preferred_element_type=jnp.float32)
        )
        value_parts.append(
            jnp.einsum(
                "rhqk,rqhd->rkhd",
                weights.astype(jnp.bfloat16),
                grad_low,
                preferred_element_type=jnp.float32,
            )
        )
    return (query_grad, jnp.concatenate(key_parts, axis=1), jnp.concatenate(value_parts, axis=1))


def gated_back(hidden_grad, gate_part, upward):
    gate_sigmoid = jax.nn.sigmoid(gate_part)
    gate_grad = hidden_grad * upward * gate_sigmoid * (1.0 + gate_part * (1.0 - gate_sigmoid))
    upward_grad = hidden_grad * gate_part * gate_sigmoid
    return jnp.concatenate([gate_grad, upward_grad], axis=-1).astype(jnp.bfloat16)


def column_blocks(values, dp_count, seq_count):
    row_count, frame_count, width = values.shape
    turned = jnp.swapaxes(values, 1, 2)
    return turned.reshape(
        row_count, dp_count, seq_count, width // (dp_count * seq_count), frame_count
    )


def own_columns(values, dp_count, seq_count, seq_place):
    width = values.shape[-1]
    shaped = values.reshape(
        values.shape[:-1] + (dp_count, seq_count, width // (dp_count * seq_count))
    )
    return lax.dynamic_index_in_dim(shaped, seq_place, axis=values.ndim, keepdims=False)


def rows_grad(moved, gradients):
    part = jnp.einsum(
        "rabf,rfn->abn", moved[:, :, 0], gradients, preferred_element_type=jnp.float32
    )
    return part.reshape(part.shape[0] * part.shape[1], part.shape[2])


def on_device(
    latents,
    context,
    clip_bounds,
    timesteps,
    self_inward,
    self_outward,
    cross_query,
    cross_keyval,
    cross_return,
    time_weight,
    expand_weight,
    shrink_weight,
    gain_attend,
    gain_cross,
    gain_feed,
    cotangent,
):
    row_count = latents.shape[0]
    frame_count = latents.shape[1]
    dp_count = lax.axis_size("dp")
    seq_count = lax.axis_size("seq")
    seq_place = lax.axis_index("seq")
    row_length = frame_count * seq_count
    text_count = context.shape[1]
    frames = seq_place * frame_count + jnp.arange(frame_count, dtype=jnp.int32)
    all_frames = jnp.arange(row_length, dtype=jnp.int32)
    second_start = clip_bounds[:, 0:1]
    third_start = clip_bounds[:, 1:2]
    clip_ids = (frames[None, :] >= second_start).astype(jnp.int32) + (
        frames[None, :] >= third_start
    ).astype(jnp.int32)
    frame_clips = (all_frames[None, :] >= second_start).astype(jnp.int32) + (
        all_frames[None, :] >= third_start
    ).astype(jnp.int32)
    token_clips = jnp.arange(CLIPS, dtype=jnp.int32)[None, :]
    key_clips = jnp.concatenate([frame_clips, token_clips], axis=1)
    clip_starts = jnp.where(clip_ids == 0, 0, jnp.where(clip_ids == 1, second_start, third_start))
    positions = (frames[None, :] - clip_starts + 1).astype(jnp.float32)
    cosine_table, sine_table = rotary_tables(positions)
    text_clips = (jnp.arange(text_count, dtype=jnp.int32) // CTX_LEN)[None, :]
    feats_low = time_features(timesteps).astype(jnp.bfloat16)
    (
        inward_full,
        outward_full,
        query_full,
        keyval_full,
        return_full,
        time_full,
        expand_full,
        shrink_full,
        attend_gain,
        cross_gain,
        feed_gain,
    ) = (
        lax.all_gather(self_inward, ("dp", "seq"), axis=0, tiled=True),
        lax.all_gather(self_outward, ("dp", "seq"), axis=0, tiled=True),
        lax.all_gather(cross_query, ("dp", "seq"), axis=0, tiled=True),
        lax.all_gather(cross_keyval, ("dp", "seq"), axis=0, tiled=True),
        lax.all_gather(cross_return, ("dp", "seq"), axis=0, tiled=True),
        lax.all_gather(time_weight, ("dp", "seq"), axis=0, tiled=True),
        lax.all_gather(expand_weight, ("dp", "seq"), axis=0, tiled=True),
        lax.all_gather(shrink_weight, ("dp", "seq"), axis=0, tiled=True),
        lax.all_gather(gain_attend, ("dp", "seq"), axis=0, tiled=True),
        lax.all_gather(gain_cross, ("dp", "seq"), axis=0, tiled=True),
        lax.all_gather(gain_feed, ("dp", "seq"), axis=0, tiled=True),
    )
    attend_gain_f = attend_gain.astype(jnp.float32)
    token = dense(feats_low, time_full)
    token_norm, token_inverse = norm_forward(token)
    token_low = (token_norm * attend_gain_f).astype(jnp.bfloat16)
    token_kv = (
        dense(token_low, inward_full[:, D:])
        .astype(jnp.bfloat16)
        .reshape(row_count, CLIPS, 2, HEADS, HEAD_DIM)
    )
    conditioned = latents.astype(jnp.float32)
    norm_one, inverse_one = norm_forward(conditioned)
    normed_one = (norm_one * attend_gain_f).astype(jnp.bfloat16)
    projected = dense(normed_one, inward_full).reshape(row_count, frame_count, 3, HEADS, HEAD_DIM)
    queries_low = rotate(projected[:, :, 0], cosine_table, sine_table).astype(jnp.bfloat16)
    keys_low = rotate(projected[:, :, 1], cosine_table, sine_table).astype(jnp.bfloat16)
    values_low = projected[:, :, 2].astype(jnp.bfloat16)
    keys_all, values_all = (
        lax.all_gather(keys_low.reshape(row_count, frame_count, D), "seq", axis=1, tiled=True),
        lax.all_gather(values_low.reshape(row_count, frame_count, D), "seq", axis=1, tiled=True),
    )
    keys_heads = jnp.concatenate(
        [keys_all.reshape(row_count, row_length, HEADS, HEAD_DIM), token_kv[:, :, 0]], axis=1
    )
    values_heads = jnp.concatenate(
        [values_all.reshape(row_count, row_length, HEADS, HEAD_DIM), token_kv[:, :, 1]], axis=1
    )
    attended, self_top, self_sum = attend_forward(
        queries_low, keys_heads, values_heads, clip_ids, key_clips
    )
    attended_low = attended.reshape(row_count, frame_count, D).astype(jnp.bfloat16)
    after_self = conditioned + dense(attended_low, outward_full)
    norm_two, inverse_two = norm_forward(after_self)
    normed_two = (norm_two * cross_gain.astype(jnp.float32)).astype(jnp.bfloat16)
    cross_heads = (
        dense(normed_two, query_full)
        .astype(jnp.bfloat16)
        .reshape(row_count, frame_count, HEADS, HEAD_DIM)
    )
    keyval = (
        jnp.einsum("rkc,cn->rkn", context, keyval_full, preferred_element_type=jnp.float32)
        .astype(jnp.bfloat16)
        .reshape(row_count, text_count, 2, HEADS, HEAD_DIM)
    )
    cross_keys = keyval[:, :, 0]
    cross_values = keyval[:, :, 1]
    crossed, cross_top, cross_sum = attend_forward(
        cross_heads, cross_keys, cross_values, clip_ids, text_clips
    )
    crossed_low = crossed.reshape(row_count, frame_count, D).astype(jnp.bfloat16)
    after_cross = after_self + dense(crossed_low, return_full)
    norm_three, inverse_three = norm_forward(after_cross)
    normed_three = (norm_three * feed_gain.astype(jnp.float32)).astype(jnp.bfloat16)
    gate_up = dense(normed_three, expand_full)
    gate_part = gate_up[..., :FF]
    upward = gate_up[..., FF:]
    hidden_low = (jax.nn.silu(gate_part) * upward).astype(jnp.bfloat16)
    block_output = (after_cross + dense(hidden_low, shrink_full)).astype(jnp.bfloat16)
    (
        inward_back,
        outward_back,
        query_back,
        return_back,
        expand_back,
        shrink_back,
        attend_back,
        cross_back,
        feed_back,
    ) = (
        lax.all_gather(self_inward, ("dp", "seq"), axis=0, tiled=True),
        lax.all_gather(self_outward, ("dp", "seq"), axis=0, tiled=True),
        lax.all_gather(cross_query, ("dp", "seq"), axis=0, tiled=True),
        lax.all_gather(cross_return, ("dp", "seq"), axis=0, tiled=True),
        lax.all_gather(expand_weight, ("dp", "seq"), axis=0, tiled=True),
        lax.all_gather(shrink_weight, ("dp", "seq"), axis=0, tiled=True),
        lax.all_gather(gain_attend, ("dp", "seq"), axis=0, tiled=True),
        lax.all_gather(gain_cross, ("dp", "seq"), axis=0, tiled=True),
        lax.all_gather(gain_feed, ("dp", "seq"), axis=0, tiled=True),
    )
    attend_back_f = attend_back.astype(jnp.float32)
    upstream = cotangent.astype(jnp.float32)
    hidden_grad = dense_back(cotangent, shrink_back)
    expand_low = gated_back(hidden_grad, gate_part, upward)
    feed_norm_grad = dense_back(expand_low, expand_back)
    feed_term, feed_gain_part = norm_backward(
        feed_norm_grad, norm_three, inverse_three, feed_back.astype(jnp.float32)
    )
    after_cross_grad = upstream + feed_term
    return_low = after_cross_grad.astype(jnp.bfloat16)
    crossed_grad = (
        dense_back(return_low, return_back)
        .astype(jnp.bfloat16)
        .reshape(row_count, frame_count, HEADS, HEAD_DIM)
    )
    cross_query_grad, cross_key_grad, cross_value_grad = attend_backward(
        cross_heads,
        cross_keys,
        cross_values,
        clip_ids,
        text_clips,
        cross_top,
        cross_sum,
        crossed_grad,
    )
    cross_query_low = cross_query_grad.reshape(row_count, frame_count, D).astype(jnp.bfloat16)
    keyval_grad_rows = jnp.stack([cross_key_grad, cross_value_grad], axis=2).reshape(
        row_count, text_count, 2 * D
    )
    cross_norm_grad = dense_back(cross_query_low, query_back)
    cross_term, cross_gain_part = norm_backward(
        cross_norm_grad, norm_two, inverse_two, cross_back.astype(jnp.float32)
    )
    after_self_grad = after_cross_grad + cross_term
    outward_low = after_self_grad.astype(jnp.bfloat16)
    attended_grad = (
        dense_back(outward_low, outward_back)
        .astype(jnp.bfloat16)
        .reshape(row_count, frame_count, HEADS, HEAD_DIM)
    )
    self_query_grad, self_key_grad, self_value_grad = attend_backward(
        queries_low,
        keys_heads,
        values_heads,
        clip_ids,
        key_clips,
        self_top,
        self_sum,
        attended_grad,
    )
    key_own, value_own = (
        lax.psum_scatter(
            self_key_grad[:, :row_length].reshape(row_count, row_length, D).astype(jnp.bfloat16),
            "seq",
            scatter_dimension=1,
            tiled=True,
        ).astype(jnp.float32),
        lax.psum_scatter(
            self_value_grad[:, :row_length].reshape(row_count, row_length, D).astype(jnp.bfloat16),
            "seq",
            scatter_dimension=1,
            tiled=True,
        ).astype(jnp.float32),
    )
    token_kv_grad = jnp.stack(
        [self_key_grad[:, row_length:], self_value_grad[:, row_length:]], axis=2
    ).reshape(row_count, CLIPS, 2 * D)
    query_turned = rotate(self_query_grad, cosine_table, -sine_table)
    key_turned = rotate(
        key_own.reshape(row_count, frame_count, HEADS, HEAD_DIM), cosine_table, -sine_table
    )
    value_heads_grad = value_own.reshape(row_count, frame_count, HEADS, HEAD_DIM)
    inward_low = (
        jnp.stack([query_turned, key_turned, value_heads_grad], axis=2)
        .reshape(row_count, frame_count, 3 * D)
        .astype(jnp.bfloat16)
    )
    attend_norm_grad = dense_back(inward_low, inward_back)
    attend_term, attend_gain_part = norm_backward(
        attend_norm_grad, norm_one, inverse_one, attend_back_f
    )
    latents_grad = after_self_grad + attend_term
    moved_inputs = (
        lax.all_to_all(
            column_blocks(hidden_low, dp_count, seq_count),
            "seq",
            split_axis=2,
            concat_axis=4,
            tiled=True,
        ),
        lax.all_to_all(
            column_blocks(normed_three, dp_count, seq_count),
            "seq",
            split_axis=2,
            concat_axis=4,
            tiled=True,
        ),
        lax.all_to_all(
            column_blocks(crossed_low, dp_count, seq_count),
            "seq",
            split_axis=2,
            concat_axis=4,
            tiled=True,
        ),
        lax.all_to_all(
            column_blocks(normed_two, dp_count, seq_count),
            "seq",
            split_axis=2,
            concat_axis=4,
            tiled=True,
        ),
        lax.all_to_all(
            column_blocks(attended_low, dp_count, seq_count),
            "seq",
            split_axis=2,
            concat_axis=4,
            tiled=True,
        ),
        lax.all_to_all(
            column_blocks(normed_one, dp_count, seq_count),
            "seq",
            split_axis=2,
            concat_axis=4,
            tiled=True,
        ),
    )
    moved_grads = (
        lax.all_gather(cotangent, "seq", axis=1, tiled=True),
        lax.all_gather(expand_low, "seq", axis=1, tiled=True),
        lax.all_gather(return_low, "seq", axis=1, tiled=True),
        lax.all_gather(cross_query_low, "seq", axis=1, tiled=True),
        lax.all_gather(outward_low, "seq", axis=1, tiled=True),
        lax.all_gather(inward_low, "seq", axis=1, tiled=True),
    )
    gain_parts = jnp.stack([attend_gain_part, cross_gain_part, feed_gain_part], axis=0)
    small_parts = (
        lax.all_gather(
            keyval_grad_rows[None].astype(jnp.bfloat16), "seq", axis=0, tiled=True
        ).astype(jnp.float32),
        lax.all_gather(token_kv_grad[None].astype(jnp.bfloat16), "seq", axis=0, tiled=True).astype(
            jnp.float32
        ),
        lax.all_gather(gain_parts[None].astype(jnp.bfloat16), "seq", axis=0, tiled=True).astype(
            jnp.float32
        ),
    )
    keyval_total = jnp.sum(small_parts[0], axis=0)
    token_total = jnp.sum(small_parts[1], axis=0)
    gain_total = jnp.sum(small_parts[2], axis=0)
    token_norm_grad = jnp.einsum(
        "rcn,dn->rcd",
        token_total,
        inward_back[:, D:].astype(jnp.float32),
        precision=PRECISE,
        preferred_element_type=jnp.float32,
    )
    token_term, token_gain_grad = norm_backward(
        token_norm_grad, token_norm, token_inverse, attend_back_f
    )
    gain_total = gain_total + jnp.stack(
        [token_gain_grad, jnp.zeros_like(token_gain_grad), jnp.zeros_like(token_gain_grad)], axis=0
    )
    gain_rows = own_columns(gain_total, dp_count, seq_count, seq_place).reshape(3, -1)
    shrink_rows = rows_grad(moved_inputs[0], moved_grads[0])
    expand_rows = rows_grad(moved_inputs[1], moved_grads[1])
    return_rows = rows_grad(moved_inputs[2], moved_grads[2])
    query_rows = rows_grad(moved_inputs[3], moved_grads[3])
    outward_rows = rows_grad(moved_inputs[4], moved_grads[4])
    inward_rows = rows_grad(moved_inputs[5], moved_grads[5])
    token_cols = own_columns(token_low.astype(jnp.float32), dp_count, seq_count, seq_place)
    token_rows = jnp.einsum(
        "rcab,rcn->abn",
        token_cols,
        token_total,
        precision=PRECISE,
        preferred_element_type=jnp.float32,
    )
    token_rows = token_rows.reshape(token_rows.shape[0] * token_rows.shape[1], 2 * D)
    inward_rows = jnp.concatenate([inward_rows[:, :D], inward_rows[:, D:] + token_rows], axis=1)
    context_cols = own_columns(context.astype(jnp.float32), dp_count, seq_count, seq_place)
    keyval_rows = jnp.einsum(
        "rkab,rkn->abn",
        context_cols,
        keyval_total,
        precision=PRECISE,
        preferred_element_type=jnp.float32,
    )
    keyval_rows = keyval_rows.reshape(keyval_rows.shape[0] * keyval_rows.shape[1], 2 * D)
    feat_cols = own_columns(feats_low.astype(jnp.float32), dp_count, seq_count, seq_place)
    time_rows = jnp.einsum(
        "rcab,rcn->abn",
        feat_cols,
        token_term,
        precision=PRECISE,
        preferred_element_type=jnp.float32,
    )
    time_rows = time_rows.reshape(time_rows.shape[0] * time_rows.shape[1], D)
    owned = (
        lax.psum_scatter(
            inward_rows.astype(jnp.bfloat16), "dp", scatter_dimension=0, tiled=True
        ).astype(jnp.float32),
        lax.psum_scatter(
            outward_rows.astype(jnp.bfloat16), "dp", scatter_dimension=0, tiled=True
        ).astype(jnp.float32),
        lax.psum_scatter(
            query_rows.astype(jnp.bfloat16), "dp", scatter_dimension=0, tiled=True
        ).astype(jnp.float32),
        lax.psum_scatter(
            keyval_rows.astype(jnp.bfloat16), "dp", scatter_dimension=0, tiled=True
        ).astype(jnp.float32),
        lax.psum_scatter(
            return_rows.astype(jnp.bfloat16), "dp", scatter_dimension=0, tiled=True
        ).astype(jnp.float32),
        lax.psum_scatter(
            time_rows.astype(jnp.bfloat16), "dp", scatter_dimension=0, tiled=True
        ).astype(jnp.float32),
        lax.psum_scatter(
            expand_rows.astype(jnp.bfloat16), "dp", scatter_dimension=0, tiled=True
        ).astype(jnp.float32),
        lax.psum_scatter(
            shrink_rows.astype(jnp.bfloat16), "dp", scatter_dimension=0, tiled=True
        ).astype(jnp.float32),
        lax.psum_scatter(
            gain_rows[0].astype(jnp.bfloat16), "dp", scatter_dimension=0, tiled=True
        ).astype(jnp.float32),
        lax.psum_scatter(
            gain_rows[1].astype(jnp.bfloat16), "dp", scatter_dimension=0, tiled=True
        ).astype(jnp.float32),
        lax.psum_scatter(
            gain_rows[2].astype(jnp.bfloat16), "dp", scatter_dimension=0, tiled=True
        ).astype(jnp.float32),
    )
    return (
        block_output,
        latents_grad,
        owned[0],
        owned[1],
        owned[2],
        owned[3],
        owned[4],
        owned[5],
        owned[6],
        owned[7],
        owned[8],
        owned[9],
        owned[10],
    )


def solution(mesh):
    return jax.shard_map(
        on_device,
        mesh=mesh,
        in_specs=(
            P("dp", "seq", None),
            P("dp", None, None),
            P("dp", None),
            P("dp", None),
            P(("dp", "seq"), None),
            P(("dp", "seq"), None),
            P(("dp", "seq"), None),
            P(("dp", "seq"), None),
            P(("dp", "seq"), None),
            P(("dp", "seq"), None),
            P(("dp", "seq"), None),
            P(("dp", "seq"), None),
            P(("dp", "seq")),
            P(("dp", "seq")),
            P(("dp", "seq")),
            P("dp", "seq", None),
        ),
        out_specs=(
            P("dp", "seq", None),
            P("dp", "seq", None),
            P(("dp", "seq"), None),
            P(("dp", "seq"), None),
            P(("dp", "seq"), None),
            P(("dp", "seq"), None),
            P(("dp", "seq"), None),
            P(("dp", "seq"), None),
            P(("dp", "seq"), None),
            P(("dp", "seq"), None),
            P(("dp", "seq")),
            P(("dp", "seq")),
            P(("dp", "seq")),
        ),
        check_vma=False,
    )
```

profile of v0, /device:TPU:0, one launch (start us, length us, event | category | flops | bytes accessed | tf_op | source)
XLA Modules:
  0.0 2683.6 jit_solution(15726724103666712043)
XLA Ops:
  11.3 42.8 %all-reduce.7 = (bf16[1536]{0:T(1024)(128)(2,1)S(1)}, bf16[1536]{0:T(1024)(128)(2,1)S(1)}, bf16[1536]{0:T(1024)(128)(2,1)S(1)}) all-reduce(bf16[1536]{0:T(1024)(128)(2,1)S(1)} %dynamic-update-slice, bf16[1536]{0:T(1024)(128)(2,1)S(1)} %dynamic-update-slice.1, ...), channel_id=1, replica_groups=mesh['dp'=8,'seq'=4] {'dp','seq'}, use_global_device_ids=true, to_apply=%add.1 | all-reduce | flops 4608 | bytes 18432
  60.4 57.3 %all-gather.17.cloned.1.call-done = bf16[1536,4608]{1,0:T(8,128)(2,1)} async-done(((bf16[48,4608]{1,0:T(8,128)(2,1)}), bf16[1536,4608]{1,0:T(8,128)(2,1)}) %all-gather.17.cloned.1.call-update) | async-done | bytes 14155792 | tf_op jit(solution)/shard_map/all_gather | solution.py:264
  158.9 97.4 %all_gather.79 = bf16[256,1536]{1,0:T(8,128)(2,1)S(1)} all-gather(bf16[8,1536]{1,0:T(8,128)(2,1)S(1)} %copy-done.56), channel_id=1, replica_groups=mesh['dp'=8,'seq'=4] {'dp','seq'}, dimensions={0}, use_global_device_ids=true | all-gather | bytes 811008 | tf_op jit(solution)/shard_map/all_gather | solution.py:269
  333.9 50.4 %all-gather.23.cloned.1.call-done = bf16[1536,1536]{1,0:T(8,128)(2,1)} async-done(((bf16[48,1536]{1,0:T(8,128)(2,1)}), bf16[1536,1536]{1,0:T(8,128)(2,1)}) %all-gather.23.cloned.1.call-update) | async-done | bytes 4718608 | tf_op jit(solution)/shard_map/all_gather | solution.py:265
  388.5 60.9 %all-gather.27.cloned.1.call-done = bf16[1536,1536]{1,0:T(8,128)(2,1)} async-done(((bf16[48,1536]{1,0:T(8,128)(2,1)}), bf16[1536,1536]{1,0:T(8,128)(2,1)}) %all-gather.27.cloned.1.call-update) | async-done | bytes 4718608 | tf_op jit(solution)/shard_map/all_gather | solution.py:266
  465.5 49.2 %all-gather.29.cloned.1.call-done = bf16[1536,1536]{1,0:T(8,128)(2,1)} async-done(((bf16[48,1536]{1,0:T(8,128)(2,1)}), bf16[1536,1536]{1,0:T(8,128)(2,1)}) %all-gather.29.cloned.1.call-update) | async-done | bytes 4718608 | tf_op jit(solution)/shard_map/all_gather | solution.py:268
  520.2 211.0 %all-gather.31.cloned.1.call-done = bf16[1536,12288]{1,0:T(8,128)(2,1)} async-done(((bf16[48,12288]{1,0:T(8,128)(2,1)}), bf16[1536,12288]{1,0:T(8,128)(2,1)}) %all-gather.31.cloned.1.call-update) | async-done | bytes 37748752 | tf_op jit(solution)/shard_map/all_gather | solution.py:270
  751.5 105.4 %all-gather.33.cloned.1.call-done = bf16[6144,1536]{1,0:T(8,128)(2,1)} async-done(((bf16[192,1536]{1,0:T(8,128)(2,1)}), bf16[6144,1536]{1,0:T(8,128)(2,1)}) %all-gather.33.cloned.1.call-update) | async-done | bytes 18874384 | tf_op jit(solution)/shard_map/all_gather | solution.py:271
  912.5 44.8 %fusion.123 = bf16[24,64,256]{2,1,0:T(8,128)(2,1)S(1)} fusion(f32[24,256,384]{2,1,0:T(8,128)} %fusion.135, bf16[1,384,2,24,64]{1,4,3,2,0:T(8,128)(2,1)} %bitcast.413, f32[24,256,384]{2,1,0:T(8,128)} %copy-done.5, f32[24,256]{1,0:T(8,128)} %copy-done.57, f32[24,256]{1,0:T(8,128)} %copy-done.54, pred[256,384]{1,0:T(8,128)(4,1)S(1)} %broadcast_compare_fusion.2), kind=kOutput, calls=%fused_computation.151 | convolution fusion | flops 337779072 | bytes 40009728 | tf_op jit(solution)/shard_map/rhqk,rkhd->rqhd/dot_general | solution.py:162
  1042.1 45.5 %fusion.114 = bf16[1,384,1,24,64]{1,4,3,2,0:T(8,128)(2,1)} fusion(bf16[256,24,64]{0,2,1:T(8,128)(2,1)S(1)} %bitcast.429, f32[24,256,384]{2,1,0:T(8,128)} %fusion.135, f32[24,256,384]{2,1,0:T(8,128)} %copy-done.5, f32[24,256]{1,0:T(8,128)S(1)} %copy-done.58, f32[24,256]{1,0:T(8,128)S(1)} %copy-done.55, pred[256,384]{1,0:T(8,128)(4,1)S(1)} %broadcast_compare_fusion.2), kind=kOutput, calls=%fused_computation.148 | convolution fusion | flops 337975680 | bytes 20987904 | tf_op jit(solution)/shard_map/rhqk,rqhd->rkhd/dot_general | solution.py:166
  1160.1 40.0 %all-to-all-done.3 = bf16[1,8,4,48,256]{4,3,1,0,2:T(8,128)(2,1)} async-done(((bf16[1,8,4,48,256]{4,3,1,0,2:T(8,128)(2,1)}), bf16[1,8,4,48,256]{4,3,1,0,2:T(8,128)(2,1)}, u32[]{:S(2)}, u32[]{:S(2)}) %all-to-all-start.3) | async-done | bytes 786464 | tf_op jit(solution)/shard_map/all_to_all | solution.py:451
  1244.4 44.2 %all_gather.89 = bf16[4,1,3,3072]{3,2,1,0:T(4,128)(2,1)S(1)} all-gather(bf16[1,1,3,3072]{3,2,1,0:T(4,128)(2,1)S(1)} %convert_element_type.501), channel_id=1, replica_groups=mesh['dp'=8,'seq'=4] {'seq'}, dimensions={0}, use_global_device_ids=true | all-gather | bytes 92160 | tf_op jit(solution)/shard_map/all_gather | solution.py:493
  1350.2 82.6 %all-gather.37.cloned.1.call-done = bf16[1,1024,1536]{2,1,0:T(8,128)(2,1)} async-done(((bf16[1,256,1536]{2,1,0:T(8,128)(2,1)}), bf16[1,1024,1536]{2,1,0:T(8,128)(2,1)}) %all-gather.37.cloned.1.call-update) | async-done | bytes 3145744 | tf_op jit(solution)/shard_map/all_gather | solution.py:485
  1440.7 56.1 %all-gather.47.cloned.1.call-done = bf16[1,1024,1536]{2,1,0:T(8,128)(2,1)} async-done(((bf16[1,256,1536]{2,1,0:T(8,128)(2,1)}), bf16[1,1024,1536]{2,1,0:T(8,128)(2,1)}) %all-gather.47.cloned.1.call-update) | async-done | bytes 3145744 | tf_op jit(solution)/shard_map/all_gather | solution.py:481
  1522.8 39.3 %all-to-all-done = bf16[1,8,4,48,256]{4,3,1,0,2:T(8,128)(2,1)S(1)} async-done(((bf16[1,8,4,48,256]{4,3,1,0,2:T(8,128)(2,1)}), bf16[1,8,4,48,256]{4,3,1,0,2:T(8,128)(2,1)S(1)}, u32[]{:S(2)}, u32[]{:S(2)}) %all-to-all-start) | async-done | bytes 786464 | tf_op jit(solution)/shard_map/all_to_all | solution.py:472
  1562.9 117.5 %all-gather.41.cloned.1.call-done = bf16[4,1,384,3072]{3,2,1,0:T(8,128)(2,1)} async-done(((bf16[1,1,384,3072]{3,2,1,0:T(8,128)(2,1)}), bf16[4,1,384,3072]{3,2,1,0:T(8,128)(2,1)}) %all-gather.41.cloned.1.call-update) | async-done | bytes 9437200 | tf_op jit(solution)/shard_map/all_gather | solution.py:490
  1690.2 156.7 %all-gather.35.cloned.1.call-done = bf16[1,1024,4608]{1,2,0:T(8,128)(2,1)} async-done(((bf16[1,256,4608]{1,2,0:T(8,128)(2,1)}), bf16[1,1024,4608]{1,2,0:T(8,128)(2,1)}) %all-gather.35.cloned.1.call-update) | async-done | bytes 9437200 | tf_op jit(solution)/shard_map/all_gather | solution.py:486
  1858.7 48.5 %all_to_all.90 = bf16[1,8,4,48,256]{4,3,1,0,2:T(8,128)(2,1)S(1)} all-to-all(bf16[1,8,4,48,256]{4,3,1,0,2:T(8,128)(2,1)S(1)} %copy.105), channel_id=1, replica_groups=mesh['dp'=8,'seq'=4] {'seq'}, dimensions={2} | all-to-all | bytes 1572864 | tf_op jit(solution)/shard_map/all_to_all | solution.py:444
  1907.9 379.3 %all-gather.45.cloned.1.call-done = bf16[1,1024,12288]{2,1,0:T(8,128)(2,1)} async-done(((bf16[1,256,12288]{2,1,0:T(8,128)(2,1)}), bf16[1,1024,12288]{2,1,0:T(8,128)(2,1)}) %all-gather.45.cloned.1.call-update) | async-done | bytes 25165840 | tf_op jit(solution)/shard_map/all_gather | solution.py:482
  2365.4 38.4 %reduce-scatter.23.cloned.1.call-done = bf16[48,1536]{1,0:T(8,128)(2,1)} async-done(((bf16[384,1536]{1,0:T(8,128)(2,1)}), bf16[48,1536]{1,0:T(8,128)(2,1)}) %reduce-scatter.23.cloned.1.call-update) | async-done | bytes 147472 | tf_op jit(solution)/shard_map/reduce_scatter | solution.py:564
  2405.5 39.3 %reduce-scatter.17.cloned.1.call-done = bf16[48,1536]{1,0:T(8,128)(2,1)} async-done(((bf16[384,1536]{1,0:T(8,128)(2,1)}), bf16[48,1536]{1,0:T(8,128)(2,1)}) %reduce-scatter.17.cloned.1.call-update) | async-done | bytes 147472 | tf_op jit(solution)/shard_map/reduce_scatter | solution.py:555
  2446.4 55.7 %reduce-scatter.29.cloned.1.call-done = bf16[192,1536]{1,0:T(8,128)(2,1)} async-done(((bf16[1536,1536]{1,0:T(8,128)(2,1)}), bf16[192,1536]{1,0:T(8,128)(2,1)}) %reduce-scatter.29.cloned.1.call-update) | async-done | bytes 589840 | tf_op jit(solution)/shard_map/reduce_scatter | solution.py:573
  2544.0 49.9 %reduce-scatter.15.cloned.1.call-done = bf16[48,4608]{1,0:T(8,128)(2,1)} async-done(((bf16[384,4608]{1,0:T(8,128)(2,1)}), bf16[48,4608]{1,0:T(8,128)(2,1)}) %reduce-scatter.15.cloned.1.call-update) | async-done | bytes 442384 | tf_op jit(solution)/shard_map/reduce_scatter | solution.py:552
  2595.9 77.9 %reduce-scatter.27.cloned.1.call-done = bf16[48,12288]{1,0:T(8,128)(2,1)} async-done(((bf16[384,12288]{1,0:T(8,128)(2,1)}), bf16[48,12288]{1,0:T(8,128)(2,1)}) %reduce-scatter.27.cloned.1.call-update) | async-done | bytes 1179664 | tf_op jit(solution)/shard_map/reduce_scatter | solution.py:570
  (432 shorter events, 676.9 us)
Async XLA Ops:
  7.9 249.4 %all-gather.25.cloned.1.call-start = ((), (), s32[]{:S(2)}) async-start(), calls=%async_computation.20 | async-start | bytes 4866048 | tf_op jit(solution)/shard_map/all_gather | solution.py:267
  8.7 264.3 %all-gather.21.cloned.1.call-start = ((), (), s32[]{:S(2)}) async-start(), calls=%async_computation.18 | async-start | bytes 3932160 | tf_op jit(solution)/shard_map/all_gather | solution.py:293
  148.5 171.4 %all-gather.19.cloned.1.call-start = ((), (), s32[]{:S(2)}) async-start(), calls=%async_computation.17 | async-start | bytes 3932160 | tf_op jit(solution)/shard_map/all_gather | solution.py:294
  151.0 233.3 %all-gather.23.cloned.1.call-start = ((), (), s32[]{:S(2)}) async-start(), calls=%async_computation.19 | async-start | bytes 4866048 | tf_op jit(solution)/shard_map/all_gather | solution.py:265
  151.6 297.8 %all-gather.27.cloned.1.call-start = ((), (), s32[]{:S(2)}) async-start(), calls=%async_computation.21 | async-start | bytes 4866048 | tf_op jit(solution)/shard_map/all_gather | solution.py:266
  152.1 362.5 %all-gather.29.cloned.1.call-start = ((), (), s32[]{:S(2)}) async-start(), calls=%async_computation.22 | async-start | bytes 4866048 | tf_op jit(solution)/shard_map/all_gather | solution.py:268
  152.9 578.3 %all-gather.31.cloned.1.call-start = ((), (), s32[]{:S(2)}) async-start(), calls=%async_computation.23 | async-start | bytes 38928384 | tf_op jit(solution)/shard_map/all_gather | solution.py:270
  153.6 703.3 %all-gather.33.cloned.1.call-start = ((), (), s32[]{:S(2)}) async-start(), calls=%async_computation.24 | async-start | bytes 19464192 | tf_op jit(solution)/shard_map/all_gather | solution.py:271
  154.4 954.4 %reduce-scatter.11.cloned.1.call-start = ((), (), s32[]{:S(2)}) async-start(), calls=%async_computation.25 | async-start | bytes 3932160 | tf_op jit(solution)/shard_map/reduce_scatter | solution.py:405
  1039.5 267.8 %all-gather.39.cloned.1.call-start = ((), (), s32[]{:S(2)}) async-start(), calls=%async_computation.31 | async-start | bytes 3932160 | tf_op jit(solution)/shard_map/all_gather | solution.py:484
  1040.1 302.7 %all-gather.43.cloned.1.call-start = ((), (), s32[]{:S(2)}) async-start(), calls=%async_computation.35 | async-start | bytes 3932160 | tf_op jit(solution)/shard_map/all_gather | solution.py:483
  1040.9 392.0 %all-gather.37.cloned.1.call-start = ((), (), s32[]{:S(2)}) async-start(), calls=%async_computation.29 | async-start | bytes 3932160 | tf_op jit(solution)/shard_map/all_gather | solution.py:485
  1041.4 455.3 %all-gather.47.cloned.1.call-start = ((), (), s32[]{:S(2)}) async-start(), calls=%async_computation.40 | async-start | bytes 3932160 | tf_op jit(solution)/shard_map/all_gather | solution.py:481
  1042.0 638.4 %all-gather.41.cloned.1.call-start = ((), (), s32[]{:S(2)}) async-start(), calls=%async_computation.33 | async-start | bytes 11796480 | tf_op jit(solution)/shard_map/all_gather | solution.py:490
  1100.2 746.7 %all-gather.35.cloned.1.call-start = ((), (), s32[]{:S(2)}) async-start(), calls=%async_computation.27 | async-start | bytes 11796480 | tf_op jit(solution)/shard_map/all_gather | solution.py:486
  1146.4 1140.8 %all-gather.45.cloned.1.call-start = ((), (), s32[]{:S(2)}) async-start(), calls=%async_computation.38 | async-start | bytes 31457280 | tf_op jit(solution)/shard_map/all_gather | solution.py:482
  1303.3 1020.2 %reduce-scatter.25.cloned.1.call-start = ((), (), s32[]{:S(2)}) async-start(), calls=%async_computation.37 | async-start | bytes 221184 | tf_op jit(solution)/shard_map/reduce_scatter | solution.py:567
  1304.4 1059.3 %reduce-scatter.19.cloned.1.call-start = ((), (), s32[]{:S(2)}) async-start(), calls=%async_computation.32 | async-start | bytes 1327104 | tf_op jit(solution)/shard_map/reduce_scatter | solution.py:558
  1311.9 1091.9 %reduce-scatter.23.cloned.1.call-start = ((), (), s32[]{:S(2)}) async-start(), calls=%async_computation.36 | async-start | bytes 1327104 | tf_op jit(solution)/shard_map/reduce_scatter | solution.py:564
  1347.4 1097.4 %reduce-scatter.17.cloned.1.call-start = ((), (), s32[]{:S(2)}) async-start(), calls=%async_computation.30 | async-start | bytes 1327104 | tf_op jit(solution)/shard_map/reduce_scatter | solution.py:555
  1437.4 1064.7 %reduce-scatter.29.cloned.1.call-start = ((), (), s32[]{:S(2)}) async-start(), calls=%async_computation.41 | async-start | bytes 5308416 | tf_op jit(solution)/shard_map/reduce_scatter | solution.py:573
  1521.9 1020.4 %reduce-scatter.21.cloned.1.call-start = ((), (), s32[]{:S(2)}) async-start(), calls=%async_computation.34 | async-start | bytes 1327104 | tf_op jit(solution)/shard_map/reduce_scatter | solution.py:561
  1690.1 903.8 %reduce-scatter.15.cloned.1.call-start = ((), (), s32[]{:S(2)}) async-start(), calls=%async_computation.28 | async-start | bytes 3981312 | tf_op jit(solution)/shard_map/reduce_scatter | solution.py:552
  1858.3 815.5 %reduce-scatter.27.cloned.1.call-start = ((), (), s32[]{:S(2)}) async-start(), calls=%async_computation.39 | async-start | bytes 10616832 | tf_op jit(solution)/shard_map/reduce_scatter | solution.py:570
  (90 other events, 2997.1 us)
Sparse Core Ops, SparseCore 0:
  10.8 106.8 all-gather.16
  120.5 63.7 all-gather.24
  186.4 69.2 all-gather.20
  257.7 62.1 all-gather.18
  322.5 61.7 all-gather.22
  387.0 62.3 all-gather.26
  452.2 62.4 all-gather.28
  517.4 213.7 all-gather.30
  734.0 122.8 all-gather.32
  1022.5 58.4 reduce-scatter.10
  1083.3 60.2 reduce-scatter.12
  1145.0 96.7 all-gather.38
  1243.4 99.3 all-gather.42
  1344.2 88.6 all-gather.36
  1434.3 62.4 all-gather.46
  1498.2 182.1 all-gather.40
  1682.4 164.4 all-gather.34
  1848.3 438.8 all-gather.44
  2326.9 36.7 reduce-scatter.18
  2408.0 36.7 reduce-scatter.16
  2448.2 53.8 reduce-scatter.28
  2505.5 36.7 reduce-scatter.20
  2545.8 48.0 reduce-scatter.14
  2597.3 76.4 reduce-scatter.26
  (2 shorter events, 69.3 us)
where the time goes:
time: 2690 us; the launch traced here: 2680 us
  waiting for transfers between devices  1840 us (68%)
  matrix products  370 us (14%)
  blocking collectives  258 us (10%)
  other arithmetic  99.5 us (4%)
  local copies, waits for them, and re-layouts  75.3 us (3%)
    all_gather x1, waiting for transfers between devices, on_device(): lax.all_gather(expand_low, 'seq', axis=1, tiled=True)  379 us
    all_gather x1, waiting for transfers between devices, on_device(): lax.all_gather(expand_weight, ('dp', 'seq'), axis=0, tiled=True)  211 us
    all_gather x1, waiting for transfers between devices, on_device(): lax.all_gather(inward_low, 'seq', axis=1, tiled=True)  157 us
    all_gather x1, waiting for transfers between devices, on_device(): lax.all_gather(keyval_grad_rows[None].astype(jnp.bfloat16), 'seq', axis=0...  118 us
    all_gather x1, waiting for transfers between devices, on_device(): lax.all_gather(shrink_weight, ('dp', 'seq'), axis=0, tiled=True)  105 us
    all_gather x1, blocking collectives, on_device(): lax.all_gather(time_weight, ('dp', 'seq'), axis=0, tiled=True)  97.4 us
    all_gather x1, waiting for transfers between devices, on_device(): lax.all_gather(outward_low, 'seq', axis=1, tiled=True)  82.6 us
    reduce_scatter x1, waiting for transfers between devices, on_device(): lax.psum_scatter(expand_rows.astype(jnp.bfloat16), 'dp', scatter_dimensio...  77.9 us
  transfers between devices with their start and end apart: 31, of which 25 were waited for; matrix products, arithmetic and copies ran while one was open for 14% of the time, Pallas kernels for 0%

commit v1 on v0

v1 whole, which is shorter than its diff:
```python
import math

import jax
import jax.numpy as jnp
from jax import lax
from jax.sharding import PartitionSpec as P

D = 1536
HEADS = 24
HEAD_DIM = 64
FF = 6144
CTX_LEN = 128
TFEAT = 256
CLIPS = 3


EPSILON = 1e-05
SCORE_SCALE = 0.125
MASKED = -1e30
PRECISE = lax.Precision.HIGHEST


def dense(activations, weight):
    return jnp.einsum("rfd,dn->rfn", activations, weight, preferred_element_type=jnp.float32)


def dense_back(gradients, weight):
    return jnp.einsum("rfn,dn->rfd", gradients, weight, preferred_element_type=jnp.float32)


def norm_forward(hidden):
    centre = jnp.mean(hidden, axis=-1, keepdims=True)
    centred = hidden - centre
    spread = jnp.mean(centred * centred, axis=-1, keepdims=True)
    scale_inv = lax.rsqrt(spread + EPSILON)
    return (centred * scale_inv, scale_inv)


def norm_backward(grad_norm, normalized, scale_inv, gain_vector):
    scaled = grad_norm * gain_vector
    gain_grad = jnp.sum(grad_norm * normalized, axis=(0, 1))
    inner = (
        scaled
        - jnp.mean(scaled, axis=-1, keepdims=True)
        - normalized * jnp.mean(scaled * normalized, axis=-1, keepdims=True)
    )
    return (scale_inv * inner, gain_grad)


def rotate(head_values, cosine_table, sine_table):
    half_width = head_values.shape[-1] // 2
    first_half = head_values[..., :half_width]
    second_half = head_values[..., half_width:]
    return jnp.concatenate(
        [
            first_half * cosine_table - second_half * sine_table,
            first_half * sine_table + second_half * cosine_table,
        ],
        axis=-1,
    )


def rotary_tables(positions):
    half_width = HEAD_DIM // 2
    frequencies = jnp.exp(
        -math.log(10000.0) * jnp.arange(half_width, dtype=jnp.float32) / half_width
    )
    angles = positions[..., None] * frequencies
    return (jnp.cos(angles)[..., None, :], jnp.sin(angles)[..., None, :])


def time_features(step_values):
    half_width = TFEAT // 2
    frequencies = jnp.exp(
        -math.log(10000.0) * jnp.arange(half_width, dtype=jnp.float32) / half_width
    )
    angles = step_values.astype(jnp.float32)[..., None] * frequencies
    return jnp.concatenate([jnp.cos(angles), jnp.sin(angles)], axis=-1)


def score_block(query_low, key_block, query_clip, key_clip):
    raw_scores = jnp.einsum(
        "rqhd,rkhd->rhqk", query_low, key_block, preferred_element_type=jnp.float32
    )
    allowed = (query_clip[:, :, None] == key_clip[:, None, :])[:, None]
    return (jnp.where(allowed, raw_scores * SCORE_SCALE, MASKED), allowed)


def attend_forward(query_low, keys_low, values_low, query_clip, key_clip):
    key_count = keys_low.shape[1]
    key_width = min(512, key_count)
    stat_shape = (query_low.shape[0], query_low.shape[2], query_low.shape[1], 1)
    row_top = jnp.full(stat_shape, MASKED, jnp.float32)
    norm_sum = jnp.zeros(stat_shape, jnp.float32)
    for offset in range(0, key_count, key_width):
        scores, allowed = score_block(
            query_low,
            keys_low[:, offset : offset + key_width],
            query_clip,
            key_clip[:, offset : offset + key_width],
        )
        next_top = jnp.maximum(row_top, jnp.max(scores, axis=-1, keepdims=True))
        norm_sum = norm_sum * jnp.exp(row_top - next_top) + jnp.sum(
            jnp.where(allowed, jnp.exp(scores - next_top), 0.0), axis=-1, keepdims=True
        )
        row_top = next_top
    mixture = jnp.zeros(query_low.shape, jnp.float32)
    for offset in range(0, key_count, key_width):
        scores, allowed = score_block(
            query_low,
            keys_low[:, offset : offset + key_width],
            query_clip,
            key_clip[:, offset : offset + key_width],
        )
        weights = jnp.where(allowed, jnp.exp(scores - row_top) / norm_sum, 0.0)
        mixture = mixture + jnp.einsum(
            "rhqk,rkhd->rqhd",
            weights.astype(jnp.bfloat16),
            values_low[:, offset : offset + key_width],
            preferred_element_type=jnp.float32,
        )
    return (mixture, row_top, norm_sum)


def attend_backward(
    query_low, keys_low, values_low, query_clip, key_clip, row_top, norm_sum, grad_low
):
    key_count = keys_low.shape[1]
    key_width = min(512, key_count)
    diagonal = jnp.zeros_like(row_top)
    for offset in range(0, key_count, key_width):
        scores, allowed = score_block(
            query_low,
            keys_low[:, offset : offset + key_width],
            query_clip,
            key_clip[:, offset : offset + key_width],
        )
        weights = jnp.where(allowed, jnp.exp(scores - row_top) / norm_sum, 0.0)
        grad_weights = jnp.einsum(
            "rqhd,rkhd->rhqk",
            grad_low,
            values_low[:, offset : offset + key_width],
            preferred_element_type=jnp.float32,
        )
        diagonal = diagonal + jnp.sum(weights * grad_weights, axis=-1, keepdims=True)
    query_grad = jnp.zeros(query_low.shape, jnp.float32)
    key_parts = []
    value_parts = []
    for offset in range(0, key_count, key_width):
        key_block = keys_low[:, offset : offset + key_width]
        scores, allowed = score_block(
            query_low, key_block, query_clip, key_clip[:, offset : offset + key_width]
        )
        weights = jnp.where(allowed, jnp.exp(scores - row_top) / norm_sum, 0.0)
        grad_weights = jnp.einsum(
            "rqhd,rkhd->rhqk",
            grad_low,
            values_low[:, offset : offset + key_width],
            preferred_element_type=jnp.float32,
        )
        score_grad = (weights * (grad_weights - diagonal) * SCORE_SCALE).astype(jnp.bfloat16)
        query_grad = query_grad + jnp.einsum(
            "rhqk,rkhd->rqhd", score_grad, key_block, preferred_element_type=jnp.float32
        )
        key_parts.append(
            jnp.einsum("rhqk,rqhd->rkhd", score_grad, query_low, preferred_element_type=jnp.float32)
        )
        value_parts.append(
            jnp.einsum(
                "rhqk,rqhd->rkhd",
                weights.astype(jnp.bfloat16),
                grad_low,
                preferred_element_type=jnp.float32,
            )
        )
    return (query_grad, jnp.concatenate(key_parts, axis=1), jnp.concatenate(value_parts, axis=1))


def gated_back(hidden_grad, gate_part, upward):
    gate_sigmoid = jax.nn.sigmoid(gate_part)
    gate_grad = hidden_grad * upward * gate_sigmoid * (1.0 + gate_part * (1.0 - gate_sigmoid))
    upward_grad = hidden_grad * gate_part * gate_sigmoid
    return jnp.concatenate([gate_grad, upward_grad], axis=-1).astype(jnp.bfloat16)


def xor_pairs(count, bit):
    return [(k, k ^ bit) for k in range(count)]


def chip_gather(values, axis):
    count = lax.axis_size(axis)
    bits = [1 << b for b in range(1, count.bit_length() - 1)]
    if len(bits) == 2 and values.shape[0] % 32 == 0:
        first, second = bits
        half = values.shape[0] // 2
        by_first = lax.ppermute(values, axis, xor_pairs(count, first))
        by_second = lax.ppermute(values, axis, xor_pairs(count, second))
        far_one = lax.ppermute(by_first[:half], axis, xor_pairs(count, second))
        far_two = lax.ppermute(by_second[half:], axis, xor_pairs(count, first))
        far = jnp.concatenate([far_one, far_two], axis=0)
        same = jnp.stack([values, by_first, by_second, far], axis=0)
    else:
        same = values[None]
        for bit in bits:
            same = jnp.concatenate([same, lax.ppermute(same, axis, xor_pairs(count, bit))], axis=0)
    if count == 1:
        return same
    other = lax.ppermute(same, axis, xor_pairs(count, 1))
    return jnp.stack([same, other], axis=1).reshape((count,) + values.shape)


def chip_scatter(parts, axis):
    count = lax.axis_size(axis)
    if count == 1:
        return parts[0].astype(jnp.float32)
    low = jnp.bfloat16
    pairs = parts.reshape((count // 2, 2) + parts.shape[1:])
    got = lax.ppermute(pairs[:, 1].astype(low), axis, xor_pairs(count, 1))
    total = pairs[:, 0].astype(jnp.float32) + got.astype(jnp.float32)
    bits = [1 << b for b in range(1, count.bit_length() - 1)]
    if len(bits) == 2 and parts.shape[1] % 32 == 0:
        first, second = bits
        half = parts.shape[1] // 2
        far_one = lax.ppermute(total[3, :half].astype(low), axis, xor_pairs(count, first))
        far_two = lax.ppermute(total[3, half:].astype(low), axis, xor_pairs(count, second))
        to_second = jnp.concatenate(
            [total[2, :half] + far_one.astype(jnp.float32), total[2, half:]], axis=0
        )
        to_first = jnp.concatenate(
            [total[1, :half], total[1, half:] + far_two.astype(jnp.float32)], axis=0
        )
        by_first = lax.ppermute(to_first.astype(low), axis, xor_pairs(count, first))
        by_second = lax.ppermute(to_second.astype(low), axis, xor_pairs(count, second))
        return total[0] + by_first.astype(jnp.float32) + by_second.astype(jnp.float32)
    for bit in reversed(bits):
        middle = total.shape[0] // 2
        got = lax.ppermute(total[middle:].astype(low), axis, xor_pairs(count, bit))
        total = total[:middle] + got.astype(jnp.float32)
    return total[0]


def place(buffer, block, dim, index):
    starts = [0] * buffer.ndim
    starts[dim] = index
    return lax.dynamic_update_slice(buffer, block, tuple(starts))


def by_order(relative, me):
    ordered = jnp.zeros(relative.shape, relative.dtype)
    for r in range(relative.shape[0]):
        ordered = place(ordered, relative[r : r + 1], 0, me ^ r)
    return ordered


def by_partner(ordered, me):
    return jnp.concatenate(
        [
            lax.dynamic_slice_in_dim(ordered, me ^ r, 1, axis=0)
            for r in range(ordered.shape[0])
        ],
        axis=0,
    )


def chip_exchange(blocks, axis, me):
    count = lax.axis_size(axis)
    result = blocks
    for r in range(1, count):
        sent = lax.dynamic_slice_in_dim(blocks, me ^ r, 1, axis=0)
        result = place(result, lax.ppermute(sent, axis, xor_pairs(count, r)), 0, me ^ r)
    return result


def line_gather(values, axis, me, dim=0):
    count = lax.axis_size(axis)
    values = jnp.expand_dims(values, dim)
    shape = list(values.shape)
    shape[dim] = count
    rightward, leftward = [values], [values]
    for step in range(1, count):
        rightward.append(
            lax.ppermute(rightward[-1], axis, [(k, k + 1) for k in range(step - 1, count - 1)])
        )
        leftward.append(
            lax.ppermute(leftward[-1], axis, [(k + 1, k) for k in range(0, count - step)])
        )
    result = place(jnp.zeros(shape, values.dtype), values, dim, me)
    for step in range(1, count):
        block = jnp.where(me >= step, rightward[step], leftward[count - step])
        result = place(result, block, dim, lax.rem(me - step + count, count))
    return result


def line_scatter(parts, axis, me, dim=0):
    count = lax.axis_size(axis)

    def part(index):
        picked = lax.dynamic_slice_in_dim(parts, index, 1, axis=dim)
        return jnp.squeeze(picked, dim).astype(jnp.float32)

    total = part(me)
    from_left = from_right = None
    for step in range(1, count):
        to_right = part(jnp.minimum(me + count - step, count - 1))
        to_left = part(jnp.maximum(me - count + step, 0))
        if step > 1:
            to_right = to_right + from_left.astype(jnp.float32)
            to_left = to_left + from_right.astype(jnp.float32)
        from_left = lax.ppermute(
            to_right.astype(jnp.bfloat16), axis, [(k, k + 1) for k in range(0, step)]
        )
        from_right = lax.ppermute(
            to_left.astype(jnp.bfloat16),
            axis,
            [(k + 1, k) for k in range(count - 1 - step, count - 1)],
        )
    if count > 1:
        total = total + from_left.astype(jnp.float32) + from_right.astype(jnp.float32)
    return total


def line_exchange(blocks, axis, me):
    count = lax.axis_size(axis)
    result = blocks
    for step in range(1, count):
        sent = lax.dynamic_slice_in_dim(blocks, lax.rem(me + step, count), 1, axis=0)
        got = lax.ppermute(sent, axis, [(k, (k + step) % count) for k in range(count)])
        result = place(result, got, 0, lax.rem(me - step + count, count))
    return result


def whole_weight(rows, dp_place, seq_place):
    column = line_gather(rows, "seq", seq_place)
    full = by_order(chip_gather(column, "dp"), dp_place)
    return full.reshape((-1,) + rows.shape[1:])


def own_rows_sum(partial, dp_place, seq_place):
    dp_count, seq_count = lax.axis_size("dp"), lax.axis_size("seq")
    rows, width = partial.shape
    shaped = partial.astype(jnp.bfloat16).reshape(dp_count, rows // dp_count, width)
    column = chip_scatter(by_partner(shaped, dp_place), "dp")
    return line_scatter(column.reshape(seq_count, -1, width), "seq", seq_place)


def on_device(
    latents,
    context,
    clip_bounds,
    timesteps,
    self_inward,
    self_outward,
    cross_query,
    cross_keyval,
    cross_return,
    time_weight,
    expand_weight,
    shrink_weight,
    gain_attend,
    gain_cross,
    gain_feed,
    cotangent,
):
    f32, bf16 = jnp.float32, jnp.bfloat16
    frame_count = latents.shape[1]
    dp_count = lax.axis_size("dp")
    seq_count = lax.axis_size("seq")
    dp_place = lax.axis_index("dp")
    seq_place = lax.axis_index("seq")
    row_length = frame_count * seq_count
    text_count = context.shape[1]
    own_heads = HEADS // seq_count
    own_width = own_heads * HEAD_DIM
    hidden_width = FF // dp_count
    place_all = dp_place * seq_count + seq_place

    all_frames = jnp.arange(row_length, dtype=jnp.int32)[None, :]
    second_start = clip_bounds[:, 0:1]
    third_start = clip_bounds[:, 1:2]
    frame_clips = (all_frames >= second_start).astype(jnp.int32) + (
        all_frames >= third_start
    ).astype(jnp.int32)
    clip_ids = lax.dynamic_slice_in_dim(frame_clips, seq_place * frame_count, frame_count, axis=1)
    token_clips = jnp.arange(CLIPS, dtype=jnp.int32)[None, :]
    key_clips = jnp.concatenate([frame_clips, token_clips], axis=1)
    clip_starts = jnp.where(
        frame_clips == 0, 0, jnp.where(frame_clips == 1, second_start, third_start)
    )
    positions = (all_frames - clip_starts + 1).astype(f32)
    cosine_table, sine_table = rotary_tables(positions)
    text_clips = (jnp.arange(text_count, dtype=jnp.int32) // CTX_LEN)[None, :]

    gains_all = lax.all_gather(
        jnp.stack([gain_attend, gain_cross, gain_feed], axis=0), ("dp", "seq"), axis=1, tiled=True
    ).astype(f32)
    time_full = lax.all_gather(time_weight, ("dp", "seq"), axis=0, tiled=True)
    steps_all = lax.all_gather(timesteps, "dp", axis=0, tiled=True)
    attend_gain, cross_gain, feed_gain = gains_all[0], gains_all[1], gains_all[2]

    inward_blocks = (
        self_inward.reshape(-1, 3, seq_count, own_width)
        .transpose(2, 0, 1, 3)
        .reshape(seq_count, -1, 3 * own_width)
    )
    row_latents = line_gather(latents[0], "seq", seq_place).reshape(row_length, D)
    inward_columns = line_exchange(inward_blocks, "seq", seq_place)
    inward_own = by_order(chip_gather(inward_columns, "dp"), dp_place).reshape(D, 3 * own_width)
    cotangent_all = chip_gather(cotangent[0], "dp").reshape(dp_count * frame_count, D)

    outward_full = whole_weight(self_outward, dp_place, seq_place)
    query_full = whole_weight(cross_query, dp_place, seq_place)
    keyval_full = whole_weight(cross_keyval, dp_place, seq_place)
    return_full = whole_weight(cross_return, dp_place, seq_place)

    expand_blocks = (
        expand_weight.reshape(-1, 2, dp_count, hidden_width)
        .transpose(2, 0, 1, 3)
        .reshape(dp_count, -1, 2 * hidden_width)
    )
    expand_part = chip_exchange(expand_blocks, "dp", dp_place)
    expand_own = line_gather(expand_part, "seq", seq_place, dim=1).reshape(D, 2 * hidden_width)
    shrink_own = line_gather(shrink_weight, "seq", seq_place).reshape(hidden_width, D)

    feats_low = time_features(timesteps[0]).astype(bf16)
    token = jnp.dot(feats_low, time_full, preferred_element_type=f32)
    token_norm, token_inverse = norm_forward(token)
    token_low = (token_norm * attend_gain).astype(bf16)
    token_kv = jnp.dot(
        token_low, inward_own[:, own_width:], preferred_element_type=f32
    ).astype(bf16)

    row_float = row_latents.astype(f32)
    row_norm, row_inverse = norm_forward(row_float)
    row_low = (row_norm * attend_gain).astype(bf16)
    projected = jnp.dot(row_low, inward_own, preferred_element_type=f32).reshape(
        1, row_length, 3, own_heads, HEAD_DIM
    )
    queries_low = rotate(projected[:, :, 0], cosine_table, sine_table).astype(bf16)
    keys_low = rotate(projected[:, :, 1], cosine_table, sine_table).astype(bf16)
    values_low = projected[:, :, 2].astype(bf16)
    token_heads = token_kv.reshape(1, CLIPS, 2, own_heads, HEAD_DIM)
    keys_heads = jnp.concatenate([keys_low, token_heads[:, :, 0]], axis=1)
    values_heads = jnp.concatenate([values_low, token_heads[:, :, 1]], axis=1)
    attended, self_top, self_sum = attend_forward(
        queries_low, keys_heads, values_heads, frame_clips, key_clips
    )
    attended_blocks = attended.astype(bf16).reshape(seq_count, frame_count, own_width)
    attended_low = (
        line_exchange(attended_blocks, "seq", seq_place)
        .transpose(1, 0, 2)
        .reshape(frame_count, D)
    )
    conditioned = latents[0].astype(f32)
    after_self = conditioned + jnp.dot(attended_low, outward_full, preferred_element_type=f32)

    norm_two, inverse_two = norm_forward(after_self)
    normed_two = (norm_two * cross_gain).astype(bf16)
    cross_heads = (
        jnp.dot(normed_two, query_full, preferred_element_type=f32)
        .astype(bf16)
        .reshape(1, frame_count, HEADS, HEAD_DIM)
    )
    keyval = (
        jnp.dot(context[0], keyval_full, preferred_element_type=f32)
        .astype(bf16)
        .reshape(1, text_count, 2, HEADS, HEAD_DIM)
    )
    cross_keys = keyval[:, :, 0]
    cross_values = keyval[:, :, 1]
    crossed, cross_top, cross_sum = attend_forward(
        cross_heads, cross_keys, cross_values, clip_ids, text_clips
    )
    crossed_low = crossed.reshape(frame_count, D).astype(bf16)
    after_cross = after_self + jnp.dot(crossed_low, return_full, preferred_element_type=f32)

    norm_three, inverse_three = norm_forward(after_cross)
    normed_three = (norm_three * feed_gain).astype(bf16)
    frames_all = chip_gather(normed_three, "dp").reshape(dp_count * frame_count, D)
    gate_up = jnp.dot(frames_all, expand_own, preferred_element_type=f32)
    gate_part = gate_up[:, :hidden_width]
    upward = gate_up[:, hidden_width:]
    hidden_low = (jax.nn.silu(gate_part) * upward).astype(bf16)
    hidden_grad = jnp.dot(cotangent_all, shrink_own.T, preferred_element_type=f32)
    expand_low = gated_back(hidden_grad, gate_part, upward)
    feed_parts = jnp.dot(expand_low, expand_own.T, preferred_element_type=f32).astype(bf16)
    feed_norm_grad = chip_scatter(feed_parts.reshape(dp_count, frame_count, D), "dp")
    out_parts = jnp.dot(hidden_low, shrink_own, preferred_element_type=f32).astype(bf16)
    fed = chip_scatter(out_parts.reshape(dp_count, frame_count, D), "dp")
    block_output = (after_cross + fed).astype(bf16)

    shrink_part = jnp.dot(hidden_low.T, cotangent_all, preferred_element_type=f32).astype(bf16)
    grad_shrink = line_scatter(
        shrink_part.reshape(seq_count, hidden_width // seq_count, D), "seq", seq_place
    )
    expand_grad = jnp.dot(frames_all.T, expand_low, preferred_element_type=f32).astype(bf16)
    expand_sum = line_scatter(
        expand_grad.reshape(dp_count, seq_count, -1, 2 * hidden_width), "seq", seq_place, dim=1
    ).astype(bf16)
    grad_expand = (
        chip_exchange(expand_sum, "dp", dp_place)
        .reshape(dp_count, -1, 2, hidden_width)
        .transpose(1, 2, 0, 3)
        .reshape(-1, 2 * FF)
        .astype(f32)
    )

    feed_term, feed_gain_part = norm_backward(
        feed_norm_grad[None], norm_three[None], inverse_three[None], feed_gain
    )
    after_cross_grad = cotangent[0].astype(f32) + feed_term[0]
    return_low = after_cross_grad.astype(bf16)
    grad_return = own_rows_sum(
        jnp.dot(crossed_low.T, return_low, preferred_element_type=f32), dp_place, seq_place
    )
    crossed_grad = (
        jnp.dot(return_low, return_full.T, preferred_element_type=f32)
        .astype(bf16)
        .reshape(1, frame_count, HEADS, HEAD_DIM)
    )
    cross_query_grad, cross_key_grad, cross_value_grad = attend_backward(
        cross_heads,
        cross_keys,
        cross_values,
        clip_ids,
        text_clips,
        cross_top,
        cross_sum,
        crossed_grad,
    )
    cross_query_low = cross_query_grad.reshape(frame_count, D).astype(bf16)
    keyval_low = (
        jnp.stack([cross_key_grad, cross_value_grad], axis=2)
        .reshape(text_count, 2 * D)
        .astype(bf16)
    )
    grad_keyval = own_rows_sum(
        jnp.dot(context[0].T, keyval_low, preferred_element_type=f32), dp_place, seq_place
    )
    grad_query = own_rows_sum(
        jnp.dot(normed_two.T, cross_query_low, preferred_element_type=f32), dp_place, seq_place
    )
    cross_norm_grad = jnp.dot(cross_query_low, query_full.T, preferred_element_type=f32)
    cross_term, cross_gain_part = norm_backward(
        cross_norm_grad[None], norm_two[None], inverse_two[None], cross_gain
    )
    after_self_grad = after_cross_grad + cross_term[0]
    outward_low = after_self_grad.astype(bf16)
    grad_outward = own_rows_sum(
        jnp.dot(attended_low.T, outward_low, preferred_element_type=f32), dp_place, seq_place
    )
    attended_grad = jnp.dot(outward_low, outward_full.T, preferred_element_type=f32).astype(bf16)
    attended_grad_own = line_exchange(
        attended_grad.reshape(frame_count, seq_count, own_width).transpose(1, 0, 2),
        "seq",
        seq_place,
    ).reshape(1, row_length, own_heads, HEAD_DIM)
    self_query_grad, self_key_grad, self_value_grad = attend_backward(
        queries_low,
        keys_heads,
        values_heads,
        frame_clips,
        key_clips,
        self_top,
        self_sum,
        attended_grad_own,
    )
    query_turned = rotate(self_query_grad, cosine_table, -sine_table)
    key_turned = rotate(self_key_grad[:, :row_length], cosine_table, -sine_table)
    inward_low = (
        jnp.stack([query_turned, key_turned, self_value_grad[:, :row_length]], axis=2)
        .reshape(row_length, 3 * own_width)
        .astype(bf16)
    )
    token_grad = jnp.stack(
        [self_key_grad[:, row_length:], self_value_grad[:, row_length:]], axis=2
    ).reshape(CLIPS, 2 * own_width)
    token_grad_low = token_grad.astype(bf16)
    attend_parts = jnp.dot(inward_low, inward_own.T, preferred_element_type=f32)
    attend_norm_grad = line_scatter(
        attend_parts.astype(bf16).reshape(seq_count, frame_count, D), "seq", seq_place
    )
    own_norm = lax.dynamic_slice_in_dim(row_norm, seq_place * frame_count, frame_count, axis=0)
    own_inverse = lax.dynamic_slice_in_dim(
        row_inverse, seq_place * frame_count, frame_count, axis=0
    )
    attend_term, _ = norm_backward(
        attend_norm_grad[None], own_norm[None], own_inverse[None], attend_gain
    )
    latents_grad = (after_self_grad + attend_term[0])[None]

    token_norm_grad = jnp.dot(
        token_grad_low, inward_own[:, own_width:].T, preferred_element_type=f32
    )
    token_term, token_gain_part = norm_backward(
        token_norm_grad[None], token_norm[None], token_inverse[None], attend_gain
    )
    attend_gain_part = jnp.sum(attend_parts * row_norm, axis=0) + token_gain_part
    small = jnp.concatenate(
        [
            token_term[0],
            attend_gain_part[None],
            cross_gain_part[None],
            feed_gain_part[None],
        ],
        axis=0,
    )
    small_all = lax.all_gather(small, ("dp", "seq"), axis=0, tiled=False)
    small_sum = jnp.sum(small_all.reshape(dp_count, seq_count, CLIPS + 3, D), axis=1)
    feats_all = time_features(steps_all).astype(bf16).astype(f32)
    time_rows = TFEAT // (dp_count * seq_count)
    feats_own = lax.dynamic_slice_in_dim(feats_all, place_all * time_rows, time_rows, axis=2)
    grad_time = jnp.einsum(
        "rct,rcn->tn",
        feats_own,
        small_sum[:, :CLIPS],
        precision=PRECISE,
        preferred_element_type=f32,
    )
    gain_width = D // (dp_count * seq_count)
    gain_sums = lax.dynamic_slice_in_dim(
        jnp.sum(small_sum[:, CLIPS:], axis=0), place_all * gain_width, gain_width, axis=1
    )

    inward_full_low = jnp.concatenate(
        [row_low, jnp.pad(token_low, ((0, 16 - CLIPS), (0, 0)))], axis=0
    )
    inward_full_grad = jnp.concatenate(
        [inward_low, jnp.pad(token_grad_low, ((0, 16 - CLIPS), (own_width, 0)))], axis=0
    )
    inward_grad = jnp.dot(inward_full_low.T, inward_full_grad, preferred_element_type=f32)
    inward_sum = chip_scatter(
        by_partner(
            inward_grad.astype(bf16).reshape(dp_count, D // dp_count, 3 * own_width), dp_place
        ),
        "dp",
    )
    grad_inward = (
        line_exchange(
            inward_sum.astype(bf16).reshape(seq_count, -1, 3 * own_width), "seq", seq_place
        )
        .reshape(seq_count, -1, 3, own_width)
        .transpose(1, 2, 0, 3)
        .reshape(-1, 3 * D)
        .astype(f32)
    )
    return (
        block_output[None],
        latents_grad,
        grad_inward,
        grad_outward,
        grad_query,
        grad_keyval,
        grad_return,
        grad_time,
        grad_expand,
        grad_shrink,
        gain_sums[0],
        gain_sums[1],
        gain_sums[2],
    )


def solution(mesh):
    return jax.shard_map(
        on_device,
        mesh=mesh,
        in_specs=(
            P("dp", "seq", None),
            P("dp", None, None),
            P("dp", None),
            P("dp", None),
            P(("dp", "seq"), None),
            P(("dp", "seq"), None),
            P(("dp", "seq"), None),
            P(("dp", "seq"), None),
            P(("dp", "seq"), None),
            P(("dp", "seq"), None),
            P(("dp", "seq"), None),
            P(("dp", "seq"), None),
            P(("dp", "seq")),
            P(("dp", "seq")),
            P(("dp", "seq")),
            P("dp", "seq", None),
        ),
        out_specs=(
            P("dp", "seq", None),
            P("dp", "seq", None),
            P(("dp", "seq"), None),
            P(("dp", "seq"), None),
            P(("dp", "seq"), None),
            P(("dp", "seq"), None),
            P(("dp", "seq"), None),
            P(("dp", "seq"), None),
            P(("dp", "seq"), None),
            P(("dp", "seq"), None),
            P(("dp", "seq")),
            P(("dp", "seq")),
            P(("dp", "seq")),
        ),
        check_vma=False,
    )
```

time: 2690 us -> 1570 us (0.58)
  waiting for transfers between devices: 1840 us -> 425 us
  starting transfers between devices: 20.9 us -> 313 us
  blocking collectives: 258 us -> 147 us
  local copies, waits for them, and re-layouts: 75.3 us -> 160 us
  other arithmetic: 99.5 us -> 181 us
  matrix products: 370 us -> 312 us
    all_gather x16 -> x1, waiting for transfers between devices: 1380 us -> 0.01 us  [on_device(): small_all = lax.all_gather(small, ('dp', 'seq'), axis=0, tiled=False)]
    ppermute x0 -> x170, waiting for transfers between devices: none -> 425 us  [the longest x12 94.2 us: line_exchange(): lax.ppermute(sent, axis, [(k, (k + step) % count) for k in range(count)])]
    reduce_scatter x10 -> x0, waiting for transfers between devices: 344 us -> none  [the longest x1 77.9 us: on_device(): lax.psum_scatter(expand_rows.astype(jnp.bfloat16), 'dp', scatter_dimensio...]
    ppermute x0 -> x170, starting transfers between devices: none -> 313 us  [the longest x21 91.8 us: line_scatter(): lax.ppermute(to_right.astype(jnp.bfloat16), axis, [(k, k + 1) for k in ra...]
    all_to_all x5 -> x0, waiting for transfers between devices: 107 us -> none  [the longest x1 40 us: on_device(): lax.all_to_all(column_blocks(crossed_low, dp_count, seq_count), 'seq', sp...]
    unnamed x2 -> x0, blocking collectives: 54.7 us -> none
    dynamic_update_slice x0 -> x72, local copies, waits for them, and re-layouts: none -> 53.4 us  [place(): return lax.dynamic_update_slice(buffer, block, tuple(starts))]
    another operation x4 -> x34, other arithmetic: 0.25 us -> 53.5 us
  transfers between devices with their start and end apart: 31 -> 171, of which waited for: 25 -> 59; matrix products, arithmetic and copies ran while one was open for 14% -> 36% of each run, Pallas kernels for 0% -> 0%
where the time goes in v1:
time: 1570 us; the launch traced here: 1560 us
  waiting for transfers between devices  425 us (27%)
  starting transfers between devices  313 us (20%)
  matrix products  312 us (20%)
  other arithmetic  181 us (12%)
  local copies, waits for them, and re-layouts  160 us (10%)
  blocking collectives  147 us (9%)
  between operations  19.2 us (1%)
    ppermute x12, waiting for transfers between devices, line_exchange(): lax.ppermute(sent, axis, [(k, (k + step) % count) for k in range(count)])  94.2 us
    ppermute x21, starting transfers between devices, line_scatter(): lax.ppermute(to_right.astype(jnp.bfloat16), axis, [(k, k + 1) for k in ra...  91.8 us
    ppermute x21, waiting for transfers between devices, line_gather(): lax.ppermute(leftward[-1], axis, [(k + 1, k) for k in range(0, count - st...  81 us
    ppermute x10, waiting for transfers between devices, chip_gather(): lax.ppermute(same, axis, xor_pairs(count, bit))  71.4 us
    all_gather x1, blocking collectives, on_device(): time_full = lax.all_gather(time_weight, ('dp', 'seq'), axis=0, tiled=True)  71.2 us
    all_gather x1, blocking collectives, on_device(): lax.all_gather(jnp.stack([gain_attend, gain_cross, gain_feed], axis=0), (...  66.8 us
    ppermute x14, waiting for transfers between devices, chip_exchange(): lax.ppermute(sent, axis, xor_pairs(count, r))  57.8 us
    dynamic_update_slice x72, local copies, waits for them, and re-layouts, place(): return lax.dynamic_update_slice(buffer, block, tuple(starts))  53.4 us
  transfers between devices with their start and end apart: 171, of which 59 were waited for; matrix products, arithmetic and copies ran while one was open for 36% of the time, Pallas kernels for 0%

profile of v1, /device:TPU:0, one launch (start us, length us, event | category | flops | bytes accessed | tf_op | source)
XLA Modules:
  0.0 1557.3 jit_solution(1522145653165759170)
XLA Ops:
  31.8 66.8 %all-gather.1 = bf16[32,48,3]{1,2,0:T(4,128)(2,1)S(1)} all-gather(bf16[1,48,3]{1,2,0:T(4,128)(2,1)S(1)} %maximum_bitcast_fusion.6), channel_id=1, replica_groups=mesh['dp'=8,'seq'=4] {'dp','seq'}, dimensions={0}, use_global_device_ids=true | all-gather | bytes 9504 | tf_op jit(solution)/shard_map/all_gather | solution.py:393
  99.9 71.2 %all_gather.16 = bf16[256,1536]{1,0:T(8,128)(2,1)S(1)} all-gather(bf16[8,1536]{1,0:T(8,128)(2,1)S(1)} %copy-done.150), channel_id=1, replica_groups=mesh['dp'=8,'seq'=4] {'dp','seq'}, dimensions={0}, use_global_device_ids=true | all-gather | bytes 811008 | tf_op jit(solution)/shard_map/all_gather | solution.py:396
  270.6 18.8 %collective-permute-done.45 = bf16[1,48,1536]{2,1,0:T(8,128)(2,1)S(1)} collective-permute-done((bf16[1,48,1536]{2,1,0:T(8,128)(2,1)S(1)}, bf16[1,48,1536]{2,1,0:T(8,128)(2,1)S(1)}, u32[]{:S(2)}, u32[]{:S(2)}) %collective-permute-start.45) | collective-permute-done | bytes 147488 | tf_op jit(solution)/shard_map/ppermute | solution.py:285
  327.6 16.7 %collective-permute-start.48 = (bf16[1,4,48,1536]{3,2,1,0:T(8,128)(2,1)S(1)}, bf16[1,4,48,1536]{3,2,1,0:T(8,128)(2,1)S(1)}, u32[]{:S(2)}, u32[]{:S(2)}) collective-permute-start(bf16[1,4,48,1536]{3,2,1,0:T(8,128)(2,1)S(1)} %bitcast_dynamic-update-slice_fusion.11), channel_id=1, source_target_pairs={{0,8},{4,12},{8,0},{12,4},{16,24},{20,28},{24,16},{28,20},{1,9},{5... | collective-permute-start | bytes 1769480 | tf_op jit(solution)/shard_map/ppermute | solution.py:205
  349.2 11.1 collective-permute-done.48
  362.5 10.4 collective-permute-done.21
  373.3 12.3 collective-permute-done.39
  431.8 22.0 %collective-permute-done.22 = bf16[2,4,48,1536]{3,2,1,0:T(8,128)(2,1)S(1)} collective-permute-done((bf16[2,4,48,1536]{3,2,1,0:T(8,128)(2,1)S(1)}, bf16[2,4,48,1536]{3,2,1,0:T(8,128)(2,1)S(1)}, u32[]{:S(2)}, u32[]{:S(2)}) %collective-permute-start.22) | collective-permute-done | bytes 1179680 | tf_op jit(solution)/shard_map/ppermute | solution.py:205
  527.4 40.4 %collective-permute-done.12 = bf16[1,256,384]{1,2,0:T(8,128)(2,1)S(1)} collective-permute-done((bf16[1,256,384]{1,2,0:T(8,128)(2,1)S(1)}, bf16[1,256,384]{1,2,0:T(8,128)(2,1)S(1)}, u32[]{:S(2)}, u32[]{:S(2)}) %collective-permute-start.12) | collective-permute-done | bytes 196640 | tf_op jit(solution)/shard_map/ppermute | solution.py:327
  569.6 17.7 %collective-permute-done.13 = bf16[1,256,384]{1,2,0:T(8,128)(2,1)S(1)} collective-permute-done((bf16[1,256,384]{1,2,0:T(8,128)(2,1)S(1)}, bf16[1,256,384]{1,2,0:T(8,128)(2,1)S(1)}, u32[]{:S(2)}, u32[]{:S(2)}) %collective-permute-start.13) | collective-permute-done | bytes 196640 | tf_op jit(solution)/shard_map/ppermute | solution.py:327
  655.9 13.3 collective-permute-done.51
  686.3 24.4 %collective-permute-done.66 = bf16[8,1,48,1536]{3,2,0,1:T(8,128)(2,1)S(1)} collective-permute-done((bf16[8,1,48,1536]{3,2,0,1:T(8,128)(2,1)}, bf16[8,1,48,1536]{3,2,0,1:T(8,128)(2,1)S(1)}, u32[]{:S(2)}, u32[]{:S(2)}) %collective-permute-start.66) | collective-permute-done | bytes 1179680 | tf_op jit(solution)/shard_map/ppermute | solution.py:285
  727.6 16.4 %fusion.266 = f32[2048,1536]{0,1:T(8,128)} fusion(bf16[2048,1536]{1,0:T(8,128)(2,1)} %bitcast.1002, bf16[1536,1536]{1,0:T(8,128)(2,1)} %bitcast.1033), kind=kOutput, calls=%fused_computation.714 | convolution fusion | flops 9663676416 | bytes 23592960 | tf_op jit(solution)/shard_map/dot_general | solution.py:479
  744.1 12.5 multiply_convert_fusion.5
  756.6 13.9 convolution_convert_fusion.6
  770.5 17.9 %convolution_convert_fusion.5 = bf16[2048,1536]{1,0:T(8,128)(2,1)} fusion(bf16[1536,1536]{1,0:T(8,128)(2,1)} %bitcast.1034, bf16[2048,768]{0,1:T(8,128)(2,1)} %get-tuple-element.33, bf16[2048,768]{0,1:T(8,128)(2,1)} %get-tuple-element.32), kind=kOutput, calls=%fused_computation.26 | convolution fusion | flops 9679405056 | bytes 17301504 | tf_op jit(solution)/shard_map/dot_general | solution.py:485
  819.3 18.5 %collective-permute-done.151 = bf16[8,48,1536]{2,1,0:T(8,128)(2,1)S(1)} collective-permute-done((bf16[8,48,1536]{2,1,0:T(8,128)(2,1)S(1)}, bf16[8,48,1536]{2,1,0:T(8,128)(2,1)S(1)}, u32[]{:S(2)}, u32[]{:S(2)}) %collective-permute-start.151) | collective-permute-done | bytes 1179680 | tf_op jit(solution)/shard_map/ppermute | solution.py:309
  917.4 10.9 collective-permute-start.153
  952.7 45.0 %fusion.85 = bf16[24,64,256]{2,1,0:T(8,128)(2,1)S(1)} fusion(f32[24,256,384]{2,1,0:T(8,128)} %fusion.115, bf16[1,384,2,24,64]{1,4,3,2,0:T(8,128)(2,1)} %bitcast.1077, f32[24,256,384]{2,1,0:T(8,128)} %copy-done.6, f32[24,256]{1,0:T(8,128)S(1)} %copy-done.155, f32[24,256]{1,0:T(8,128)S(1)} %copy-done.134, pred[256,384]{1,0:T(8,128)(4,1)S(1)} %copy-done.101), kind=kOutput, calls=%fused_computation.183 | convolution fusion | flops 337779072 | bytes 40009728 | tf_op jit(solution)/shard_map/rhqk,rkhd->rqhd/dot_general | solution.py:162
  1010.2 45.9 %fusion.76 = bf16[1,384,1,24,64]{1,4,3,2,0:T(8,128)(2,1)} fusion(bf16[256,24,64]{0,2,1:T(8,128)(2,1)S(1)} %bitcast.1069, f32[24,256,384]{2,1,0:T(8,128)} %fusion.115, f32[24,256,384]{2,1,0:T(8,128)} %copy-done.6, f32[24,256]{1,0:T(8,128)S(1)} %copy-done.155, f32[24,256]{1,0:T(8,128)S(1)} %copy-done.134, pred[256,384]{1,0:T(8,128)(4,1)S(1)} %copy-done.101), kind=kOutput, calls=%fused_computation.180 | convolution fusion | flops 337975680 | bytes 20987904 | tf_op jit(solution)/shard_map/rhqk,rqhd->rkhd/dot_general | solution.py:166
  1154.0 19.7 %multiply_reduce_fusion = (f32[6,1024]{1,0:T(8,128)}, f32[6,1024]{1,0:T(8,128)}, f32[6,1024,512]{1,2,0:T(8,128)}) fusion(f32[6,1024]{1,0:T(8,128)S(1)} %copy-done.111, f32[6,1024]{1,0:T(8,128)S(1)} %copy-done.94, f32[6,1024,512]{1,2,0:T(8,128)} %copy-done.1, pred[1024,512]{0,1:T(8,128)(4,1)S(1)} %copy-done.39, f32[6,1024,512]{1,2,0:T(8,128)} %fusion.166, ...), kind=kOutput, calls=%fused_computation.3 | convolution fusion | flops 446681088 | bytes 52674560 | tf_op jit(solution)/shard_map/rqhd,rkhd->rhqk/dot_general | solution.py:139
  1174.6 18.5 %multiply_convert_fusion.1 = (bf16[6,1024,512]{1,2,0:T(8,128)(2,1)S(1)}, bf16[6,1024,512]{1,2,0:T(8,128)(2,1)S(1)}) fusion(f32[6,1024,512]{1,2,0:T(8,128)} %fusion.166, f32[6,1024]{1,0:T(8,128)S(1)} %add_add_fusion, f32[6,1024]{1,0:T(8,128)S(1)} %copy-done.111, f32[6,1024]{1,0:T(8,128)S(1)} %copy-done.94, f32[6,1024,512]{1,2,0:T(8,128)} %copy-done.2, ...), kind=kLoop, calls=%fused_computation.2 | loop fusion | flops 56623104 | bytes 64036864 | tf_op jit(solution)/shard_map/convert_element_type | solution.py:161
  1304.1 13.9 collective-permute-done.94
  1394.9 13.7 collective-permute-done.104
  (1164 shorter events, 965.8 us)
Async XLA Ops:
  7.3 1349.3 %all-gather.6.cloned.1.call-start = ((), (), s32[]{:S(2)}) async-start(), calls=%async_computation | async-start | bytes 1622016 | tf_op jit(solution)/shard_map/all_gather | solution.py:607
  7.3 249.4 %collective-permute-start.43 = (bf16[1,48,1536]{2,1,0:T(8,128)(2,1)}, bf16[1,48,1536]{2,1,0:T(8,128)(2,1)}, u32[]{:S(2)}, u32[]{:S(2)}) collective-permute-start(bf16[1,48,1536]{2,1,0:T(8,128)(2,1)} %bitcast.1097), channel_id=1, source_target_pairs={{1,0},{2,1},{3,2},{5,4},{6,5},{7,6},{9,8},{10,9},{11,10},{13,12},{... | collective-permute-start | bytes 442376 | tf_op jit(solution)/shard_map/ppermute | solution.py:285
  8.7 254.6 %collective-permute-start.42 = (bf16[1,48,1536]{2,1,0:T(8,128)(2,1)}, bf16[1,48,1536]{2,1,0:T(8,128)(2,1)}, u32[]{:S(2)}, u32[]{:S(2)}) collective-permute-start(bf16[1,48,1536]{2,1,0:T(8,128)(2,1)} %bitcast.1098), channel_id=1, source_target_pairs={{0,1},{1,2},{2,3},{4,5},{5,6},{6,7},{8,9},{9,10},{10,11},{12,13},{... | collective-permute-start | bytes 442376 | tf_op jit(solution)/shard_map/ppermute | solution.py:282
  15.0 225.0 %collective-permute-start.25 = (bf16[1,24,3072]{2,1,0:T(8,128)(2,1)}, bf16[1,24,3072]{2,1,0:T(8,128)(2,1)}, u32[]{:S(2)}, u32[]{:S(2)}) collective-permute-start(bf16[1,24,3072]{2,1,0:T(8,128)(2,1)} %bitcast.1095), channel_id=1, source_target_pairs={{1,0},{2,1},{3,2},{5,4},{6,5},{7,6},{9,8},{10,9},{11,10},{13,12},{... | collective-permute-start | bytes 442376 | tf_op jit(solution)/shard_map/ppermute | solution.py:285
  16.2 245.1 %collective-permute-start.24 = (bf16[1,24,3072]{2,1,0:T(8,128)(2,1)}, bf16[1,24,3072]{2,1,0:T(8,128)(2,1)}, u32[]{:S(2)}, u32[]{:S(2)}) collective-permute-start(bf16[1,24,3072]{2,1,0:T(8,128)(2,1)} %bitcast.1096), channel_id=1, source_target_pairs={{0,1},{1,2},{2,3},{4,5},{5,6},{6,7},{8,9},{9,10},{10,11},{12,13},{... | collective-permute-start | bytes 442376 | tf_op jit(solution)/shard_map/ppermute | solution.py:282
  24.0 171.1 %collective-permute-start.6 = (bf16[1,48,1152]{2,1,0:T(8,128)(2,1)}, bf16[1,48,1152]{2,1,0:T(8,128)(2,1)}, u32[]{:S(2)}, u32[]{:S(2)}) collective-permute-start(bf16[1,48,1152]{2,1,0:T(8,128)(2,1)} %get-tuple-element.173), channel_id=1, source_target_pairs={{0,1},{1,2},{2,3},{3,0},{4,5},{5,6},{6,7},{7,4},{8,9},{9,10},{10,1... | collective-permute-start | bytes 331784 | tf_op jit(solution)/shard_map/ppermute | solution.py:327
  263.4 98.5 %collective-permute-start.1 = (bf16[1,256,1536]{2,1,0:T(8,128)(2,1)S(1)}, bf16[1,256,1536]{2,1,0:T(8,128)(2,1)S(1)}, u32[]{:S(2)}, u32[]{:S(2)}) collective-permute-start(bf16[1,256,1536]{2,1,0:T(8,128)(2,1)S(1)} %copy-done.62), channel_id=1, source_target_pairs={{1,0},{2,1},{3,2},{5,4},{6,5},{7,6},{9,8},{10,9},{11,10},{13,12},{... | collective-permute-start | bytes 2359304 | tf_op jit(solution)/shard_map/ppermute | solution.py:285
  409.7 102.5 %collective-permute-start.70 = (bf16[1,192,1536]{2,1,0:T(8,128)(2,1)}, bf16[1,192,1536]{2,1,0:T(8,128)(2,1)}, u32[]{:S(2)}, u32[]{:S(2)}) collective-permute-start(bf16[1,192,1536]{2,1,0:T(8,128)(2,1)} %bitcast.111), channel_id=1, source_target_pairs={{1,0},{2,1},{3,2},{5,4},{6,5},{7,6},{9,8},{10,9},{11,10},{13,12},{... | collective-permute-start | bytes 1769480 | tf_op jit(solution)/shard_map/ppermute | solution.py:285
  428.5 97.6 %collective-permute-start.40 = (bf16[2,4,48,1536]{3,2,1,0:T(8,128)(2,1)}, bf16[2,4,48,1536]{3,2,1,0:T(8,128)(2,1)}, u32[]{:S(2)}, u32[]{:S(2)}) collective-permute-start(bf16[2,4,48,1536]{3,2,1,0:T(8,128)(2,1)} %pad_maximum_fusion.20), channel_id=1, source_target_pairs={{0,16},{4,20},{8,24},{12,28},{16,0},{20,4},{24,8},{28,12},{1,17},{... | collective-permute-start | bytes 3538952 | tf_op jit(solution)/shard_map/ppermute | solution.py:205
  453.8 65.1 %collective-permute-start.31 = (bf16[2,4,24,3072]{3,2,1,0:T(8,128)(2,1)}, bf16[2,4,24,3072]{3,2,1,0:T(8,128)(2,1)}, u32[]{:S(2)}, u32[]{:S(2)}) collective-permute-start(bf16[2,4,24,3072]{3,2,1,0:T(8,128)(2,1)} %pad_maximum_fusion.19), channel_id=1, source_target_pairs={{0,16},{4,20},{8,24},{12,28},{16,0},{20,4},{24,8},{28,12},{1,17},{... | collective-permute-start | bytes 3538952 | tf_op jit(solution)/shard_map/ppermute | solution.py:205
  459.0 140.9 %collective-permute-start.50 = (bf16[4,4,48,1536]{3,2,1,0:T(8,128)(2,1)}, bf16[4,4,48,1536]{3,2,1,0:T(8,128)(2,1)}, u32[]{:S(2)}, u32[]{:S(2)}) collective-permute-start(bf16[4,4,48,1536]{3,2,1,0:T(8,128)(2,1)} %get-tuple-element.110), channel_id=1, source_target_pairs={{0,4},{4,0},{8,12},{12,8},{16,20},{20,16},{24,28},{28,24},{1,5},{5... | collective-permute-start | bytes 7077896 | tf_op jit(solution)/shard_map/ppermute | solution.py:208
  461.9 142.0 %collective-permute-start.23 = (bf16[4,4,48,1536]{3,2,1,0:T(8,128)(2,1)}, bf16[4,4,48,1536]{3,2,1,0:T(8,128)(2,1)}, u32[]{:S(2)}, u32[]{:S(2)}) collective-permute-start(bf16[4,4,48,1536]{3,2,1,0:T(8,128)(2,1)} %get-tuple-element.116), channel_id=1, source_target_pairs={{0,4},{4,0},{8,12},{12,8},{16,20},{20,16},{24,28},{28,24},{1,5},{5... | collective-permute-start | bytes 7077896 | tf_op jit(solution)/shard_map/ppermute | solution.py:208
  512.3 86.3 %collective-permute-start.64 = (bf16[8,1,48,1536]{3,2,0,1:T(8,128)(2,1)}, bf16[8,1,48,1536]{3,2,0,1:T(8,128)(2,1)}, u32[]{:S(2)}, u32[]{:S(2)}) collective-permute-start(bf16[8,1,48,1536]{3,2,0,1:T(8,128)(2,1)} %bitcast_dynamic-update-slice_fusion.4), channel_id=1, source_target_pairs={{1,0},{2,1},{3,2},{5,4},{6,5},{7,6},{9,8},{10,9},{11,10},{13,12},{... | collective-permute-start | bytes 3538952 | tf_op jit(solution)/shard_map/ppermute | solution.py:285
  526.1 69.7 %collective-permute-start.71 = (bf16[1,192,1536]{2,1,0:T(8,128)(2,1)}, bf16[1,192,1536]{2,1,0:T(8,128)(2,1)S(1)}, u32[]{:S(2)}, u32[]{:S(2)}) collective-permute-start(bf16[1,192,1536]{2,1,0:T(8,128)(2,1)} %collective-permute-done.70), channel_id=1, source_target_pairs={{1,0},{2,1},{5,4},{6,5},{9,8},{10,9},{13,12},{14,13},{17,16},{18,1... | collective-permute-start | bytes 1769480 | tf_op jit(solution)/shard_map/ppermute | solution.py:285
  593.5 57.9 %collective-permute-start.69 = (bf16[1,192,1536]{2,1,0:T(8,128)(2,1)}, bf16[1,192,1536]{2,1,0:T(8,128)(2,1)}, u32[]{:S(2)}, u32[]{:S(2)}) collective-permute-start(bf16[1,192,1536]{2,1,0:T(8,128)(2,1)} %bitcast.111), channel_id=1, source_target_pairs={{0,1},{1,2},{2,3},{4,5},{5,6},{6,7},{8,9},{9,10},{10,11},{12,13},{... | collective-permute-start | bytes 1769480 | tf_op jit(solution)/shard_map/ppermute | solution.py:282
  599.9 71.9 %collective-permute-start.65 = (bf16[8,1,48,1536]{3,2,0,1:T(8,128)(2,1)}, bf16[8,1,48,1536]{3,2,0,1:T(8,128)(2,1)}, u32[]{:S(2)}, u32[]{:S(2)}) collective-permute-start(bf16[8,1,48,1536]{3,2,0,1:T(8,128)(2,1)} %collective-permute-done.64), channel_id=1, source_target_pairs={{1,0},{2,1},{5,4},{6,5},{9,8},{10,9},{13,12},{14,13},{17,16},{18,1... | collective-permute-start | bytes 3538952 | tf_op jit(solution)/shard_map/ppermute | solution.py:285
  807.5 65.0 %collective-permute-start.154 = (bf16[8,48,1536]{2,1,0:T(8,128)(2,1)}, bf16[8,48,1536]{2,1,0:T(8,128)(2,1)}, u32[]{:S(2)}, u32[]{:S(2)}) collective-permute-start(bf16[8,48,1536]{2,1,0:T(8,128)(2,1)} %get-tuple-element.58), channel_id=1, source_target_pairs={{3,2},{7,6},{11,10},{15,14},{19,18},{23,22},{27,26},{31,30}} | collective-permute-start | bytes 3538952 | tf_op jit(solution)/shard_map/ppermute | solution.py:312
  819.3 63.0 %collective-permute-start.75 = (bf16[4,256,1536]{2,1,0:T(8,128)(2,1)}, bf16[4,256,1536]{2,1,0:T(8,128)(2,1)}, u32[]{:S(2)}, u32[]{:S(2)}) collective-permute-start(bf16[4,256,1536]{2,1,0:T(8,128)(2,1)} %slice_bitcast_fusion.2), channel_id=1, source_target_pairs={{0,4},{4,0},{8,12},{12,8},{16,20},{20,16},{24,28},{28,24},{1,5},{5... | collective-permute-start | bytes 9437192 | tf_op jit(solution)/shard_map/ppermute | solution.py:218
  917.4 324.8 %collective-permute-start.153 = (bf16[8,48,1536]{2,1,0:T(8,128)(2,1)}, bf16[8,48,1536]{2,1,0:T(8,128)(2,1)}, u32[]{:S(2)}, u32[]{:S(2)}) collective-permute-start(bf16[8,48,1536]{2,1,0:T(8,128)(2,1)} %get-tuple-element.55), channel_id=1, source_target_pairs={{0,1},{1,2},{2,3},{4,5},{5,6},{6,7},{8,9},{9,10},{10,11},{12,13},{... | collective-permute-start | bytes 3538952 | tf_op jit(solution)/shard_map/ppermute | solution.py:309
  931.3 311.0 %collective-permute-start.156 = (bf16[8,48,1536]{2,1,0:T(8,128)(2,1)}, bf16[8,48,1536]{2,1,0:T(8,128)(2,1)}, u32[]{:S(2)}, u32[]{:S(2)}) collective-permute-start(bf16[8,48,1536]{2,1,0:T(8,128)(2,1)} %fusion.41), channel_id=1, source_target_pairs={{1,0},{2,1},{3,2},{5,4},{6,5},{7,6},{9,8},{10,9},{11,10},{13,12},{... | collective-permute-start | bytes 3538952 | tf_op jit(solution)/shard_map/ppermute | solution.py:312
  1113.0 215.3 %collective-permute-start.140 = (bf16[4,192,1536]{2,1,0:T(8,128)(2,1)}, bf16[4,192,1536]{2,1,0:T(8,128)(2,1)}, u32[]{:S(2)}, u32[]{:S(2)}) collective-permute-start(bf16[4,192,1536]{2,1,0:T(8,128)(2,1)} %slice_bitcast_fusion.4), channel_id=1, source_target_pairs={{0,4},{4,0},{8,12},{12,8},{16,20},{20,16},{24,28},{28,24},{1,5},{5... | collective-permute-start | bytes 7077896 | tf_op jit(solution)/shard_map/ppermute | solution.py:218
  1123.3 226.7 %collective-permute-start.129 = (bf16[4,96,3072]{2,1,0:T(8,128)(2,1)}, bf16[4,96,3072]{2,1,0:T(8,128)(2,1)}, u32[]{:S(2)}, u32[]{:S(2)}) collective-permute-start(bf16[4,96,3072]{2,1,0:T(8,128)(2,1)} %slice_bitcast_fusion.6), channel_id=1, source_target_pairs={{0,4},{4,0},{8,12},{12,8},{16,20},{20,16},{24,28},{28,24},{1,5},{5... | collective-permute-start | bytes 7077896 | tf_op jit(solution)/shard_map/ppermute | solution.py:218
  1328.3 134.4 %collective-permute-start.95 = (bf16[256,1536]{1,0:T(8,128)(2,1)}, bf16[256,1536]{1,0:T(8,128)(2,1)S(1)}, u32[]{:S(2)}, u32[]{:S(2)}) collective-permute-start(bf16[256,1536]{1,0:T(8,128)(2,1)} %get-tuple-element.73), channel_id=1, source_target_pairs={{0,1},{1,2},{2,3},{4,5},{5,6},{6,7},{8,9},{9,10},{10,11},{12,13},{... | collective-permute-start | bytes 2359304 | tf_op jit(solution)/shard_map/ppermute | solution.py:309
  1382.7 83.9 %collective-permute-start.98 = (bf16[256,1536]{1,0:T(8,128)(2,1)}, bf16[256,1536]{1,0:T(8,128)(2,1)}, u32[]{:S(2)}, u32[]{:S(2)}) collective-permute-start(bf16[256,1536]{1,0:T(8,128)(2,1)} %fusion.65), channel_id=1, source_target_pairs={{1,0},{2,1},{3,2},{5,4},{6,5},{7,6},{9,8},{10,9},{11,10},{13,12},{... | collective-permute-start | bytes 2359304 | tf_op jit(solution)/shard_map/ppermute | solution.py:312
  (351 other events, 8067.8 us)
Sparse Core Ops, SparseCore 0:
  1235.0 56.5 all-gather.5

commit v2 on v1

v2 whole, which is shorter than its diff:
```python
import math

import jax
import jax.numpy as jnp
from jax import lax
from jax.experimental import pallas as pl
from jax.experimental.pallas import tpu as pltpu
from jax.sharding import PartitionSpec as P

D = 1536
HEADS = 24
HEAD_DIM = 64
FF = 6144
CTX_LEN = 128
TFEAT = 256
CLIPS = 3
TOKEN_ROWS = 128


EPSILON = 1e-05
SCORE_SCALE = 0.125
MASKED = -1e30
PRECISE = lax.Precision.HIGHEST


def contract_last(left, right):
    return lax.dot_general(left, right, (((1,), (1,)), ((), ())), preferred_element_type=jnp.float32)


def contract(left, right):
    return lax.dot_general(left, right, (((1,), (0,)), ((), ())), preferred_element_type=jnp.float32)


def lane_of(width=2 * HEAD_DIM):
    return lax.broadcasted_iota(jnp.int32, (1, width), 1)


def attend_rows(query, keys, value_pair, query_clip, key_clip):
    first = lane_of() < HEAD_DIM
    allowed = query_clip == key_clip
    zero = jnp.zeros((), query.dtype)
    outs, tops = [], []
    for head in range(2):
        mine = first if head == 0 else jnp.logical_not(first)
        scores = contract_last(jnp.where(mine, query, zero), keys)
        scores = jnp.where(allowed, scores, MASKED)
        top = jnp.max(scores, axis=1, keepdims=True)
        weights = jnp.exp(scores - top).astype(jnp.bfloat16)
        mixed = contract(weights, value_pair[head])
        place_sum = HEAD_DIM if head == 0 else 0
        total = mixed[:, place_sum : place_sum + 1]
        outs.append(mixed / total)
        tops.append(top + jnp.log(total))
    mixture = jnp.where(first, outs[0], outs[1])
    return mixture, jnp.where(first, tops[0], tops[1])


def value_with_ones(values):
    first = lane_of() < HEAD_DIM
    one = jnp.ones((), values.dtype)
    return jnp.where(first, values, one), jnp.where(first, one, values)


def attend_rows_back(query, keys, keys_turned, values, grads, mixture, level, query_clip, key_clip):
    first = lane_of() < HEAD_DIM
    allowed = key_clip == query_clip
    zero = jnp.zeros((), query.dtype)
    product = jnp.transpose(grads.astype(jnp.float32) * mixture)
    level_turned = jnp.transpose(level)
    head_rows = lax.broadcasted_iota(jnp.int32, (2 * HEAD_DIM, 1), 0) < HEAD_DIM
    parts = []
    for head in range(2):
        mine = first if head == 0 else jnp.logical_not(first)
        low, high = head * HEAD_DIM, (head + 1) * HEAD_DIM
        query_own = jnp.where(mine, query, zero)
        grads_own = jnp.where(mine, grads, zero)
        scores = contract_last(keys, query_own)
        scores = jnp.where(allowed, scores, MASKED)
        weights = jnp.exp(scores - level_turned[low : low + 1])
        grad_weights = contract_last(values, grads_own)
        diagonal = jnp.sum(product[low:high], axis=0, keepdims=True)
        grad_scores = (weights * (grad_weights - diagonal)).astype(jnp.bfloat16)
        key_grad = contract(grad_scores, query_own)
        value_grad = contract(weights.astype(jnp.bfloat16), grads_own)
        parts.append((contract(keys_turned, grad_scores), key_grad, value_grad))
    query_turned = jnp.where(head_rows, parts[0][0], parts[1][0])
    return query_turned, parts[0][1] + parts[1][1], parts[0][2] + parts[1][2]


def swap_halves(values):
    quarter = HEAD_DIM // 2
    down = pltpu.roll(values, 2 * HEAD_DIM - quarter, 1)
    up = pltpu.roll(values, quarter, 1)
    return jnp.where(lane_of() % HEAD_DIM < quarter, down, up)


def self_forward_kernel(
    projected, cosine, sine, clip_column, clip_row, mixed, mixed_wide, level, low, value_pair
):
    rows = mixed.shape[0]
    pair = 2 * HEAD_DIM
    block = min(256, rows)
    for part, scale in ((0, SCORE_SCALE), (1, 1.0)):
        values = projected[:, part * pair : (part + 1) * pair]
        turned = values * cosine[...] + swap_halves(values) * sine[...]
        low[:, part * pair : (part + 1) * pair] = turned.astype(jnp.bfloat16) * jnp.bfloat16(scale)
    values = projected[:, 2 * pair : 3 * pair].astype(jnp.bfloat16)
    low[:, 2 * pair : 3 * pair] = values
    value_pair[0], value_pair[1] = value_with_ones(values)

    def step(index, carry):
        place = pl.ds(pl.multiple_of(index * block, block), block)
        mixture, tops = attend_rows(
            low[place, 0:pair],
            low[:, pair : 2 * pair],
            (value_pair[0], value_pair[1]),
            clip_column[place, :],
            clip_row[...],
        )
        mixed[place, :] = mixture.astype(jnp.bfloat16)
        mixed_wide[place, :] = mixture
        level[place, :] = tops
        return carry

    lax.fori_loop(0, rows // block, step, 0)


def self_backward_kernel(
    low, grads, mixed_wide, level, cosine, sine, clip_column, clip_row, out, keys_turned, totals
):
    rows = grads.shape[0]
    pair = 2 * HEAD_DIM
    block = min(256, rows)
    keys_turned[...] = jnp.transpose(low[:, pair : 2 * pair])
    totals[...] = jnp.zeros_like(totals)
    out[rows:, 0:pair] = jnp.zeros((out.shape[0] - rows, pair), jnp.bfloat16)

    def step(index, carry):
        start = pl.multiple_of(index * block, block)
        place = pl.ds(start, block)
        query_turned, key_grad, value_grad = attend_rows_back(
            low[place, 0:pair],
            low[:, pair : 2 * pair],
            keys_turned[...],
            low[:, 2 * pair : 3 * pair],
            grads[place, :],
            mixed_wide[place, :],
            level[place, :],
            clip_row[:, place],
            clip_column[...],
        )
        query_grad = jnp.transpose(query_turned) * SCORE_SCALE
        back = query_grad * cosine[place, :] - swap_halves(query_grad) * sine[place, :]
        out[place, 0:pair] = back.astype(jnp.bfloat16)
        totals[0] += key_grad
        totals[1] += value_grad
        return carry

    lax.fori_loop(0, rows // block, step, 0)
    key_grad = totals[0]
    back = key_grad * cosine[...] - swap_halves(key_grad) * sine[...]
    out[:, pair : 2 * pair] = back.astype(jnp.bfloat16)
    out[:, 2 * pair : 3 * pair] = totals[1].astype(jnp.bfloat16)


def cross_forward_kernel(query, keys, values, clip_column, clip_row, mixed, mixed_wide, level):
    mixture, tops = attend_rows(
        query[...] * jnp.bfloat16(SCORE_SCALE),
        keys[...],
        value_with_ones(values[...]),
        clip_column[...],
        clip_row[...],
    )
    mixed[...] = mixture.astype(jnp.bfloat16)
    mixed_wide[...] = mixture
    level[...] = tops


def cross_backward_kernel(
    query, keys, values, grads, mixed_wide, level, clip_column, clip_row, query_out, key_out, value_out
):
    query_turned, key_grad, value_grad = attend_rows_back(
        query[...] * jnp.bfloat16(SCORE_SCALE),
        keys[...],
        jnp.transpose(keys[...]),
        values[...],
        grads[...],
        mixed_wide[...],
        level[...],
        clip_row[...],
        clip_column[...],
    )
    query_out[...] = (jnp.transpose(query_turned) * SCORE_SCALE).astype(jnp.bfloat16)
    key_out[...] = key_grad.astype(jnp.bfloat16)
    value_out[...] = value_grad.astype(jnp.bfloat16)


def whole(array):
    return pl.BlockSpec(array.shape, lambda p: (0,) * array.ndim)


def lanes(rows, width=2 * HEAD_DIM, offset=0):
    return pl.BlockSpec((rows, width), lambda p: (0, p + offset))


KERNEL_PARAMS = pltpu.CompilerParams(
    dimension_semantics=("arbitrary",), vmem_limit_bytes=48 * 1024 * 1024
)


def cost(heads, queries, keys, dots):
    return pl.CostEstimate(
        flops=2 * dots * heads * queries * keys * 2 * HEAD_DIM,
        bytes_accessed=heads * HEAD_DIM * (queries + keys) * 16,
        transcendentals=heads * queries * keys,
    )


def self_forward(projected, cosine, sine, clip_column, clip_row, rows):
    total, width = projected.shape
    pair = 2 * HEAD_DIM
    pairs = width // (3 * pair)
    return pl.pallas_call(
        self_forward_kernel,
        grid=(pairs,),
        in_specs=[
            lanes(total, 3 * pair),
            whole(cosine),
            whole(sine),
            whole(clip_column),
            whole(clip_row),
        ],
        out_specs=[lanes(rows), lanes(rows), lanes(rows), lanes(total, 3 * pair)],
        out_shape=[
            jax.ShapeDtypeStruct((rows, pairs * pair), jnp.bfloat16),
            jax.ShapeDtypeStruct((rows, pairs * pair), jnp.float32),
            jax.ShapeDtypeStruct((rows, pairs * pair), jnp.float32),
            jax.ShapeDtypeStruct((total, width), jnp.bfloat16),
        ],
        scratch_shapes=[pltpu.VMEM((2, total, pair), jnp.bfloat16)],
        compiler_params=KERNEL_PARAMS,
        cost_estimate=cost(2 * pairs, rows, total, 2),
    )(projected, cosine, sine, clip_column, clip_row)


def self_backward(low, grads, mixed_wide, level, cosine, sine, clip_column, clip_row):
    total, width = low.shape
    rows = grads.shape[0]
    pair = 2 * HEAD_DIM
    pairs = width // (3 * pair)
    return pl.pallas_call(
        self_backward_kernel,
        grid=(pairs,),
        in_specs=[
            lanes(total, 3 * pair),
            lanes(rows),
            lanes(rows),
            lanes(rows),
            whole(cosine),
            whole(sine),
            whole(clip_column),
            whole(clip_row),
        ],
        out_specs=lanes(total, 3 * pair),
        out_shape=jax.ShapeDtypeStruct((total, width), jnp.bfloat16),
        scratch_shapes=[
            pltpu.VMEM((pair, total), jnp.bfloat16),
            pltpu.VMEM((2, total, pair), jnp.float32),
        ],
        compiler_params=KERNEL_PARAMS,
        cost_estimate=cost(2 * pairs, rows, total, 5),
    )(low, grads, mixed_wide, level, cosine, sine, clip_column, clip_row)


def cross_forward(query, keyval, clip_column, clip_row):
    rows, width = query.shape
    keys = keyval.shape[0]
    pair = 2 * HEAD_DIM
    pairs = width // pair
    return pl.pallas_call(
        cross_forward_kernel,
        grid=(pairs,),
        in_specs=[
            lanes(rows),
            lanes(keys),
            lanes(keys, offset=pairs),
            whole(clip_column),
            whole(clip_row),
        ],
        out_specs=[lanes(rows), lanes(rows), lanes(rows)],
        out_shape=[
            jax.ShapeDtypeStruct((rows, width), jnp.bfloat16),
            jax.ShapeDtypeStruct((rows, width), jnp.float32),
            jax.ShapeDtypeStruct((rows, width), jnp.float32),
        ],
        compiler_params=KERNEL_PARAMS,
        cost_estimate=cost(2 * pairs, rows, keys, 2),
    )(query, keyval, keyval, clip_column, clip_row)


def cross_backward(query, keyval, grads, mixed_wide, level, clip_column, clip_row):
    rows, width = query.shape
    keys = keyval.shape[0]
    pair = 2 * HEAD_DIM
    pairs = width // pair
    return pl.pallas_call(
        cross_backward_kernel,
        grid=(pairs,),
        in_specs=[
            lanes(rows),
            lanes(keys),
            lanes(keys, offset=pairs),
            lanes(rows),
            lanes(rows),
            lanes(rows),
            whole(clip_column),
            whole(clip_row),
        ],
        out_specs=[lanes(rows), lanes(keys), lanes(keys)],
        out_shape=[
            jax.ShapeDtypeStruct((rows, width), jnp.bfloat16),
            jax.ShapeDtypeStruct((keys, width), jnp.bfloat16),
            jax.ShapeDtypeStruct((keys, width), jnp.bfloat16),
        ],
        compiler_params=KERNEL_PARAMS,
        cost_estimate=cost(2 * pairs, rows, keys, 5),
    )(query, keyval, keyval, grads, mixed_wide, level, clip_column, clip_row)


def norm_forward(hidden):
    centre = jnp.mean(hidden, axis=-1, keepdims=True)
    centred = hidden - centre
    spread = jnp.mean(centred * centred, axis=-1, keepdims=True)
    scale_inv = lax.rsqrt(spread + EPSILON)
    return (centred * scale_inv, scale_inv)


def norm_backward(grad_norm, normalized, scale_inv, gain_vector):
    scaled = grad_norm * gain_vector
    gain_grad = jnp.sum(grad_norm * normalized, axis=0)
    inner = (
        scaled
        - jnp.mean(scaled, axis=-1, keepdims=True)
        - normalized * jnp.mean(scaled * normalized, axis=-1, keepdims=True)
    )
    return (scale_inv * inner, gain_grad)


def rotary_tables(positions):
    half_width = HEAD_DIM // 2
    frequencies = jnp.exp(
        -math.log(10000.0) * jnp.arange(half_width, dtype=jnp.float32) / half_width
    )
    angles = positions[:, None] * frequencies
    cosine, sine = jnp.cos(angles), jnp.sin(angles)
    return (
        jnp.concatenate([cosine, cosine, cosine, cosine], axis=1),
        jnp.concatenate([-sine, sine, -sine, sine], axis=1),
    )


def time_features(step_values):
    half_width = TFEAT // 2
    frequencies = jnp.exp(
        -math.log(10000.0) * jnp.arange(half_width, dtype=jnp.float32) / half_width
    )
    angles = step_values.astype(jnp.float32)[..., None] * frequencies
    return jnp.concatenate([jnp.cos(angles), jnp.sin(angles)], axis=-1)


def gated_back(hidden_grad, gate_part, upward):
    gate_sigmoid = jax.nn.sigmoid(gate_part)
    gate_grad = hidden_grad * upward * gate_sigmoid * (1.0 + gate_part * (1.0 - gate_sigmoid))
    upward_grad = hidden_grad * gate_part * gate_sigmoid
    return jnp.concatenate([gate_grad, upward_grad], axis=-1).astype(jnp.bfloat16)


def xor_pairs(count, bit):
    return [(k, k ^ bit) for k in range(count)]


def place(buffer, block, dim, index):
    starts = [0] * buffer.ndim
    starts[dim] = index
    return lax.dynamic_update_slice(buffer, block, tuple(starts))


def take(array, index, dim=0):
    return lax.dynamic_slice_in_dim(array, index, 1, axis=dim)


def plane_bits(count):
    return [1 << b for b in range(1, count.bit_length() - 1)]


def chip_gather(values, axis):
    count = lax.axis_size(axis)
    bits = plane_bits(count)
    if len(bits) == 2 and values.shape[0] % 32 == 0:
        first, second = bits
        half = values.shape[0] // 2
        by_first = lax.ppermute(values, axis, xor_pairs(count, first))
        by_second = lax.ppermute(values, axis, xor_pairs(count, second))
        far_one = lax.ppermute(by_first[:half], axis, xor_pairs(count, second))
        far_two = lax.ppermute(by_second[half:], axis, xor_pairs(count, first))
        far = jnp.concatenate([far_one, far_two], axis=0)
        same = jnp.stack([values, by_first, by_second, far], axis=0)
    else:
        same = values[None]
        for bit in bits:
            same = jnp.concatenate([same, lax.ppermute(same, axis, xor_pairs(count, bit))], axis=0)
    if count == 1:
        return same
    other = lax.ppermute(same, axis, xor_pairs(count, 1))
    return jnp.stack([same, other], axis=1).reshape((count,) + values.shape)


def chip_gather_ordered(values, axis, me):
    count = lax.axis_size(axis)
    bits = plane_bits(count)
    if len(bits) == 2 and values.shape[0] % 2 == 0:
        first, second = bits
        half = values.shape[0] // 2
        chip, core = me // 2, me % 2
        by_first = lax.ppermute(values, axis, xor_pairs(count, first))
        by_second = lax.ppermute(values, axis, xor_pairs(count, second))
        far_one = lax.ppermute(by_first[:half], axis, xor_pairs(count, second))
        far_two = lax.ppermute(by_second[half:], axis, xor_pairs(count, first))
        same = jnp.zeros((count // 2,) + values.shape, values.dtype)
        same = place(same, values[None], 0, chip)
        same = place(same, by_first[None], 0, chip ^ 1)
        same = place(same, by_second[None], 0, chip ^ 2)
        far = jnp.concatenate([far_one, far_two], axis=0)
        same = place(same, far[None], 0, chip ^ 3)
        other = lax.ppermute(same, axis, xor_pairs(count, 1))
        result = jnp.zeros((count // 2, 2) + values.shape, values.dtype)
        result = place(result, same[:, None], 1, core)
        result = place(result, other[:, None], 1, 1 - core)
        return result.reshape((count,) + values.shape)
    return lax.all_gather(values, axis)


def chip_scatter(parts, axis):
    count = lax.axis_size(axis)
    if count == 1:
        return parts[0].astype(jnp.float32)
    low = jnp.bfloat16
    pairs = parts.reshape((count // 2, 2) + parts.shape[1:])
    got = lax.ppermute(pairs[:, 1].astype(low), axis, xor_pairs(count, 1))
    total = pairs[:, 0].astype(jnp.float32) + got.astype(jnp.float32)
    return sum_over_chips([total[r] for r in range(count // 2)], axis)


def chip_scatter_ordered(parts, axis, me):
    count = lax.axis_size(axis)
    if count == 1:
        return parts[0].astype(jnp.float32)
    low = jnp.bfloat16
    chip, core = me // 2, me % 2
    pairs = parts.reshape((count // 2, 2) + parts.shape[1:])
    got = lax.ppermute(take(pairs, 1 - core, 1).astype(low), axis, xor_pairs(count, 1))
    total = (take(pairs, core, 1).astype(jnp.float32) + got.astype(jnp.float32))[:, 0]
    return sum_over_chips([take(total, chip ^ r)[0] for r in range(count // 2)], axis)


def sum_over_chips(blocks, axis):
    count = lax.axis_size(axis)
    bits = plane_bits(count)
    low, wide = jnp.bfloat16, jnp.float32
    if len(bits) == 2 and blocks[0].shape[0] % 2 == 0:
        first, second = bits
        half = blocks[0].shape[0] // 2
        far_one = lax.ppermute(blocks[3][:half].astype(low), axis, xor_pairs(count, first))
        far_two = lax.ppermute(blocks[3][half:].astype(low), axis, xor_pairs(count, second))
        to_second = jnp.concatenate(
            [(blocks[2][:half] + far_one.astype(wide)).astype(low), blocks[2][half:].astype(low)],
            axis=0,
        )
        to_first = jnp.concatenate(
            [blocks[1][:half].astype(low), (blocks[1][half:] + far_two.astype(wide)).astype(low)],
            axis=0,
        )
        by_first = lax.ppermute(to_first, axis, xor_pairs(count, first))
        by_second = lax.ppermute(to_second, axis, xor_pairs(count, second))
        return blocks[0] + by_first.astype(wide) + by_second.astype(wide)
    total = jnp.stack(blocks, axis=0)
    for bit in reversed(bits):
        middle = total.shape[0] // 2
        got = lax.ppermute(total[middle:].astype(low), axis, xor_pairs(count, bit))
        total = total[:middle] + got.astype(wide)
    return total[0]


def line_send(blocks, axis, me):
    count = lax.axis_size(axis)
    return [
        lax.ppermute(
            take(blocks, lax.rem(me + step, count)),
            axis,
            [(k, (k + step) % count) for k in range(count)],
        )
        for step in range(1, count)
    ]


def line_exchange(blocks, axis, me):
    count = lax.axis_size(axis)
    result = blocks
    for step, got in enumerate(line_send(blocks, axis, me), 1):
        result = place(result, got, 0, lax.rem(me - step + count, count))
    return result


def line_gather(values, axis, me):
    count = lax.axis_size(axis)
    result = place(jnp.zeros((count,) + values.shape, values.dtype), values[None], 0, me)
    for step in range(1, count):
        got = lax.ppermute(values, axis, [(k, (k + step) % count) for k in range(count)])
        result = place(result, got[None], 0, lax.rem(me - step + count, count))
    return result


def line_scatter(parts, axis, me):
    count = lax.axis_size(axis)

    def part(index):
        return take(parts, index)[0].astype(jnp.float32)

    total = part(me)
    from_left = from_right = None
    for step in range(1, count):
        to_right = part(jnp.minimum(me + count - step, count - 1))
        to_left = part(jnp.maximum(me - count + step, 0))
        if step > 1:
            to_right = to_right + from_left.astype(jnp.float32)
            to_left = to_left + from_right.astype(jnp.float32)
        from_left = lax.ppermute(
            to_right.astype(jnp.bfloat16), axis, [(k, k + 1) for k in range(0, step)]
        )
        from_right = lax.ppermute(
            to_left.astype(jnp.bfloat16),
            axis,
            [(k + 1, k) for k in range(count - 1 - step, count - 1)],
        )
    if count > 1:
        total = total + from_left.astype(jnp.float32) + from_right.astype(jnp.float32)
    return total


def dot(left, right):
    return jnp.dot(left, right, preferred_element_type=jnp.float32)


def on_device(
    latents,
    context,
    clip_bounds,
    timesteps,
    self_inward,
    self_outward,
    cross_query,
    cross_keyval,
    cross_return,
    time_weight,
    expand_weight,
    shrink_weight,
    gain_attend,
    gain_cross,
    gain_feed,
    cotangent,
):
    f32, bf16 = jnp.float32, jnp.bfloat16
    frame_count = latents.shape[1]
    dp_count = lax.axis_size("dp")
    seq_count = lax.axis_size("seq")
    dp_place = lax.axis_index("dp")
    seq_place = lax.axis_index("seq")
    row_length = frame_count * seq_count
    text_count = context.shape[1]
    own_heads = HEADS // seq_count
    pairs = (own_heads + 1) // 2
    own_width = own_heads * HEAD_DIM
    pair_width = 2 * HEAD_DIM
    padded = pairs * pair_width
    hidden_width = FF // dp_count
    shard = D // (dp_count * seq_count)
    time_shard = TFEAT // (dp_count * seq_count)
    place_all = dp_place * seq_count + seq_place

    all_frames = jnp.arange(row_length, dtype=jnp.int32)
    second_start, third_start = clip_bounds[0, 0], clip_bounds[0, 1]
    frame_clips = (all_frames >= second_start).astype(jnp.int32) + (
        all_frames >= third_start
    ).astype(jnp.int32)
    clip_starts = jnp.where(
        frame_clips == 0, 0, jnp.where(frame_clips == 1, second_start, third_start)
    )
    token_slots = jnp.arange(TOKEN_ROWS, dtype=jnp.int32)
    clips = jnp.concatenate(
        [frame_clips, jnp.where(token_slots < CLIPS, token_slots, -1)]
    ).astype(f32)
    positions = jnp.concatenate(
        [all_frames - clip_starts + 1, jnp.zeros(TOKEN_ROWS, jnp.int32)]
    ).astype(f32)
    cosine, sine = rotary_tables(positions)
    clip_column, clip_row = clips[:, None], clips[None, :]
    own_clips = lax.dynamic_slice_in_dim(clips, seq_place * frame_count, frame_count)
    text_clips = (jnp.arange(text_count, dtype=jnp.int32) // CTX_LEN).astype(f32)

    inward_blocks = (
        self_inward.reshape(shard, 3, seq_count, own_width)
        .transpose(2, 0, 1, 3)
        .reshape(seq_count, shard, 3 * own_width)
    )
    extra = jnp.concatenate([time_weight.reshape(-1), gain_attend, gain_cross, gain_feed])
    extra_rows = -(-extra.shape[0] // (3 * own_width))
    sent_rows = -(-(shard + extra_rows) // 16) * 16
    extra = jnp.pad(extra, (0, (sent_rows - shard) * 3 * own_width - extra.shape[0]))
    extra = jnp.broadcast_to(
        extra.reshape(1, sent_rows - shard, 3 * own_width),
        (seq_count, sent_rows - shard, 3 * own_width),
    )
    inward_columns = line_exchange(
        jnp.concatenate([inward_blocks, extra], axis=1), "seq", seq_place
    )
    row_latents = line_gather(latents[0], "seq", seq_place).reshape(row_length, D)
    inward_all = chip_gather_ordered(inward_columns, "dp", dp_place)
    inward_own = inward_all[:, :, :shard].reshape(D, 3, own_width)
    inward_own = jnp.pad(inward_own, ((0, 0), (0, 0), (0, padded - own_width)))
    inward_own = (
        inward_own.reshape(D, 3, pairs, pair_width).transpose(0, 2, 1, 3).reshape(D, 3 * padded)
    )
    extra_all = inward_all[:, :, shard:].reshape(dp_count, seq_count, -1)
    time_full = extra_all[:, :, : time_shard * D].reshape(TFEAT, D)
    gains_all = extra_all[:, :, time_shard * D : time_shard * D + 3 * shard]
    gains_all = gains_all.reshape(dp_count, seq_count, 3, shard).astype(f32)
    attend_gain = gains_all[:, :, 0].reshape(D)
    cross_gain = gains_all[:, :, 1].reshape(D)
    feed_gain = gains_all[:, :, 2].reshape(D)
    steps_all = lax.all_gather(timesteps, "dp", axis=0, tiled=True)

    packed = jnp.concatenate(
        [
            self_outward,
            cross_keyval[:, :D],
            cross_keyval[:, D:],
            cross_query,
            cross_return,
        ],
        axis=0,
    )
    lined = lax.all_gather(packed, "seq")
    cotangent_all = chip_gather(cotangent[0], "dp").reshape(dp_count * frame_count, D)
    outward_full = chip_gather_ordered(lined[:, :shard], "dp", dp_place).reshape(D, D)
    keyval_rows = chip_gather_ordered(lined[:, shard : 2 * shard], "dp", dp_place)
    keyval_full = jnp.concatenate(
        [
            keyval_rows[:, :, : shard // 2].reshape(D // 2, D),
            keyval_rows[:, :, shard // 2 :].reshape(D // 2, D),
        ],
        axis=1,
    )
    query_full = chip_gather_ordered(lined[:, 2 * shard : 3 * shard], "dp", dp_place).reshape(D, D)
    return_full = chip_gather_ordered(lined[:, 3 * shard :], "dp", dp_place).reshape(D, D)

    expand_blocks = (
        expand_weight.reshape(shard, 2, dp_count, hidden_width)
        .transpose(2, 0, 1, 3)
        .reshape(dp_count, shard, 2 * hidden_width)
    )
    expand_part = lax.all_to_all(expand_blocks, "dp", 0, 0, tiled=True)
    expand_own = (
        lax.all_gather(expand_part, "seq", axis=1).reshape(D, 2 * hidden_width)
    )
    shrink_own = lax.all_gather(shrink_weight, "seq", tiled=True)

    feats_low = time_features(timesteps[0]).astype(bf16)
    token = dot(feats_low, time_full)
    token_norm, token_inverse = norm_forward(token)
    token_low = jnp.pad(
        (token_norm * attend_gain).astype(bf16), ((0, TOKEN_ROWS - CLIPS), (0, 0))
    )
    row_norm, row_inverse = norm_forward(row_latents.astype(f32))
    row_low = jnp.concatenate([(row_norm * attend_gain).astype(bf16), token_low], axis=0)
    projected = dot(row_low, inward_own)
    attended, attended_wide, self_level, projected_low = self_forward(
        projected, cosine, sine, clip_column, clip_row, row_length
    )
    attended_low = (
        line_exchange(
            attended[:, :own_width].reshape(seq_count, frame_count, own_width), "seq", seq_place
        )
        .transpose(1, 0, 2)
        .reshape(frame_count, D)
    )
    after_self = latents[0].astype(f32) + dot(attended_low, outward_full)

    norm_two, inverse_two = norm_forward(after_self)
    normed_two = (norm_two * cross_gain).astype(bf16)
    cross_heads = dot(normed_two, query_full).astype(bf16)
    keyval = dot(context[0], keyval_full).astype(bf16)
    crossed, crossed_wide, cross_level = cross_forward(
        cross_heads, keyval, own_clips[:, None], text_clips[None, :]
    )
    after_cross = after_self + dot(crossed, return_full)

    norm_three, inverse_three = norm_forward(after_cross)
    normed_three = (norm_three * feed_gain).astype(bf16)
    frames_all = chip_gather(normed_three, "dp").reshape(dp_count * frame_count, D)
    gate_up = dot(frames_all, expand_own)
    gate_part = gate_up[:, :hidden_width]
    upward = gate_up[:, hidden_width:]
    hidden_low = (jax.nn.silu(gate_part) * upward).astype(bf16)
    hidden_grad = dot(cotangent_all, shrink_own.T)
    expand_low = gated_back(hidden_grad, gate_part, upward)
    feed_parts = dot(expand_low, expand_own.T).astype(bf16)
    feed_norm_grad = chip_scatter(feed_parts.reshape(dp_count, frame_count, D), "dp")
    expand_grad = dot(frames_all.T, expand_low).astype(bf16)
    expand_sum = lax.psum_scatter(
        expand_grad.reshape(dp_count, seq_count, shard, 2 * hidden_width).transpose(1, 0, 2, 3),
        "seq",
        scatter_dimension=0,
    )
    shrink_part = dot(hidden_low.T, cotangent_all).astype(bf16)
    grad_shrink = lax.psum_scatter(
        shrink_part, "seq", scatter_dimension=0, tiled=True
    ).astype(f32)
    out_parts = dot(hidden_low, shrink_own).astype(bf16)
    fed = chip_scatter(out_parts.reshape(dp_count, frame_count, D), "dp")
    block_output = (after_cross + fed).astype(bf16)
    grad_expand = (
        lax.all_to_all(expand_sum, "dp", 0, 0, tiled=True)
        .reshape(dp_count, shard, 2, hidden_width)
        .transpose(1, 2, 0, 3)
        .reshape(shard, 2 * FF)
        .astype(f32)
    )

    feed_term, feed_gain_part = norm_backward(
        feed_norm_grad, norm_three, inverse_three, feed_gain
    )
    after_cross_grad = cotangent[0].astype(f32) + feed_term
    return_low = after_cross_grad.astype(bf16)
    crossed_grad = dot(return_low, return_full.T).astype(bf16)
    cross_query_low, cross_key_low, cross_value_low = cross_backward(
        cross_heads,
        keyval,
        crossed_grad,
        crossed_wide,
        cross_level,
        text_clips[:, None],
        own_clips[None, :],
    )
    cross_norm_grad = dot(cross_query_low, query_full.T)
    cross_term, cross_gain_part = norm_backward(
        cross_norm_grad, norm_two, inverse_two, cross_gain
    )
    after_self_grad = after_cross_grad + cross_term
    outward_low = after_self_grad.astype(bf16)
    attended_grad = dot(outward_low, outward_full.T).astype(bf16)
    attended_grad_own = line_exchange(
        attended_grad.reshape(frame_count, seq_count, own_width).transpose(1, 0, 2),
        "seq",
        seq_place,
    ).reshape(row_length, own_width)
    attended_grad_own = jnp.pad(attended_grad_own, ((0, 0), (0, padded - own_width)))

    def column_sum(partial):
        shaped = partial.astype(bf16).reshape(dp_count, seq_count, -1, D)
        return chip_scatter_ordered(shaped, "dp", dp_place)

    columns = jnp.concatenate(
        [
            column_sum(dot(crossed.T, return_low)),
            column_sum(dot(context[0].T, cross_key_low)),
            column_sum(dot(context[0].T, cross_value_low)),
            column_sum(dot(normed_two.T, cross_query_low)),
            column_sum(dot(attended_low.T, outward_low)),
        ],
        axis=1,
    )
    whole_sums = lax.psum_scatter(columns.astype(bf16), "seq", scatter_dimension=0).astype(f32)
    grad_return = whole_sums[:shard]
    grad_keyval = jnp.concatenate(
        [whole_sums[shard : shard + shard // 2], whole_sums[shard + shard // 2 : 2 * shard]],
        axis=1,
    )
    grad_query = whole_sums[2 * shard : 3 * shard]
    grad_outward = whole_sums[3 * shard :]

    inward_low = self_backward(
        projected_low,
        attended_grad_own,
        attended_wide,
        self_level,
        cosine,
        sine,
        clip_column,
        clip_row,
    )
    attend_parts = dot(inward_low, inward_own.T)
    attend_norm_grad = line_scatter(
        attend_parts[:row_length].reshape(seq_count, frame_count, D), "seq", seq_place
    )
    own_norm = lax.dynamic_slice_in_dim(row_norm, seq_place * frame_count, frame_count, axis=0)
    own_inverse = lax.dynamic_slice_in_dim(
        row_inverse, seq_place * frame_count, frame_count, axis=0
    )
    attend_term, _ = norm_backward(attend_norm_grad, own_norm, own_inverse, attend_gain)
    latents_grad = (after_self_grad + attend_term)[None]

    inward_grad = dot(row_low.T, inward_low).astype(bf16)
    inward_grad = (
        inward_grad.reshape(D, pairs, 3, pair_width)
        .transpose(0, 2, 1, 3)
        .reshape(D, 3, padded)[:, :, :own_width]
    )
    inward_sum = chip_scatter_ordered(
        inward_grad.reshape(dp_count, seq_count, shard, 3 * own_width), "dp", dp_place
    )
    grad_inward = (
        line_exchange(inward_sum.astype(bf16), "seq", seq_place)
        .reshape(seq_count, shard, 3, own_width)
        .transpose(1, 2, 0, 3)
        .reshape(shard, 3 * D)
        .astype(f32)
    )

    token_term, token_gain_part = norm_backward(
        attend_parts[row_length : row_length + CLIPS], token_norm, token_inverse, attend_gain
    )
    attend_gain_part = jnp.sum(attend_parts[:row_length] * row_norm, axis=0) + token_gain_part
    small = jnp.concatenate(
        [token_term, attend_gain_part[None], cross_gain_part[None], feed_gain_part[None]], axis=0
    )
    device_count = dp_count * seq_count
    small_all = lax.all_to_all(
        jnp.broadcast_to(small[None], (device_count,) + small.shape),
        ("dp", "seq"),
        0,
        0,
        tiled=True,
    )
    small_sum = jnp.sum(small_all.reshape(dp_count, seq_count, CLIPS + 3, D), axis=1)
    feats_all = time_features(steps_all).astype(bf16).astype(f32)
    feats_own = lax.dynamic_slice_in_dim(feats_all, place_all * time_shard, time_shard, axis=2)
    grad_time = jnp.einsum(
        "rct,rcn->tn",
        feats_own,
        small_sum[:, :CLIPS],
        precision=PRECISE,
        preferred_element_type=f32,
    )
    gain_sums = lax.dynamic_slice_in_dim(
        jnp.sum(small_sum[:, CLIPS:], axis=0), place_all * shard, shard, axis=1
    )
    return (
        block_output[None],
        latents_grad,
        grad_inward,
        grad_outward,
        grad_query,
        grad_keyval,
        grad_return,
        grad_time,
        grad_expand,
        grad_shrink,
        gain_sums[0],
        gain_sums[1],
        gain_sums[2],
    )


def solution(mesh):
    return jax.shard_map(
        on_device,
        mesh=mesh,
        in_specs=(
            P("dp", "seq", None),
            P("dp", None, None),
            P("dp", None),
            P("dp", None),
            P(("dp", "seq"), None),
            P(("dp", "seq"), None),
            P(("dp", "seq"), None),
            P(("dp", "seq"), None),
            P(("dp", "seq"), None),
            P(("dp", "seq"), None),
            P(("dp", "seq"), None),
            P(("dp", "seq"), None),
            P(("dp", "seq")),
            P(("dp", "seq")),
            P(("dp", "seq")),
            P("dp", "seq", None),
        ),
        out_specs=(
            P("dp", "seq", None),
            P("dp", "seq", None),
            P(("dp", "seq"), None),
            P(("dp", "seq"), None),
            P(("dp", "seq"), None),
            P(("dp", "seq"), None),
            P(("dp", "seq"), None),
            P(("dp", "seq"), None),
            P(("dp", "seq"), None),
            P(("dp", "seq"), None),
            P(("dp", "seq")),
            P(("dp", "seq")),
            P(("dp", "seq")),
        ),
        check_vma=False,
    )
```

time: 1570 us -> 1000 us (0.64)
  matrix products: 312 us -> 117 us
  starting transfers between devices: 313 us -> 142 us
  blocking collectives: 147 us -> 8.96 us
  other arithmetic: 181 us -> 92 us
  Pallas kernels: 0 us -> 72.8 us
  waiting for transfers between devices: 425 us -> 390 us
    dot_general x47 -> x22, matrix products: 311 us -> 116 us  [dot(): return jnp.dot(left, right, preferred_element_type=jnp.float32)]
    all_gather x2 -> x0, blocking collectives: 138 us -> none  [the longest x1 71.2 us: on_device(): time_full = lax.all_gather(time_weight, ('dp', 'seq'), axis=0, tiled=True)]
    ppermute x106 -> x78, starting transfers between devices: 168 us -> 87.9 us  [the longest x12 18.8 us: line_send(): lax.ppermute(take(blocks, lax.rem(me + step, count)), axis, [(k, (k + ste...]
    pallas_call x0 -> x4, Pallas kernels: none -> 72.8 us  [the longest x1 23.9 us: self_backward(): pl.pallas_call(self_backward_kernel, grid=(pairs,), in_specs=[lanes(total...]
    ppermute x21 -> x3, starting transfers between devices: 91.8 us -> 26.6 us  [line_scatter(): lax.ppermute(to_right.astype(jnp.bfloat16), axis, [(k, k + 1) for k in ra...]
    ppermute x21 -> x3, waiting for transfers between devices: 45.4 us -> 0.01 us  [line_scatter(): lax.ppermute(to_right.astype(jnp.bfloat16), axis, [(k, k + 1) for k in ra...]
    ppermute x21 -> x3, starting transfers between devices: 37.5 us -> 4.35 us  [line_scatter(): lax.ppermute(to_left.astype(jnp.bfloat16), axis, [(k + 1, k) for k in ran...]
    dynamic_update_slice x72 -> x40, local copies, waits for them, and re-layouts: 53.4 us -> 24.1 us  [place(): return lax.dynamic_update_slice(buffer, block, tuple(starts))]
  transfers between devices with their start and end apart: 171 -> 105, of which waited for: 59 -> 49; matrix products, arithmetic and copies ran while one was open for 36% -> 31% of each run, Pallas kernels for 0% -> 7%
where the time goes in v2:
time: 1000 us; the launch traced here: 994 us
  waiting for transfers between devices  390 us (39%)
  local copies, waits for them, and re-layouts  154 us (15%)
  starting transfers between devices  142 us (14%)
  matrix products  117 us (12%)
  other arithmetic  92 us (9%)
  Pallas kernels  72.8 us (7%)
  between operations  17.1 us (2%)
    ppermute x12, waiting for transfers between devices, line_send(): lax.ppermute(take(blocks, lax.rem(me + step, count)), axis, [(k, (k + ste...  158 us
    dot_general x22, matrix products, dot(): return jnp.dot(left, right, preferred_element_type=jnp.float32)  116 us
    ppermute x8, waiting for transfers between devices, sum_over_chips(): by_first = lax.ppermute(to_first, axis, xor_pairs(count, first))  49.8 us
    ppermute x5, waiting for transfers between devices, chip_gather_ordered(): by_first = lax.ppermute(values, axis, xor_pairs(count, first))  39.8 us
    ppermute x8, waiting for transfers between devices, sum_over_chips(): lax.ppermute(blocks[3][half:].astype(low), axis, xor_pairs(count, second))  31.2 us
    unnamed x253, local copies, waits for them, and re-layouts  29.3 us
    ppermute x3, starting transfers between devices, line_scatter(): lax.ppermute(to_right.astype(jnp.bfloat16), axis, [(k, k + 1) for k in ra...  26.6 us
    dynamic_update_slice x40, local copies, waits for them, and re-layouts, place(): return lax.dynamic_update_slice(buffer, block, tuple(starts))  24.1 us
  transfers between devices with their start and end apart: 105, of which 49 were waited for; matrix products, arithmetic and copies ran while one was open for 31% of the time, Pallas kernels for 7%

profile of v2, /device:TPU:0, one launch (start us, length us, event | category | flops | bytes accessed | tf_op | source)
XLA Modules:
  0.0 994.3 jit_solution(4076830683811024129)
XLA Ops:
  41.4 62.0 %collective-permute-done.3 = bf16[1,64,1152]{2,1,0:T(8,128)(2,1)} collective-permute-done((bf16[1,64,1152]{2,1,0:T(8,128)(2,1)}, bf16[1,64,1152]{2,1,0:T(8,128)(2,1)}, u32[]{:S(2)}, u32[]{:S(2)}) %collective-permute-start.3) | collective-permute-done | bytes 147488 | tf_op jit(solution)/shard_map/ppermute | solution.py:497
  104.3 24.0 %collective-permute-done.4 = bf16[1,64,1152]{2,1,0:T(8,128)(2,1)} collective-permute-done((bf16[1,64,1152]{2,1,0:T(8,128)(2,1)}, bf16[1,64,1152]{2,1,0:T(8,128)(2,1)}, u32[]{:S(2)}, u32[]{:S(2)}) %collective-permute-start.4) | collective-permute-done | bytes 147488 | tf_op jit(solution)/shard_map/ppermute | solution.py:497
  156.8 11.3 %collective-permute-done.9 = bf16[2,64,1152]{2,1,0:T(8,128)(2,1)S(1)} collective-permute-done((bf16[2,64,1152]{2,1,0:T(8,128)(2,1)S(1)}, bf16[2,64,1152]{2,1,0:T(8,128)(2,1)S(1)}, u32[]{:S(2)}, u32[]{:S(2)}) %collective-permute-start.9) | collective-permute-done | bytes 294944 | tf_op jit(solution)/shard_map/ppermute | solution.py:428
  225.3 23.3 %shard_map.255 = (bf16[1024,384]{1,0:T(8,128)(2,1)S(1)}, f32[1024,384]{1,0:T(8,128)S(1)}, f32[1024,384]{1,0:T(8,128)S(1)}, bf16[1152,1152]{1,0:T(8,128)(2,1)}) custom-call(f32[1152,1152]{1,0:T(8,128)} %fusion.14.projected, f32[1152,128]{1,0:T(8,128)S(1)} %pad_maximum_fusion.12.cosine, f32[1152,128]{1,0:T(8,128)S(1)} %pad_maximum_fusion.13.sine, ...), custom_call_target="tpu_custom_call" | custom-call | flops 3623878656 | bytes 13369344 | tf_op jit(solution)/shard_map/pallas_call | solution.py:223
  268.9 9.7 collective-permute-done.12
  283.1 11.8 %collective-permute-done.14 = bf16[4,48,1536]{2,1,0:T(8,128)(2,1)S(1)} collective-permute-done((bf16[4,48,1536]{2,1,0:T(8,128)(2,1)S(1)}, bf16[4,48,1536]{2,1,0:T(8,128)(2,1)S(1)}, u32[]{:S(2)}, u32[]{:S(2)}) %collective-permute-start.14) | collective-permute-done | bytes 589856 | tf_op jit(solution)/shard_map/ppermute | solution.py:425
  297.4 10.1 %collective-permute-done.19 = bf16[4,48,1536]{2,1,0:T(8,128)(2,1)S(1)} collective-permute-done((bf16[4,48,1536]{2,1,0:T(8,128)(2,1)S(1)}, bf16[4,48,1536]{2,1,0:T(8,128)(2,1)S(1)}, u32[]{:S(2)}, u32[]{:S(2)}) %collective-permute-start.19) | collective-permute-done | bytes 589856 | tf_op jit(solution)/shard_map/ppermute | solution.py:425
  310.2 10.0 %collective-permute-done.29 = bf16[4,48,1536]{2,1,0:T(8,128)(2,1)S(1)} collective-permute-done((bf16[4,48,1536]{2,1,0:T(8,128)(2,1)S(1)}, bf16[4,48,1536]{2,1,0:T(8,128)(2,1)S(1)}, u32[]{:S(2)}, u32[]{:S(2)}) %collective-permute-start.29) | collective-permute-done | bytes 589856 | tf_op jit(solution)/shard_map/ppermute | solution.py:425
  322.7 10.0 %collective-permute-done.16 = bf16[2,48,1536]{2,1,0:T(8,128)(2,1)S(1)} collective-permute-done((bf16[2,48,1536]{2,1,0:T(8,128)(2,1)S(1)}, bf16[2,48,1536]{2,1,0:T(8,128)(2,1)S(1)}, u32[]{:S(2)}, u32[]{:S(2)}) %collective-permute-start.16) | collective-permute-done | bytes 294944 | tf_op jit(solution)/shard_map/ppermute | solution.py:427
  373.9 12.5 %shard_map.256 = (bf16[256,1536]{1,0:T(8,128)(2,1)S(1)}, f32[256,1536]{1,0:T(8,128)S(1)}, f32[256,1536]{1,0:T(8,128)S(1)}) custom-call(bf16[256,1536]{1,0:T(8,128)(2,1)S(1)} %convolution_convert_fusion.12.query, bf16[384,3072]{1,0:T(8,128)(2,1)} %fusion.9.keys.values, bf16[384,3072]{1,0:T(8,128)(2,1)} %fusion.9.keys.values, f32[256,1]{1,0:T(8,128)S(1)} %copy.267.clip_column, ...), custom_call_target="tpu_custom_call" | custom-call | flops 1207959552 | bytes 15728640 | tf_op jit(solution)/shard_map/pallas_call | solution.py:280
  400.9 14.7 %collective-permute-done.34 = bf16[256,1536]{1,0:T(8,128)(2,1)S(1)} collective-permute-done((bf16[256,1536]{1,0:T(8,128)(2,1)S(1)}, bf16[256,1536]{1,0:T(8,128)(2,1)S(1)}, u32[]{:S(2)}, u32[]{:S(2)}) %collective-permute-start.34) | collective-permute-done | bytes 786464 | tf_op jit(solution)/shard_map/ppermute | solution.py:402
  452.1 16.1 %fusion.158 = f32[2048,1536]{0,1:T(8,128)} fusion(bf16[2048,1536]{1,0:T(8,128)(2,1)} %bitcast.615, bf16[1536,1536]{1,0:T(8,128)(2,1)} %bitcast.663), kind=kOutput, calls=%fused_computation.442 | convolution fusion | flops 9663676416 | bytes 23592960 | tf_op jit(solution)/shard_map/dot_general | solution.py:551
  468.2 15.3 %all-gather.7.cloned.1.call-done = bf16[768,1536]{1,0:T(8,128)(2,1)} async-done(((bf16[192,1536]{1,0:T(8,128)(2,1)}), bf16[768,1536]{1,0:T(8,128)(2,1)}) %all-gather.7.cloned.1.call-update) | async-done | bytes 2359312 | tf_op jit(solution)/shard_map/all_gather | solution.py:675
  483.5 14.1 %multiply_convert_fusion.1 = (bf16[2048,768]{0,1:T(8,128)(2,1)S(1)}, bf16[2048,768]{0,1:T(8,128)(2,1)S(1)}, bf16[2048,768]{0,1:T(8,128)(2,1)}) fusion(f32[2048,1536]{0,1:T(8,128)} %fusion.158, bf16[2048,1536]{1,0:T(8,128)(2,1)} %bitcast.611, bf16[768,1536]{1,0:T(8,128)(2,1)} %all-gather.7.cloned.1.call-done), kind=kOutput, calls=%fused_computation.18 | convolution fusion | flops 4857004032 | bytes 30670848 | tf_op jit(solution)/shard_map/dot_general | solution.py:551
  497.7 13.6 %convolution_convert_fusion.6 = bf16[1536,1536]{1,0:T(8,128)(2,1)} fusion(bf16[2048,1536]{1,0:T(8,128)(2,1)S(1)} %bitcast.616, bf16[2048,768]{0,1:T(8,128)(2,1)S(1)} %get-tuple-element.47, bf16[2048,768]{0,1:T(8,128)(2,1)S(1)} %get-tuple-element.46), kind=kOutput, calls=%fused_computation.6 | convolution fusion | flops 9678618624 | bytes 17301504 | tf_op jit(solution)/shard_map/dot_general | solution.py:551
  511.4 13.9 %convolution_convert_fusion.5 = bf16[2048,1536]{1,0:T(8,128)(2,1)S(1)} fusion(bf16[1536,1536]{1,0:T(8,128)(2,1)} %bitcast.664, bf16[2048,768]{0,1:T(8,128)(2,1)} %copy-done.108, bf16[2048,768]{0,1:T(8,128)(2,1)} %copy-done.107), kind=kOutput, calls=%fused_computation.5 | convolution fusion | flops 9679405056 | bytes 17301504 | tf_op jit(solution)/shard_map/dot_general | solution.py:551
  576.3 14.4 %collective-permute-done.51 = bf16[256,1536]{1,0:T(8,128)(2,1)S(1)} collective-permute-done((bf16[256,1536]{1,0:T(8,128)(2,1)S(1)}, bf16[256,1536]{1,0:T(8,128)(2,1)S(1)}, u32[]{:S(2)}, u32[]{:S(2)}) %collective-permute-start.51) | collective-permute-done | bytes 786464 | tf_op jit(solution)/shard_map/ppermute | solution.py:483
  591.5 14.7 %collective-permute-done.41 = bf16[256,1536]{1,0:T(8,128)(2,1)S(1)} collective-permute-done((bf16[256,1536]{1,0:T(8,128)(2,1)S(1)}, bf16[256,1536]{1,0:T(8,128)(2,1)S(1)}, u32[]{:S(2)}, u32[]{:S(2)}) %collective-permute-start.41) | collective-permute-done | bytes 786464 | tf_op jit(solution)/shard_map/ppermute | solution.py:483
  609.5 13.2 %shard_map.257 = (bf16[256,1536]{1,0:T(8,128)(2,1)S(1)}, bf16[384,1536]{1,0:T(8,128)(2,1)S(1)}, bf16[384,1536]{1,0:T(8,128)(2,1)S(1)}) custom-call(bf16[256,1536]{1,0:T(8,128)(2,1)S(1)} %copy-done.4, bf16[384,3072]{1,0:T(8,128)(2,1)} %fusion.9.keys.values, bf16[384,3072]{1,0:T(8,128)(2,1)} %fusion.9.keys.values, ...), custom_call_target="tpu_custom_call" | custom-call | flops 3019898880 | bytes 15728640 | tf_op jit(solution)/shard_map/pallas_call | solution.py:306
  649.6 11.6 %collective-permute-done.55 = bf16[1,256,384]{2,1,0:T(8,128)(2,1)S(1)} collective-permute-done((bf16[1,256,384]{2,1,0:T(8,128)(2,1)S(1)}, bf16[1,256,384]{2,1,0:T(8,128)(2,1)S(1)}, u32[]{:S(2)}, u32[]{:S(2)}) %collective-permute-start.55) | collective-permute-done | bytes 196640 | tf_op jit(solution)/shard_map/ppermute | solution.py:497
  661.3 23.9 %shard_map.258 = bf16[1152,1152]{1,0:T(8,128)(2,1)} custom-call(bf16[1152,1152]{1,0:T(8,128)(2,1)} %get-tuple-element.28.low, bf16[1024,384]{1,0:T(8,128)(2,1)S(1)} %bitcast.572, f32[1024,384]{1,0:T(8,128)S(1)} %copy-done.10, f32[1024,384]{1,0:T(8,128)S(1)} %copy-done.12, f32[1152,128]{1,0:T(8,128)S(1)} %pad_maximum_fusion.12.cosine, ...), custom_call_target="tpu_custom_call" | custom-call | flops 9059696640 | bytes 13369344 | tf_op jit(solution)/shard_map/pallas_call | solution.py:251
  696.5 16.9 %collective-permute-start.57 = (bf16[256,1536]{1,0:T(8,128)(2,1)S(1)}, bf16[256,1536]{1,0:T(8,128)(2,1)S(1)}, u32[]{:S(2)}, u32[]{:S(2)}) collective-permute-start(bf16[256,1536]{1,0:T(8,128)(2,1)S(1)} %get-tuple-element.57), channel_id=1, source_target_pairs={{0,1},{4,5},{8,9},{12,13},{16,17},{20,21},{24,25},{28,29}} | collective-permute-start | bytes 2359304 | tf_op jit(solution)/shard_map/ppermute | solution.py:537
  747.2 14.7 %reduce-scatter.8.cloned.1.call-done = bf16[192,1536]{1,0:T(8,128)(2,1)} async-done(((bf16[768,1536]{1,0:T(8,128)(2,1)}), bf16[192,1536]{1,0:T(8,128)(2,1)}) %reduce-scatter.8.cloned.1.call-update) | async-done | bytes 589840 | tf_op jit(solution)/shard_map/reduce_scatter | solution.py:725
  934.8 41.3 %collective-permute-done.69 = bf16[1,48,1152]{2,1,0:T(8,128)(2,1)S(1)} collective-permute-done((bf16[1,48,1152]{2,1,0:T(8,128)(2,1)S(1)}, bf16[1,48,1152]{2,1,0:T(8,128)(2,1)S(1)}, u32[]{:S(2)}, u32[]{:S(2)}) %collective-permute-start.69) | collective-permute-done | bytes 110624 | tf_op jit(solution)/shard_map/ppermute | solution.py:497
  (745 shorter events, 554.1 us)
Async XLA Ops:
  7.2 252.2 %all-gather.9.cloned.1.call-start = ((), (), s32[]{:S(2)}) async-start(), calls=%async_computation.8 | async-start | bytes 2949120 | tf_op jit(solution)/shard_map/all_gather | solution.py:652
  7.3 142.5 %collective-permute-start = (bf16[256,1536]{1,0:T(8,128)(2,1)}, bf16[256,1536]{1,0:T(8,128)(2,1)}, u32[]{:S(2)}, u32[]{:S(2)}) collective-permute-start(bf16[256,1536]{1,0:T(8,128)(2,1)} %bitcast.636), channel_id=1, source_target_pairs={{0,1},{1,2},{2,3},{3,0},{4,5},{5,6},{6,7},{7,4},{8,9},{9,10},{10,1... | collective-permute-start | bytes 2359304 | tf_op jit(solution)/shard_map/ppermute | solution.py:518
  10.4 158.5 %collective-permute-start.1 = (bf16[256,1536]{1,0:T(8,128)(2,1)}, bf16[256,1536]{1,0:T(8,128)(2,1)}, u32[]{:S(2)}, u32[]{:S(2)}) collective-permute-start(bf16[256,1536]{1,0:T(8,128)(2,1)} %bitcast.637), channel_id=1, source_target_pairs={{0,2},{1,3},{2,0},{3,1},{4,6},{5,7},{6,4},{7,5},{8,10},{9,11},{10,... | collective-permute-start | bytes 2359304 | tf_op jit(solution)/shard_map/ppermute | solution.py:518
  12.9 157.1 %collective-permute-start.2 = (bf16[256,1536]{1,0:T(8,128)(2,1)}, bf16[256,1536]{1,0:T(8,128)(2,1)}, u32[]{:S(2)}, u32[]{:S(2)}) collective-permute-start(bf16[256,1536]{1,0:T(8,128)(2,1)} %bitcast.638), channel_id=1, source_target_pairs={{0,3},{1,0},{2,1},{3,2},{4,7},{5,4},{6,5},{7,6},{8,11},{9,8},{10,9... | collective-permute-start | bytes 2359304 | tf_op jit(solution)/shard_map/ppermute | solution.py:518
  22.7 80.7 %collective-permute-start.3 = (bf16[1,64,1152]{2,1,0:T(8,128)(2,1)}, bf16[1,64,1152]{2,1,0:T(8,128)(2,1)}, u32[]{:S(2)}, u32[]{:S(2)}) collective-permute-start(bf16[1,64,1152]{2,1,0:T(8,128)(2,1)} %get-tuple-element.128), channel_id=1, source_target_pairs={{0,1},{1,2},{2,3},{3,0},{4,5},{5,6},{6,7},{7,4},{8,9},{9,10},{10,1... | collective-permute-start | bytes 442376 | tf_op jit(solution)/shard_map/ppermute | solution.py:497
  23.3 105.0 %collective-permute-start.4 = (bf16[1,64,1152]{2,1,0:T(8,128)(2,1)}, bf16[1,64,1152]{2,1,0:T(8,128)(2,1)}, u32[]{:S(2)}, u32[]{:S(2)}) collective-permute-start(bf16[1,64,1152]{2,1,0:T(8,128)(2,1)} %get-tuple-element.129), channel_id=1, source_target_pairs={{0,2},{1,3},{2,0},{3,1},{4,6},{5,7},{6,4},{7,5},{8,10},{9,11},{10,... | collective-permute-start | bytes 442376 | tf_op jit(solution)/shard_map/ppermute | solution.py:497
  26.4 151.3 %all-to-all-start = ((bf16[8,48,1536]{2,1,0:T(8,128)(2,1)}), bf16[8,48,1536]{2,1,0:T(8,128)(2,1)}, u32[]{:S(2)}, u32[]{:S(2)}) async-start(bf16[8,48,1536]{2,1,0:T(8,128)(2,1)} %reshape.545), calls=%async_computation | async-start | bytes 2359296 | tf_op jit(solution)/shard_map/all_to_all | solution.py:671
  30.8 421.3 %all-gather.11.cloned.1.call-start = ((), (), s32[]{:S(2)}) async-start(), calls=%async_computation.9 | async-start | bytes 5898240 | tf_op jit(solution)/shard_map/all_gather | solution.py:673
  174.5 222.4 %collective-permute-start.46 = (bf16[128,1536]{1,0:T(8,128)(2,1)}, bf16[128,1536]{1,0:T(8,128)(2,1)}, u32[]{:S(2)}, u32[]{:S(2)}) collective-permute-start(bf16[128,1536]{1,0:T(8,128)(2,1)} %slice.599), channel_id=1, source_target_pairs={{0,16},{4,20},{8,24},{12,28},{16,0},{20,4},{24,8},{28,12},{1,17},{... | collective-permute-start | bytes 1179656 | tf_op jit(solution)/shard_map/ppermute | solution.py:404
  177.7 305.8 %all-gather.7.cloned.1.call-start = ((), (), s32[]{:S(2)}) async-start(), calls=%async_computation.5 | async-start | bytes 2949120 | tf_op jit(solution)/shard_map/all_gather | solution.py:675
  336.4 60.5 %collective-permute-start.47 = (bf16[128,1536]{1,0:T(8,128)(2,1)S(1)}, bf16[128,1536]{1,0:T(8,128)(2,1)S(1)}, u32[]{:S(2)}, u32[]{:S(2)}) collective-permute-start(bf16[128,1536]{1,0:T(8,128)(2,1)S(1)} %copy-done.65), channel_id=1, source_target_pairs={{0,8},{4,12},{8,0},{12,4},{16,24},{20,28},{24,16},{28,20},{1,9},{5... | collective-permute-start | bytes 1179656 | tf_op jit(solution)/shard_map/ppermute | solution.py:405
  429.5 311.2 %all-reduce.6.cloned.1.call-start = ((), (), s32[]{:S(2)}) async-start(), calls=%async_computation.10 | async-start | bytes 9437184
  511.3 250.6 %reduce-scatter.8.cloned.1.call-start = ((), (), s32[]{:S(2)}) async-start(), calls=%async_computation.7 | async-start | bytes 2949120 | tf_op jit(solution)/shard_map/reduce_scatter | solution.py:725
  639.9 176.5 %collective-permute-start.91 = (bf16[4,1,4,48,1536]{4,3,2,1,0:T(8,128)(2,1)}, bf16[4,1,4,48,1536]{4,3,2,1,0:T(8,128)(2,1)}, u32[]{:S(2)}, u32[]{:S(2)}) collective-permute-start(bf16[4,1,4,48,1536]{4,3,2,1,0:T(8,128)(2,1)} %constant_dynamic-slice_fusion.3), channel_id=1, source_target_pairs={{0,4},{4,0},{8,12},{12,8},{16,20},{20,16},{24,28},{28,24},{1,5},{5... | collective-permute-start | bytes 7077896 | tf_op jit(solution)/shard_map/ppermute | solution.py:461
  641.6 179.8 %collective-permute-start.86 = (bf16[4,1,4,48,1536]{4,3,2,1,0:T(8,128)(2,1)}, bf16[4,1,4,48,1536]{4,3,2,1,0:T(8,128)(2,1)}, u32[]{:S(2)}, u32[]{:S(2)}) collective-permute-start(bf16[4,1,4,48,1536]{4,3,2,1,0:T(8,128)(2,1)} %constant_dynamic-slice_fusion.4), channel_id=1, source_target_pairs={{0,4},{4,0},{8,12},{12,8},{16,20},{20,16},{24,28},{28,24},{1,5},{5... | collective-permute-start | bytes 7077896 | tf_op jit(solution)/shard_map/ppermute | solution.py:461
  649.5 117.3 %collective-permute-start.81 = (bf16[4,1,4,24,1536]{4,3,2,1,0:T(8,128)(2,1)}, bf16[4,1,4,24,1536]{4,3,2,1,0:T(8,128)(2,1)}, u32[]{:S(2)}, u32[]{:S(2)}) collective-permute-start(bf16[4,1,4,24,1536]{4,3,2,1,0:T(8,128)(2,1)} %constant_dynamic-slice_fusion.5), channel_id=1, source_target_pairs={{0,4},{4,0},{8,12},{12,8},{16,20},{20,16},{24,28},{28,24},{1,5},{5... | collective-permute-start | bytes 3538952 | tf_op jit(solution)/shard_map/ppermute | solution.py:461
  661.2 107.4 %collective-permute-start.76 = (bf16[4,1,4,24,1536]{4,3,2,1,0:T(8,128)(2,1)}, bf16[4,1,4,24,1536]{4,3,2,1,0:T(8,128)(2,1)}, u32[]{:S(2)}, u32[]{:S(2)}) collective-permute-start(bf16[4,1,4,24,1536]{4,3,2,1,0:T(8,128)(2,1)} %constant_dynamic-slice_fusion.6), channel_id=1, source_target_pairs={{0,4},{4,0},{8,12},{12,8},{16,20},{20,16},{24,28},{28,24},{1,5},{5... | collective-permute-start | bytes 3538952 | tf_op jit(solution)/shard_map/ppermute | solution.py:461
  696.5 67.7 %collective-permute-start.57 = (bf16[256,1536]{1,0:T(8,128)(2,1)S(1)}, bf16[256,1536]{1,0:T(8,128)(2,1)S(1)}, u32[]{:S(2)}, u32[]{:S(2)}) collective-permute-start(bf16[256,1536]{1,0:T(8,128)(2,1)S(1)} %get-tuple-element.57), channel_id=1, source_target_pairs={{0,1},{4,5},{8,9},{12,13},{16,17},{20,21},{24,25},{28,29}} | collective-permute-start | bytes 2359304 | tf_op jit(solution)/shard_map/ppermute | solution.py:537
  792.7 115.5 %all-to-all-start.1 = ((f32[32,6,1536]{2,1,0:T(8,128)}), f32[32,6,1536]{2,1,0:T(8,128)S(1)}, u32[]{:S(2)}, u32[]{:S(2)}) async-start(f32[32,6,1536]{2,1,0:T(8,128)} %broadcast_in_dim.222), calls=%async_computation.2 | async-start | bytes 3145728 | tf_op jit(solution)/shard_map/all_to_all | solution.py:837
  797.6 186.8 %reduce-scatter.6.cloned.1.call-start = ((), (), s32[]{:S(2)}) async-start(), calls=%async_computation.6 | async-start | bytes 2949120 | tf_op jit(solution)/shard_map/reduce_scatter | solution.py:782
  806.8 69.9 %collective-permute-start.83 = (bf16[4,24,1536]{2,1,0:T(8,128)(2,1)S(1)}, bf16[4,24,1536]{2,1,0:T(8,128)(2,1)S(1)}, u32[]{:S(2)}, u32[]{:S(2)}) collective-permute-start(bf16[4,24,1536]{2,1,0:T(8,128)(2,1)S(1)} %copy-done.69), channel_id=1, source_target_pairs={{0,8},{4,12},{8,0},{12,4},{16,24},{20,28},{24,16},{28,20},{1,9},{5... | collective-permute-start | bytes 884744 | tf_op jit(solution)/shard_map/ppermute | solution.py:483
  812.6 65.5 %collective-permute-start.85 = (bf16[4,24,1536]{2,1,0:T(8,128)(2,1)S(1)}, bf16[4,24,1536]{2,1,0:T(8,128)(2,1)S(1)}, u32[]{:S(2)}, u32[]{:S(2)}) collective-permute-start(bf16[4,24,1536]{2,1,0:T(8,128)(2,1)S(1)} %copy-done.68), channel_id=1, source_target_pairs={{0,16},{4,20},{8,24},{12,28},{16,0},{20,4},{24,8},{28,12},{1,17},{... | collective-permute-start | bytes 884744 | tf_op jit(solution)/shard_map/ppermute | solution.py:484
  886.5 91.9 %collective-permute-start.59 = (bf16[256,1536]{1,0:T(8,128)(2,1)}, bf16[256,1536]{1,0:T(8,128)(2,1)}, u32[]{:S(2)}, u32[]{:S(2)}) collective-permute-start(bf16[256,1536]{1,0:T(8,128)(2,1)} %get-tuple-element.55), channel_id=1, source_target_pairs={{0,1},{1,2},{2,3},{4,5},{5,6},{6,7},{8,9},{9,10},{10,11},{12,13},{... | collective-permute-start | bytes 2359304 | tf_op jit(solution)/shard_map/ppermute | solution.py:537
  922.5 55.8 %collective-permute-start.62 = (bf16[256,1536]{1,0:T(8,128)(2,1)}, bf16[256,1536]{1,0:T(8,128)(2,1)}, u32[]{:S(2)}, u32[]{:S(2)}) collective-permute-start(bf16[256,1536]{1,0:T(8,128)(2,1)} %fusion.23), channel_id=1, source_target_pairs={{1,0},{2,1},{3,2},{5,4},{6,5},{7,6},{9,8},{10,9},{11,10},{13,12},{... | collective-permute-start | bytes 2359304 | tf_op jit(solution)/shard_map/ppermute | solution.py:540
  (204 other events, 3316.7 us)
Sparse Core Ops, SparseCore 0:
  19.8 89.2 all-gather.8
  177.8 104.0 all-gather.10
  429.7 53.8 all-gather.6
  511.4 187.3 all-reduce.5
  701.0 60.8 reduce-scatter.7
  901.5 74.2 reduce-scatter.5

commit v3 on v2

--- a/solution.py
+++ b/solution.py
@@ -199,8 +199,8 @@
     return pl.BlockSpec(array.shape, lambda p: (0,) * array.ndim)
 
 
-def lanes(rows, width=2 * HEAD_DIM, offset=0):
-    return pl.BlockSpec((rows, width), lambda p: (0, p + offset))
+def lanes(rows, width=2 * HEAD_DIM, second=False):
+    return pl.BlockSpec((rows, width), lambda p: (1 if second else 0, p))
 
 
 KERNEL_PARAMS = pltpu.CompilerParams(
@@ -208,11 +208,9 @@
 )
 
 
-def cost(heads, queries, keys, dots):
+def cost(microseconds):
     return pl.CostEstimate(
-        flops=2 * dots * heads * queries * keys * 2 * HEAD_DIM,
-        bytes_accessed=heads * HEAD_DIM * (queries + keys) * 16,
-        transcendentals=heads * queries * keys,
+        flops=int(microseconds * 1e9), bytes_accessed=2**20, transcendentals=0
     )
 
 
@@ -239,7 +237,7 @@
         ],
         scratch_shapes=[pltpu.VMEM((2, total, pair), jnp.bfloat16)],
         compiler_params=KERNEL_PARAMS,
-        cost_estimate=cost(2 * pairs, rows, total, 2),
+        cost_estimate=cost(120),
     )(projected, cosine, sine, clip_column, clip_row)
 
 
@@ -268,13 +266,13 @@
             pltpu.VMEM((2, total, pair), jnp.float32),
         ],
         compiler_params=KERNEL_PARAMS,
-        cost_estimate=cost(2 * pairs, rows, total, 5),
+        cost_estimate=cost(15),
     )(low, grads, mixed_wide, level, cosine, sine, clip_column, clip_row)
 
 
 def cross_forward(query, keyval, clip_column, clip_row):
     rows, width = query.shape
-    keys = keyval.shape[0]
+    keys = keyval.shape[0] // 2
     pair = 2 * HEAD_DIM
     pairs = width // pair
     return pl.pallas_call(
@@ -283,7 +281,7 @@
         in_specs=[
             lanes(rows),
             lanes(keys),
-            lanes(keys, offset=pairs),
+            lanes(keys, second=True),
             whole(clip_column),
             whole(clip_row),
         ],
@@ -294,13 +292,13 @@
             jax.ShapeDtypeStruct((rows, width), jnp.float32),
         ],
         compiler_params=KERNEL_PARAMS,
-        cost_estimate=cost(2 * pairs, rows, keys, 2),
+        cost_estimate=cost(20),
     )(query, keyval, keyval, clip_column, clip_row)
 
 
 def cross_backward(query, keyval, grads, mixed_wide, level, clip_column, clip_row):
     rows, width = query.shape
-    keys = keyval.shape[0]
+    keys = keyval.shape[0] // 2
     pair = 2 * HEAD_DIM
     pairs = width // pair
     return pl.pallas_call(
@@ -309,7 +307,7 @@
         in_specs=[
             lanes(rows),
             lanes(keys),
-            lanes(keys, offset=pairs),
+            lanes(keys, second=True),
             lanes(rows),
             lanes(rows),
             lanes(rows),
@@ -323,7 +321,7 @@
             jax.ShapeDtypeStruct((keys, width), jnp.bfloat16),
         ],
         compiler_params=KERNEL_PARAMS,
-        cost_estimate=cost(2 * pairs, rows, keys, 5),
+        cost_estimate=cost(120),
     )(query, keyval, keyval, grads, mixed_wide, level, clip_column, clip_row)
 
 
@@ -391,104 +389,6 @@
 
 def plane_bits(count):
     return [1 << b for b in range(1, count.bit_length() - 1)]
-
-
-def chip_gather(values, axis):
-    count = lax.axis_size(axis)
-    bits = plane_bits(count)
-    if len(bits) == 2 and values.shape[0] % 32 == 0:
-        first, second = bits
-        half = values.shape[0] // 2
-        by_first = lax.ppermute(values, axis, xor_pairs(count, first))
-        by_second = lax.ppermute(values, axis, xor_pairs(count, second))
-        far_one = lax.ppermute(by_first[:half], axis, xor_pairs(count, second))
-        far_two = lax.ppermute(by_second[half:], axis, xor_pairs(count, first))
-        far = jnp.concatenate([far_one, far_two], axis=0)
-        same = jnp.stack([values, by_first, by_second, far], axis=0)
-    else:
-        same = values[None]
-        for bit in bits:
-            same = jnp.concatenate([same, lax.ppermute(same, axis, xor_pairs(count, bit))], axis=0)
-    if count == 1:
-        return same
-    other = lax.ppermute(same, axis, xor_pairs(count, 1))
-    return jnp.stack([same, other], axis=1).reshape((count,) + values.shape)
-
-
-def chip_gather_ordered(values, axis, me):
-    count = lax.axis_size(axis)
-    bits = plane_bits(count)
-    if len(bits) == 2 and values.shape[0] % 2 == 0:
-        first, second = bits
-        half = values.shape[0] // 2
-        chip, core = me // 2, me % 2
-        by_first = lax.ppermute(values, axis, xor_pairs(count, first))
-        by_second = lax.ppermute(values, axis, xor_pairs(count, second))
-        far_one = lax.ppermute(by_first[:half], axis, xor_pairs(count, second))
-        far_two = lax.ppermute(by_second[half:], axis, xor_pairs(count, first))
-        same = jnp.zeros((count // 2,) + values.shape, values.dtype)
-        same = place(same, values[None], 0, chip)
-        same = place(same, by_first[None], 0, chip ^ 1)
-        same = place(same, by_second[None], 0, chip ^ 2)
-        far = jnp.concatenate([far_one, far_two], axis=0)
-        same = place(same, far[None], 0, chip ^ 3)
-        other = lax.ppermute(same, axis, xor_pairs(count, 1))
-        result = jnp.zeros((count // 2, 2) + values.shape, values.dtype)
-        result = place(result, same[:, None], 1, core)
-        result = place(result, other[:, None], 1, 1 - core)
-        return result.reshape((count,) + values.shape)
-    return lax.all_gather(values, axis)
-
-
-def chip_scatter(parts, axis):
-    count = lax.axis_size(axis)
-    if count == 1:
-        return parts[0].astype(jnp.float32)
-    low = jnp.bfloat16
-    pairs = parts.reshape((count // 2, 2) + parts.shape[1:])
-    got = lax.ppermute(pairs[:, 1].astype(low), axis, xor_pairs(count, 1))
-    total = pairs[:, 0].astype(jnp.float32) + got.astype(jnp.float32)
-    return sum_over_chips([total[r] for r in range(count // 2)], axis)
-
-
-def chip_scatter_ordered(parts, axis, me):
-    count = lax.axis_size(axis)
-    if count == 1:
-        return parts[0].astype(jnp.float32)
-    low = jnp.bfloat16
-    chip, core = me // 2, me % 2
-    pairs = parts.reshape((count // 2, 2) + parts.shape[1:])
-    got = lax.ppermute(take(pairs, 1 - core, 1).astype(low), axis, xor_pairs(count, 1))
-    total = (take(pairs, core, 1).astype(jnp.float32) + got.astype(jnp.float32))[:, 0]
-    return sum_over_chips([take(total, chip ^ r)[0] for r in range(count // 2)], axis)
-
-
-def sum_over_chips(blocks, axis):
-    count = lax.axis_size(axis)
-    bits = plane_bits(count)
-    low, wide = jnp.bfloat16, jnp.float32
-    if len(bits) == 2 and blocks[0].shape[0] % 2 == 0:
-        first, second = bits
-        half = blocks[0].shape[0] // 2
-        far_one = lax.ppermute(blocks[3][:half].astype(low), axis, xor_pairs(count, first))
-        far_two = lax.ppermute(blocks[3][half:].astype(low), axis, xor_pairs(count, second))
-        to_second = jnp.concatenate(
-            [(blocks[2][:half] + far_one.astype(wide)).astype(low), blocks[2][half:].astype(low)],
-            axis=0,
-        )
-        to_first = jnp.concatenate(
-            [blocks[1][:half].astype(low), (blocks[1][half:] + far_two.astype(wide)).astype(low)],
-            axis=0,
-        )
-        by_first = lax.ppermute(to_first, axis, xor_pairs(count, first))
-        by_second = lax.ppermute(to_second, axis, xor_pairs(count, second))
-        return blocks[0] + by_first.astype(wide) + by_second.astype(wide)
-    total = jnp.stack(blocks, axis=0)
-    for bit in reversed(bits):
-        middle = total.shape[0] // 2
-        got = lax.ppermute(total[middle:].astype(low), axis, xor_pairs(count, bit))
-        total = total[:middle] + got.astype(wide)
-    return total[0]
 
 
 def line_send(blocks, axis, me):
@@ -511,44 +411,250 @@
     return result
 
 
-def line_gather(values, axis, me):
-    count = lax.axis_size(axis)
-    result = place(jnp.zeros((count,) + values.shape, values.dtype), values[None], 0, me)
-    for step in range(1, count):
-        got = lax.ppermute(values, axis, [(k, (k + step) % count) for k in range(count)])
-        result = place(result, got[None], 0, lax.rem(me - step + count, count))
-    return result
-
-
-def line_scatter(parts, axis, me):
-    count = lax.axis_size(axis)
-
-    def part(index):
-        return take(parts, index)[0].astype(jnp.float32)
-
-    total = part(me)
-    from_left = from_right = None
-    for step in range(1, count):
-        to_right = part(jnp.minimum(me + count - step, count - 1))
-        to_left = part(jnp.maximum(me - count + step, 0))
-        if step > 1:
-            to_right = to_right + from_left.astype(jnp.float32)
-            to_left = to_left + from_right.astype(jnp.float32)
-        from_left = lax.ppermute(
-            to_right.astype(jnp.bfloat16), axis, [(k, k + 1) for k in range(0, step)]
-        )
-        from_right = lax.ppermute(
-            to_left.astype(jnp.bfloat16),
-            axis,
-            [(k + 1, k) for k in range(count - 1 - step, count - 1)],
-        )
-    if count > 1:
-        total = total + from_left.astype(jnp.float32) + from_right.astype(jnp.float32)
-    return total
-
-
 def dot(left, right):
     return jnp.dot(left, right, preferred_element_type=jnp.float32)
+
+
+def tie(*values):
+    return lax.optimization_barrier(values)
+
+
+def flip(values, bit):
+    return lax.ppermute(values, "dp", xor_pairs(lax.axis_size("dp"), bit))
+
+
+def two_by_two():
+    return lax.axis_size("dp") == 8
+
+
+def assemble(pieces, shapes, moves, places):
+    count = len(pieces)
+
+    def kernel(places_ref, *refs):
+        given, results, semaphores = refs[:count], refs[count:-1], refs[-1]
+        copies = []
+        for number, (piece, source, result, target) in enumerate(moves):
+            copy = pltpu.make_async_copy(
+                given[piece].at[source(places_ref)],
+                results[result].at[target(places_ref)],
+                semaphores.at[number],
+            )
+            copy.start()
+            copies.append(copy)
+        for copy in copies:
+            copy.wait()
+
+    size = sum(2 * math.prod(shape) for shape in shapes)
+    return pl.pallas_call(
+        kernel,
+        in_specs=[pl.BlockSpec(memory_space=pltpu.SMEM)]
+        + [pl.BlockSpec(memory_space=pl.ANY)] * count,
+        out_specs=[pl.BlockSpec(memory_space=pltpu.VMEM)] * len(shapes),
+        out_shape=[jax.ShapeDtypeStruct(shape, jnp.bfloat16) for shape in shapes],
+        scratch_shapes=[pltpu.SemaphoreType.DMA((len(moves),))],
+        compiler_params=pltpu.CompilerParams(vmem_limit_bytes=48 * 1024 * 1024),
+        cost_estimate=pl.CostEstimate(flops=0, bytes_accessed=2 * size, transcendentals=0),
+    )(places, *pieces)
+
+
+def everything(places):
+    return slice(None)
+
+
+def at(*index):
+    return lambda places: index
+
+
+def plane_open(values):
+    if not two_by_two():
+        return (values,)
+    return (values, flip(values, 2), flip(values, 4))
+
+
+def plane_relay(state):
+    if not two_by_two():
+        return state
+    values, by_first, by_second = state
+    half = values.shape[0] // 2
+    return state + (flip(by_first[:half], 4), flip(by_second[half:], 2))
+
+
+def plane_chips(state, chip=None):
+    values = state[0]
+    chips = lax.axis_size("dp") // 2
+    if not two_by_two():
+        same = values[None]
+        for bit in plane_bits(2 * chips):
+            same = jnp.concatenate([same, flip(same, bit)], axis=0)
+        if chip is None:
+            return same
+        ordered = jnp.zeros(same.shape, same.dtype)
+        for r in range(chips):
+            ordered = place(ordered, same[r : r + 1], 0, chip ^ r)
+        return ordered
+    half = values.shape[0] // 2
+    rest = values.shape[0] - half
+
+    def target(r, *more):
+        if chip is None:
+            return at(r, *more)
+        return lambda places: (places[0] ^ r,) + more
+
+    moves = [(r, everything, 0, target(r)) for r in range(3)]
+    moves.append((3, everything, 0, target(3, pl.ds(0, half))))
+    moves.append((4, everything, 0, target(3, pl.ds(half, rest))))
+    places = jnp.zeros((1,), jnp.int32) if chip is None else chip.reshape(1).astype(jnp.int32)
+    return assemble(state, [(chips,) + values.shape], moves, places)[0]
+
+
+def both_cores(same, other, core, rows):
+    chips, line, _, width = same.shape
+    if two_by_two() and all(count % 16 == 0 for count in rows):
+        moves, start = [], 0
+        for result, count in enumerate(rows):
+            part = at(slice(None), slice(None), pl.ds(start, count))
+            moves.append((0, part, result, lambda places: (slice(None), places[0])))
+            moves.append((1, part, result, lambda places: (slice(None), 1 - places[0])))
+            start += count
+        return assemble(
+            [same, other],
+            [(chips, 2, line, count, width) for count in rows],
+            moves,
+            core.reshape(1).astype(jnp.int32),
+        )
+    full = jnp.zeros((chips, 2) + same.shape[1:], same.dtype)
+    full = place(place(full, same[:, None], 1, core), other[:, None], 1, 1 - core)
+    results, start = [], 0
+    for count in rows:
+        results.append(full[:, :, :, start : start + count])
+        start += count
+    return results
+
+
+def plane_far(blocks):
+    if not two_by_two():
+        return None
+    half = blocks[3].shape[0] // 2
+    low = jnp.bfloat16
+    return (flip(blocks[3][:half].astype(low), 2), flip(blocks[3][half:].astype(low), 4))
+
+
+def plane_near(blocks, far):
+    low, wide = jnp.bfloat16, jnp.float32
+    if not two_by_two():
+        total = jnp.stack([block.astype(wide) for block in blocks], axis=0)
+        for bit in reversed(plane_bits(lax.axis_size("dp"))):
+            middle = total.shape[0] // 2
+            got = flip(total[middle:].astype(low), bit)
+            total = total[:middle] + got.astype(wide)
+        return (total[0],)
+    half = blocks[3].shape[0] // 2
+    to_first = jnp.concatenate(
+        [
+            blocks[1][:half].astype(low),
+            (blocks[1][half:].astype(wide) + far[1].astype(wide)).astype(low),
+        ],
+        axis=0,
+    )
+    to_second = jnp.concatenate(
+        [
+            (blocks[2][:half].astype(wide) + far[0].astype(wide)).astype(low),
+            blocks[2][half:].astype(low),
+        ],
+        axis=0,
+    )
+    return (blocks[0], flip(to_first, 2), flip(to_second, 4))
+
+
+def plane_total(near):
+    total = near[0].astype(jnp.float32)
+    for got in near[1:]:
+        total = total + got.astype(jnp.float32)
+    return total
+
+
+def relay_step(state, step):
+    count = lax.axis_size("seq")
+    rightward, leftward = state
+    return (
+        rightward
+        + [lax.ppermute(rightward[-1], "seq", [(k, k + 1) for k in range(step - 1, count - 1)])],
+        leftward
+        + [lax.ppermute(leftward[-1], "seq", [(k + 1, k) for k in range(0, count - step)])],
+    )
+
+
+def relay_join(state, me):
+    rightward, leftward = state
+    count = len(rightward)
+    shape = rightward[0].shape
+
+    def kernel(me_ref, *refs):
+        right, left, result = refs[:count], refs[count : 2 * count - 1], refs[-1]
+        index = me_ref[0]
+        result[pl.ds(index, 1)] = right[0][...][None]
+        for step in range(1, count):
+            target = lax.rem(index - step + count, count)
+
+            @pl.when(index >= step)
+            def _(step=step, target=target):
+                result[pl.ds(target, 1)] = right[step][...][None]
+
+            @pl.when(index < step)
+            def _(step=step, target=target):
+                result[pl.ds(target, 1)] = left[count - step - 1][...][None]
+
+    return pl.pallas_call(
+        kernel,
+        in_specs=[pl.BlockSpec(memory_space=pltpu.SMEM)]
+        + [pl.BlockSpec(memory_space=pltpu.VMEM)] * (2 * count - 1),
+        out_specs=pl.BlockSpec(memory_space=pltpu.VMEM),
+        out_shape=jax.ShapeDtypeStruct((count,) + shape, rightward[0].dtype),
+        compiler_params=pltpu.CompilerParams(vmem_limit_bytes=48 * 1024 * 1024),
+        cost_estimate=pl.CostEstimate(
+            flops=0, bytes_accessed=6 * count * math.prod(shape), transcendentals=0
+        ),
+    )(me.reshape(1).astype(jnp.int32), *rightward, *leftward[1:])
+
+
+def line_join(blocks, got, me):
+    count = len(got) + 1
+    alone = blocks.shape[0] != count
+    moves = [
+        (
+            0,
+            everything if alone else lambda places: pl.ds(places[0], 1),
+            0,
+            lambda places: pl.ds(places[0], 1),
+        )
+    ]
+    for step in range(1, count):
+        moves.append(
+            (
+                step,
+                everything,
+                0,
+                lambda places, step=step: pl.ds(lax.rem(places[0] - step + count, count), 1),
+            )
+        )
+    shape = (count,) + blocks.shape[1:]
+    return assemble([blocks] + got, [shape], moves, me.reshape(1).astype(jnp.int32))[0]
+
+
+def sum_step(parts, me, step, came):
+    count = lax.axis_size("seq")
+    to_right = take(parts, jnp.minimum(me + count - step, count - 1))[0].astype(jnp.float32)
+    to_left = take(parts, jnp.maximum(me - count + step, 0))[0].astype(jnp.float32)
+    if came is not None:
+        to_right = to_right + came[0].astype(jnp.float32)
+        to_left = to_left + came[1].astype(jnp.float32)
+    low = jnp.bfloat16
+    return (
+        lax.ppermute(to_right.astype(low), "seq", [(k, k + 1) for k in range(0, step)]),
+        lax.ppermute(
+            to_left.astype(low), "seq", [(k + 1, k) for k in range(count - 1 - step, count - 1)]
+        ),
+    )
 
 
 def on_device(
@@ -586,6 +692,8 @@
     shard = D // (dp_count * seq_count)
     time_shard = TFEAT // (dp_count * seq_count)
     place_all = dp_place * seq_count + seq_place
+    chip_place, core_place = dp_place // 2, dp_place % 2
+    chips = dp_count // 2
 
     all_frames = jnp.arange(row_length, dtype=jnp.int32)
     second_start, third_start = clip_bounds[0, 0], clip_bounds[0, 1]
@@ -607,141 +715,226 @@
     own_clips = lax.dynamic_slice_in_dim(clips, seq_place * frame_count, frame_count)
     text_clips = (jnp.arange(text_count, dtype=jnp.int32) // CTX_LEN).astype(f32)
 
-    inward_blocks = (
-        self_inward.reshape(shard, 3, seq_count, own_width)
+    def by_pairs(blocks):
+        blocks = jnp.pad(blocks, ((0, 0),) * 3 + ((0, padded - own_width),))
+        return (
+            blocks.reshape(seq_count, shard, 3, pairs, pair_width)
+            .transpose(0, 1, 3, 2, 4)
+            .reshape(seq_count, shard, 3 * padded)
+        )
+
+    def from_pairs(blocks):
+        return (
+            blocks.reshape(seq_count, shard, pairs, 3, pair_width)
+            .transpose(0, 1, 3, 2, 4)
+            .reshape(seq_count, shard, 3, padded)[..., :own_width]
+        )
+
+    inward_blocks = by_pairs(
+        self_inward.reshape(shard, 3, seq_count, own_width).transpose(2, 0, 1, 3)
+    )
+    extra = jnp.concatenate([time_weight.reshape(-1), gain_attend, gain_cross, gain_feed])
+    extra_rows = -(-extra.shape[0] // (16 * 3 * padded)) * 16
+    extra = jnp.pad(extra, (0, extra_rows * 3 * padded - extra.shape[0]))
+    extra = jnp.broadcast_to(
+        extra.reshape(1, extra_rows, 3 * padded), (seq_count, extra_rows, 3 * padded)
+    )
+    inward_send = jnp.concatenate([inward_blocks, extra], axis=1)
+    expand_blocks = (
+        expand_weight.reshape(shard, 2, dp_count, hidden_width)
         .transpose(2, 0, 1, 3)
-        .reshape(seq_count, shard, 3 * own_width)
-    )
-    extra = jnp.concatenate([time_weight.reshape(-1), gain_attend, gain_cross, gain_feed])
-    extra_rows = -(-extra.shape[0] // (3 * own_width))
-    sent_rows = -(-(shard + extra_rows) // 16) * 16
-    extra = jnp.pad(extra, (0, (sent_rows - shard) * 3 * own_width - extra.shape[0]))
-    extra = jnp.broadcast_to(
-        extra.reshape(1, sent_rows - shard, 3 * own_width),
-        (seq_count, sent_rows - shard, 3 * own_width),
-    )
-    inward_columns = line_exchange(
-        jnp.concatenate([inward_blocks, extra], axis=1), "seq", seq_place
-    )
-    row_latents = line_gather(latents[0], "seq", seq_place).reshape(row_length, D)
-    inward_all = chip_gather_ordered(inward_columns, "dp", dp_place)
-    inward_own = inward_all[:, :, :shard].reshape(D, 3, own_width)
-    inward_own = jnp.pad(inward_own, ((0, 0), (0, 0), (0, padded - own_width)))
-    inward_own = (
-        inward_own.reshape(D, 3, pairs, pair_width).transpose(0, 2, 1, 3).reshape(D, 3 * padded)
-    )
-    extra_all = inward_all[:, :, shard:].reshape(dp_count, seq_count, -1)
+        .reshape(dp_count, shard, 2 * hidden_width)
+    )
+
+    inward_got = line_send(inward_send, "seq", seq_place)
+    inward_got, latents = tie(inward_got, latents)
+
+    moving = ([latents[0]], [latents[0]])
+    for step in range(1, seq_count - 2):
+        moving = relay_step(moving, step)
+    inward_columns = line_join(inward_send, inward_got, seq_place)
+    inward_state = plane_open(inward_columns)
+    packed = jnp.concatenate(
+        [self_outward, cross_keyval[:, :D], cross_keyval[:, D:], cross_query, cross_return],
+        axis=0,
+    )
+    inward_state, moving, cosine, sine, packed, expand_blocks = tie(
+        inward_state, moving, cosine, sine, packed, expand_blocks
+    )
+
+    moving = relay_step(moving, seq_count - 2)
+    inward_state = plane_relay(inward_state)
+    inward_same = plane_chips(inward_state, chip_place)
+    inward_same, moving, packed = tie(inward_same, moving, packed)
+
+    moving = relay_step(moving, seq_count - 1)
+    lined = lax.all_gather(packed, "seq")
+    inward_other = flip(inward_same, 1)
+    expand_part = lax.all_to_all(expand_blocks, "dp", 0, 0, tiled=True)
+    spread_rows = jnp.arange(D, dtype=jnp.int32)[None, :]
+    context_rows = jnp.arange(D // 2, dtype=jnp.int32)[:, None]
+    group, within = context_rows // (shard // 2), context_rows % (shard // 2)
+    spread_keys = (spread_rows == group * shard + within).astype(bf16)
+    spread_values = (spread_rows == group * shard + shard // 2 + within).astype(bf16)
+    context_spread = jnp.concatenate(
+        [dot(context[0], spread_keys).astype(bf16), dot(context[0], spread_values).astype(bf16)],
+        axis=0,
+    )
+    inward_same, inward_other, context_spread, expand_part, moving = tie(
+        inward_same, inward_other, context_spread, expand_part, moving
+    )
+
+    inward_own, extra_all = both_cores(
+        inward_same, inward_other, core_place, [shard, extra_rows]
+    )
+    inward_own = inward_own.reshape(D, 3 * padded)
+    extra_all = extra_all.reshape(dp_count, seq_count, extra_rows * 3 * padded)
     time_full = extra_all[:, :, : time_shard * D].reshape(TFEAT, D)
     gains_all = extra_all[:, :, time_shard * D : time_shard * D + 3 * shard]
     gains_all = gains_all.reshape(dp_count, seq_count, 3, shard).astype(f32)
     attend_gain = gains_all[:, :, 0].reshape(D)
     cross_gain = gains_all[:, :, 1].reshape(D)
     feed_gain = gains_all[:, :, 2].reshape(D)
-    steps_all = lax.all_gather(timesteps, "dp", axis=0, tiled=True)
-
-    packed = jnp.concatenate(
-        [
-            self_outward,
-            cross_keyval[:, :D],
-            cross_keyval[:, D:],
-            cross_query,
-            cross_return,
-        ],
-        axis=0,
-    )
-    lined = lax.all_gather(packed, "seq")
-    cotangent_all = chip_gather(cotangent[0], "dp").reshape(dp_count * frame_count, D)
-    outward_full = chip_gather_ordered(lined[:, :shard], "dp", dp_place).reshape(D, D)
-    keyval_rows = chip_gather_ordered(lined[:, shard : 2 * shard], "dp", dp_place)
-    keyval_full = jnp.concatenate(
-        [
-            keyval_rows[:, :, : shard // 2].reshape(D // 2, D),
-            keyval_rows[:, :, shard // 2 :].reshape(D // 2, D),
-        ],
-        axis=1,
-    )
-    query_full = chip_gather_ordered(lined[:, 2 * shard : 3 * shard], "dp", dp_place).reshape(D, D)
-    return_full = chip_gather_ordered(lined[:, 3 * shard :], "dp", dp_place).reshape(D, D)
-
-    expand_blocks = (
-        expand_weight.reshape(shard, 2, dp_count, hidden_width)
-        .transpose(2, 0, 1, 3)
-        .reshape(dp_count, shard, 2 * hidden_width)
-    )
-    expand_part = lax.all_to_all(expand_blocks, "dp", 0, 0, tiled=True)
-    expand_own = (
-        lax.all_gather(expand_part, "seq", axis=1).reshape(D, 2 * hidden_width)
-    )
-    shrink_own = lax.all_gather(shrink_weight, "seq", tiled=True)
-
     feats_low = time_features(timesteps[0]).astype(bf16)
     token = dot(feats_low, time_full)
     token_norm, token_inverse = norm_forward(token)
     token_low = jnp.pad(
         (token_norm * attend_gain).astype(bf16), ((0, TOKEN_ROWS - CLIPS), (0, 0))
     )
+    row_latents = relay_join(moving, seq_place).reshape(row_length, D)
     row_norm, row_inverse = norm_forward(row_latents.astype(f32))
     row_low = jnp.concatenate([(row_norm * attend_gain).astype(bf16), token_low], axis=0)
     projected = dot(row_low, inward_own)
+    projected, lined, shrink_weight = tie(projected, lined, shrink_weight)
+    shrink_own = lax.all_gather(shrink_weight, "seq", tiled=True)
+    expand_lined = lax.all_gather(expand_part, "seq")
+    first_state = plane_open(lined[:, : 3 * shard])
     attended, attended_wide, self_level, projected_low = self_forward(
         projected, cosine, sine, clip_column, clip_row, row_length
     )
+    attended, first_state = tie(attended, first_state)
+
+    attended_blocks = attended[:, :own_width].reshape(seq_count, frame_count, own_width)
+    attended_got = line_send(attended_blocks, "seq", seq_place)
+    first_state = plane_relay(first_state)
+    second_state = plane_open(lined[:, 3 * shard :])
+    first_same = plane_chips(first_state, chip_place)
+    attended_got, first_same, second_state, cotangent, shrink_own = tie(
+        attended_got, first_same, second_state, cotangent, shrink_own
+    )
+
+    first_other = flip(first_same, 1)
+    second_state = plane_relay(second_state)
     attended_low = (
-        line_exchange(
-            attended[:, :own_width].reshape(seq_count, frame_count, own_width), "seq", seq_place
-        )
+        line_join(attended_blocks, attended_got, seq_place)
         .transpose(1, 0, 2)
         .reshape(frame_count, D)
     )
+    first_other, second_state, attended_low = tie(first_other, second_state, attended_low)
+
+    cotangent_state = plane_open(cotangent[0])
+    outward_full, keyval_full, query_full = [
+        weight.reshape(D, D)
+        for weight in both_cores(first_same, first_other, core_place, [shard] * 3)
+    ]
+    second_same = plane_chips(second_state, chip_place)
+    second_other = flip(second_same, 1)
+    keyval = dot(context_spread, keyval_full).astype(bf16)
     after_self = latents[0].astype(f32) + dot(attended_low, outward_full)
-
     norm_two, inverse_two = norm_forward(after_self)
     normed_two = (norm_two * cross_gain).astype(bf16)
     cross_heads = dot(normed_two, query_full).astype(bf16)
-    keyval = dot(context[0], keyval_full).astype(bf16)
+    cross_heads, keyval, second_other, cotangent_state = tie(
+        cross_heads, keyval, second_other, cotangent_state
+    )
+
+    cotangent_state = plane_relay(cotangent_state)
+    cotangent_same = plane_chips(cotangent_state)
+    cotangent_other = flip(cotangent_same, 1)
+    return_full = both_cores(second_same, second_other, core_place, [shard])[0].reshape(D, D)
     crossed, crossed_wide, cross_level = cross_forward(
         cross_heads, keyval, own_clips[:, None], text_clips[None, :]
     )
+    crossed, return_full, cotangent_other, expand_lined = tie(
+        crossed, return_full, cotangent_other, expand_lined
+    )
     after_cross = after_self + dot(crossed, return_full)
-
     norm_three, inverse_three = norm_forward(after_cross)
     normed_three = (norm_three * feed_gain).astype(bf16)
-    frames_all = chip_gather(normed_three, "dp").reshape(dp_count * frame_count, D)
-    gate_up = dot(frames_all, expand_own)
-    gate_part = gate_up[:, :hidden_width]
-    upward = gate_up[:, hidden_width:]
-    hidden_low = (jax.nn.silu(gate_part) * upward).astype(bf16)
-    hidden_grad = dot(cotangent_all, shrink_own.T)
-    expand_low = gated_back(hidden_grad, gate_part, upward)
-    feed_parts = dot(expand_low, expand_own.T).astype(bf16)
-    feed_norm_grad = chip_scatter(feed_parts.reshape(dp_count, frame_count, D), "dp")
-    expand_grad = dot(frames_all.T, expand_low).astype(bf16)
-    expand_sum = lax.psum_scatter(
-        expand_grad.reshape(dp_count, seq_count, shard, 2 * hidden_width).transpose(1, 0, 2, 3),
-        "seq",
-        scatter_dimension=0,
-    )
-    shrink_part = dot(hidden_low.T, cotangent_all).astype(bf16)
-    grad_shrink = lax.psum_scatter(
-        shrink_part, "seq", scatter_dimension=0, tiled=True
-    ).astype(f32)
-    out_parts = dot(hidden_low, shrink_own).astype(bf16)
-    fed = chip_scatter(out_parts.reshape(dp_count, frame_count, D), "dp")
-    block_output = (after_cross + fed).astype(bf16)
-    grad_expand = (
-        lax.all_to_all(expand_sum, "dp", 0, 0, tiled=True)
-        .reshape(dp_count, shard, 2, hidden_width)
-        .transpose(1, 2, 0, 3)
-        .reshape(shard, 2 * FF)
-        .astype(f32)
-    )
-
+    frames_state = plane_relay(plane_open(normed_three))
+
+    expand_own = (
+        expand_lined.reshape(seq_count, dp_count, shard, 2 * hidden_width)
+        .transpose(1, 0, 2, 3)
+        .reshape(D, 2 * hidden_width)
+    )
+    half_frames = chips * frame_count
+    frames_same = plane_chips(frames_state)
+    frames_other = flip(frames_same, 1)
+    frames = [frames_same.reshape(half_frames, D), frames_other.reshape(half_frames, D)]
+    tangents = [cotangent_same.reshape(half_frames, D), cotangent_other.reshape(half_frames, D)]
+    hidden_low, expand_low = [], []
+    for side in range(2):
+        gate_up = dot(frames[side], expand_own)
+        gate_part = gate_up[:, :hidden_width]
+        upward = gate_up[:, hidden_width:]
+        hidden_low.append((jax.nn.silu(gate_part) * upward).astype(bf16))
+        hidden_grad = dot(tangents[side], shrink_own.T)
+        expand_low.append(gated_back(hidden_grad, gate_part, upward))
+
+    def sides(array):
+        return array.astype(bf16).reshape(chips, frame_count, D)
+
+    feed_other = sides(dot(expand_low[1], expand_own.T))
+    feed_got = flip(feed_other, 1)
+    feed_same = sides(dot(expand_low[0], expand_own.T))
+    feed_same, feed_got, hidden_low, expand_low = tie(feed_same, feed_got, hidden_low, expand_low)
+    feed_blocks = [feed_same[r].astype(f32) + feed_got[r].astype(f32) for r in range(chips)]
+    feed_far = plane_far(feed_blocks)
+    shrink_part = (
+        dot(hidden_low[0].T, tangents[0]) + dot(hidden_low[1].T, tangents[1])
+    ).astype(bf16)
+    feed_far, shrink_part, expand_low = tie(feed_far, shrink_part, expand_low)
+    grad_shrink = lax.psum_scatter(shrink_part, "seq", scatter_dimension=0, tiled=True)
+
+    feed_near = plane_near(feed_blocks, feed_far)
+    expand_grad = (dot(frames[0].T, expand_low[0]) + dot(frames[1].T, expand_low[1])).astype(bf16)
+    expand_grad = expand_grad.reshape(dp_count, seq_count, shard, 2 * hidden_width)
+    expand_grad = expand_grad.transpose(1, 0, 2, 3).reshape(D, 2 * hidden_width)
+    feed_near, expand_grad, hidden_low = tie(feed_near, expand_grad, hidden_low)
+    expand_sum = lax.psum_scatter(expand_grad, "seq", scatter_dimension=0, tiled=True)
+    expand_sum = expand_sum.reshape(dp_count, shard, 2 * hidden_width)
+
+    def open_grad(grad):
+        grad = grad.astype(bf16).reshape(chips, 2, seq_count, shard, -1)
+        return grad, flip(take(grad, 1 - core_place, 1), 1)
+
+    def side_blocks(opened):
+        return [
+            jnp.concatenate(
+                [
+                    (
+                        take(take(grad, core_place, 1), chip_place ^ r)[0, 0].astype(f32)
+                        + take(got, chip_place ^ r)[0, 0].astype(f32)
+                    ).astype(bf16)
+                    for grad, got in opened
+                ],
+                axis=1,
+            )
+            for r in range(chips)
+        ]
+
+    feed_norm_grad = plane_total(feed_near)
     feed_term, feed_gain_part = norm_backward(
         feed_norm_grad, norm_three, inverse_three, feed_gain
     )
     after_cross_grad = cotangent[0].astype(f32) + feed_term
     return_low = after_cross_grad.astype(bf16)
     crossed_grad = dot(return_low, return_full.T).astype(bf16)
+    return_grad = open_grad(dot(crossed.T, return_low))
+    crossed_grad, return_grad = tie(crossed_grad, return_grad)
+    return_blocks = side_blocks([return_grad])
+    return_far = plane_far(return_blocks)
     cross_query_low, cross_key_low, cross_value_low = cross_backward(
         cross_heads,
         keyval,
@@ -751,6 +944,13 @@
         text_clips[:, None],
         own_clips[None, :],
     )
+    cross_query_low, cross_key_low, cross_value_low, return_far, grad_shrink = tie(
+        cross_query_low, cross_key_low, cross_value_low, return_far, grad_shrink
+    )
+    return_near = plane_near(return_blocks, return_far)
+    keyval_low = jnp.concatenate([cross_key_low, cross_value_low], axis=0)
+    keyval_grad = open_grad(dot(context_spread.T, keyval_low))
+    query_grad = open_grad(dot(normed_two.T, cross_query_low))
     cross_norm_grad = dot(cross_query_low, query_full.T)
     cross_term, cross_gain_part = norm_backward(
         cross_norm_grad, norm_two, inverse_two, cross_gain
@@ -758,36 +958,20 @@
     after_self_grad = after_cross_grad + cross_term
     outward_low = after_self_grad.astype(bf16)
     attended_grad = dot(outward_low, outward_full.T).astype(bf16)
-    attended_grad_own = line_exchange(
-        attended_grad.reshape(frame_count, seq_count, own_width).transpose(1, 0, 2),
-        "seq",
-        seq_place,
-    ).reshape(row_length, own_width)
+    attended_grad, return_near, outward_low, keyval_grad, query_grad = tie(
+        attended_grad, return_near, outward_low, keyval_grad, query_grad
+    )
+
+    grad_blocks = attended_grad.reshape(frame_count, seq_count, own_width).transpose(1, 0, 2)
+    grad_got = line_send(grad_blocks, "seq", seq_place)
+    outward_grad = open_grad(dot(attended_low.T, outward_low))
+    rest_blocks = side_blocks([keyval_grad, query_grad, outward_grad])
+    grad_got, rest_blocks = tie(grad_got, rest_blocks)
+
+    rest_far = plane_far(rest_blocks)
+    attended_grad_own = line_join(grad_blocks, grad_got, seq_place)
+    attended_grad_own = attended_grad_own.reshape(row_length, own_width)
     attended_grad_own = jnp.pad(attended_grad_own, ((0, 0), (0, padded - own_width)))
-
-    def column_sum(partial):
-        shaped = partial.astype(bf16).reshape(dp_count, seq_count, -1, D)
-        return chip_scatter_ordered(shaped, "dp", dp_place)
-
-    columns = jnp.concatenate(
-        [
-            column_sum(dot(crossed.T, return_low)),
-            column_sum(dot(context[0].T, cross_key_low)),
-            column_sum(dot(context[0].T, cross_value_low)),
-            column_sum(dot(normed_two.T, cross_query_low)),
-            column_sum(dot(attended_low.T, outward_low)),
-        ],
-        axis=1,
-    )
-    whole_sums = lax.psum_scatter(columns.astype(bf16), "seq", scatter_dimension=0).astype(f32)
-    grad_return = whole_sums[:shard]
-    grad_keyval = jnp.concatenate(
-        [whole_sums[shard : shard + shard // 2], whole_sums[shard + shard // 2 : 2 * shard]],
-        axis=1,
-    )
-    grad_query = whole_sums[2 * shard : 3 * shard]
-    grad_outward = whole_sums[3 * shard :]
-
     inward_low = self_backward(
         projected_low,
         attended_grad_own,
@@ -798,41 +982,43 @@
         clip_column,
         clip_row,
     )
+    inward_low, rest_far, expand_sum = tie(inward_low, rest_far, expand_sum)
+
+    rest_near = plane_near(rest_blocks, rest_far)
     attend_parts = dot(inward_low, inward_own.T)
-    attend_norm_grad = line_scatter(
-        attend_parts[:row_length].reshape(seq_count, frame_count, D), "seq", seq_place
-    )
-    own_norm = lax.dynamic_slice_in_dim(row_norm, seq_place * frame_count, frame_count, axis=0)
-    own_inverse = lax.dynamic_slice_in_dim(
-        row_inverse, seq_place * frame_count, frame_count, axis=0
-    )
-    attend_term, _ = norm_backward(attend_norm_grad, own_norm, own_inverse, attend_gain)
-    latents_grad = (after_self_grad + attend_term)[None]
-
-    inward_grad = dot(row_low.T, inward_low).astype(bf16)
-    inward_grad = (
-        inward_grad.reshape(D, pairs, 3, pair_width)
-        .transpose(0, 2, 1, 3)
-        .reshape(D, 3, padded)[:, :, :own_width]
-    )
-    inward_sum = chip_scatter_ordered(
-        inward_grad.reshape(dp_count, seq_count, shard, 3 * own_width), "dp", dp_place
-    )
-    grad_inward = (
-        line_exchange(inward_sum.astype(bf16), "seq", seq_place)
-        .reshape(seq_count, shard, 3, own_width)
-        .transpose(1, 2, 0, 3)
-        .reshape(shard, 3 * D)
-        .astype(f32)
-    )
-
+    attend_blocks = attend_parts[:row_length].reshape(seq_count, frame_count, D)
+    came = sum_step(attend_blocks, seq_place, 1, None)
+    inward_grad = open_grad(dot(row_low.T, inward_low))
+    came, inward_grad = tie(came, inward_grad)
+
+    for step in range(2, seq_count - 1):
+        came = sum_step(attend_blocks, seq_place, step, came)
+    inward_blocks = side_blocks([inward_grad])
+    inward_far = plane_far(inward_blocks)
     token_term, token_gain_part = norm_backward(
         attend_parts[row_length : row_length + CLIPS], token_norm, token_inverse, attend_gain
     )
     attend_gain_part = jnp.sum(attend_parts[:row_length] * row_norm, axis=0) + token_gain_part
+    feats_row = jnp.pad(feats_low.astype(f32).reshape(1, -1), ((0, 0), (0, D - CLIPS * TFEAT)))
     small = jnp.concatenate(
-        [token_term, attend_gain_part[None], cross_gain_part[None], feed_gain_part[None]], axis=0
-    )
+        [
+            token_term,
+            attend_gain_part[None],
+            cross_gain_part[None],
+            feed_gain_part[None],
+            feats_row,
+            jnp.zeros((1, D), f32),
+        ],
+        axis=0,
+    )
+    came, inward_far, rest_near, small = tie(came, inward_far, rest_near, small)
+
+    whole_column = jnp.concatenate(
+        [plane_total(return_near).astype(bf16), plane_total(rest_near).astype(bf16)], axis=1
+    )
+    whole_sums = lax.psum_scatter(whole_column, "seq", scatter_dimension=0).astype(f32)
+    came = sum_step(attend_blocks, seq_place, seq_count - 1, came)
+    inward_near = plane_near(inward_blocks, inward_far)
     device_count = dp_count * seq_count
     small_all = lax.all_to_all(
         jnp.broadcast_to(small[None], (device_count,) + small.shape),
@@ -841,8 +1027,53 @@
         0,
         tiled=True,
     )
-    small_sum = jnp.sum(small_all.reshape(dp_count, seq_count, CLIPS + 3, D), axis=1)
-    feats_all = time_features(steps_all).astype(bf16).astype(f32)
+    fed_other = sides(dot(hidden_low[1], shrink_own))
+    fed_got = flip(fed_other, 1)
+    fed_same = sides(dot(hidden_low[0], shrink_own))
+    inward_near, came, fed_got, fed_same, expand_sum = tie(
+        inward_near, came, fed_got, fed_same, expand_sum
+    )
+
+    fed_blocks = [fed_same[r].astype(f32) + fed_got[r].astype(f32) for r in range(chips)]
+    fed_far = plane_far(fed_blocks)
+    inward_sum = plane_total(inward_near).astype(bf16)
+    inward_moved = line_send(inward_sum, "seq", seq_place)
+    attend_norm_grad = take(attend_blocks, seq_place)[0]
+    attend_norm_grad = attend_norm_grad + came[0].astype(f32) + came[1].astype(f32)
+    own_norm = lax.dynamic_slice_in_dim(row_norm, seq_place * frame_count, frame_count, axis=0)
+    own_inverse = lax.dynamic_slice_in_dim(
+        row_inverse, seq_place * frame_count, frame_count, axis=0
+    )
+    attend_term, _ = norm_backward(attend_norm_grad, own_norm, own_inverse, attend_gain)
+    latents_grad = (after_self_grad + attend_term)[None]
+    grad_expand = (
+        lax.all_to_all(expand_sum, "dp", 0, 0, tiled=True)
+        .reshape(dp_count, shard, 2, hidden_width)
+        .transpose(1, 2, 0, 3)
+        .reshape(shard, 2 * FF)
+        .astype(f32)
+    )
+    fed_far, inward_moved, latents_grad, grad_expand = tie(
+        fed_far, inward_moved, latents_grad, grad_expand
+    )
+
+    fed_near = plane_near(fed_blocks, fed_far)
+    inward_rows = line_join(inward_sum, inward_moved, seq_place)
+    grad_inward = (
+        from_pairs(inward_rows).transpose(1, 2, 0, 3).reshape(shard, 3 * D).astype(f32)
+    )
+    block_output = (after_cross + plane_total(fed_near)).astype(bf16)
+    grad_return = whole_sums[:shard]
+    grad_keyval = jnp.concatenate(
+        [whole_sums[shard : shard + shard // 2], whole_sums[shard + shard // 2 : 2 * shard]],
+        axis=1,
+    )
+    grad_query = whole_sums[2 * shard : 3 * shard]
+    grad_outward = whole_sums[3 * shard :]
+    grad_shrink = grad_shrink.astype(f32)
+    small_sum = jnp.sum(small_all.reshape(dp_count, seq_count, 8, D), axis=1)
+    feats_all = small_all.reshape(dp_count, seq_count, 8, D)[:, 0, CLIPS + 3, : CLIPS * TFEAT]
+    feats_all = feats_all.reshape(dp_count, CLIPS, TFEAT)
     feats_own = lax.dynamic_slice_in_dim(feats_all, place_all * time_shard, time_shard, axis=2)
     grad_time = jnp.einsum(
         "rct,rcn->tn",
@@ -852,7 +1083,7 @@
         preferred_element_type=f32,
     )
     gain_sums = lax.dynamic_slice_in_dim(
-        jnp.sum(small_sum[:, CLIPS:], axis=0), place_all * shard, shard, axis=1
+        jnp.sum(small_sum[:, CLIPS : CLIPS + 3], axis=0), place_all * shard, shard, axis=1
     )
     return (
         block_output[None],

time: 1000 us -> 852 us (0.85)
  waiting for transfers between devices: 390 us -> 243 us
  Pallas kernels: 72.8 us -> 109 us
  local copies, waits for them, and re-layouts: 154 us -> 118 us
  starting transfers between devices: 142 us -> 122 us
  matrix products: 117 us -> 129 us
  other arithmetic: 92 us -> 103 us
    ppermute x12, waiting for transfers between devices: 158 us -> 11.7 us  [line_send(): lax.ppermute(take(blocks, lax.rem(me + step, count)), axis, [(k, (k + ste...]
    pallas_call x0 -> x13, Pallas kernels: none -> 36.8 us  [the longest x12 32.5 us: assemble(): pl.pallas_call(kernel, in_specs=[pl.BlockSpec(memory_space=pltpu.SMEM)] +...]
    dynamic_update_slice x40 -> x0, local copies, waits for them, and re-layouts: 24.1 us -> none  [place(): return lax.dynamic_update_slice(buffer, block, tuple(starts))]
    convert_element_type x15 -> x23, other arithmetic: 19.5 us -> 38.6 us  [the longest x5 14.5 us: side_blocks(): return [jnp.concatenate([(take(take(grad, core_place, 1), chip_place ^ r)...]
    another operation x15 -> x4, local copies, waits for them, and re-layouts: 19.5 us -> 2.5 us  [the longest x1 9.53 us: chip_scatter_ordered(): pairs = parts.reshape((count // 2, 2) + parts.shape[1:])]
    reshape x5 -> x4, local copies, waits for them, and re-layouts: 20.7 us -> 4.54 us  [the longest x1 2.53 us: on_device(): expand_grad.reshape(dp_count, seq_count, shard, 2 * hidden_width)]
    add x10 -> x3, other arithmetic: 22 us -> 6.54 us  [the longest x1 3.9 us: on_device(): fed_same[r].astype(f32) + fed_got[r].astype(f32)]
    all_gather x1, waiting for transfers between devices: 15.3 us -> 0.01 us  [on_device(): shrink_own = lax.all_gather(shrink_weight, 'seq', tiled=True)]
  transfers between devices with their start and end apart: 105 -> 85, of which waited for: 49 -> 33; matrix products, arithmetic and copies ran while one was open for 31% -> 33% of each run, Pallas kernels for 7% -> 13%
where the time goes in v3:
time: 852 us; the launch traced here: 840 us
  waiting for transfers between devices  243 us (29%)
  matrix products  129 us (15%)
  starting transfers between devices  122 us (14%)
  local copies, waits for them, and re-layouts  118 us (14%)
  Pallas kernels  109 us (13%)
  other arithmetic  103 us (12%)
  between operations  16.7 us (2%)
    dot_general x29, matrix products, dot(): return jnp.dot(left, right, preferred_element_type=jnp.float32)  128 us
    ppermute x52, waiting for transfers between devices, flip(): return lax.ppermute(values, 'dp', xor_pairs(lax.axis_size('dp'), bit))  127 us
    ppermute x52, starting transfers between devices, flip(): return lax.ppermute(values, 'dp', xor_pairs(lax.axis_size('dp'), bit))  47 us
    unnamed x310, local copies, waits for them, and re-layouts  40.4 us
    pallas_call x12, Pallas kernels, assemble(): pl.pallas_call(kernel, in_specs=[pl.BlockSpec(memory_space=pltpu.SMEM)] +...  32.5 us
    ppermute x3, starting transfers between devices, sum_step(): lax.ppermute(to_right.astype(low), 'seq', [(k, k + 1) for k in range(0, s...  31 us
    ppermute x3, waiting for transfers between devices, relay_step(): lax.ppermute(leftward[-1], 'seq', [(k + 1, k) for k in range(0, count - s...  28.3 us
    ppermute x3, waiting for transfers between devices, sum_step(): lax.ppermute(to_left.astype(low), 'seq', [(k + 1, k) for k in range(count...  25.6 us
  transfers between devices with their start and end apart: 85, of which 33 were waited for; matrix products, arithmetic and copies ran while one was open for 33% of the time, Pallas kernels for 13%

profile of v3, /device:TPU:0, one launch (start us, length us, event | category | flops | bytes accessed | tf_op | source)
XLA Modules:
  0.0 840.5 jit_solution(4043935908589433312)
XLA Ops:
  95.0 7.6 all-to-all-done
  102.6 22.9 %collective-permute-done.13.refs_6_ = bf16[256,1536]{1,0:T(8,128)(2,1)} collective-permute-done((bf16[256,1536]{1,0:T(8,128)(2,1)}, bf16[256,1536]{1,0:T(8,128)(2,1)}, u32[]{:S(2)}, u32[]{:S(2)}) %collective-permute-start.13) | collective-permute-done | bytes 786464 | tf_op jit(solution)/shard_map/ppermute | solution.py:583
  163.5 23.3 %shard_map.259 = (bf16[1024,384]{1,0:T(8,128)(2,1)S(1)}, f32[1024,384]{1,0:T(8,128)S(1)}, f32[1024,384]{1,0:T(8,128)S(1)}, bf16[1152,1152]{1,0:T(8,128)(2,1)}) custom-call(f32[1152,1152]{1,0:T(8,128)} %fusion.15.projected, f32[1152,128]{1,0:T(8,128)S(1)} %copy-done.20, f32[1152,128]{1,0:T(8,128)S(1)} %copy-done.18, f32[1152,1]{1,0:T(8,128)S(1)} %copy-done.22, ...), custom_call_target="tpu_custom_call" | custom-call | flops 120000004096 | bytes 1048576 | tf_op jit(solution)/shard_map/pallas_call | solution.py:221
  186.8 7.5 collective-permute-done.14.refs_1_
  203.6 15.9 %collective-permute-done.19.refs_3_ = bf16[2,144,1536]{2,1,0:T(8,128)(2,1)S(1)} collective-permute-done((bf16[2,144,1536]{2,1,0:T(8,128)(2,1)S(1)}, bf16[2,144,1536]{2,1,0:T(8,128)(2,1)S(1)}, u32[]{:S(2)}, u32[]{:S(2)}) %collective-permute-start.19) | collective-permute-done | bytes 884768 | tf_op jit(solution)/shard_map/ppermute | solution.py:423
  244.9 8.9 %shard_map.262 = (bf16[4,2,4,48,1536]{4,3,2,1,0:T(8,128)(2,1)S(1)}, bf16[4,2,4,48,1536]{4,3,2,1,0:T(8,128)(2,1)}, bf16[4,2,4,48,1536]{4,3,2,1,0:T(8,128)(2,1)}) custom-call(s32[1]{0:T(128)} %bitcast.12.places_ref, bf16[4,4,144,1536]{3,2,1,0:T(8,128)(2,1)} %shard_map.260.refs_0_, bf16[4,4,144,1536]{3,2,1,0:T(8,128)(2,1)} %collective-permute-done.23.refs_1_), custom_call_target="tpu_custom_call" | custom-call | bytes 28311552 | tf_op jit(solution)/shard_map/pallas_call | solution.py:448
  272.3 8.4 collective-permute-done.29.refs_3_
  290.7 12.1 %shard_map.264 = (bf16[256,1536]{1,0:T(8,128)(2,1)S(1)}, f32[256,1536]{1,0:T(8,128)S(1)}, f32[256,1536]{1,0:T(8,128)S(1)}) custom-call(bf16[256,1536]{1,0:T(8,128)(2,1)S(1)} %copy-done.36, bf16[768,1536]{1,0:T(8,128)(2,1)} %convolution_convert_fusion.9.keys.values, bf16[768,1536]{1,0:T(8,128)(2,1)} %convolution_convert_fusion.9.keys.values, ...), custom_call_target="tpu_custom_call" | custom-call | flops 20000000000 | bytes 1048576 | tf_op jit(solution)/shard_map/pallas_call | solution.py:278
  304.1 14.1 %all-gather.10.cloned.1.call-done = bf16[32,48,1536]{2,1,0:T(8,128)(2,1)} async-done(((bf16[8,48,1536]{2,1,0:T(8,128)(2,1)}), bf16[32,48,1536]{2,1,0:T(8,128)(2,1)}) %all-gather.10.cloned.1.call-update) | async-done | bytes 4718608 | tf_op jit(solution)/shard_map/all_gather | solution.py:810
  326.2 16.4 %collective-permute-done.32.refs_1_ = bf16[256,1536]{1,0:T(8,128)(2,1)S(1)} collective-permute-done((bf16[256,1536]{1,0:T(8,128)(2,1)S(1)}, bf16[256,1536]{1,0:T(8,128)(2,1)S(1)}, u32[]{:S(2)}, u32[]{:S(2)}) %collective-permute-start.32) | collective-permute-done | bytes 786464 | tf_op jit(solution)/shard_map/ppermute | solution.py:423
  362.5 7.3 fusion.110
  427.4 9.5 %fusion.112 = f32[1536,1536]{1,0:T(8,128)} fusion(bf16[1024,1536]{1,0:T(8,128)(2,1)} %bitcast.36, bf16[1024,1536]{0,1:T(8,128)(2,1)S(1)} %copy-done.75), kind=kOutput, calls=%fused_computation.345 | convolution fusion | flops 4831838208 | bytes 15728640 | tf_op jit(solution)/shard_map/dot_general | solution.py:415
  437.0 9.6 %add_convert_fusion = bf16[1536,1536]{1,0:T(8,128)(2,1)S(1)} fusion(f32[1536,1536]{1,0:T(8,128)} %fusion.112, bf16[1024,1536]{1,0:T(8,128)(2,1)} %bitcast.391, bf16[1024,1536]{0,1:T(8,128)(2,1)} %pad_maximum_fusion), kind=kOutput, calls=%fused_computation | convolution fusion | flops 4836556800 | bytes 20447232 | tf_op jit(solution)/shard_map/dot_general | solution.py:415
  471.1 13.0 %shard_map.268 = (bf16[256,1536]{1,0:T(8,128)(2,1)S(1)}, bf16[384,1536]{1,0:T(8,128)(2,1)S(1)}, bf16[384,1536]{1,0:T(8,128)(2,1)S(1)}) custom-call(bf16[256,1536]{1,0:T(8,128)(2,1)S(1)} %copy-done.37, bf16[768,1536]{1,0:T(8,128)(2,1)} %convolution_convert_fusion.9.keys.values, bf16[768,1536]{1,0:T(8,128)(2,1)} %convolution_convert_fusion.9.keys.values, ...), custom_call_target="tpu_custom_call" | custom-call | flops 120000004096 | bytes 1048576 | tf_op jit(solution)/shard_map/pallas_call | solution.py:304
  509.0 9.7 %collective-permute-done.46 = bf16[4,48,1536]{2,1,0:T(8,128)(2,1)S(1)} collective-permute-done((bf16[4,48,1536]{2,1,0:T(8,128)(2,1)S(1)}, bf16[4,48,1536]{2,1,0:T(8,128)(2,1)S(1)}, u32[]{:S(2)}, u32[]{:S(2)}) %collective-permute-start.46) | collective-permute-done | bytes 589856 | tf_op jit(solution)/shard_map/ppermute | solution.py:423
  552.4 10.5 %collective-permute-done.50.refs_2_ = bf16[1,256,384]{2,1,0:T(8,128)(2,1)S(1)} collective-permute-done((bf16[1,256,384]{2,1,0:T(8,128)(2,1)}, bf16[1,256,384]{2,1,0:T(8,128)(2,1)S(1)}, u32[]{:S(2)}, u32[]{:S(2)}) %collective-permute-start.50) | collective-permute-done | bytes 196640 | tf_op jit(solution)/shard_map/ppermute | solution.py:397
  569.6 23.8 %shard_map.270 = bf16[1152,1152]{1,0:T(8,128)(2,1)} custom-call(bf16[1152,1152]{1,0:T(8,128)(2,1)} %get-tuple-element.235.low, bf16[1024,384]{1,0:T(8,128)(2,1)S(1)} %bitcast.348, f32[1024,384]{1,0:T(8,128)S(1)} %copy-done.41, f32[1024,384]{1,0:T(8,128)S(1)} %copy-done.43, f32[1152,128]{1,0:T(8,128)S(1)} %copy-done.21, f32[1152,128]{1,0:T(8,128)S(1)} %copy-done.19, ...), custom_call_target="tpu_custom_call" | custom-call | flops 15000000512 | bytes 1048576 | tf_op jit(solution)/shard_map/pallas_call | solution.py:249
  593.4 7.7 fusion.113
  609.8 21.3 %collective-permute-start.55 = (bf16[256,1536]{1,0:T(8,128)(2,1)}, bf16[256,1536]{1,0:T(8,128)(2,1)}, u32[]{:S(2)}, u32[]{:S(2)}) collective-permute-start(bf16[256,1536]{1,0:T(8,128)(2,1)} %get-tuple-element.366), channel_id=1, source_target_pairs={{0,1},{4,5},{8,9},{12,13},{16,17},{20,21},{24,25},{28,29}} | collective-permute-start | bytes 2359304 | tf_op jit(solution)/shard_map/ppermute | solution.py:653
  658.9 19.3 %collective-permute-done.62 = bf16[4,144,1536]{2,1,0:T(8,128)(2,1)} collective-permute-done((bf16[4,144,1536]{2,1,0:T(8,128)(2,1)}, bf16[4,144,1536]{2,1,0:T(8,128)(2,1)}, u32[]{:S(2)}, u32[]{:S(2)}) %collective-permute-start.62) | collective-permute-done | bytes 1769504 | tf_op jit(solution)/shard_map/ppermute | solution.py:423
  678.8 7.6 collective-permute-done.63
  707.4 9.3 %collective-permute-done.66 = bf16[256,1536]{1,0:T(8,128)(2,1)} collective-permute-done((bf16[256,1536]{1,0:T(8,128)(2,1)}, bf16[256,1536]{1,0:T(8,128)(2,1)}, u32[]{:S(2)}, u32[]{:S(2)}) %collective-permute-start.66) | collective-permute-done | bytes 786464 | tf_op jit(solution)/shard_map/ppermute | solution.py:653
  716.7 25.6 %collective-permute-done.67 = bf16[256,1536]{1,0:T(8,128)(2,1)} collective-permute-done((bf16[256,1536]{1,0:T(8,128)(2,1)}, bf16[256,1536]{1,0:T(8,128)(2,1)}, u32[]{:S(2)}, u32[]{:S(2)}) %collective-permute-start.67) | collective-permute-done | bytes 786464 | tf_op jit(solution)/shard_map/ppermute | solution.py:654
  767.5 12.2 %all-to-all-done.1 = bf16[8,48,1536]{2,1,0:T(8,128)(2,1)} async-done(((bf16[8,48,1536]{2,1,0:T(8,128)(2,1)}), bf16[8,48,1536]{2,1,0:T(8,128)(2,1)}, u32[]{:S(2)}, u32[]{:S(2)}) %all-to-all-start.1) | async-done | bytes 1179680 | tf_op jit(solution)/shard_map/all_to_all | solution.py:1050
  (710 shorter events, 500.0 us)
Async XLA Ops:
  78.1 47.4 %collective-permute-start.11 = (bf16[4,4,64,1152]{3,2,1,0:T(8,128)(2,1)S(1)}, bf16[4,4,64,1152]{3,2,1,0:T(8,128)(2,1)}, u32[]{:S(2)}, u32[]{:S(2)}) collective-permute-start(bf16[4,4,64,1152]{3,2,1,0:T(8,128)(2,1)S(1)} %shard_map.256.refs_0_), channel_id=1, source_target_pairs={{0,4},{4,0},{8,12},{12,8},{16,20},{20,16},{24,28},{28,24},{1,5},{5... | collective-permute-start | bytes 7077896 | tf_op jit(solution)/shard_map/ppermute | solution.py:423
  85.8 69.2 %all-gather.8.cloned.1.call-start = ((), (), s32[]{:S(2)}) async-start(), calls=%async_computation.10 | async-start | bytes 2949120 | tf_op jit(solution)/shard_map/all_gather | solution.py:771
  89.7 35.8 %collective-permute-start.13 = (bf16[256,1536]{1,0:T(8,128)(2,1)}, bf16[256,1536]{1,0:T(8,128)(2,1)}, u32[]{:S(2)}, u32[]{:S(2)}) collective-permute-start(bf16[256,1536]{1,0:T(8,128)(2,1)} %collective-permute-done.10.refs_5_), channel_id=1, source_target_pairs={{1,0},{5,4},{9,8},{13,12},{17,16},{21,20},{25,24},{29,28}} | collective-permute-start | bytes 2359304 | tf_op jit(solution)/shard_map/ppermute | solution.py:583
  94.8 134.3 %all-gather.6.cloned.1.call-start = ((), (), s32[]{:S(2)}) async-start(), calls=%async_computation.6 | async-start | bytes 2949120 | tf_op jit(solution)/shard_map/all_gather | solution.py:809
  156.6 37.7 %collective-permute-start.14 = (bf16[4,144,1536]{2,1,0:T(8,128)(2,1)S(1)}, bf16[4,144,1536]{2,1,0:T(8,128)(2,1)S(1)}, u32[]{:S(2)}, u32[]{:S(2)}) collective-permute-start(bf16[4,144,1536]{2,1,0:T(8,128)(2,1)S(1)} %slice.333.refs_0_), channel_id=1, source_target_pairs={{0,8},{4,12},{8,0},{12,4},{16,24},{20,28},{24,16},{28,20},{1,9},{5... | collective-permute-start | bytes 5308424 | tf_op jit(solution)/shard_map/ppermute | solution.py:423
  158.7 38.1 %collective-permute-start.15 = (bf16[4,144,1536]{2,1,0:T(8,128)(2,1)S(1)}, bf16[4,144,1536]{2,1,0:T(8,128)(2,1)}, u32[]{:S(2)}, u32[]{:S(2)}) collective-permute-start(bf16[4,144,1536]{2,1,0:T(8,128)(2,1)S(1)} %slice.333.refs_0_), channel_id=1, source_target_pairs={{0,16},{4,20},{8,24},{12,28},{16,0},{20,4},{24,8},{28,12},{1,17},{... | collective-permute-start | bytes 5308424 | tf_op jit(solution)/shard_map/ppermute | solution.py:423
  160.2 158.0 %all-gather.10.cloned.1.call-start = ((), (), s32[]{:S(2)}) async-start(), calls=%async_computation.11 | async-start | bytes 5898240 | tf_op jit(solution)/shard_map/all_gather | solution.py:810
  229.1 256.8 %reduce-scatter.4.cloned.1.call-start = ((), (), s32[]{:S(2)}) async-start(), calls=%async_computation.7 | async-start | bytes 2949120 | tf_op jit(solution)/shard_map/reduce_scatter | solution.py:898
  285.4 32.7 %collective-permute-start.31 = (bf16[4,256,1536]{2,1,0:T(8,128)(2,1)}, bf16[4,256,1536]{2,1,0:T(8,128)(2,1)}, u32[]{:S(2)}, u32[]{:S(2)}) collective-permute-start(bf16[4,256,1536]{2,1,0:T(8,128)(2,1)} %shard_map.266), channel_id=1, source_target_pairs={{0,4},{4,0},{8,12},{12,8},{16,20},{20,16},{24,28},{28,24},{1,5},{5... | collective-permute-start | bytes 9437192 | tf_op jit(solution)/shard_map/ppermute | solution.py:423
  437.0 156.4 %reduce-scatter.6.cloned.1.call-start = ((), (), s32[]{:S(2)}) async-start(), calls=%async_computation.8 | async-start | bytes 5898240 | tf_op jit(solution)/shard_map/reduce_scatter | solution.py:905
  458.7 371.9 %reduce-scatter.8.cloned.1.call-start = ((), (), s32[]{:S(2)}) async-start(), calls=%async_computation.9 | async-start | bytes 2949120 | tf_op jit(solution)/shard_map/reduce_scatter | solution.py:1019
  529.9 177.6 %collective-permute-start.68 = (bf16[4,256,1536]{2,1,0:T(8,128)(2,1)}, bf16[4,256,1536]{2,1,0:T(8,128)(2,1)}, u32[]{:S(2)}, u32[]{:S(2)}) collective-permute-start(bf16[4,256,1536]{2,1,0:T(8,128)(2,1)} %bitcast.94), channel_id=1, source_target_pairs={{0,4},{4,0},{8,12},{12,8},{16,20},{20,16},{24,28},{28,24},{1,5},{5... | collective-permute-start | bytes 9437192 | tf_op jit(solution)/shard_map/ppermute | solution.py:423
  609.8 37.3 %collective-permute-start.55 = (bf16[256,1536]{1,0:T(8,128)(2,1)}, bf16[256,1536]{1,0:T(8,128)(2,1)}, u32[]{:S(2)}, u32[]{:S(2)}) collective-permute-start(bf16[256,1536]{1,0:T(8,128)(2,1)} %get-tuple-element.366), channel_id=1, source_target_pairs={{0,1},{4,5},{8,9},{12,13},{16,17},{20,21},{24,25},{28,29}} | collective-permute-start | bytes 2359304 | tf_op jit(solution)/shard_map/ppermute | solution.py:653
  636.9 41.3 %collective-permute-start.62 = (bf16[4,144,1536]{2,1,0:T(8,128)(2,1)}, bf16[4,144,1536]{2,1,0:T(8,128)(2,1)}, u32[]{:S(2)}, u32[]{:S(2)}) collective-permute-start(bf16[4,144,1536]{2,1,0:T(8,128)(2,1)} %pad_maximum_fusion.8), channel_id=1, source_target_pairs={{0,8},{4,12},{8,0},{12,4},{16,24},{20,28},{24,16},{28,20},{1,9},{5... | collective-permute-start | bytes 5308424 | tf_op jit(solution)/shard_map/ppermute | solution.py:423
  647.2 39.3 %collective-permute-start.63 = (bf16[4,144,1536]{2,1,0:T(8,128)(2,1)S(1)}, bf16[4,144,1536]{2,1,0:T(8,128)(2,1)S(1)}, u32[]{:S(2)}, u32[]{:S(2)}) collective-permute-start(bf16[4,144,1536]{2,1,0:T(8,128)(2,1)S(1)} %pad_maximum_fusion.9), channel_id=1, source_target_pairs={{0,16},{4,20},{8,24},{12,28},{16,0},{20,4},{24,8},{28,12},{1,17},{... | collective-permute-start | bytes 5308424 | tf_op jit(solution)/shard_map/ppermute | solution.py:423
  650.7 41.6 %collective-permute-start.58 = (bf16[256,1536]{1,0:T(8,128)(2,1)S(1)}, bf16[256,1536]{1,0:T(8,128)(2,1)S(1)}, u32[]{:S(2)}, u32[]{:S(2)}) collective-permute-start(bf16[256,1536]{1,0:T(8,128)(2,1)S(1)} %get-tuple-element.364), channel_id=1, source_target_pairs={{0,1},{1,2},{4,5},{5,6},{8,9},{9,10},{12,13},{13,14},{16,17},{17,1... | collective-permute-start | bytes 2359304 | tf_op jit(solution)/shard_map/ppermute | solution.py:653
  655.2 37.2 %collective-permute-start.59 = (bf16[256,1536]{1,0:T(8,128)(2,1)S(1)}, bf16[256,1536]{1,0:T(8,128)(2,1)S(1)}, u32[]{:S(2)}, u32[]{:S(2)}) collective-permute-start(bf16[256,1536]{1,0:T(8,128)(2,1)S(1)} %get-tuple-element.363), channel_id=1, source_target_pairs={{2,1},{3,2},{6,5},{7,6},{10,9},{11,10},{14,13},{15,14},{18,17},{19... | collective-permute-start | bytes 2359304 | tf_op jit(solution)/shard_map/ppermute | solution.py:654
  702.2 40.2 %collective-permute-start.67 = (bf16[256,1536]{1,0:T(8,128)(2,1)}, bf16[256,1536]{1,0:T(8,128)(2,1)}, u32[]{:S(2)}, u32[]{:S(2)}) collective-permute-start(bf16[256,1536]{1,0:T(8,128)(2,1)} %get-tuple-element.361), channel_id=1, source_target_pairs={{1,0},{2,1},{3,2},{5,4},{6,5},{7,6},{9,8},{10,9},{11,10},{13,12},{... | collective-permute-start | bytes 2359304 | tf_op jit(solution)/shard_map/ppermute | solution.py:654
  747.2 47.3 %collective-permute-start.69 = (bf16[128,1536]{1,0:T(8,128)(2,1)}, bf16[128,1536]{1,0:T(8,128)(2,1)}, u32[]{:S(2)}, u32[]{:S(2)}) collective-permute-start(bf16[128,1536]{1,0:T(8,128)(2,1)} %get-tuple-element.387), channel_id=1, source_target_pairs={{0,8},{4,12},{8,0},{12,4},{16,24},{20,28},{24,16},{28,20},{1,9},{5... | collective-permute-start | bytes 1179656 | tf_op jit(solution)/shard_map/ppermute | solution.py:423
  748.6 45.9 %collective-permute-start.70 = (bf16[128,1536]{1,0:T(8,128)(2,1)}, bf16[128,1536]{1,0:T(8,128)(2,1)}, u32[]{:S(2)}, u32[]{:S(2)}) collective-permute-start(bf16[128,1536]{1,0:T(8,128)(2,1)} %get-tuple-element.386), channel_id=1, source_target_pairs={{0,16},{4,20},{8,24},{12,28},{16,0},{20,4},{24,8},{28,12},{1,17},{... | collective-permute-start | bytes 1179656 | tf_op jit(solution)/shard_map/ppermute | solution.py:423
  751.9 42.7 %collective-permute-start.71 = (bf16[1,48,1152]{2,1,0:T(8,128)(2,1)}, bf16[1,48,1152]{2,1,0:T(8,128)(2,1)S(1)}, u32[]{:S(2)}, u32[]{:S(2)}) collective-permute-start(bf16[1,48,1152]{2,1,0:T(8,128)(2,1)} %get-tuple-element.403), channel_id=1, source_target_pairs={{0,1},{1,2},{2,3},{3,0},{4,5},{5,6},{6,7},{7,4},{8,9},{9,10},{10,1... | collective-permute-start | bytes 331784 | tf_op jit(solution)/shard_map/ppermute | solution.py:397
  751.9 42.7 %collective-permute-start.72 = (bf16[1,48,1152]{2,1,0:T(8,128)(2,1)}, bf16[1,48,1152]{2,1,0:T(8,128)(2,1)S(1)}, u32[]{:S(2)}, u32[]{:S(2)}) collective-permute-start(bf16[1,48,1152]{2,1,0:T(8,128)(2,1)} %get-tuple-element.402), channel_id=1, source_target_pairs={{0,2},{1,3},{2,0},{3,1},{4,6},{5,7},{6,4},{7,5},{8,10},{9,11},{10,... | collective-permute-start | bytes 331784 | tf_op jit(solution)/shard_map/ppermute | solution.py:397
  751.9 42.7 %collective-permute-start.73 = (bf16[1,48,1152]{2,1,0:T(8,128)(2,1)}, bf16[1,48,1152]{2,1,0:T(8,128)(2,1)S(1)}, u32[]{:S(2)}, u32[]{:S(2)}) collective-permute-start(bf16[1,48,1152]{2,1,0:T(8,128)(2,1)} %get-tuple-element.401), channel_id=1, source_target_pairs={{0,3},{1,0},{2,1},{3,2},{4,7},{5,4},{6,5},{7,6},{8,11},{9,8},{10,9... | collective-permute-start | bytes 331784 | tf_op jit(solution)/shard_map/ppermute | solution.py:397
  781.1 47.3 %all-to-all-start.2 = ((f32[32,8,1536]{2,1,0:T(8,128)}), f32[32,8,1536]{2,1,0:T(8,128)S(1)}, u32[]{:S(2)}, u32[]{:S(2)}) async-start(f32[32,8,1536]{2,1,0:T(8,128)} %broadcast_in_dim.40), calls=%async_computation.5 | async-start | bytes 3145728 | tf_op jit(solution)/shard_map/all_to_all | solution.py:1023
  (213 other events, 2370.8 us)
Sparse Core Ops, SparseCore 0:
  94.9 55.1 all-gather.7
  160.3 48.8 all-gather.5
  229.2 88.9 all-gather.9
  437.1 46.1 reduce-scatter.3
  485.4 97.3 reduce-scatter.5
  707.5 58.3 reduce-scatter.7

commit v4 on v3

--- a/solution.py
+++ b/solution.py
@@ -391,24 +391,8 @@
     return [1 << b for b in range(1, count.bit_length() - 1)]
 
 
-def line_send(blocks, axis, me):
-    count = lax.axis_size(axis)
-    return [
-        lax.ppermute(
-            take(blocks, lax.rem(me + step, count)),
-            axis,
-            [(k, (k + step) % count) for k in range(count)],
-        )
-        for step in range(1, count)
-    ]
-
-
-def line_exchange(blocks, axis, me):
-    count = lax.axis_size(axis)
-    result = blocks
-    for step, got in enumerate(line_send(blocks, axis, me), 1):
-        result = place(result, got, 0, lax.rem(me - step + count, count))
-    return result
+def line_swap(blocks, split=0, join=0):
+    return lax.all_to_all(blocks, "seq", split, join, tiled=True)
 
 
 def dot(left, right):
@@ -571,90 +555,6 @@
     for got in near[1:]:
         total = total + got.astype(jnp.float32)
     return total
-
-
-def relay_step(state, step):
-    count = lax.axis_size("seq")
-    rightward, leftward = state
-    return (
-        rightward
-        + [lax.ppermute(rightward[-1], "seq", [(k, k + 1) for k in range(step - 1, count - 1)])],
-        leftward
-        + [lax.ppermute(leftward[-1], "seq", [(k + 1, k) for k in range(0, count - step)])],
-    )
-
-
-def relay_join(state, me):
-    rightward, leftward = state
-    count = len(rightward)
-    shape = rightward[0].shape
-
-    def kernel(me_ref, *refs):
-        right, left, result = refs[:count], refs[count : 2 * count - 1], refs[-1]
-        index = me_ref[0]
-        result[pl.ds(index, 1)] = right[0][...][None]
-        for step in range(1, count):
-            target = lax.rem(index - step + count, count)
-
-            @pl.when(index >= step)
-            def _(step=step, target=target):
-                result[pl.ds(target, 1)] = right[step][...][None]
-
-            @pl.when(index < step)
-            def _(step=step, target=target):
-                result[pl.ds(target, 1)] = left[count - step - 1][...][None]
-
-    return pl.pallas_call(
-        kernel,
-        in_specs=[pl.BlockSpec(memory_space=pltpu.SMEM)]
-        + [pl.BlockSpec(memory_space=pltpu.VMEM)] * (2 * count - 1),
-        out_specs=pl.BlockSpec(memory_space=pltpu.VMEM),
-        out_shape=jax.ShapeDtypeStruct((count,) + shape, rightward[0].dtype),
-        compiler_params=pltpu.CompilerParams(vmem_limit_bytes=48 * 1024 * 1024),
-        cost_estimate=pl.CostEstimate(
-            flops=0, bytes_accessed=6 * count * math.prod(shape), transcendentals=0
-        ),
-    )(me.reshape(1).astype(jnp.int32), *rightward, *leftward[1:])
-
-
-def line_join(blocks, got, me):
-    count = len(got) + 1
-    alone = blocks.shape[0] != count
-    moves = [
-        (
-            0,
-            everything if alone else lambda places: pl.ds(places[0], 1),
-            0,
-            lambda places: pl.ds(places[0], 1),
-        )
-    ]
-    for step in range(1, count):
-        moves.append(
-            (
-                step,
-                everything,
-                0,
-                lambda places, step=step: pl.ds(lax.rem(places[0] - step + count, count), 1),
-            )
-        )
-    shape = (count,) + blocks.shape[1:]
-    return assemble([blocks] + got, [shape], moves, me.reshape(1).astype(jnp.int32))[0]
-
-
-def sum_step(parts, me, step, came):
-    count = lax.axis_size("seq")
-    to_right = take(parts, jnp.minimum(me + count - step, count - 1))[0].astype(jnp.float32)
-    to_left = take(parts, jnp.maximum(me - count + step, 0))[0].astype(jnp.float32)
-    if came is not None:
-        to_right = to_right + came[0].astype(jnp.float32)
-        to_left = to_left + came[1].astype(jnp.float32)
-    low = jnp.bfloat16
-    return (
-        lax.ppermute(to_right.astype(low), "seq", [(k, k + 1) for k in range(0, step)]),
-        lax.ppermute(
-            to_left.astype(low), "seq", [(k + 1, k) for k in range(count - 1 - step, count - 1)]
-        ),
-    )
 
 
 def on_device(
@@ -746,43 +646,57 @@
         .reshape(dp_count, shard, 2 * hidden_width)
     )
 
-    inward_got = line_send(inward_send, "seq", seq_place)
-    inward_got, latents = tie(inward_got, latents)
-
-    moving = ([latents[0]], [latents[0]])
-    for step in range(1, seq_count - 2):
-        moving = relay_step(moving, step)
-    inward_columns = line_join(inward_send, inward_got, seq_place)
-    inward_state = plane_open(inward_columns)
-    packed = jnp.concatenate(
-        [self_outward, cross_keyval[:, :D], cross_keyval[:, D:], cross_query, cross_return],
-        axis=0,
-    )
-    inward_state, moving, cosine, sine, packed, expand_blocks = tie(
-        inward_state, moving, cosine, sine, packed, expand_blocks
-    )
-
-    moving = relay_step(moving, seq_count - 2)
-    inward_state = plane_relay(inward_state)
-    inward_same = plane_chips(inward_state, chip_place)
-    inward_same, moving, packed = tie(inward_same, moving, packed)
-
-    moving = relay_step(moving, seq_count - 1)
-    lined = lax.all_gather(packed, "seq")
-    inward_other = flip(inward_same, 1)
-    expand_part = lax.all_to_all(expand_blocks, "dp", 0, 0, tiled=True)
     spread_rows = jnp.arange(D, dtype=jnp.int32)[None, :]
     context_rows = jnp.arange(D // 2, dtype=jnp.int32)[:, None]
     group, within = context_rows // (shard // 2), context_rows % (shard // 2)
     spread_keys = (spread_rows == group * shard + within).astype(bf16)
     spread_values = (spread_rows == group * shard + shard // 2 + within).astype(bf16)
+    stacked = jnp.concatenate(
+        [
+            latents[0],
+            self_outward,
+            cross_query,
+            cross_keyval[:, :D],
+            cross_keyval[:, D:],
+            cross_return,
+        ],
+        axis=0,
+    )
+    lined = lax.all_gather(stacked, "seq")
+    inward_columns = line_swap(inward_send)
+    inward_columns, cotangent = tie(inward_columns, cotangent)
+
+    inward_state = plane_open(inward_columns)
+    cotangent_state = plane_open(cotangent[0])
+    context_other = flip(context, 1)
     context_spread = jnp.concatenate(
         [dot(context[0], spread_keys).astype(bf16), dot(context[0], spread_values).astype(bf16)],
         axis=0,
     )
-    inward_same, inward_other, context_spread, expand_part, moving = tie(
-        inward_same, inward_other, context_spread, expand_part, moving
-    )
+    inward_state, cotangent_state, context_spread, context_other = tie(
+        inward_state, cotangent_state, context_spread, context_other
+    )
+
+    inward_state = plane_relay(inward_state)
+    cotangent_state = plane_relay(cotangent_state)
+    inward_same = plane_chips(inward_state, chip_place)
+    core_rows = jnp.arange(D // 2, dtype=jnp.int32)[None, :]
+    core_rows = (
+        core_rows // (seq_count * shard) * 2 + core_place
+    ) * seq_count * shard + core_rows % (seq_count * shard)
+    core_keys = (core_rows == group * shard + within).astype(bf16)
+    core_values = (core_rows == group * shard + shard // 2 + within).astype(bf16)
+    context_core = [
+        jnp.concatenate(
+            [dot(side[0], core_keys).astype(bf16), dot(side[0], core_values).astype(bf16)], axis=0
+        )
+        for side in (context, context_other)
+    ]
+    inward_same, cotangent_state, context_core = tie(inward_same, cotangent_state, context_core)
+
+    inward_other = flip(inward_same, 1)
+    cotangent_same = plane_chips(cotangent_state)
+    inward_other, cosine, sine, cotangent_same = tie(inward_other, cosine, sine, cotangent_same)
 
     inward_own, extra_all = both_cores(
         inward_same, inward_other, core_place, [shard, extra_rows]
@@ -801,75 +715,89 @@
     token_low = jnp.pad(
         (token_norm * attend_gain).astype(bf16), ((0, TOKEN_ROWS - CLIPS), (0, 0))
     )
-    row_latents = relay_join(moving, seq_place).reshape(row_length, D)
+    shrink_own = lax.all_gather(shrink_weight, "seq", tiled=True)
+    cotangent_other = flip(cotangent_same, 1)
+    cotangent_other, inward_own, token_low, lined, cross_gain, feed_gain = tie(
+        cotangent_other, inward_own, token_low, lined, cross_gain, feed_gain
+    )
+
+    def weight_rows(first, count):
+        start = frame_count + first * shard
+        return lined[:, start : start + count * shard]
+
+    first_state = plane_open(weight_rows(0, 2))
+    row_latents = lined[:, :frame_count].reshape(row_length, D)
     row_norm, row_inverse = norm_forward(row_latents.astype(f32))
     row_low = jnp.concatenate([(row_norm * attend_gain).astype(bf16), token_low], axis=0)
     projected = dot(row_low, inward_own)
-    projected, lined, shrink_weight = tie(projected, lined, shrink_weight)
-    shrink_own = lax.all_gather(shrink_weight, "seq", tiled=True)
-    expand_lined = lax.all_gather(expand_part, "seq")
-    first_state = plane_open(lined[:, : 3 * shard])
+    projected, first_state, expand_blocks = tie(projected, first_state, expand_blocks)
+
+    first_state = plane_relay(first_state)
+    keyval_state = plane_open(weight_rows(2, 1))
+    expand_part = lax.all_to_all(expand_blocks, "dp", 0, 0, tiled=True)
     attended, attended_wide, self_level, projected_low = self_forward(
         projected, cosine, sine, clip_column, clip_row, row_length
     )
-    attended, first_state = tie(attended, first_state)
-
-    attended_blocks = attended[:, :own_width].reshape(seq_count, frame_count, own_width)
-    attended_got = line_send(attended_blocks, "seq", seq_place)
-    first_state = plane_relay(first_state)
-    second_state = plane_open(lined[:, 3 * shard :])
+    attended, first_state, keyval_state, shrink_own, expand_part = tie(
+        attended, first_state, keyval_state, shrink_own, expand_part
+    )
+
+    attended_low = line_swap(attended[:, :own_width], 0, 1)
     first_same = plane_chips(first_state, chip_place)
-    attended_got, first_same, second_state, cotangent, shrink_own = tie(
-        attended_got, first_same, second_state, cotangent, shrink_own
-    )
-
     first_other = flip(first_same, 1)
-    second_state = plane_relay(second_state)
-    attended_low = (
-        line_join(attended_blocks, attended_got, seq_place)
-        .transpose(1, 0, 2)
-        .reshape(frame_count, D)
-    )
-    first_other, second_state, attended_low = tie(first_other, second_state, attended_low)
-
-    cotangent_state = plane_open(cotangent[0])
-    outward_full, keyval_full, query_full = [
+    keyval_state = plane_relay(keyval_state)
+    return_state = plane_open(weight_rows(3, 1))
+    attended_low, first_same, first_other, keyval_state, return_state, expand_part = tie(
+        attended_low, first_same, first_other, keyval_state, return_state, expand_part
+    )
+
+    expand_lined = lax.all_gather(expand_part, "seq")
+    outward_full, query_full = [
         weight.reshape(D, D)
-        for weight in both_cores(first_same, first_other, core_place, [shard] * 3)
+        for weight in both_cores(first_same, first_other, core_place, [shard] * 2)
     ]
-    second_same = plane_chips(second_state, chip_place)
-    second_other = flip(second_same, 1)
-    keyval = dot(context_spread, keyval_full).astype(bf16)
+    keyval_same = plane_chips(keyval_state, chip_place)
+    keyval_other = flip(keyval_same, 1)
+    return_state = plane_relay(return_state)
     after_self = latents[0].astype(f32) + dot(attended_low, outward_full)
     norm_two, inverse_two = norm_forward(after_self)
     normed_two = (norm_two * cross_gain).astype(bf16)
     cross_heads = dot(normed_two, query_full).astype(bf16)
-    cross_heads, keyval, second_other, cotangent_state = tie(
-        cross_heads, keyval, second_other, cotangent_state
-    )
-
-    cotangent_state = plane_relay(cotangent_state)
-    cotangent_same = plane_chips(cotangent_state)
-    cotangent_other = flip(cotangent_same, 1)
-    return_full = both_cores(second_same, second_other, core_place, [shard])[0].reshape(D, D)
+    attended_other = flip(attended_low, 1)
+    cross_heads, keyval_same, keyval_other, return_state, attended_other = tie(
+        cross_heads, keyval_same, keyval_other, return_state, attended_other
+    )
+
+    keyval_full = both_cores(keyval_same, keyval_other, core_place, [shard])[0].reshape(D, D)
+    return_same = plane_chips(return_state, chip_place)
+    return_other = flip(return_same, 1)
+    keyval = dot(context_spread, keyval_full).astype(bf16)
     crossed, crossed_wide, cross_level = cross_forward(
         cross_heads, keyval, own_clips[:, None], text_clips[None, :]
     )
-    crossed, return_full, cotangent_other, expand_lined = tie(
-        crossed, return_full, cotangent_other, expand_lined
-    )
+    return_full = both_cores(return_same, return_other, core_place, [shard])[0].reshape(D, D)
+    normed_two_other = flip(normed_two, 1)
+    crossed, return_full, normed_two_other = tie(crossed, return_full, normed_two_other)
+
     after_cross = after_self + dot(crossed, return_full)
     norm_three, inverse_three = norm_forward(after_cross)
     normed_three = (norm_three * feed_gain).astype(bf16)
+    crossed_other = flip(crossed, 1)
     frames_state = plane_relay(plane_open(normed_three))
-
-    expand_own = (
-        expand_lined.reshape(seq_count, dp_count, shard, 2 * hidden_width)
-        .transpose(1, 0, 2, 3)
-        .reshape(D, 2 * hidden_width)
-    )
+    frames_same = plane_chips(frames_state)
+    frames_same, expand_lined, crossed_other = tie(frames_same, expand_lined, crossed_other)
+
+    if two_by_two():
+        expand_own = assemble(
+            [expand_lined],
+            [(dp_count, seq_count, shard, 2 * hidden_width)],
+            [(0, at(line), 0, at(slice(None), line)) for line in range(seq_count)],
+            jnp.zeros((1,), jnp.int32),
+        )[0]
+    else:
+        expand_own = expand_lined.transpose(1, 0, 2, 3)
+    expand_own = expand_own.reshape(D, 2 * hidden_width)
     half_frames = chips * frame_count
-    frames_same = plane_chips(frames_state)
     frames_other = flip(frames_same, 1)
     frames = [frames_same.reshape(half_frames, D), frames_other.reshape(half_frames, D)]
     tangents = [cotangent_same.reshape(half_frames, D), cotangent_other.reshape(half_frames, D)]
@@ -909,20 +837,26 @@
         grad = grad.astype(bf16).reshape(chips, 2, seq_count, shard, -1)
         return grad, flip(take(grad, 1 - core_place, 1), 1)
 
+    def side_block(opened, r):
+        return jnp.concatenate(
+            [
+                (
+                    take(take(grad, core_place, 1), chip_place ^ r)[0, 0].astype(f32)
+                    + take(got, chip_place ^ r)[0, 0].astype(f32)
+                ).astype(bf16)
+                for grad, got in opened
+            ],
+            axis=1,
+        )
+
     def side_blocks(opened):
-        return [
-            jnp.concatenate(
-                [
-                    (
-                        take(take(grad, core_place, 1), chip_place ^ r)[0, 0].astype(f32)
-                        + take(got, chip_place ^ r)[0, 0].astype(f32)
-                    ).astype(bf16)
-                    for grad, got in opened
-                ],
-                axis=1,
-            )
-            for r in range(chips)
-        ]
+        return [side_block(opened, r) for r in range(chips)]
+
+    def both_grad(left, left_other, right, right_other):
+        return (dot(left.T, right) + dot(left_other.T, right_other)).astype(bf16)
+
+    def own_core(grad):
+        return take(grad.reshape(chips, 2, seq_count, shard, D), core_place, 1)[:, 0]
 
     feed_norm_grad = plane_total(feed_near)
     feed_term, feed_gain_part = norm_backward(
@@ -931,10 +865,8 @@
     after_cross_grad = cotangent[0].astype(f32) + feed_term
     return_low = after_cross_grad.astype(bf16)
     crossed_grad = dot(return_low, return_full.T).astype(bf16)
-    return_grad = open_grad(dot(crossed.T, return_low))
-    crossed_grad, return_grad = tie(crossed_grad, return_grad)
-    return_blocks = side_blocks([return_grad])
-    return_far = plane_far(return_blocks)
+    return_other = flip(return_low, 1)
+    crossed_grad, return_low, return_other = tie(crossed_grad, return_low, return_other)
     cross_query_low, cross_key_low, cross_value_low = cross_backward(
         cross_heads,
         keyval,
@@ -944,13 +876,9 @@
         text_clips[:, None],
         own_clips[None, :],
     )
-    cross_query_low, cross_key_low, cross_value_low, return_far, grad_shrink = tie(
-        cross_query_low, cross_key_low, cross_value_low, return_far, grad_shrink
-    )
-    return_near = plane_near(return_blocks, return_far)
-    keyval_low = jnp.concatenate([cross_key_low, cross_value_low], axis=0)
-    keyval_grad = open_grad(dot(context_spread.T, keyval_low))
-    query_grad = open_grad(dot(normed_two.T, cross_query_low))
+    cross_query_low, cross_key_low, cross_value_low = tie(
+        cross_query_low, cross_key_low, cross_value_low
+    )
     cross_norm_grad = dot(cross_query_low, query_full.T)
     cross_term, cross_gain_part = norm_backward(
         cross_norm_grad, norm_two, inverse_two, cross_gain
@@ -958,19 +886,33 @@
     after_self_grad = after_cross_grad + cross_term
     outward_low = after_self_grad.astype(bf16)
     attended_grad = dot(outward_low, outward_full.T).astype(bf16)
-    attended_grad, return_near, outward_low, keyval_grad, query_grad = tie(
-        attended_grad, return_near, outward_low, keyval_grad, query_grad
-    )
-
-    grad_blocks = attended_grad.reshape(frame_count, seq_count, own_width).transpose(1, 0, 2)
-    grad_got = line_send(grad_blocks, "seq", seq_place)
-    outward_grad = open_grad(dot(attended_low.T, outward_low))
-    rest_blocks = side_blocks([keyval_grad, query_grad, outward_grad])
-    grad_got, rest_blocks = tie(grad_got, rest_blocks)
-
-    rest_far = plane_far(rest_blocks)
-    attended_grad_own = line_join(grad_blocks, grad_got, seq_place)
-    attended_grad_own = attended_grad_own.reshape(row_length, own_width)
+    keyval_low = jnp.concatenate([cross_key_low, cross_value_low], axis=0)
+    keyval_low_other = flip(keyval_low, 1)
+    cross_query_other = flip(cross_query_low, 1)
+    attended_grad, outward_low, keyval_low, keyval_low_other, cross_query_other, return_other = tie(
+        attended_grad, outward_low, keyval_low, keyval_low_other, cross_query_other, return_other
+    )
+
+    attended_grad_own = line_swap(attended_grad, 1, 0)
+    outward_other = flip(outward_low, 1)
+    keyval_grad = both_grad(context_core[0], context_core[1], keyval_low, keyval_low_other)
+    whole_grads = [
+        own_core(both_grad(crossed, crossed_other, return_low, return_other)),
+        keyval_grad.reshape(chips, seq_count, shard, D),
+        own_core(both_grad(normed_two, normed_two_other, cross_query_low, cross_query_other)),
+        own_core(both_grad(attended_low, attended_other, outward_low, outward_other)),
+    ]
+    halves = [
+        [
+            jnp.concatenate([take(grad, chip_place ^ r)[0] for grad in group], axis=1)
+            for r in range(chips)
+        ]
+        for group in (whole_grads[:2], whole_grads[2:])
+    ]
+    half_far = [plane_far(blocks) for blocks in halves]
+    attended_grad_own, half_far, grad_shrink = tie(attended_grad_own, half_far, grad_shrink)
+
+    near_early = plane_near(halves[0], half_far[0])
     attended_grad_own = jnp.pad(attended_grad_own, ((0, 0), (0, padded - own_width)))
     inward_low = self_backward(
         projected_low,
@@ -982,87 +924,82 @@
         clip_column,
         clip_row,
     )
-    inward_low, rest_far, expand_sum = tie(inward_low, rest_far, expand_sum)
-
-    rest_near = plane_near(rest_blocks, rest_far)
+    inward_low, near_early = tie(inward_low, near_early)
+
+    near_late = plane_near(halves[1], half_far[1])
     attend_parts = dot(inward_low, inward_own.T)
-    attend_blocks = attend_parts[:row_length].reshape(seq_count, frame_count, D)
-    came = sum_step(attend_blocks, seq_place, 1, None)
-    inward_grad = open_grad(dot(row_low.T, inward_low))
-    came, inward_grad = tie(came, inward_grad)
-
-    for step in range(2, seq_count - 1):
-        came = sum_step(attend_blocks, seq_place, step, came)
-    inward_blocks = side_blocks([inward_grad])
+    attend_low = attend_parts[:row_length].astype(bf16)
+    attend_low, inward_low, attend_parts, near_late, expand_sum, hidden_low = tie(
+        attend_low, inward_low, attend_parts, near_late, expand_sum, hidden_low
+    )
+
+    attend_sum = lax.psum_scatter(attend_low, "seq", scatter_dimension=0, tiled=True)
+    expand_rows = lax.all_to_all(expand_sum, "dp", 0, 0, tiled=True)
+    inward_blocks = side_blocks([open_grad(dot(row_low.T, inward_low))])
     inward_far = plane_far(inward_blocks)
+    whole_column = jnp.concatenate(
+        [plane_total(near_early).astype(bf16), plane_total(near_late).astype(bf16)], axis=1
+    )
     token_term, token_gain_part = norm_backward(
         attend_parts[row_length : row_length + CLIPS], token_norm, token_inverse, attend_gain
     )
     attend_gain_part = jnp.sum(attend_parts[:row_length] * row_norm, axis=0) + token_gain_part
-    feats_row = jnp.pad(feats_low.astype(f32).reshape(1, -1), ((0, 0), (0, D - CLIPS * TFEAT)))
+    feats_row = feats_low.astype(f32).reshape(-1)
+    device_count = dp_count * seq_count
+    gain_parts = jnp.stack([attend_gain_part, cross_gain_part, feed_gain_part], axis=0)
+    gain_parts = gain_parts.reshape(3, device_count, shard).transpose(1, 0, 2)
+    common = jnp.concatenate([token_term.reshape(-1), feats_row]).astype(bf16)
     small = jnp.concatenate(
         [
-            token_term,
-            attend_gain_part[None],
-            cross_gain_part[None],
-            feed_gain_part[None],
-            feats_row,
-            jnp.zeros((1, D), f32),
-        ],
-        axis=0,
-    )
-    came, inward_far, rest_near, small = tie(came, inward_far, rest_near, small)
-
-    whole_column = jnp.concatenate(
-        [plane_total(return_near).astype(bf16), plane_total(rest_near).astype(bf16)], axis=1
-    )
-    whole_sums = lax.psum_scatter(whole_column, "seq", scatter_dimension=0).astype(f32)
-    came = sum_step(attend_blocks, seq_place, seq_count - 1, came)
-    inward_near = plane_near(inward_blocks, inward_far)
-    device_count = dp_count * seq_count
-    small_all = lax.all_to_all(
-        jnp.broadcast_to(small[None], (device_count,) + small.shape),
-        ("dp", "seq"),
-        0,
-        0,
-        tiled=True,
-    )
+            jnp.broadcast_to(common[None], (device_count,) + common.shape),
+            gain_parts.reshape(device_count, 3 * shard).astype(bf16),
+        ],
+        axis=1,
+    )
+    small = jnp.pad(small, ((0, 0), (0, -small.shape[1] % 2048)))
+    small = small.reshape(device_count, -1, 128)
     fed_other = sides(dot(hidden_low[1], shrink_own))
     fed_got = flip(fed_other, 1)
     fed_same = sides(dot(hidden_low[0], shrink_own))
-    inward_near, came, fed_got, fed_same, expand_sum = tie(
-        inward_near, came, fed_got, fed_same, expand_sum
-    )
-
+    inward_far, fed_got, fed_same, small, expand_rows, whole_column = tie(
+        inward_far, fed_got, fed_same, small, expand_rows, whole_column
+    )
+
+    whole_sums = lax.psum_scatter(whole_column, "seq", scatter_dimension=0)
+    small_all = lax.all_to_all(small, ("dp", "seq"), 0, 0, tiled=True).astype(f32)
+    inward_near = plane_near(inward_blocks, inward_far)
     fed_blocks = [fed_same[r].astype(f32) + fed_got[r].astype(f32) for r in range(chips)]
     fed_far = plane_far(fed_blocks)
-    inward_sum = plane_total(inward_near).astype(bf16)
-    inward_moved = line_send(inward_sum, "seq", seq_place)
-    attend_norm_grad = take(attend_blocks, seq_place)[0]
-    attend_norm_grad = attend_norm_grad + came[0].astype(f32) + came[1].astype(f32)
+    inward_near, fed_far, expand_rows, small_all, attend_sum = tie(
+        inward_near, fed_far, expand_rows, small_all, attend_sum
+    )
+
+    inward_rows = line_swap(plane_total(inward_near).astype(bf16))
+    fed_near = plane_near(fed_blocks, fed_far)
+    grad_expand = (
+        expand_rows.reshape(dp_count, shard, 2, hidden_width)
+        .transpose(1, 2, 0, 3)
+        .reshape(shard, 2 * FF)
+        .astype(f32)
+    )
+    inward_rows, fed_near, grad_expand, whole_sums = tie(
+        inward_rows, fed_near, grad_expand, whole_sums
+    )
+    whole_sums = whole_sums.astype(f32)
+
+    block_output = (after_cross + plane_total(fed_near)).astype(bf16)
     own_norm = lax.dynamic_slice_in_dim(row_norm, seq_place * frame_count, frame_count, axis=0)
     own_inverse = lax.dynamic_slice_in_dim(
         row_inverse, seq_place * frame_count, frame_count, axis=0
     )
-    attend_term, _ = norm_backward(attend_norm_grad, own_norm, own_inverse, attend_gain)
+    attend_term, _ = norm_backward(
+        attend_sum.astype(f32), own_norm, own_inverse, attend_gain
+    )
     latents_grad = (after_self_grad + attend_term)[None]
-    grad_expand = (
-        lax.all_to_all(expand_sum, "dp", 0, 0, tiled=True)
-        .reshape(dp_count, shard, 2, hidden_width)
-        .transpose(1, 2, 0, 3)
-        .reshape(shard, 2 * FF)
-        .astype(f32)
-    )
-    fed_far, inward_moved, latents_grad, grad_expand = tie(
-        fed_far, inward_moved, latents_grad, grad_expand
-    )
-
-    fed_near = plane_near(fed_blocks, fed_far)
-    inward_rows = line_join(inward_sum, inward_moved, seq_place)
+    grad_shrink = grad_shrink.astype(f32)
     grad_inward = (
         from_pairs(inward_rows).transpose(1, 2, 0, 3).reshape(shard, 3 * D).astype(f32)
     )
-    block_output = (after_cross + plane_total(fed_near)).astype(bf16)
     grad_return = whole_sums[:shard]
     grad_keyval = jnp.concatenate(
         [whole_sums[shard : shard + shard // 2], whole_sums[shard + shard // 2 : 2 * shard]],
@@ -1070,21 +1007,25 @@
     )
     grad_query = whole_sums[2 * shard : 3 * shard]
     grad_outward = whole_sums[3 * shard :]
-    grad_shrink = grad_shrink.astype(f32)
-    small_sum = jnp.sum(small_all.reshape(dp_count, seq_count, 8, D), axis=1)
-    feats_all = small_all.reshape(dp_count, seq_count, 8, D)[:, 0, CLIPS + 3, : CLIPS * TFEAT]
+    small_all = small_all.reshape(device_count, -1)
+    token_count, feats_count = CLIPS * D, CLIPS * TFEAT
+    token_sum = jnp.sum(
+        small_all[:, :token_count].reshape(dp_count, seq_count, CLIPS, D), axis=1
+    )
+    feats_all = small_all.reshape(dp_count, seq_count, -1)[:, 0]
+    feats_all = feats_all[:, token_count : token_count + feats_count]
     feats_all = feats_all.reshape(dp_count, CLIPS, TFEAT)
     feats_own = lax.dynamic_slice_in_dim(feats_all, place_all * time_shard, time_shard, axis=2)
     grad_time = jnp.einsum(
         "rct,rcn->tn",
         feats_own,
-        small_sum[:, :CLIPS],
+        token_sum,
         precision=PRECISE,
         preferred_element_type=f32,
     )
-    gain_sums = lax.dynamic_slice_in_dim(
-        jnp.sum(small_sum[:, CLIPS : CLIPS + 3], axis=0), place_all * shard, shard, axis=1
-    )
+    gain_start = token_count + feats_count
+    gain_sums = jnp.sum(small_all[:, gain_start : gain_start + 3 * shard], axis=0)
+    gain_sums = gain_sums.reshape(3, shard)
     return (
         block_output[None],
         latents_grad,

time: 852 us -> 746 us (0.88)
  waiting for transfers between devices: 243 us -> 185 us
  starting transfers between devices: 122 us -> 82.4 us
  matrix products: 129 us -> 160 us
  local copies, waits for them, and re-layouts: 118 us -> 96.2 us
  other arithmetic: 103 us -> 92.6 us
    ppermute x24 -> x0, waiting for transfers between devices: 81.5 us -> none  [the longest x3 28.3 us: relay_step(): lax.ppermute(leftward[-1], 'seq', [(k + 1, k) for k in range(0, count - s...]
    ppermute x24 -> x0, starting transfers between devices: 63.2 us -> none  [the longest x3 31 us: sum_step(): lax.ppermute(to_right.astype(low), 'seq', [(k, k + 1) for k in range(0, s...]
    all_to_all x2 -> x6, waiting for transfers between devices: 12.2 us -> 54.1 us  [the longest x4 34.6 us: line_swap(): return lax.all_to_all(blocks, 'seq', split, join, tiled=True)]
    dot_general x29 -> x37, matrix products: 128 us -> 159 us  [dot(): return jnp.dot(left, right, preferred_element_type=jnp.float32)]
    reduce_scatter x1 -> x2, waiting for transfers between devices: 0.01 us -> 23.4 us  [the longest x1 23.4 us: on_device(): whole_sums = lax.psum_scatter(whole_column, 'seq', scatter_dimension=0)]
    ppermute x52 -> x61, waiting for transfers between devices: 127 us -> 105 us  [flip(): return lax.ppermute(values, 'dp', xor_pairs(lax.axis_size('dp'), bit))]
    all_to_all x2 -> x6, starting transfers between devices: 6.95 us -> 27.6 us  [the longest x4 18.2 us: line_swap(): return lax.all_to_all(blocks, 'seq', split, join, tiled=True)]
    convert_element_type x11 -> x9, other arithmetic: 24.8 us -> 12.5 us  [the longest x1 2.62 us: side_block(): return jnp.concatenate([(take(take(grad, core_place, 1), chip_place ^ r)[...]
  transfers between devices with their start and end apart: 85 -> 75, of which waited for: 33 -> 27; matrix products, arithmetic and copies ran while one was open for 33% -> 37% of each run, Pallas kernels for 13% -> 13%
where the time goes in v4:
time: 746 us; the launch traced here: 736 us
  waiting for transfers between devices  185 us (25%)
  matrix products  160 us (21%)
  Pallas kernels  102 us (14%)
  local copies, waits for them, and re-layouts  96.2 us (13%)
  other arithmetic  92.6 us (12%)
  starting transfers between devices  82.4 us (11%)
  between operations  17.4 us (2%)
    dot_general x37, matrix products, dot(): return jnp.dot(left, right, preferred_element_type=jnp.float32)  159 us
    ppermute x61, waiting for transfers between devices, flip(): return lax.ppermute(values, 'dp', xor_pairs(lax.axis_size('dp'), bit))  105 us
    ppermute x61, starting transfers between devices, flip(): return lax.ppermute(values, 'dp', xor_pairs(lax.axis_size('dp'), bit))  49.9 us
    all_to_all x4, waiting for transfers between devices, line_swap(): return lax.all_to_all(blocks, 'seq', split, join, tiled=True)  34.6 us
    unnamed x307, local copies, waits for them, and re-layouts  32.6 us
    pallas_call x11, Pallas kernels, assemble(): pl.pallas_call(kernel, in_specs=[pl.BlockSpec(memory_space=pltpu.SMEM)] +...  29.8 us
    pallas_call x1, Pallas kernels, self_backward(): pl.pallas_call(self_backward_kernel, grid=(pairs,), in_specs=[lanes(total...  23.5 us
    reduce_scatter x1, waiting for transfers between devices, on_device(): whole_sums = lax.psum_scatter(whole_column, 'seq', scatter_dimension=0)  23.4 us
  transfers between devices with their start and end apart: 75, of which 27 were waited for; matrix products, arithmetic and copies ran while one was open for 37% of the time, Pallas kernels for 13%

profile of v4, /device:TPU:0, one launch (start us, length us, event | category | flops | bytes accessed | tf_op | source)
XLA Modules:
  0.0 735.6 jit_solution(6272934087128573089)
XLA Ops:
  15.0 6.3 all-to-all-start
  26.9 27.4 %all-to-all-done.refs_0_ = bf16[4,64,1152]{2,1,0:T(8,128)(2,1)S(1)} async-done(((bf16[4,64,1152]{2,1,0:T(8,128)(2,1)}), bf16[4,64,1152]{2,1,0:T(8,128)(2,1)S(1)}, u32[]{:S(2)}, u32[]{:S(2)}) %all-to-all-start) | async-done | bytes 589856 | tf_op jit(solution)/shard_map/all_to_all | solution.py:395
  65.4 14.6 %collective-permute-done.refs_1_ = bf16[4,64,1152]{2,1,0:T(8,128)(2,1)} collective-permute-done((bf16[4,64,1152]{2,1,0:T(8,128)(2,1)S(1)}, bf16[4,64,1152]{2,1,0:T(8,128)(2,1)}, u32[]{:S(2)}, u32[]{:S(2)}) %collective-permute-start) | collective-permute-done | bytes 589856 | tf_op jit(solution)/shard_map/ppermute | solution.py:407
  145.5 7.4 %fusion.24.projected = f32[1152,1152]{1,0:T(8,128)} fusion(bf16[1536,1152]{1,0:T(8,128)(2,1)S(1)} %bitcast.378, bf16[128,1536]{1,0:T(8,128)(2,1)S(1)} %pad.14, bf16[1024,1536]{1,0:T(8,128)(2,1)S(1)} %get-tuple-element.346), kind=kOutput, calls=%fused_computation.65 | convolution fusion | flops 4083941376 | bytes 12386304 | tf_op jit(solution)/shard_map/dot_general | solution.py:399
  152.9 11.3 %collective-permute-done.11.refs_1_ = bf16[4,96,1536]{2,1,0:T(8,128)(2,1)S(1)} collective-permute-done((bf16[4,96,1536]{2,1,0:T(8,128)(2,1)S(1)}, bf16[4,96,1536]{2,1,0:T(8,128)(2,1)S(1)}, u32[]{:S(2)}, u32[]{:S(2)}) %collective-permute-start.11) | collective-permute-done | bytes 1179680 | tf_op jit(solution)/shard_map/ppermute | solution.py:407
  175.8 23.2 %shard_map.258 = (bf16[1024,384]{1,0:T(8,128)(2,1)S(1)}, f32[1024,384]{1,0:T(8,128)S(1)}, f32[1024,384]{1,0:T(8,128)S(1)}, bf16[1152,1152]{1,0:T(8,128)(2,1)}) custom-call(f32[1152,1152]{1,0:T(8,128)} %fusion.24.projected, f32[1152,128]{1,0:T(8,128)S(1)} %copy-done.24, f32[1152,128]{1,0:T(8,128)S(1)} %copy-done.22, f32[1152,1]{1,0:T(8,128)S(1)} %copy-done.26, ...), custom_call_target="tpu_custom_call" | custom-call | flops 120000004096 | bytes 1048576 | tf_op jit(solution)/shard_map/pallas_call | solution.py:221
  220.9 10.0 %collective-permute-done.20.refs_1_ = bf16[4,48,1536]{2,1,0:T(8,128)(2,1)S(1)} collective-permute-done((bf16[4,48,1536]{2,1,0:T(8,128)(2,1)S(1)}, bf16[4,48,1536]{2,1,0:T(8,128)(2,1)S(1)}, u32[]{:S(2)}, u32[]{:S(2)}) %collective-permute-start.20) | collective-permute-done | bytes 589856 | tf_op jit(solution)/shard_map/ppermute | solution.py:407
  242.2 6.1 shard_map.260
  267.1 8.3 %convolution_convert_fusion.5.keys.values = bf16[768,1536]{1,0:T(8,128)(2,1)} fusion(bf16[768,1536]{1,0:T(8,128)(2,1)} %pad_maximum_fusion.3, bf16[1536,1536]{1,0:T(8,128)(2,1)} %bitcast.335), kind=kOutput, calls=%fused_computation.25 | convolution fusion | flops 3625058304 | bytes 9437184 | tf_op jit(solution)/shard_map/dot_general | solution.py:399
  275.4 12.2 %shard_map.263 = (bf16[256,1536]{1,0:T(8,128)(2,1)S(1)}, f32[256,1536]{1,0:T(8,128)S(1)}, f32[256,1536]{1,0:T(8,128)S(1)}) custom-call(bf16[256,1536]{1,0:T(8,128)(2,1)S(1)} %convolution_convert_fusion.8.query, bf16[768,1536]{1,0:T(8,128)(2,1)} %convolution_convert_fusion.5.keys.values, bf16[768,1536]{1,0:T(8,128)(2,1)} %convolution_convert_fusion.5.keys.values, ...), custom_call_target="tpu_custom_call" | custom-call | flops 20000000000 | bytes 1048576 | tf_op jit(solution)/shard_map/pallas_call | solution.py:278
  296.4 19.1 %collective-permute-done.28.refs_1_ = bf16[256,1536]{1,0:T(8,128)(2,1)S(1)} collective-permute-done((bf16[256,1536]{1,0:T(8,128)(2,1)S(1)}, bf16[256,1536]{1,0:T(8,128)(2,1)S(1)}, u32[]{:S(2)}, u32[]{:S(2)}) %collective-permute-start.28) | collective-permute-done | bytes 786464 | tf_op jit(solution)/shard_map/ppermute | solution.py:407
  317.4 9.1 %collective-permute-done.30.refs_3_ = bf16[128,1536]{1,0:T(8,128)(2,1)S(1)} collective-permute-done((bf16[128,1536]{1,0:T(8,128)(2,1)S(1)}, bf16[128,1536]{1,0:T(8,128)(2,1)S(1)}, u32[]{:S(2)}, u32[]{:S(2)}) %collective-permute-start.30) | collective-permute-done | bytes 393248 | tf_op jit(solution)/shard_map/ppermute | solution.py:407
  337.8 7.1 fusion.133
  356.5 7.1 fusion.132
  363.6 5.8 multiply_convert_fusion.6
  401.1 8.8 %fusion.135 = f32[1536,1536]{1,0:T(8,128)S(1)} fusion(bf16[1024,1536]{1,0:T(8,128)(2,1)} %bitcast.37, bf16[1024,1536]{0,1:T(8,128)(2,1)} %pad_maximum_fusion.2), kind=kOutput, calls=%fused_computation.348 | convolution fusion | flops 4831838208 | bytes 15728640 | tf_op jit(solution)/shard_map/dot_general | solution.py:399
  430.5 12.9 %shard_map.268 = (bf16[256,1536]{1,0:T(8,128)(2,1)S(1)}, bf16[384,1536]{1,0:T(8,128)(2,1)S(1)}, bf16[384,1536]{1,0:T(8,128)(2,1)S(1)}) custom-call(bf16[256,1536]{1,0:T(8,128)(2,1)S(1)} %copy-done.33, bf16[768,1536]{1,0:T(8,128)(2,1)} %convolution_convert_fusion.5.keys.values, bf16[768,1536]{1,0:T(8,128)(2,1)} %convolution_convert_fusion.5.keys.values, ...), custom_call_target="tpu_custom_call" | custom-call | flops 120000004096 | bytes 1048576 | tf_op jit(solution)/shard_map/pallas_call | solution.py:304
  499.9 7.2 all-to-all-done.3
  524.6 23.5 %shard_map.269 = bf16[1152,1152]{1,0:T(8,128)(2,1)} custom-call(bf16[1152,1152]{1,0:T(8,128)(2,1)} %get-tuple-element.230.low, bf16[1024,384]{1,0:T(8,128)(2,1)S(1)} %bitcast.313, f32[1024,384]{1,0:T(8,128)S(1)} %copy-done.35, f32[1024,384]{1,0:T(8,128)S(1)} %copy-done.37, f32[1152,128]{1,0:T(8,128)S(1)} %copy-done.25, f32[1152,128]{1,0:T(8,128)S(1)} %copy-done.23, ...), custom_call_target="tpu_custom_call" | custom-call | flops 15000000512 | bytes 1048576 | tf_op jit(solution)/shard_map/pallas_call | solution.py:249
  548.2 8.5 %fusion.140 = f32[1152,1536]{1,0:T(8,128)S(1)} fusion(bf16[1152,1152]{1,0:T(8,128)(2,1)} %shard_map.269, bf16[1536,1152]{1,0:T(8,128)(2,1)} %bitcast.377), kind=kOutput, calls=%fused_computation.353 | convolution fusion | flops 4076863488 | bytes 13271040 | tf_op jit(solution)/shard_map/dot_general | solution.py:399
  597.6 6.6 convolution_convert_fusion.1
  628.1 5.8 all-to-all-start.5
  636.7 19.5 %all-to-all-done.5 = bf16[32,48,128]{2,1,0:T(8,128)(2,1)} async-done(((bf16[32,48,128]{2,1,0:T(8,128)(2,1)}), bf16[32,48,128]{2,1,0:T(8,128)(2,1)}, u32[]{:S(2)}, u32[]{:S(2)}) %all-to-all-start.5) | async-done | bytes 393248 | tf_op jit(solution)/shard_map/all_to_all | solution.py:969
  690.6 23.4 %reduce-scatter.11.cloned.1.call-done = bf16[1,192,1536]{2,1,0:T(8,128)(2,1)} async-done(((bf16[4,192,1536]{2,1,0:T(8,128)(2,1)}), bf16[1,192,1536]{2,1,0:T(8,128)(2,1)}) %reduce-scatter.11.cloned.1.call-update) | async-done | bytes 589840 | tf_op jit(solution)/shard_map/reduce_scatter | solution.py:968
  (687 shorter events, 426.9 us)
Async XLA Ops:
  7.3 123.9 %all-gather.8.cloned.1.call-start = ((), (), s32[]{:S(2)}) async-start(), calls=%async_computation.16 | async-start | bytes 6881280 | tf_op jit(solution)/shard_map/all_gather | solution.py:665
  15.0 39.2 %all-to-all-start = ((bf16[4,64,1152]{2,1,0:T(8,128)(2,1)}), bf16[4,64,1152]{2,1,0:T(8,128)(2,1)S(1)}, u32[]{:S(2)}, u32[]{:S(2)}) async-start(bf16[4,64,1152]{2,1,0:T(8,128)(2,1)} %pad_maximum_fusion.21), calls=%async_computation | async-start | bytes 1179648 | tf_op jit(solution)/shard_map/all_to_all | solution.py:395
  21.3 180.9 %all-gather.6.cloned.1.call-start = ((), (), s32[]{:S(2)}) async-start(), calls=%async_computation.11 | async-start | bytes 2949120 | tf_op jit(solution)/shard_map/all_gather | solution.py:718
  21.3 44.1 %collective-permute-start.4 = (bf16[1,384,768]{2,1,0:T(8,128)(2,1)}, bf16[1,384,768]{2,1,0:T(8,128)(2,1)}, u32[]{:S(2)}, u32[]{:S(2)}) collective-permute-start(bf16[1,384,768]{2,1,0:T(8,128)(2,1)} %param.17), channel_id=1, source_target_pairs={{0,4},{4,0},{8,12},{12,8},{16,20},{20,16},{24,28},{28,24},{1,5},{5... | collective-permute-start | bytes 1769480 | tf_op jit(solution)/shard_map/ppermute | solution.py:407
  137.4 64.8 %collective-permute-start.15 = (bf16[4,48,1536]{2,1,0:T(8,128)(2,1)}, bf16[4,48,1536]{2,1,0:T(8,128)(2,1)}, u32[]{:S(2)}, u32[]{:S(2)}) collective-permute-start(bf16[4,48,1536]{2,1,0:T(8,128)(2,1)} %get-tuple-element.210.refs_0_), channel_id=1, source_target_pairs={{0,8},{4,12},{8,0},{12,4},{16,24},{20,28},{24,16},{28,20},{1,9},{5... | collective-permute-start | bytes 1769480 | tf_op jit(solution)/shard_map/ppermute | solution.py:407
  138.8 63.4 %collective-permute-start.16 = (bf16[4,48,1536]{2,1,0:T(8,128)(2,1)}, bf16[4,48,1536]{2,1,0:T(8,128)(2,1)}, u32[]{:S(2)}, u32[]{:S(2)}) collective-permute-start(bf16[4,48,1536]{2,1,0:T(8,128)(2,1)} %get-tuple-element.210.refs_0_), channel_id=1, source_target_pairs={{0,16},{4,20},{8,24},{12,28},{16,0},{20,4},{24,8},{28,12},{1,17},{... | collective-permute-start | bytes 1769480 | tf_op jit(solution)/shard_map/ppermute | solution.py:407
  165.3 36.9 %collective-permute-start.13 = (bf16[2,96,1536]{2,1,0:T(8,128)(2,1)}, bf16[2,96,1536]{2,1,0:T(8,128)(2,1)}, u32[]{:S(2)}, u32[]{:S(2)}) collective-permute-start(bf16[2,96,1536]{2,1,0:T(8,128)(2,1)} %slice.331), channel_id=1, source_target_pairs={{0,16},{4,20},{8,24},{12,28},{16,0},{20,4},{24,8},{28,12},{1,17},{... | collective-permute-start | bytes 1769480 | tf_op jit(solution)/shard_map/ppermute | solution.py:407
  166.8 35.4 %collective-permute-start.14 = (bf16[2,96,1536]{2,1,0:T(8,128)(2,1)}, bf16[2,96,1536]{2,1,0:T(8,128)(2,1)}, u32[]{:S(2)}, u32[]{:S(2)}) collective-permute-start(bf16[2,96,1536]{2,1,0:T(8,128)(2,1)} %slice.332), channel_id=1, source_target_pairs={{0,8},{4,12},{8,0},{12,4},{16,24},{20,28},{24,16},{28,20},{1,9},{5... | collective-permute-start | bytes 1769480 | tf_op jit(solution)/shard_map/ppermute | solution.py:407
  168.3 33.9 %all-to-all-start.1 = ((bf16[8,48,1536]{2,1,0:T(8,128)(2,1)}), bf16[8,48,1536]{2,1,0:T(8,128)(2,1)}, u32[]{:S(2)}, u32[]{:S(2)}) async-start(bf16[8,48,1536]{2,1,0:T(8,128)(2,1)} %reshape.674), calls=%async_computation.1 | async-start | bytes 2359296 | tf_op jit(solution)/shard_map/all_to_all | solution.py:737
  207.7 31.1 %collective-permute-start.17 = (bf16[4,4,96,1536]{3,2,1,0:T(8,128)(2,1)}, bf16[4,4,96,1536]{3,2,1,0:T(8,128)(2,1)}, u32[]{:S(2)}, u32[]{:S(2)}) collective-permute-start(bf16[4,4,96,1536]{3,2,1,0:T(8,128)(2,1)} %shard_map.259.refs_0_), channel_id=1, source_target_pairs={{0,4},{4,0},{8,12},{12,8},{16,20},{20,16},{24,28},{28,24},{1,5},{5... | collective-permute-start | bytes 14155784 | tf_op jit(solution)/shard_map/ppermute | solution.py:407
  214.6 117.2 %all-gather.10.cloned.1.call-start = ((), (), s32[]{:S(2)}) async-start(), calls=%async_computation.17 | async-start | bytes 5898240 | tf_op jit(solution)/shard_map/all_gather | solution.py:754
  242.1 257.8 %reduce-scatter.5.cloned.1.call-start = ((), (), s32[]{:S(2)}) async-start(), calls=%async_computation.12 | async-start | bytes 2949120 | tf_op jit(solution)/shard_map/reduce_scatter | solution.py:826
  254.7 36.0 %collective-permute-start.27 = (bf16[256,1536]{1,0:T(8,128)(2,1)S(1)}, bf16[256,1536]{1,0:T(8,128)(2,1)S(1)}, u32[]{:S(2)}, u32[]{:S(2)}) collective-permute-start(bf16[256,1536]{1,0:T(8,128)(2,1)S(1)} %multiply_convert_fusion.8), channel_id=1, source_target_pairs={{0,4},{4,0},{8,12},{12,8},{16,20},{20,16},{24,28},{28,24},{1,5},{5... | collective-permute-start | bytes 2359304 | tf_op jit(solution)/shard_map/ppermute | solution.py:407
  296.4 32.7 %collective-permute-start.32 = (bf16[256,1536]{1,0:T(8,128)(2,1)S(1)}, bf16[256,1536]{1,0:T(8,128)(2,1)}, u32[]{:S(2)}, u32[]{:S(2)}) collective-permute-start(bf16[256,1536]{1,0:T(8,128)(2,1)S(1)} %get-tuple-element.228), channel_id=1, source_target_pairs={{0,4},{4,0},{8,12},{12,8},{16,20},{20,16},{24,28},{28,24},{1,5},{5... | collective-permute-start | bytes 2359304 | tf_op jit(solution)/shard_map/ppermute | solution.py:407
  398.3 170.8 %reduce-scatter.7.cloned.1.call-start = ((), (), s32[]{:S(2)}) async-start(), calls=%async_computation.13 | async-start | bytes 5898240 | tf_op jit(solution)/shard_map/reduce_scatter | solution.py:833
  463.5 43.7 %all-to-all-start.3 = ((bf16[256,4,384]{2,0,1:T(8,128)(2,1)}), bf16[256,4,384]{2,0,1:T(8,128)(2,1)S(1)}, u32[]{:S(2)}, u32[]{:S(2)}) async-start(bf16[256,4,384]{2,0,1:T(8,128)(2,1)} %bitcast.301), calls=%async_computation.3 | async-start | bytes 1572864 | tf_op jit(solution)/shard_map/all_to_all | solution.py:395
  467.0 190.3 %reduce-scatter.9.cloned.1.call-start = ((), (), s32[]{:S(2)}) async-start(), calls=%async_computation.14 | async-start | bytes 3932160 | tf_op jit(solution)/shard_map/reduce_scatter | solution.py:936
  513.5 34.7 %collective-permute-start.47 = (bf16[4,96,1536]{2,1,0:T(8,128)(2,1)S(1)}, bf16[4,96,1536]{2,1,0:T(8,128)(2,1)S(1)}, u32[]{:S(2)}, u32[]{:S(2)}) collective-permute-start(bf16[4,96,1536]{2,1,0:T(8,128)(2,1)S(1)} %pad_maximum_fusion.10), channel_id=1, source_target_pairs={{0,8},{4,12},{8,0},{12,4},{16,24},{20,28},{24,16},{28,20},{1,9},{5... | collective-permute-start | bytes 3538952 | tf_op jit(solution)/shard_map/ppermute | solution.py:407
  516.7 31.5 %collective-permute-start.48 = (bf16[4,96,1536]{2,1,0:T(8,128)(2,1)S(1)}, bf16[4,96,1536]{2,1,0:T(8,128)(2,1)S(1)}, u32[]{:S(2)}, u32[]{:S(2)}) collective-permute-start(bf16[4,96,1536]{2,1,0:T(8,128)(2,1)S(1)} %fusion.45), channel_id=1, source_target_pairs={{0,16},{4,20},{8,24},{12,28},{16,0},{20,4},{24,8},{28,12},{1,17},{... | collective-permute-start | bytes 3538952 | tf_op jit(solution)/shard_map/ppermute | solution.py:407
  519.1 47.2 %collective-permute-start.49 = (bf16[4,96,1536]{2,1,0:T(8,128)(2,1)S(1)}, bf16[4,96,1536]{2,1,0:T(8,128)(2,1)}, u32[]{:S(2)}, u32[]{:S(2)}) collective-permute-start(bf16[4,96,1536]{2,1,0:T(8,128)(2,1)S(1)} %pad_maximum_fusion.12), channel_id=1, source_target_pairs={{0,8},{4,12},{8,0},{12,4},{16,24},{20,28},{24,16},{28,20},{1,9},{5... | collective-permute-start | bytes 3538952 | tf_op jit(solution)/shard_map/ppermute | solution.py:407
  522.3 46.9 %collective-permute-start.50 = (bf16[4,96,1536]{2,1,0:T(8,128)(2,1)}, bf16[4,96,1536]{2,1,0:T(8,128)(2,1)}, u32[]{:S(2)}, u32[]{:S(2)}) collective-permute-start(bf16[4,96,1536]{2,1,0:T(8,128)(2,1)} %fusion.47), channel_id=1, source_target_pairs={{0,16},{4,20},{8,24},{12,28},{16,0},{20,4},{24,8},{28,12},{1,17},{... | collective-permute-start | bytes 3538952 | tf_op jit(solution)/shard_map/ppermute | solution.py:407
  593.6 120.4 %reduce-scatter.11.cloned.1.call-start = ((), (), s32[]{:S(2)}) async-start(), calls=%async_computation.15 | async-start | bytes 2949120 | tf_op jit(solution)/shard_map/reduce_scatter | solution.py:968
  616.9 40.4 %collective-permute-start.55 = (bf16[4,48,1152]{2,1,0:T(8,128)(2,1)}, bf16[4,48,1152]{2,1,0:T(8,128)(2,1)}, u32[]{:S(2)}, u32[]{:S(2)}) collective-permute-start(bf16[4,48,1152]{2,1,0:T(8,128)(2,1)} %pad_maximum_fusion.24), channel_id=1, source_target_pairs={{0,8},{4,12},{8,0},{12,4},{16,24},{20,28},{24,16},{28,20},{1,9},{5... | collective-permute-start | bytes 1327112 | tf_op jit(solution)/shard_map/ppermute | solution.py:407
  618.3 39.0 %collective-permute-start.56 = (bf16[4,48,1152]{2,1,0:T(8,128)(2,1)}, bf16[4,48,1152]{2,1,0:T(8,128)(2,1)}, u32[]{:S(2)}, u32[]{:S(2)}) collective-permute-start(bf16[4,48,1152]{2,1,0:T(8,128)(2,1)} %pad_maximum_fusion.25), channel_id=1, source_target_pairs={{0,16},{4,20},{8,24},{12,28},{16,0},{20,4},{24,8},{28,12},{1,17},{... | collective-permute-start | bytes 1327112 | tf_op jit(solution)/shard_map/ppermute | solution.py:407
  (198 other events, 1962.9 us)
Sparse Core Ops, SparseCore 0:
  12.7 113.7 all-gather.7
  128.0 49.8 all-gather.5
  242.2 89.4 all-gather.9
  398.4 46.3 reduce-scatter.4
  446.9 97.3 reduce-scatter.6
  589.2 66.7 reduce-scatter.8
  658.3 55.6 reduce-scatter.10

commit v5 on v4

--- a/solution.py
+++ b/solution.py
@@ -35,15 +35,20 @@
     return lax.broadcasted_iota(jnp.int32, (1, width), 1)
 
 
-def attend_rows(query, keys, value_pair, query_clip, key_clip):
+def clip_features(clips):
+    slot = (lane_of() % HEAD_DIM).astype(jnp.float32)
+    used = slot < CLIPS + 1
+    of_query = jnp.where(used & (slot != clips), MASKED, 0.0)
+    of_key = jnp.where(used & (slot == jnp.where(clips < 0, float(CLIPS), clips)), 1.0, 0.0)
+    return of_query.astype(jnp.bfloat16), of_key.astype(jnp.bfloat16)
+
+
+def attend_rows(query, query_clips, key_pair, value_pair):
     first = lane_of() < HEAD_DIM
-    allowed = query_clip == key_clip
-    zero = jnp.zeros((), query.dtype)
     outs, tops = [], []
     for head in range(2):
         mine = first if head == 0 else jnp.logical_not(first)
-        scores = contract_last(jnp.where(mine, query, zero), keys)
-        scores = jnp.where(allowed, scores, MASKED)
+        scores = contract_last(jnp.where(mine, query, query_clips), key_pair[head])
         top = jnp.max(scores, axis=1, keepdims=True)
         weights = jnp.exp(scores - top).astype(jnp.bfloat16)
         mixed = contract(weights, value_pair[head])
@@ -61,9 +66,13 @@
     return jnp.where(first, values, one), jnp.where(first, one, values)
 
 
-def attend_rows_back(query, keys, keys_turned, values, grads, mixture, level, query_clip, key_clip):
+def key_with_clips(keys, key_clips):
     first = lane_of() < HEAD_DIM
-    allowed = key_clip == query_clip
+    return jnp.where(first, keys, key_clips), jnp.where(first, key_clips, keys)
+
+
+def attend_rows_back(query, query_clips, key_pair, keys_turned, values, grads, mixture, level):
+    first = lane_of() < HEAD_DIM
     zero = jnp.zeros((), query.dtype)
     product = jnp.transpose(grads.astype(jnp.float32) * mixture)
     level_turned = jnp.transpose(level)
@@ -74,8 +83,7 @@
         low, high = head * HEAD_DIM, (head + 1) * HEAD_DIM
         query_own = jnp.where(mine, query, zero)
         grads_own = jnp.where(mine, grads, zero)
-        scores = contract_last(keys, query_own)
-        scores = jnp.where(allowed, scores, MASKED)
+        scores = contract_last(key_pair[head], jnp.where(mine, query, query_clips))
         weights = jnp.exp(scores - level_turned[low : low + 1])
         grad_weights = contract_last(values, grads_own)
         diagonal = jnp.sum(product[low:high], axis=0, keepdims=True)
@@ -95,7 +103,7 @@
 
 
 def self_forward_kernel(
-    projected, cosine, sine, clip_column, clip_row, mixed, mixed_wide, level, low, value_pair
+    projected, cosine, sine, clip_column, mixed, mixed_wide, level, low, key_pair, value_pair
 ):
     rows = mixed.shape[0]
     pair = 2 * HEAD_DIM
@@ -107,47 +115,51 @@
     values = projected[:, 2 * pair : 3 * pair].astype(jnp.bfloat16)
     low[:, 2 * pair : 3 * pair] = values
     value_pair[0], value_pair[1] = value_with_ones(values)
+    _, key_clips = clip_features(clip_column[...])
+    key_pair[0], key_pair[1] = key_with_clips(low[:, pair : 2 * pair], key_clips)
 
     def step(index, carry):
         place = pl.ds(pl.multiple_of(index * block, block), block)
+        query_clips, _ = clip_features(clip_column[place, :])
         mixture, tops = attend_rows(
             low[place, 0:pair],
-            low[:, pair : 2 * pair],
+            query_clips,
+            (key_pair[0], key_pair[1]),
             (value_pair[0], value_pair[1]),
-            clip_column[place, :],
-            clip_row[...],
         )
         mixed[place, :] = mixture.astype(jnp.bfloat16)
         mixed_wide[place, :] = mixture
         level[place, :] = tops
         return carry
 
-    lax.fori_loop(0, rows // block, step, 0)
+    lax.fori_loop(0, rows // block, step, 0, unroll=True)
 
 
 def self_backward_kernel(
-    low, grads, mixed_wide, level, cosine, sine, clip_column, clip_row, out, keys_turned, totals
+    low, grads, mixed_wide, level, cosine, sine, clip_column, out, key_pair, keys_turned, totals
 ):
     rows = grads.shape[0]
     pair = 2 * HEAD_DIM
     block = min(256, rows)
     keys_turned[...] = jnp.transpose(low[:, pair : 2 * pair])
+    _, key_clips = clip_features(clip_column[...])
+    key_pair[0], key_pair[1] = key_with_clips(low[:, pair : 2 * pair], key_clips)
     totals[...] = jnp.zeros_like(totals)
     out[rows:, 0:pair] = jnp.zeros((out.shape[0] - rows, pair), jnp.bfloat16)
 
     def step(index, carry):
         start = pl.multiple_of(index * block, block)
         place = pl.ds(start, block)
+        query_clips, _ = clip_features(clip_column[place, :])
         query_turned, key_grad, value_grad = attend_rows_back(
             low[place, 0:pair],
-            low[:, pair : 2 * pair],
+            query_clips,
+            (key_pair[0], key_pair[1]),
             keys_turned[...],
             low[:, 2 * pair : 3 * pair],
             grads[place, :],
             mixed_wide[place, :],
             level[place, :],
-            clip_row[:, place],
-            clip_column[...],
         )
         query_grad = jnp.transpose(query_turned) * SCORE_SCALE
         back = query_grad * cosine[place, :] - swap_halves(query_grad) * sine[place, :]
@@ -156,43 +168,51 @@
         totals[1] += value_grad
         return carry
 
-    lax.fori_loop(0, rows // block, step, 0)
+    lax.fori_loop(0, rows // block, step, 0, unroll=True)
     key_grad = totals[0]
     back = key_grad * cosine[...] - swap_halves(key_grad) * sine[...]
     out[:, pair : 2 * pair] = back.astype(jnp.bfloat16)
     out[:, 2 * pair : 3 * pair] = totals[1].astype(jnp.bfloat16)
 
 
-def cross_forward_kernel(query, keys, values, clip_column, clip_row, mixed, mixed_wide, level):
-    mixture, tops = attend_rows(
-        query[...] * jnp.bfloat16(SCORE_SCALE),
-        keys[...],
-        value_with_ones(values[...]),
-        clip_column[...],
-        clip_row[...],
-    )
-    mixed[...] = mixture.astype(jnp.bfloat16)
-    mixed_wide[...] = mixture
-    level[...] = tops
+def cross_forward_kernel(query, keys, values, clip_column, text_column, mixed, mixed_wide, level):
+    pair = 2 * HEAD_DIM
+    query_clips, _ = clip_features(clip_column[...])
+    _, key_clips = clip_features(text_column[...])
+    for start in range(0, query.shape[1], pair):
+        part = slice(start, start + pair)
+        mixture, tops = attend_rows(
+            query[:, part] * jnp.bfloat16(SCORE_SCALE),
+            query_clips,
+            key_with_clips(keys[:, part], key_clips),
+            value_with_ones(values[:, part]),
+        )
+        mixed[:, part] = mixture.astype(jnp.bfloat16)
+        mixed_wide[:, part] = mixture
+        level[:, part] = tops
 
 
 def cross_backward_kernel(
-    query, keys, values, grads, mixed_wide, level, clip_column, clip_row, query_out, key_out, value_out
+    query, keys, values, grads, mixed_wide, level, clip_column, text_column, query_out, key_out, value_out
 ):
-    query_turned, key_grad, value_grad = attend_rows_back(
-        query[...] * jnp.bfloat16(SCORE_SCALE),
-        keys[...],
-        jnp.transpose(keys[...]),
-        values[...],
-        grads[...],
-        mixed_wide[...],
-        level[...],
-        clip_row[...],
-        clip_column[...],
-    )
-    query_out[...] = (jnp.transpose(query_turned) * SCORE_SCALE).astype(jnp.bfloat16)
-    key_out[...] = key_grad.astype(jnp.bfloat16)
-    value_out[...] = value_grad.astype(jnp.bfloat16)
+    pair = 2 * HEAD_DIM
+    query_clips, _ = clip_features(clip_column[...])
+    _, key_clips = clip_features(text_column[...])
+    for start in range(0, query.shape[1], pair):
+        part = slice(start, start + pair)
+        query_turned, key_grad, value_grad = attend_rows_back(
+            query[:, part] * jnp.bfloat16(SCORE_SCALE),
+            query_clips,
+            key_with_clips(keys[:, part], key_clips),
+            jnp.transpose(keys[:, part]),
+            values[:, part],
+            grads[:, part],
+            mixed_wide[:, part],
+            level[:, part],
+        )
+        query_out[:, part] = (jnp.transpose(query_turned) * SCORE_SCALE).astype(jnp.bfloat16)
+        key_out[:, part] = key_grad.astype(jnp.bfloat16)
+        value_out[:, part] = value_grad.astype(jnp.bfloat16)
 
 
 def whole(array):
@@ -203,6 +223,7 @@
     return pl.BlockSpec((rows, width), lambda p: (1 if second else 0, p))
 
 
+CROSS_PAIRS = 3
 KERNEL_PARAMS = pltpu.CompilerParams(
     dimension_semantics=("arbitrary",), vmem_limit_bytes=48 * 1024 * 1024
 )
@@ -214,7 +235,7 @@
     )
 
 
-def self_forward(projected, cosine, sine, clip_column, clip_row, rows):
+def self_forward(projected, cosine, sine, clip_column, rows):
     total, width = projected.shape
     pair = 2 * HEAD_DIM
     pairs = width // (3 * pair)
@@ -226,7 +247,6 @@
             whole(cosine),
             whole(sine),
             whole(clip_column),
-            whole(clip_row),
         ],
         out_specs=[lanes(rows), lanes(rows), lanes(rows), lanes(total, 3 * pair)],
         out_shape=[
@@ -235,13 +255,16 @@
             jax.ShapeDtypeStruct((rows, pairs * pair), jnp.float32),
             jax.ShapeDtypeStruct((total, width), jnp.bfloat16),
         ],
-        scratch_shapes=[pltpu.VMEM((2, total, pair), jnp.bfloat16)],
+        scratch_shapes=[
+            pltpu.VMEM((2, total, pair), jnp.bfloat16),
+            pltpu.VMEM((2, total, pair), jnp.bfloat16),
+        ],
         compiler_params=KERNEL_PARAMS,
         cost_estimate=cost(120),
-    )(projected, cosine, sine, clip_column, clip_row)
-
-
-def self_backward(low, grads, mixed_wide, level, cosine, sine, clip_column, clip_row):
+    )(projected, cosine, sine, clip_column)
+
+
+def self_backward(low, grads, mixed_wide, level, cosine, sine, clip_column):
     total, width = low.shape
     rows = grads.shape[0]
     pair = 2 * HEAD_DIM
@@ -257,35 +280,35 @@
             whole(cosine),
             whole(sine),
             whole(clip_column),
-            whole(clip_row),
         ],
         out_specs=lanes(total, 3 * pair),
         out_shape=jax.ShapeDtypeStruct((total, width), jnp.bfloat16),
         scratch_shapes=[
+            pltpu.VMEM((2, total, pair), jnp.bfloat16),
             pltpu.VMEM((pair, total), jnp.bfloat16),
             pltpu.VMEM((2, total, pair), jnp.float32),
         ],
         compiler_params=KERNEL_PARAMS,
-        cost_estimate=cost(15),
-    )(low, grads, mixed_wide, level, cosine, sine, clip_column, clip_row)
-
-
-def cross_forward(query, keyval, clip_column, clip_row):
+        cost_estimate=cost(2),
+    )(low, grads, mixed_wide, level, cosine, sine, clip_column)
+
+
+def cross_forward(query, keyval, clip_column, text_column):
     rows, width = query.shape
     keys = keyval.shape[0] // 2
-    pair = 2 * HEAD_DIM
-    pairs = width // pair
+    group = 2 * HEAD_DIM * CROSS_PAIRS
+    steps = width // group
     return pl.pallas_call(
         cross_forward_kernel,
-        grid=(pairs,),
+        grid=(steps,),
         in_specs=[
-            lanes(rows),
-            lanes(keys),
-            lanes(keys, second=True),
+            lanes(rows, group),
+            lanes(keys, group),
+            lanes(keys, group, second=True),
             whole(clip_column),
-            whole(clip_row),
-        ],
-        out_specs=[lanes(rows), lanes(rows), lanes(rows)],
+            whole(text_column),
+        ],
+        out_specs=[lanes(rows, group), lanes(rows, group), lanes(rows, group)],
         out_shape=[
             jax.ShapeDtypeStruct((rows, width), jnp.bfloat16),
             jax.ShapeDtypeStruct((rows, width), jnp.float32),
@@ -293,28 +316,28 @@
         ],
         compiler_params=KERNEL_PARAMS,
         cost_estimate=cost(20),
-    )(query, keyval, keyval, clip_column, clip_row)
-
-
-def cross_backward(query, keyval, grads, mixed_wide, level, clip_column, clip_row):
+    )(query, keyval, keyval, clip_column, text_column)
+
+
+def cross_backward(query, keyval, grads, mixed_wide, level, clip_column, text_column):
     rows, width = query.shape
     keys = keyval.shape[0] // 2
-    pair = 2 * HEAD_DIM
-    pairs = width // pair
+    group = 2 * HEAD_DIM * CROSS_PAIRS
+    steps = width // group
     return pl.pallas_call(
         cross_backward_kernel,
-        grid=(pairs,),
+        grid=(steps,),
         in_specs=[
-            lanes(rows),
-            lanes(keys),
-            lanes(keys, second=True),
-            lanes(rows),
-            lanes(rows),
-            lanes(rows),
+            lanes(rows, group),
+            lanes(keys, group),
+            lanes(keys, group, second=True),
+            lanes(rows, group),
+            lanes(rows, group),
+            lanes(rows, group),
             whole(clip_column),
-            whole(clip_row),
-        ],
-        out_specs=[lanes(rows), lanes(keys), lanes(keys)],
+            whole(text_column),
+        ],
+        out_specs=[lanes(rows, group), lanes(keys, group), lanes(keys, group)],
         out_shape=[
             jax.ShapeDtypeStruct((rows, width), jnp.bfloat16),
             jax.ShapeDtypeStruct((keys, width), jnp.bfloat16),
@@ -322,7 +345,7 @@
         ],
         compiler_params=KERNEL_PARAMS,
         cost_estimate=cost(120),
-    )(query, keyval, keyval, grads, mixed_wide, level, clip_column, clip_row)
+    )(query, keyval, keyval, grads, mixed_wide, level, clip_column, text_column)
 
 
 def norm_forward(hidden):
@@ -555,6 +578,92 @@
     for got in near[1:]:
         total = total + got.astype(jnp.float32)
     return total
+
+
+def spread_pairs(blocks, own_width):
+    line, rows, _ = blocks.shape
+    pair = 2 * HEAD_DIM
+
+    def kernel(given, result):
+        for source in range(line):
+            for number in range(own_width // pair):
+                for part in range(3):
+                    start = part * D + source * own_width + number * pair
+                    taken = (3 * number + part) * pair
+                    result[:, start : start + pair] = given[
+                        source, :, taken : taken + pair
+                    ].astype(jnp.float32)
+
+    return pl.pallas_call(
+        kernel,
+        out_shape=jax.ShapeDtypeStruct((rows, 3 * D), jnp.float32),
+        cost_estimate=cost(1),
+    )(blocks)
+
+
+def whole_grad_kernel(places, *refs):
+    lefts, rights, outs = refs[:8], refs[8:16], refs[16:]
+    for weight in range(4):
+        total = None
+        for side in range(2):
+            left, right = lefts[2 * weight + side], rights[2 * weight + side]
+            half = left.shape[1] // 2
+            rows = jnp.where(places[1] == 0, left[:, :half], left[:, half:])
+            part = lax.dot_general(
+                rows, right[...], (((0,), (0,)), ((), ())), preferred_element_type=jnp.float32
+            )
+            total = part if total is None else total + part
+        out = outs[weight // 2]
+        line, count = out.shape[1], out.shape[2] // 2
+        start = weight % 2 * count
+        for place_of in range(line):
+            out[0, place_of, start : start + count, :] = total[
+                place_of * count : (place_of + 1) * count
+            ].astype(jnp.bfloat16)
+
+
+def whole_grad_blocks(lefts, rights, chip, core):
+    chips, line = lax.axis_size("dp") // 2, lax.axis_size("seq")
+    shard = D // (2 * chips * line)
+    if two_by_two() and shard % 16 == 0:
+        width = 2 * line * shard
+
+        def left_spec(array):
+            return pl.BlockSpec((array.shape[0], width), lambda r, places: (0, places[0] ^ r))
+
+        def right_spec(array):
+            return pl.BlockSpec(
+                array.shape, lambda r, places: (0, 0), pipeline_mode=pl.Buffered(1)
+            )
+
+        flat_lefts = [side for pair in lefts for side in pair]
+        flat_rights = [side for pair in rights for side in pair]
+        out_shape = (chips, line, 2 * shard, D)
+        outs = pl.pallas_call(
+            whole_grad_kernel,
+            grid_spec=pltpu.PrefetchScalarGridSpec(
+                num_scalar_prefetch=1,
+                grid=(chips,),
+                in_specs=[left_spec(array) for array in flat_lefts]
+                + [right_spec(array) for array in flat_rights],
+                out_specs=[
+                    pl.BlockSpec((1,) + out_shape[1:], lambda r, places: (r, 0, 0, 0))
+                    for _ in range(2)
+                ],
+            ),
+            out_shape=[jax.ShapeDtypeStruct(out_shape, jnp.bfloat16) for _ in range(2)],
+            compiler_params=KERNEL_PARAMS,
+            cost_estimate=cost(0.1),
+        )(jnp.stack([chip, core]).astype(jnp.int32), *flat_lefts, *flat_rights)
+        return [[out[r] for r in range(chips)] for out in outs]
+    grads = []
+    for (left, left_other), (right, right_other) in zip(lefts, rights):
+        grad = (dot(left.T, right) + dot(left_other.T, right_other)).astype(jnp.bfloat16)
+        grads.append(take(grad.reshape(chips, 2, line, shard, D), core, 1)[:, 0])
+    return [
+        [jnp.concatenate([take(grad, chip ^ r)[0] for grad in group], axis=1) for r in range(chips)]
+        for group in (grads[:2], grads[2:])
+    ]
 
 
 def on_device(
@@ -611,7 +720,7 @@
         [all_frames - clip_starts + 1, jnp.zeros(TOKEN_ROWS, jnp.int32)]
     ).astype(f32)
     cosine, sine = rotary_tables(positions)
-    clip_column, clip_row = clips[:, None], clips[None, :]
+    clip_column = clips[:, None]
     own_clips = lax.dynamic_slice_in_dim(clips, seq_place * frame_count, frame_count)
     text_clips = (jnp.arange(text_count, dtype=jnp.int32) // CTX_LEN).astype(f32)
 
@@ -664,39 +773,27 @@
     )
     lined = lax.all_gather(stacked, "seq")
     inward_columns = line_swap(inward_send)
-    inward_columns, cotangent = tie(inward_columns, cotangent)
-
-    inward_state = plane_open(inward_columns)
-    cotangent_state = plane_open(cotangent[0])
-    context_other = flip(context, 1)
     context_spread = jnp.concatenate(
         [dot(context[0], spread_keys).astype(bf16), dot(context[0], spread_values).astype(bf16)],
         axis=0,
     )
-    inward_state, cotangent_state, context_spread, context_other = tie(
-        inward_state, cotangent_state, context_spread, context_other
-    )
+    inward_columns, cotangent, expand_blocks, context_spread, cosine, sine = tie(
+        inward_columns, cotangent, expand_blocks, context_spread, cosine, sine
+    )
+
+    inward_state = plane_open(inward_columns)
+    cotangent_state = plane_open(cotangent[0])
+    expand_part = lax.all_to_all(expand_blocks, "dp", 0, 0, tiled=True)
+    inward_state, cotangent_state = tie(inward_state, cotangent_state)
 
     inward_state = plane_relay(inward_state)
     cotangent_state = plane_relay(cotangent_state)
     inward_same = plane_chips(inward_state, chip_place)
-    core_rows = jnp.arange(D // 2, dtype=jnp.int32)[None, :]
-    core_rows = (
-        core_rows // (seq_count * shard) * 2 + core_place
-    ) * seq_count * shard + core_rows % (seq_count * shard)
-    core_keys = (core_rows == group * shard + within).astype(bf16)
-    core_values = (core_rows == group * shard + shard // 2 + within).astype(bf16)
-    context_core = [
-        jnp.concatenate(
-            [dot(side[0], core_keys).astype(bf16), dot(side[0], core_values).astype(bf16)], axis=0
-        )
-        for side in (context, context_other)
-    ]
-    inward_same, cotangent_state, context_core = tie(inward_same, cotangent_state, context_core)
+    inward_same, cotangent_state, expand_part = tie(inward_same, cotangent_state, expand_part)
 
     inward_other = flip(inward_same, 1)
     cotangent_same = plane_chips(cotangent_state)
-    inward_other, cosine, sine, cotangent_same = tie(inward_other, cosine, sine, cotangent_same)
+    inward_other, cotangent_same = tie(inward_other, cotangent_same)
 
     inward_own, extra_all = both_cores(
         inward_same, inward_other, core_place, [shard, extra_rows]
@@ -715,7 +812,14 @@
     token_low = jnp.pad(
         (token_norm * attend_gain).astype(bf16), ((0, TOKEN_ROWS - CLIPS), (0, 0))
     )
-    shrink_own = lax.all_gather(shrink_weight, "seq", tiled=True)
+    joined = two_by_two() and 2 * hidden_width == D and shard % 16 == 0
+    early_parts = dp_count // 4 if joined else 0
+    ffn_early = shrink_weight
+    if joined:
+        ffn_early = jnp.concatenate(
+            [shrink_weight, expand_part[:early_parts].reshape(early_parts * shard, D)], axis=0
+        )
+    ffn_early = lax.all_gather(ffn_early, "seq")
     cotangent_other = flip(cotangent_same, 1)
     cotangent_other, inward_own, token_low, lined, cross_gain, feed_gain = tie(
         cotangent_other, inward_own, token_low, lined, cross_gain, feed_gain
@@ -730,52 +834,50 @@
     row_norm, row_inverse = norm_forward(row_latents.astype(f32))
     row_low = jnp.concatenate([(row_norm * attend_gain).astype(bf16), token_low], axis=0)
     projected = dot(row_low, inward_own)
-    projected, first_state, expand_blocks = tie(projected, first_state, expand_blocks)
+    projected, first_state, lined = tie(projected, first_state, lined)
 
     first_state = plane_relay(first_state)
-    keyval_state = plane_open(weight_rows(2, 1))
-    expand_part = lax.all_to_all(expand_blocks, "dp", 0, 0, tiled=True)
+    second_state = plane_open(weight_rows(2, 2))
     attended, attended_wide, self_level, projected_low = self_forward(
-        projected, cosine, sine, clip_column, clip_row, row_length
-    )
-    attended, first_state, keyval_state, shrink_own, expand_part = tie(
-        attended, first_state, keyval_state, shrink_own, expand_part
+        projected, cosine, sine, clip_column, row_length
+    )
+    attended, first_state, second_state, ffn_early = tie(
+        attended, first_state, second_state, ffn_early
     )
 
     attended_low = line_swap(attended[:, :own_width], 0, 1)
     first_same = plane_chips(first_state, chip_place)
     first_other = flip(first_same, 1)
-    keyval_state = plane_relay(keyval_state)
-    return_state = plane_open(weight_rows(3, 1))
-    attended_low, first_same, first_other, keyval_state, return_state, expand_part = tie(
-        attended_low, first_same, first_other, keyval_state, return_state, expand_part
-    )
-
-    expand_lined = lax.all_gather(expand_part, "seq")
+    second_state = plane_relay(second_state)
+    attended_low, first_same, first_other, second_state, expand_part = tie(
+        attended_low, first_same, first_other, second_state, expand_part
+    )
+
+    expand_lined = lax.all_gather(expand_part[early_parts:], "seq")
     outward_full, query_full = [
         weight.reshape(D, D)
         for weight in both_cores(first_same, first_other, core_place, [shard] * 2)
     ]
-    keyval_same = plane_chips(keyval_state, chip_place)
-    keyval_other = flip(keyval_same, 1)
-    return_state = plane_relay(return_state)
+    second_same = plane_chips(second_state, chip_place)
+    second_other = flip(second_same, 1)
+    context_other = flip(context_spread, 1)
     after_self = latents[0].astype(f32) + dot(attended_low, outward_full)
     norm_two, inverse_two = norm_forward(after_self)
     normed_two = (norm_two * cross_gain).astype(bf16)
     cross_heads = dot(normed_two, query_full).astype(bf16)
     attended_other = flip(attended_low, 1)
-    cross_heads, keyval_same, keyval_other, return_state, attended_other = tie(
-        cross_heads, keyval_same, keyval_other, return_state, attended_other
-    )
-
-    keyval_full = both_cores(keyval_same, keyval_other, core_place, [shard])[0].reshape(D, D)
-    return_same = plane_chips(return_state, chip_place)
-    return_other = flip(return_same, 1)
+    cross_heads, second_same, second_other, attended_other, context_other = tie(
+        cross_heads, second_same, second_other, attended_other, context_other
+    )
+
+    keyval_full, return_full = [
+        weight.reshape(D, D)
+        for weight in both_cores(second_same, second_other, core_place, [shard] * 2)
+    ]
     keyval = dot(context_spread, keyval_full).astype(bf16)
     crossed, crossed_wide, cross_level = cross_forward(
-        cross_heads, keyval, own_clips[:, None], text_clips[None, :]
-    )
-    return_full = both_cores(return_same, return_other, core_place, [shard])[0].reshape(D, D)
+        cross_heads, keyval, own_clips[:, None], text_clips[:, None]
+    )
     normed_two_other = flip(normed_two, 1)
     crossed, return_full, normed_two_other = tie(crossed, return_full, normed_two_other)
 
@@ -787,15 +889,26 @@
     frames_same = plane_chips(frames_state)
     frames_same, expand_lined, crossed_other = tie(frames_same, expand_lined, crossed_other)
 
-    if two_by_two():
-        expand_own = assemble(
-            [expand_lined],
-            [(dp_count, seq_count, shard, 2 * hidden_width)],
-            [(0, at(line), 0, at(slice(None), line)) for line in range(seq_count)],
+    if joined:
+        moves = [(0, at(slice(None), pl.ds(0, hidden_width // seq_count)), 1, everything)]
+        for line in range(seq_count):
+            target = at(pl.ds(early_parts, dp_count - early_parts), line)
+            moves.append((1, at(line), 0, target))
+            for part in range(early_parts):
+                rows = pl.ds(hidden_width // seq_count + part * shard, shard)
+                moves.append((0, at(line, rows), 0, at(part, line)))
+        expand_own, shrink_own = assemble(
+            [ffn_early, expand_lined],
+            [
+                (dp_count, seq_count, shard, 2 * hidden_width),
+                (seq_count, hidden_width // seq_count, D),
+            ],
+            moves,
             jnp.zeros((1,), jnp.int32),
-        )[0]
+        )
     else:
-        expand_own = expand_lined.transpose(1, 0, 2, 3)
+        expand_own, shrink_own = expand_lined.transpose(1, 0, 2, 3), ffn_early
+    shrink_own = shrink_own.reshape(hidden_width, D)
     expand_own = expand_own.reshape(D, 2 * hidden_width)
     half_frames = chips * frame_count
     frames_other = flip(frames_same, 1)
@@ -813,23 +926,27 @@
     def sides(array):
         return array.astype(bf16).reshape(chips, frame_count, D)
 
+    shrink_part = (
+        dot(hidden_low[0].T, tangents[0]) + dot(hidden_low[1].T, tangents[1])
+    ).astype(bf16)
+    shrink_part, hidden_low, expand_low = tie(shrink_part, hidden_low, expand_low)
+    grad_shrink = lax.psum_scatter(shrink_part, "seq", scatter_dimension=0, tiled=True)
     feed_other = sides(dot(expand_low[1], expand_own.T))
     feed_got = flip(feed_other, 1)
     feed_same = sides(dot(expand_low[0], expand_own.T))
     feed_same, feed_got, hidden_low, expand_low = tie(feed_same, feed_got, hidden_low, expand_low)
     feed_blocks = [feed_same[r].astype(f32) + feed_got[r].astype(f32) for r in range(chips)]
     feed_far = plane_far(feed_blocks)
-    shrink_part = (
-        dot(hidden_low[0].T, tangents[0]) + dot(hidden_low[1].T, tangents[1])
-    ).astype(bf16)
-    feed_far, shrink_part, expand_low = tie(feed_far, shrink_part, expand_low)
-    grad_shrink = lax.psum_scatter(shrink_part, "seq", scatter_dimension=0, tiled=True)
+    fed_other = sides(dot(hidden_low[1], shrink_own))
+    fed_got = flip(fed_other, 1)
+    fed_same = sides(dot(hidden_low[0], shrink_own))
+    feed_far, fed_got, fed_same, expand_low = tie(feed_far, fed_got, fed_same, expand_low)
 
     feed_near = plane_near(feed_blocks, feed_far)
     expand_grad = (dot(frames[0].T, expand_low[0]) + dot(frames[1].T, expand_low[1])).astype(bf16)
     expand_grad = expand_grad.reshape(dp_count, seq_count, shard, 2 * hidden_width)
     expand_grad = expand_grad.transpose(1, 0, 2, 3).reshape(D, 2 * hidden_width)
-    feed_near, expand_grad, hidden_low = tie(feed_near, expand_grad, hidden_low)
+    feed_near, expand_grad = tie(feed_near, expand_grad)
     expand_sum = lax.psum_scatter(expand_grad, "seq", scatter_dimension=0, tiled=True)
     expand_sum = expand_sum.reshape(dp_count, shard, 2 * hidden_width)
 
@@ -852,12 +969,6 @@
     def side_blocks(opened):
         return [side_block(opened, r) for r in range(chips)]
 
-    def both_grad(left, left_other, right, right_other):
-        return (dot(left.T, right) + dot(left_other.T, right_other)).astype(bf16)
-
-    def own_core(grad):
-        return take(grad.reshape(chips, 2, seq_count, shard, D), core_place, 1)[:, 0]
-
     feed_norm_grad = plane_total(feed_near)
     feed_term, feed_gain_part = norm_backward(
         feed_norm_grad, norm_three, inverse_three, feed_gain
@@ -866,15 +977,17 @@
     return_low = after_cross_grad.astype(bf16)
     crossed_grad = dot(return_low, return_full.T).astype(bf16)
     return_other = flip(return_low, 1)
-    crossed_grad, return_low, return_other = tie(crossed_grad, return_low, return_other)
+    crossed_grad, return_low, return_other, grad_shrink = tie(
+        crossed_grad, return_low, return_other, grad_shrink
+    )
     cross_query_low, cross_key_low, cross_value_low = cross_backward(
         cross_heads,
         keyval,
         crossed_grad,
         crossed_wide,
         cross_level,
+        own_clips[:, None],
         text_clips[:, None],
-        own_clips[None, :],
     )
     cross_query_low, cross_key_low, cross_value_low = tie(
         cross_query_low, cross_key_low, cross_value_low
@@ -889,30 +1002,23 @@
     keyval_low = jnp.concatenate([cross_key_low, cross_value_low], axis=0)
     keyval_low_other = flip(keyval_low, 1)
     cross_query_other = flip(cross_query_low, 1)
-    attended_grad, outward_low, keyval_low, keyval_low_other, cross_query_other, return_other = tie(
-        attended_grad, outward_low, keyval_low, keyval_low_other, cross_query_other, return_other
+    queries_in, returns_in = (cross_query_low, cross_query_other), (return_low, return_other)
+    attended_grad, outward_low, keyval_low, keyval_low_other, queries_in, returns_in = tie(
+        attended_grad, outward_low, keyval_low, keyval_low_other, queries_in, returns_in
     )
 
     attended_grad_own = line_swap(attended_grad, 1, 0)
     outward_other = flip(outward_low, 1)
-    keyval_grad = both_grad(context_core[0], context_core[1], keyval_low, keyval_low_other)
-    whole_grads = [
-        own_core(both_grad(crossed, crossed_other, return_low, return_other)),
-        keyval_grad.reshape(chips, seq_count, shard, D),
-        own_core(both_grad(normed_two, normed_two_other, cross_query_low, cross_query_other)),
-        own_core(both_grad(attended_low, attended_other, outward_low, outward_other)),
-    ]
-    halves = [
-        [
-            jnp.concatenate([take(grad, chip_place ^ r)[0] for grad in group], axis=1)
-            for r in range(chips)
-        ]
-        for group in (whole_grads[:2], whole_grads[2:])
-    ]
+    halves = whole_grad_blocks(
+        [(crossed, crossed_other), (context_spread, context_other)]
+        + [(normed_two, normed_two_other), (attended_low, attended_other)],
+        [returns_in, (keyval_low, keyval_low_other), queries_in, (outward_low, outward_other)],
+        chip_place,
+        core_place,
+    )
+    attended_grad_own, halves = tie(attended_grad_own, halves)
     half_far = [plane_far(blocks) for blocks in halves]
-    attended_grad_own, half_far, grad_shrink = tie(attended_grad_own, half_far, grad_shrink)
-
-    near_early = plane_near(halves[0], half_far[0])
+
     attended_grad_own = jnp.pad(attended_grad_own, ((0, 0), (0, padded - own_width)))
     inward_low = self_backward(
         projected_low,
@@ -922,24 +1028,28 @@
         cosine,
         sine,
         clip_column,
-        clip_row,
-    )
-    inward_low, near_early = tie(inward_low, near_early)
-
-    near_late = plane_near(halves[1], half_far[1])
+    )
     attend_parts = dot(inward_low, inward_own.T)
     attend_low = attend_parts[:row_length].astype(bf16)
-    attend_low, inward_low, attend_parts, near_late, expand_sum, hidden_low = tie(
-        attend_low, inward_low, attend_parts, near_late, expand_sum, hidden_low
-    )
-
+    inward_low, attend_parts, attend_low, halves, half_far, expand_sum = tie(
+        inward_low, attend_parts, attend_low, halves, half_far, expand_sum
+    )
+
+    near_early = plane_near(halves[0], half_far[0])
     attend_sum = lax.psum_scatter(attend_low, "seq", scatter_dimension=0, tiled=True)
-    expand_rows = lax.all_to_all(expand_sum, "dp", 0, 0, tiled=True)
-    inward_blocks = side_blocks([open_grad(dot(row_low.T, inward_low))])
-    inward_far = plane_far(inward_blocks)
+    near_late = plane_near(halves[1], half_far[1])
+    inward_grad = open_grad(dot(row_low.T, inward_low))
+    inward_grad, attend_parts, near_early, near_late = tie(
+        inward_grad, attend_parts, near_early, near_late
+    )
+
     whole_column = jnp.concatenate(
         [plane_total(near_early).astype(bf16), plane_total(near_late).astype(bf16)], axis=1
     )
+    whole_sums = lax.psum_scatter(whole_column, "seq", scatter_dimension=0)
+    expand_rows = lax.all_to_all(expand_sum, "dp", 0, 0, tiled=True)
+    inward_blocks = side_blocks([inward_grad])
+    inward_far = plane_far(inward_blocks)
     token_term, token_gain_part = norm_backward(
         attend_parts[row_length : row_length + CLIPS], token_norm, token_inverse, attend_gain
     )
@@ -958,21 +1068,14 @@
     )
     small = jnp.pad(small, ((0, 0), (0, -small.shape[1] % 2048)))
     small = small.reshape(device_count, -1, 128)
-    fed_other = sides(dot(hidden_low[1], shrink_own))
-    fed_got = flip(fed_other, 1)
-    fed_same = sides(dot(hidden_low[0], shrink_own))
-    inward_far, fed_got, fed_same, small, expand_rows, whole_column = tie(
-        inward_far, fed_got, fed_same, small, expand_rows, whole_column
-    )
-
-    whole_sums = lax.psum_scatter(whole_column, "seq", scatter_dimension=0)
-    small_all = lax.all_to_all(small, ("dp", "seq"), 0, 0, tiled=True).astype(f32)
+    inward_far, fed_got, fed_same, small, expand_rows = tie(
+        inward_far, fed_got, fed_same, small, expand_rows
+    )
+
     inward_near = plane_near(inward_blocks, inward_far)
     fed_blocks = [fed_same[r].astype(f32) + fed_got[r].astype(f32) for r in range(chips)]
     fed_far = plane_far(fed_blocks)
-    inward_near, fed_far, expand_rows, small_all, attend_sum = tie(
-        inward_near, fed_far, expand_rows, small_all, attend_sum
-    )
+    inward_near, fed_far = tie(inward_near, fed_far)
 
     inward_rows = line_swap(plane_total(inward_near).astype(bf16))
     fed_near = plane_near(fed_blocks, fed_far)
@@ -982,11 +1085,11 @@
         .reshape(shard, 2 * FF)
         .astype(f32)
     )
-    inward_rows, fed_near, grad_expand, whole_sums = tie(
-        inward_rows, fed_near, grad_expand, whole_sums
-    )
-    whole_sums = whole_sums.astype(f32)
-
+    inward_rows, fed_near, grad_expand, attend_sum, small = tie(
+        inward_rows, fed_near, grad_expand, attend_sum, small
+    )
+
+    small_all = lax.all_to_all(small, ("dp", "seq"), 0, 0, tiled=True).astype(f32)
     block_output = (after_cross + plane_total(fed_near)).astype(bf16)
     own_norm = lax.dynamic_slice_in_dim(row_norm, seq_place * frame_count, frame_count, axis=0)
     own_inverse = lax.dynamic_slice_in_dim(
@@ -997,9 +1100,16 @@
     )
     latents_grad = (after_self_grad + attend_term)[None]
     grad_shrink = grad_shrink.astype(f32)
-    grad_inward = (
-        from_pairs(inward_rows).transpose(1, 2, 0, 3).reshape(shard, 3 * D).astype(f32)
-    )
+    if own_width % pair_width == 0:
+        grad_inward = spread_pairs(inward_rows, own_width)
+    else:
+        grad_inward = (
+            from_pairs(inward_rows).transpose(1, 2, 0, 3).reshape(shard, 3 * D).astype(f32)
+        )
+    grad_inward, block_output, latents_grad, whole_sums = tie(
+        grad_inward, block_output, latents_grad, whole_sums
+    )
+    whole_sums = whole_sums.astype(f32)
     grad_return = whole_sums[:shard]
     grad_keyval = jnp.concatenate(
         [whole_sums[shard : shard + shard // 2], whole_sums[shard + shard // 2 : 2 * shard]],

time: 746 us -> 724 us (0.971)
  matrix products: 160 us -> 119 us
  waiting for transfers between devices: 185 us -> 226 us
  other arithmetic: 92.6 us -> 76.5 us
  Pallas kernels: 102 us -> 114 us
  local copies, waits for them, and re-layouts: 96.2 us -> 84.9 us
    ppermute x61 -> x56, waiting for transfers between devices: 105 us -> 149 us  [flip(): return lax.ppermute(values, 'dp', xor_pairs(lax.axis_size('dp'), bit))]
    dot_general x37 -> x25, matrix products: 159 us -> 118 us  [dot(): return jnp.dot(left, right, preferred_element_type=jnp.float32)]
    all_to_all x4, waiting for transfers between devices: 34.6 us -> 68.9 us  [line_swap(): return lax.all_to_all(blocks, 'seq', split, join, tiled=True)]
    reduce_scatter x1, waiting for transfers between devices: 23.4 us -> 0.01 us  [on_device(): whole_sums = lax.psum_scatter(whole_column, 'seq', scatter_dimension=0)]
    all_to_all x1, waiting for transfers between devices: 19.5 us -> 4.75 us  [on_device(): lax.all_to_all(small, ('dp', 'seq'), 0, 0, tiled=True).astype(f32)]
    pallas_call x2 -> x4, Pallas kernels: 25.1 us -> 38.5 us  [the longest x1 15 us: whole_grad_blocks(): pl.pallas_call(whole_grad_kernel, grid_spec=pltpu.PrefetchScalarGridSpec(...]
    convert_element_type x5 -> x0, local copies, waits for them, and re-layouts: 8.18 us -> none  [on_device(): from_pairs(inward_rows).transpose(1, 2, 0, 3).reshape(shard, 3 * D)]
    unnamed x307 -> x315, local copies, waits for them, and re-layouts: 32.6 us -> 38.6 us
  transfers between devices with their start and end apart: 75 -> 70, of which waited for: 27 -> 29; matrix products, arithmetic and copies ran while one was open for 37% -> 29% of each run, Pallas kernels for 13% -> 15%
where the time goes in v5:
time: 724 us; the launch traced here: 714 us
  waiting for transfers between devices  226 us (31%)
  matrix products  119 us (16%)
  Pallas kernels  114 us (16%)
  local copies, waits for them, and re-layouts  84.9 us (12%)
  starting transfers between devices  77.6 us (11%)
  other arithmetic  76.5 us (11%)
  between operations  17.1 us (2%)
    ppermute x56, waiting for transfers between devices, flip(): return lax.ppermute(values, 'dp', xor_pairs(lax.axis_size('dp'), bit))  149 us
    dot_general x25, matrix products, dot(): return jnp.dot(left, right, preferred_element_type=jnp.float32)  118 us
    all_to_all x4, waiting for transfers between devices, line_swap(): return lax.all_to_all(blocks, 'seq', split, join, tiled=True)  68.9 us
    ppermute x56, starting transfers between devices, flip(): return lax.ppermute(values, 'dp', xor_pairs(lax.axis_size('dp'), bit))  48.1 us
    unnamed x315, local copies, waits for them, and re-layouts  38.6 us
    pallas_call x9, Pallas kernels, assemble(): pl.pallas_call(kernel, in_specs=[pl.BlockSpec(memory_space=pltpu.SMEM)] +...  35 us
    pallas_call x1, Pallas kernels, self_backward(): pl.pallas_call(self_backward_kernel, grid=(pairs,), in_specs=[lanes(total...  21.1 us
    pallas_call x1, Pallas kernels, self_forward(): pl.pallas_call(self_forward_kernel, grid=(pairs,), in_specs=[lanes(total,...  19.1 us
  transfers between devices with their start and end apart: 70, of which 29 were waited for; matrix products, arithmetic and copies ran while one was open for 29% of the time, Pallas kernels for 15%

profile of v5, /device:TPU:0, one launch (start us, length us, event | category | flops | bytes accessed | tf_op | source)
XLA Modules:
  0.0 714.1 jit_solution(16141995456669887994)
XLA Ops:
  33.4 19.1 %all-to-all-done.refs_0_ = bf16[4,64,1152]{2,1,0:T(8,128)(2,1)S(1)} async-done(((bf16[4,64,1152]{2,1,0:T(8,128)(2,1)}), bf16[4,64,1152]{2,1,0:T(8,128)(2,1)S(1)}, u32[]{:S(2)}, u32[]{:S(2)}) %all-to-all-start) | async-done | bytes 589856 | tf_op jit(solution)/shard_map/all_to_all | solution.py:418
  63.5 27.1 %collective-permute-done.refs_1_ = bf16[4,64,1152]{2,1,0:T(8,128)(2,1)S(1)} collective-permute-done((bf16[4,64,1152]{2,1,0:T(8,128)(2,1)S(1)}, bf16[4,64,1152]{2,1,0:T(8,128)(2,1)S(1)}, u32[]{:S(2)}, u32[]{:S(2)}) %collective-permute-start) | collective-permute-done | bytes 589856 | tf_op jit(solution)/shard_map/ppermute | solution.py:430
  98.6 8.3 %collective-permute-done.4.refs_3_ = bf16[2,64,1152]{2,1,0:T(8,128)(2,1)S(1)} collective-permute-done((bf16[2,64,1152]{2,1,0:T(8,128)(2,1)S(1)}, bf16[2,64,1152]{2,1,0:T(8,128)(2,1)S(1)}, u32[]{:S(2)}, u32[]{:S(2)}) %collective-permute-start.4) | collective-permute-done | bytes 294944 | tf_op jit(solution)/shard_map/ppermute | solution.py:430
  145.4 7.0 fusion.9.projected
  152.4 14.0 %collective-permute-done.10.refs_1_ = bf16[4,96,1536]{2,1,0:T(8,128)(2,1)S(1)} collective-permute-done((bf16[4,96,1536]{2,1,0:T(8,128)(2,1)S(1)}, bf16[4,96,1536]{2,1,0:T(8,128)(2,1)S(1)}, u32[]{:S(2)}, u32[]{:S(2)}) %collective-permute-start.10) | collective-permute-done | bytes 1179680 | tf_op jit(solution)/shard_map/ppermute | solution.py:430
  172.8 19.1 %shard_map.258 = (bf16[1024,384]{1,0:T(8,128)(2,1)S(1)}, f32[1024,384]{1,0:T(8,128)S(1)}, f32[1024,384]{1,0:T(8,128)S(1)}, bf16[1152,1152]{1,0:T(8,128)(2,1)}) custom-call(f32[1152,1152]{1,0:T(8,128)} %fusion.9.projected, f32[1152,128]{1,0:T(8,128)S(1)} %copy-done.19, f32[1152,128]{1,0:T(8,128)S(1)} %copy-done.17, f32[1152,1]{1,0:T(8,128)S(1)} %copy-done.21), custom_call_target="tpu_custom_call" | custom-call | flops 120000004096 | bytes 1048576 | tf_op jit(solution)/shard_map/pallas_call | solution.py:242
  196.0 11.8 %collective-permute-done.12.refs_3_ = bf16[2,96,1536]{2,1,0:T(8,128)(2,1)} collective-permute-done((bf16[2,96,1536]{2,1,0:T(8,128)(2,1)}, bf16[2,96,1536]{2,1,0:T(8,128)(2,1)}, u32[]{:S(2)}, u32[]{:S(2)}) %collective-permute-start.12) | collective-permute-done | bytes 589856 | tf_op jit(solution)/shard_map/ppermute | solution.py:430
  223.2 16.0 %all-to-all-done.2 = bf16[4,256,384]{2,1,0:T(8,128)(2,1)S(1)} async-done(((bf16[4,256,384]{2,1,0:T(8,128)(2,1)}), bf16[4,256,384]{2,1,0:T(8,128)(2,1)S(1)}, u32[]{:S(2)}, u32[]{:S(2)}) %all-to-all-start.2) | async-done | bytes 786464 | tf_op jit(solution)/shard_map/all_to_all | solution.py:418
  262.4 7.2 %shard_map.262 = (bf16[4,2,4,48,1536]{4,3,2,1,0:T(8,128)(2,1)S(1)}, bf16[4,2,4,48,1536]{4,3,2,1,0:T(8,128)(2,1)}) custom-call(s32[1]{0:T(128)} %bitcast.10.places_ref, bf16[4,4,96,1536]{3,2,1,0:T(8,128)(2,1)} %shard_map.261.refs_0_, bf16[4,4,96,1536]{3,2,1,0:T(8,128)(2,1)} %collective-permute-done.19.refs_1_), custom_call_target="tpu_custom_call" | custom-call | bytes 18874368 | tf_op jit(solution)/shard_map/pallas_call | solution.py:455
  269.6 7.4 %convolution_convert_fusion.5.keys.values = bf16[768,1536]{1,0:T(8,128)(2,1)} fusion(bf16[768,1536]{1,0:T(8,128)(2,1)} %pad_maximum_fusion.3.refs_2_, bf16[1536,1536]{1,0:T(8,128)(2,1)S(1)} %bitcast.263), kind=kOutput, calls=%fused_computation.18 | convolution fusion | flops 3625058304 | bytes 9437184 | tf_op jit(solution)/shard_map/dot_general | solution.py:422
  277.0 10.6 %shard_map.263 = (bf16[256,1536]{1,0:T(8,128)(2,1)}, f32[256,1536]{1,0:T(8,128)S(1)}, f32[256,1536]{1,0:T(8,128)S(1)}) custom-call(bf16[256,1536]{1,0:T(8,128)(2,1)S(1)} %convolution_convert_fusion.8.query, bf16[768,1536]{1,0:T(8,128)(2,1)} %convolution_convert_fusion.5.keys.values, bf16[768,1536]{1,0:T(8,128)(2,1)} %convolution_convert_fusion.5.keys.values, ...), custom_call_target="tpu_custom_call" | custom-call | flops 20000000000 | bytes 1048576 | tf_op jit(solution)/shard_map/pallas_call | solution.py:301
  294.3 17.6 %collective-permute-done.23.refs_1_ = bf16[256,1536]{1,0:T(8,128)(2,1)S(1)} collective-permute-done((bf16[256,1536]{1,0:T(8,128)(2,1)S(1)}, bf16[256,1536]{1,0:T(8,128)(2,1)S(1)}, u32[]{:S(2)}, u32[]{:S(2)}) %collective-permute-start.23) | collective-permute-done | bytes 786464 | tf_op jit(solution)/shard_map/ppermute | solution.py:430
  314.3 8.4 %collective-permute-done.25.refs_3_ = bf16[128,1536]{1,0:T(8,128)(2,1)S(1)} collective-permute-done((bf16[128,1536]{1,0:T(8,128)(2,1)S(1)}, bf16[128,1536]{1,0:T(8,128)(2,1)S(1)}, u32[]{:S(2)}, u32[]{:S(2)}) %collective-permute-start.25) | collective-permute-done | bytes 393248 | tf_op jit(solution)/shard_map/ppermute | solution.py:430
  332.1 7.8 %fusion.67 = f32[1024,1536]{1,0:T(8,128)S(1)} fusion(bf16[1024,1536]{1,0:T(8,128)(2,1)S(1)} %bitcast.286, bf16[1536,1536]{1,0:T(8,128)(2,1)} %bitcast.320), kind=kOutput, calls=%fused_computation.254 | convolution fusion | flops 4831838208 | bytes 14155776 | tf_op jit(solution)/shard_map/dot_general | solution.py:422
  366.2 7.8 %convolution_convert_fusion.3 = bf16[1024,1536]{1,0:T(8,128)(2,1)S(1)} fusion(bf16[1024,1536]{1,0:T(8,128)(2,1)S(1)} %pad_maximum_fusion.2, bf16[1536,1536]{1,0:T(8,128)(2,1)} %bitcast.321), kind=kOutput, calls=%fused_computation.15 | convolution fusion | flops 4833411072 | bytes 11010048 | tf_op jit(solution)/shard_map/dot_general | solution.py:422
  374.6 9.0 %convolution_convert_fusion.4 = bf16[1024,1536]{1,0:T(8,128)(2,1)} fusion(bf16[1024,1536]{1,0:T(8,128)(2,1)S(1)} %copy-done.80, bf16[1536,1536]{1,0:T(8,128)(2,1)} %bitcast.322), kind=kOutput, calls=%fused_computation.16 | convolution fusion | flops 4833411072 | bytes 11010048 | tf_op jit(solution)/shard_map/dot_general | solution.py:422
  434.7 10.8 %shard_map.266 = (bf16[256,1536]{1,0:T(8,128)(2,1)S(1)}, bf16[384,1536]{1,0:T(8,128)(2,1)S(1)}, bf16[384,1536]{1,0:T(8,128)(2,1)S(1)}) custom-call(bf16[256,1536]{1,0:T(8,128)(2,1)S(1)} %copy-done.51, bf16[768,1536]{1,0:T(8,128)(2,1)} %convolution_convert_fusion.5.keys.values, bf16[768,1536]{1,0:T(8,128)(2,1)} %convolution_convert_fusion.5.keys.values, ...), custom_call_target="tpu_custom_call" | custom-call | flops 120000004096 | bytes 1048576 | tf_op jit(solution)/shard_map/pallas_call | solution.py:327
  467.8 15.0 %shard_map.267 = (bf16[4,4,96,1536]{3,2,1,0:T(8,128)(2,1)}, bf16[4,4,96,1536]{3,2,1,0:T(8,128)(2,1)}) custom-call(s32[2]{0:T(128)S(1)} %pad_add_fusion.1.places, bf16[256,1536]{1,0:T(8,128)(2,1)} %get-tuple-element.241.refs_0_, bf16[256,1536]{1,0:T(8,128)(2,1)} %collective-permute-done.27.refs_1_, bf16[768,1536]{1,0:T(8,128)(2,1)} %pad_maximum_fusion.3.refs_2_, ...), custom_call_target="tpu_custom_call" | custom-call | flops 100000000 | bytes 1048576 | tf_op jit(solution)/shard_map/pallas_call | solution.py:642
  489.9 17.7 %all-to-all-done.3 = bf16[256,4,384]{2,0,1:T(8,128)(2,1)S(1)} async-done(((bf16[256,4,384]{2,0,1:T(8,128)(2,1)}), bf16[256,4,384]{2,0,1:T(8,128)(2,1)S(1)}, u32[]{:S(2)}, u32[]{:S(2)}) %all-to-all-start.3) | async-done | bytes 786464 | tf_op jit(solution)/shard_map/all_to_all | solution.py:418
  515.4 21.1 %shard_map.268 = bf16[1152,1152]{1,0:T(8,128)(2,1)} custom-call(bf16[1152,1152]{1,0:T(8,128)(2,1)} %get-tuple-element.207.low, bf16[1024,384]{1,0:T(8,128)(2,1)S(1)} %bitcast.259, f32[1024,384]{1,0:T(8,128)S(1)} %copy-done.26, f32[1024,384]{1,0:T(8,128)S(1)} %copy-done.28, f32[1152,128]{1,0:T(8,128)S(1)} %copy-done.20, f32[1152,128]{1,0:T(8,128)S(1)} %copy-done.18, ...), custom_call_target="tpu_custom_call" | custom-call | flops 2000000000 | bytes 1048576 | tf_op jit(solution)/shard_map/pallas_call | solution.py:272
  536.5 6.6 fusion.71
  583.5 21.6 %collective-permute-done.45 = bf16[4,96,1536]{2,1,0:T(8,128)(2,1)} collective-permute-done((bf16[4,96,1536]{2,1,0:T(8,128)(2,1)}, bf16[4,96,1536]{2,1,0:T(8,128)(2,1)}, u32[]{:S(2)}, u32[]{:S(2)}) %collective-permute-start.45) | collective-permute-done | bytes 1179680 | tf_op jit(solution)/shard_map/ppermute | solution.py:430
  643.0 7.6 %collective-permute-done.51 = bf16[4,48,1152]{2,1,0:T(8,128)(2,1)S(1)} collective-permute-done((bf16[4,48,1152]{2,1,0:T(8,128)(2,1)S(1)}, bf16[4,48,1152]{2,1,0:T(8,128)(2,1)S(1)}, u32[]{:S(2)}, u32[]{:S(2)}) %collective-permute-start.51) | collective-permute-done | bytes 442400 | tf_op jit(solution)/shard_map/ppermute | solution.py:430
  668.0 16.1 %all-to-all-done.5.given = bf16[4,48,1152]{2,1,0:T(8,128)(2,1)} async-done(((bf16[4,48,1152]{2,1,0:T(8,128)(2,1)}), bf16[4,48,1152]{2,1,0:T(8,128)(2,1)}, u32[]{:S(2)}, u32[]{:S(2)}) %all-to-all-start.5) | async-done | bytes 442400 | tf_op jit(solution)/shard_map/all_to_all | solution.py:418
  (659 shorter events, 382.2 us)
Async XLA Ops:
  7.2 126.7 %all-gather.7.cloned.1.call-start = ((), (), s32[]{:S(2)}) async-start(), calls=%async_computation.15 | async-start | bytes 6881280 | tf_op jit(solution)/shard_map/all_gather | solution.py:774
  13.2 39.3 %all-to-all-start = ((bf16[4,64,1152]{2,1,0:T(8,128)(2,1)}), bf16[4,64,1152]{2,1,0:T(8,128)(2,1)S(1)}, u32[]{:S(2)}, u32[]{:S(2)}) async-start(bf16[4,64,1152]{2,1,0:T(8,128)(2,1)} %pad_maximum_fusion.16), calls=%async_computation | async-start | bytes 1179648 | tf_op jit(solution)/shard_map/all_to_all | solution.py:418
  52.5 39.2 %collective-permute-start.2 = (bf16[256,1536]{1,0:T(8,128)(2,1)S(1)}, bf16[256,1536]{1,0:T(8,128)(2,1)S(1)}, u32[]{:S(2)}, u32[]{:S(2)}) collective-permute-start(bf16[256,1536]{1,0:T(8,128)(2,1)S(1)} %bitcast.256), channel_id=1, source_target_pairs={{0,8},{4,12},{8,0},{12,4},{16,24},{20,28},{24,16},{28,20},{1,9},{5... | collective-permute-start | bytes 2359304 | tf_op jit(solution)/shard_map/ppermute | solution.py:430
  54.0 37.7 %collective-permute-start.3 = (bf16[256,1536]{1,0:T(8,128)(2,1)S(1)}, bf16[256,1536]{1,0:T(8,128)(2,1)}, u32[]{:S(2)}, u32[]{:S(2)}) collective-permute-start(bf16[256,1536]{1,0:T(8,128)(2,1)S(1)} %bitcast.257), channel_id=1, source_target_pairs={{0,16},{4,20},{8,24},{12,28},{16,0},{20,4},{24,8},{28,12},{1,17},{... | collective-permute-start | bytes 2359304 | tf_op jit(solution)/shard_map/ppermute | solution.py:430
  55.5 60.8 %all-to-all-start.1 = ((bf16[8,48,1536]{2,1,0:T(8,128)(2,1)}), bf16[8,48,1536]{2,1,0:T(8,128)(2,1)}, u32[]{:S(2)}, u32[]{:S(2)}) async-start(bf16[8,48,1536]{2,1,0:T(8,128)(2,1)} %reshape.530), calls=%async_computation.1 | async-start | bytes 2359296 | tf_op jit(solution)/shard_map/all_to_all | solution.py:786
  59.8 136.2 %all-gather.9.cloned.1.call-start = ((), (), s32[]{:S(2)}) async-start(), calls=%async_computation.16 | async-start | bytes 4423680 | tf_op jit(solution)/shard_map/all_gather | solution.py:822
  167.0 40.8 %collective-permute-start.14 = (bf16[4,96,1536]{2,1,0:T(8,128)(2,1)S(1)}, bf16[4,96,1536]{2,1,0:T(8,128)(2,1)S(1)}, u32[]{:S(2)}, u32[]{:S(2)}) collective-permute-start(bf16[4,96,1536]{2,1,0:T(8,128)(2,1)S(1)} %slice.354.refs_0_), channel_id=1, source_target_pairs={{0,8},{4,12},{8,0},{12,4},{16,24},{20,28},{24,16},{28,20},{1,9},{5... | collective-permute-start | bytes 3538952 | tf_op jit(solution)/shard_map/ppermute | solution.py:430
  168.3 39.6 %collective-permute-start.15 = (bf16[4,96,1536]{2,1,0:T(8,128)(2,1)S(1)}, bf16[4,96,1536]{2,1,0:T(8,128)(2,1)}, u32[]{:S(2)}, u32[]{:S(2)}) collective-permute-start(bf16[4,96,1536]{2,1,0:T(8,128)(2,1)S(1)} %slice.354.refs_0_), channel_id=1, source_target_pairs={{0,16},{4,20},{8,24},{12,28},{16,0},{20,4},{24,8},{28,12},{1,17},{... | collective-permute-start | bytes 3538952 | tf_op jit(solution)/shard_map/ppermute | solution.py:430
  169.9 37.9 %collective-permute-start.12 = (bf16[2,96,1536]{2,1,0:T(8,128)(2,1)}, bf16[2,96,1536]{2,1,0:T(8,128)(2,1)}, u32[]{:S(2)}, u32[]{:S(2)}) collective-permute-start(bf16[2,96,1536]{2,1,0:T(8,128)(2,1)} %slice.352), channel_id=1, source_target_pairs={{0,16},{4,20},{8,24},{12,28},{16,0},{20,4},{24,8},{28,12},{1,17},{... | collective-permute-start | bytes 1769480 | tf_op jit(solution)/shard_map/ppermute | solution.py:430
  172.0 35.8 %collective-permute-start.13 = (bf16[2,96,1536]{2,1,0:T(8,128)(2,1)}, bf16[2,96,1536]{2,1,0:T(8,128)(2,1)}, u32[]{:S(2)}, u32[]{:S(2)}) collective-permute-start(bf16[2,96,1536]{2,1,0:T(8,128)(2,1)} %slice.353), channel_id=1, source_target_pairs={{0,8},{4,12},{8,0},{12,4},{16,24},{20,28},{24,16},{28,20},{1,9},{5... | collective-permute-start | bytes 1769480 | tf_op jit(solution)/shard_map/ppermute | solution.py:430
  218.2 108.8 %all-gather.11.cloned.1.call-start = ((), (), s32[]{:S(2)}) async-start(), calls=%async_computation.17 | async-start | bytes 4423680 | tf_op jit(solution)/shard_map/all_gather | solution.py:856
  258.5 176.1 %reduce-scatter.5.cloned.1.call-start = ((), (), s32[]{:S(2)}) async-start(), calls=%async_computation.11 | async-start | bytes 2949120 | tf_op jit(solution)/shard_map/reduce_scatter | solution.py:933
  387.7 160.4 %reduce-scatter.7.cloned.1.call-start = ((), (), s32[]{:S(2)}) async-start(), calls=%async_computation.12 | async-start | bytes 5898240 | tf_op jit(solution)/shard_map/reduce_scatter | solution.py:950
  462.0 45.7 %all-to-all-start.3 = ((bf16[256,4,384]{2,0,1:T(8,128)(2,1)}), bf16[256,4,384]{2,0,1:T(8,128)(2,1)S(1)}, u32[]{:S(2)}, u32[]{:S(2)}) async-start(bf16[256,4,384]{2,0,1:T(8,128)(2,1)} %bitcast.288), calls=%async_computation.4 | async-start | bytes 1572864 | tf_op jit(solution)/shard_map/all_to_all | solution.py:418
  510.2 37.9 %collective-permute-start.39 = (bf16[2,96,1536]{2,1,0:T(8,128)(2,1)}, bf16[2,96,1536]{2,1,0:T(8,128)(2,1)}, u32[]{:S(2)}, u32[]{:S(2)}) collective-permute-start(bf16[2,96,1536]{2,1,0:T(8,128)(2,1)} %get-tuple-element.398), channel_id=1, source_target_pairs={{0,8},{4,12},{8,0},{12,4},{16,24},{20,28},{24,16},{28,20},{1,9},{5... | collective-permute-start | bytes 1769480 | tf_op jit(solution)/shard_map/ppermute | solution.py:430
  511.4 36.7 %collective-permute-start.40 = (bf16[2,96,1536]{2,1,0:T(8,128)(2,1)}, bf16[2,96,1536]{2,1,0:T(8,128)(2,1)S(1)}, u32[]{:S(2)}, u32[]{:S(2)}) collective-permute-start(bf16[2,96,1536]{2,1,0:T(8,128)(2,1)} %get-tuple-element.397), channel_id=1, source_target_pairs={{0,16},{4,20},{8,24},{12,28},{16,0},{20,4},{24,8},{28,12},{1,17},{... | collective-permute-start | bytes 1769480 | tf_op jit(solution)/shard_map/ppermute | solution.py:430
  513.9 34.1 %collective-permute-start.41 = (bf16[2,96,1536]{2,1,0:T(8,128)(2,1)}, bf16[2,96,1536]{2,1,0:T(8,128)(2,1)}, u32[]{:S(2)}, u32[]{:S(2)}) collective-permute-start(bf16[2,96,1536]{2,1,0:T(8,128)(2,1)} %get-tuple-element.396), channel_id=1, source_target_pairs={{0,8},{4,12},{8,0},{12,4},{16,24},{20,28},{24,16},{28,20},{1,9},{5... | collective-permute-start | bytes 1769480 | tf_op jit(solution)/shard_map/ppermute | solution.py:430
  514.5 33.6 %collective-permute-start.42 = (bf16[2,96,1536]{2,1,0:T(8,128)(2,1)}, bf16[2,96,1536]{2,1,0:T(8,128)(2,1)}, u32[]{:S(2)}, u32[]{:S(2)}) collective-permute-start(bf16[2,96,1536]{2,1,0:T(8,128)(2,1)} %get-tuple-element.395), channel_id=1, source_target_pairs={{0,16},{4,20},{8,24},{12,28},{16,0},{20,4},{24,8},{28,12},{1,17},{... | collective-permute-start | bytes 1769480 | tf_op jit(solution)/shard_map/ppermute | solution.py:430
  558.2 46.9 %collective-permute-start.45 = (bf16[4,96,1536]{2,1,0:T(8,128)(2,1)}, bf16[4,96,1536]{2,1,0:T(8,128)(2,1)}, u32[]{:S(2)}, u32[]{:S(2)}) collective-permute-start(bf16[4,96,1536]{2,1,0:T(8,128)(2,1)} %pad_maximum_fusion.8), channel_id=1, source_target_pairs={{0,16},{4,20},{8,24},{12,28},{16,0},{20,4},{24,8},{28,12},{1,17},{... | collective-permute-start | bytes 3538952 | tf_op jit(solution)/shard_map/ppermute | solution.py:430
  567.3 41.5 %collective-permute-start.43 = (bf16[4,1,4,48,1152]{4,3,2,1,0:T(8,128)(2,1)}, bf16[4,1,4,48,1152]{4,3,2,1,0:T(8,128)(2,1)S(1)}, u32[]{:S(2)}, u32[]{:S(2)}) collective-permute-start(bf16[4,1,4,48,1152]{4,3,2,1,0:T(8,128)(2,1)} %constant_dynamic-slice_fusion.1), channel_id=1, source_target_pairs={{0,4},{4,0},{8,12},{12,8},{16,20},{20,16},{24,28},{28,24},{1,5},{5... | collective-permute-start | bytes 5308424 | tf_op jit(solution)/shard_map/ppermute | solution.py:430
  568.6 40.2 %collective-permute-start.44 = (bf16[4,96,1536]{2,1,0:T(8,128)(2,1)}, bf16[4,96,1536]{2,1,0:T(8,128)(2,1)}, u32[]{:S(2)}, u32[]{:S(2)}) collective-permute-start(bf16[4,96,1536]{2,1,0:T(8,128)(2,1)} %pad_maximum_fusion.7), channel_id=1, source_target_pairs={{0,8},{4,12},{8,0},{12,4},{16,24},{20,28},{24,16},{28,20},{1,9},{5... | collective-permute-start | bytes 3538952 | tf_op jit(solution)/shard_map/ppermute | solution.py:430
  569.4 57.8 %all-to-all-start.4 = ((bf16[8,48,1536]{2,1,0:T(8,128)(2,1)}), bf16[8,48,1536]{2,1,0:T(8,128)(2,1)S(1)}, u32[]{:S(2)}, u32[]{:S(2)}) async-start(bf16[8,48,1536]{2,1,0:T(8,128)(2,1)} %bitcast.301), calls=%async_computation.6 | async-start | bytes 2359296 | tf_op jit(solution)/shard_map/all_to_all | solution.py:1050
  573.0 111.1 %reduce-scatter.9.cloned.1.call-start = ((), (), s32[]{:S(2)}) async-start(), calls=%async_computation.13 | async-start | bytes 3932160 | tf_op jit(solution)/shard_map/reduce_scatter | solution.py:1039
  573.6 123.0 %reduce-scatter.11.cloned.1.call-start = ((), (), s32[]{:S(2)}) async-start(), calls=%async_computation.14 | async-start | bytes 2949120 | tf_op jit(solution)/shard_map/reduce_scatter | solution.py:1049
  (196 other events, 2033.6 us)
Sparse Core Ops, SparseCore 0:
  10.8 113.7 all-gather.6
  126.8 69.1 all-gather.8
  258.7 68.2 all-gather.10
  387.8 46.7 reduce-scatter.4
  436.8 97.3 reduce-scatter.6
  575.9 61.3 reduce-scatter.8
  639.5 56.5 reduce-scatter.10

commit v6 on v5

--- a/solution.py
+++ b/solution.py
@@ -1031,25 +1031,14 @@
     )
     attend_parts = dot(inward_low, inward_own.T)
     attend_low = attend_parts[:row_length].astype(bf16)
-    inward_low, attend_parts, attend_low, halves, half_far, expand_sum = tie(
-        inward_low, attend_parts, attend_low, halves, half_far, expand_sum
+    attend_sum = lax.psum_scatter(attend_low, "seq", scatter_dimension=0, tiled=True)
+    inward_low, attend_parts, halves, half_far, expand_sum = tie(
+        inward_low, attend_parts, halves, half_far, expand_sum
     )
 
     near_early = plane_near(halves[0], half_far[0])
-    attend_sum = lax.psum_scatter(attend_low, "seq", scatter_dimension=0, tiled=True)
     near_late = plane_near(halves[1], half_far[1])
     inward_grad = open_grad(dot(row_low.T, inward_low))
-    inward_grad, attend_parts, near_early, near_late = tie(
-        inward_grad, attend_parts, near_early, near_late
-    )
-
-    whole_column = jnp.concatenate(
-        [plane_total(near_early).astype(bf16), plane_total(near_late).astype(bf16)], axis=1
-    )
-    whole_sums = lax.psum_scatter(whole_column, "seq", scatter_dimension=0)
-    expand_rows = lax.all_to_all(expand_sum, "dp", 0, 0, tiled=True)
-    inward_blocks = side_blocks([inward_grad])
-    inward_far = plane_far(inward_blocks)
     token_term, token_gain_part = norm_backward(
         attend_parts[row_length : row_length + CLIPS], token_norm, token_inverse, attend_gain
     )
@@ -1068,14 +1057,28 @@
     )
     small = jnp.pad(small, ((0, 0), (0, -small.shape[1] % 2048)))
     small = small.reshape(device_count, -1, 128)
-    inward_far, fed_got, fed_same, small, expand_rows = tie(
-        inward_far, fed_got, fed_same, small, expand_rows
+    inward_grad, small, near_early, near_late, attend_sum = tie(
+        inward_grad, small, near_early, near_late, attend_sum
+    )
+
+    whole_column = jnp.concatenate(
+        [plane_total(near_early).astype(bf16), plane_total(near_late).astype(bf16)], axis=1
+    )
+    whole_sums = lax.psum_scatter(whole_column, "seq", scatter_dimension=0)
+    expand_rows = lax.all_to_all(expand_sum, "dp", 0, 0, tiled=True)
+    inward_blocks = side_blocks([inward_grad])
+    inward_far = plane_far(inward_blocks)
+    inward_blocks, inward_far, small, expand_rows = tie(
+        inward_blocks, inward_far, small, expand_rows
     )
 
     inward_near = plane_near(inward_blocks, inward_far)
+    small_all = lax.all_to_all(small, ("dp", "seq"), 0, 0, tiled=True).astype(f32)
     fed_blocks = [fed_same[r].astype(f32) + fed_got[r].astype(f32) for r in range(chips)]
     fed_far = plane_far(fed_blocks)
-    inward_near, fed_far = tie(inward_near, fed_far)
+    inward_near, small_all, fed_far, attend_sum = tie(
+        inward_near, small_all, fed_far, attend_sum
+    )
 
     inward_rows = line_swap(plane_total(inward_near).astype(bf16))
     fed_near = plane_near(fed_blocks, fed_far)
@@ -1085,11 +1088,10 @@
         .reshape(shard, 2 * FF)
         .astype(f32)
     )
-    inward_rows, fed_near, grad_expand, attend_sum, small = tie(
-        inward_rows, fed_near, grad_expand, attend_sum, small
-    )
-
-    small_all = lax.all_to_all(small, ("dp", "seq"), 0, 0, tiled=True).astype(f32)
+    inward_rows, fed_near, grad_expand, whole_sums = tie(
+        inward_rows, fed_near, grad_expand, whole_sums
+    )
+
     block_output = (after_cross + plane_total(fed_near)).astype(bf16)
     own_norm = lax.dynamic_slice_in_dim(row_norm, seq_place * frame_count, frame_count, axis=0)
     own_inverse = lax.dynamic_slice_in_dim(

time: 724 us -> 719 us (level)
  waiting for transfers between devices: 226 us -> 209 us
  local copies, waits for them, and re-layouts: 84.9 us -> 94.7 us
    all_to_all x4, waiting for transfers between devices: 68.9 us -> 52.7 us  [line_swap(): return lax.all_to_all(blocks, 'seq', split, join, tiled=True)]
    unnamed x315 -> x345, local copies, waits for them, and re-layouts: 38.6 us -> 39.4 us
  transfers between devices with their start and end apart: 70 -> 70, of which waited for: 29 -> 27; matrix products, arithmetic and copies ran while one was open for 29% -> 31% of each run, Pallas kernels for 15% -> 15%
where the time goes in v6:
time: 719 us; the launch traced here: 709 us
  waiting for transfers between devices  209 us (29%)
  matrix products  116 us (16%)
  Pallas kernels  114 us (16%)
  local copies, waits for them, and re-layouts  94.7 us (13%)
  starting transfers between devices  80.2 us (11%)
  other arithmetic  77.3 us (11%)
  between operations  17.1 us (2%)
    ppermute x56, waiting for transfers between devices, flip(): return lax.ppermute(values, 'dp', xor_pairs(lax.axis_size('dp'), bit))  144 us
    dot_general x25, matrix products, dot(): return jnp.dot(left, right, preferred_element_type=jnp.float32)  115 us
    all_to_all x4, waiting for transfers between devices, line_swap(): return lax.all_to_all(blocks, 'seq', split, join, tiled=True)  52.7 us
    ppermute x56, starting transfers between devices, flip(): return lax.ppermute(values, 'dp', xor_pairs(lax.axis_size('dp'), bit))  50.1 us
    unnamed x345, local copies, waits for them, and re-layouts  39.4 us
    pallas_call x9, Pallas kernels, assemble(): pl.pallas_call(kernel, in_specs=[pl.BlockSpec(memory_space=pltpu.SMEM)] +...  35 us
    pallas_call x1, Pallas kernels, self_backward(): pl.pallas_call(self_backward_kernel, grid=(pairs,), in_specs=[lanes(total...  21.2 us
    pallas_call x1, Pallas kernels, self_forward(): pl.pallas_call(self_forward_kernel, grid=(pairs,), in_specs=[lanes(total,...  19.1 us
  transfers between devices with their start and end apart: 70, of which 27 were waited for; matrix products, arithmetic and copies ran while one was open for 31% of the time, Pallas kernels for 15%

profile of v6, /device:TPU:0, one launch (start us, length us, event | category | flops | bytes accessed | tf_op | source)
XLA Modules:
  0.0 709.3 jit_solution(2201569371198467325)
XLA Ops:
  33.4 19.1 %all-to-all-done.refs_0_ = bf16[4,64,1152]{2,1,0:T(8,128)(2,1)S(1)} async-done(((bf16[4,64,1152]{2,1,0:T(8,128)(2,1)}), bf16[4,64,1152]{2,1,0:T(8,128)(2,1)S(1)}, u32[]{:S(2)}, u32[]{:S(2)}) %all-to-all-start) | async-done | bytes 589856 | tf_op jit(solution)/shard_map/all_to_all | solution.py:418
  63.5 27.1 %collective-permute-done.refs_1_ = bf16[4,64,1152]{2,1,0:T(8,128)(2,1)S(1)} collective-permute-done((bf16[4,64,1152]{2,1,0:T(8,128)(2,1)S(1)}, bf16[4,64,1152]{2,1,0:T(8,128)(2,1)S(1)}, u32[]{:S(2)}, u32[]{:S(2)}) %collective-permute-start) | collective-permute-done | bytes 589856 | tf_op jit(solution)/shard_map/ppermute | solution.py:430
  98.6 8.4 %collective-permute-done.4.refs_3_ = bf16[2,64,1152]{2,1,0:T(8,128)(2,1)S(1)} collective-permute-done((bf16[2,64,1152]{2,1,0:T(8,128)(2,1)S(1)}, bf16[2,64,1152]{2,1,0:T(8,128)(2,1)S(1)}, u32[]{:S(2)}, u32[]{:S(2)}) %collective-permute-start.4) | collective-permute-done | bytes 294944 | tf_op jit(solution)/shard_map/ppermute | solution.py:430
  145.3 7.0 fusion.9.projected
  152.4 13.9 %collective-permute-done.10.refs_1_ = bf16[4,96,1536]{2,1,0:T(8,128)(2,1)S(1)} collective-permute-done((bf16[4,96,1536]{2,1,0:T(8,128)(2,1)S(1)}, bf16[4,96,1536]{2,1,0:T(8,128)(2,1)S(1)}, u32[]{:S(2)}, u32[]{:S(2)}) %collective-permute-start.10) | collective-permute-done | bytes 1179680 | tf_op jit(solution)/shard_map/ppermute | solution.py:430
  172.8 19.1 %shard_map.258 = (bf16[1024,384]{1,0:T(8,128)(2,1)S(1)}, f32[1024,384]{1,0:T(8,128)S(1)}, f32[1024,384]{1,0:T(8,128)S(1)}, bf16[1152,1152]{1,0:T(8,128)(2,1)}) custom-call(f32[1152,1152]{1,0:T(8,128)} %fusion.9.projected, f32[1152,128]{1,0:T(8,128)S(1)} %copy-done.19, f32[1152,128]{1,0:T(8,128)S(1)} %copy-done.17, f32[1152,1]{1,0:T(8,128)S(1)} %copy-done.21), custom_call_target="tpu_custom_call" | custom-call | flops 120000004096 | bytes 1048576 | tf_op jit(solution)/shard_map/pallas_call | solution.py:242
  196.0 11.8 %collective-permute-done.12.refs_3_ = bf16[2,96,1536]{2,1,0:T(8,128)(2,1)} collective-permute-done((bf16[2,96,1536]{2,1,0:T(8,128)(2,1)}, bf16[2,96,1536]{2,1,0:T(8,128)(2,1)}, u32[]{:S(2)}, u32[]{:S(2)}) %collective-permute-start.12) | collective-permute-done | bytes 589856 | tf_op jit(solution)/shard_map/ppermute | solution.py:430
  223.2 16.0 %all-to-all-done.2 = bf16[4,256,384]{2,1,0:T(8,128)(2,1)S(1)} async-done(((bf16[4,256,384]{2,1,0:T(8,128)(2,1)}), bf16[4,256,384]{2,1,0:T(8,128)(2,1)S(1)}, u32[]{:S(2)}, u32[]{:S(2)}) %all-to-all-start.2) | async-done | bytes 786464 | tf_op jit(solution)/shard_map/all_to_all | solution.py:418
  262.4 7.2 %shard_map.262 = (bf16[4,2,4,48,1536]{4,3,2,1,0:T(8,128)(2,1)S(1)}, bf16[4,2,4,48,1536]{4,3,2,1,0:T(8,128)(2,1)}) custom-call(s32[1]{0:T(128)} %bitcast.10.places_ref, bf16[4,4,96,1536]{3,2,1,0:T(8,128)(2,1)} %shard_map.261.refs_0_, bf16[4,4,96,1536]{3,2,1,0:T(8,128)(2,1)} %collective-permute-done.19.refs_1_), custom_call_target="tpu_custom_call" | custom-call | bytes 18874368 | tf_op jit(solution)/shard_map/pallas_call | solution.py:455
  269.6 7.4 %convolution_convert_fusion.5.keys.values = bf16[768,1536]{1,0:T(8,128)(2,1)} fusion(bf16[768,1536]{1,0:T(8,128)(2,1)} %pad_maximum_fusion.3.refs_2_, bf16[1536,1536]{1,0:T(8,128)(2,1)S(1)} %bitcast.254), kind=kOutput, calls=%fused_computation.18 | convolution fusion | flops 3625058304 | bytes 9437184 | tf_op jit(solution)/shard_map/dot_general | solution.py:422
  277.1 10.6 %shard_map.263 = (bf16[256,1536]{1,0:T(8,128)(2,1)}, f32[256,1536]{1,0:T(8,128)S(1)}, f32[256,1536]{1,0:T(8,128)S(1)}) custom-call(bf16[256,1536]{1,0:T(8,128)(2,1)S(1)} %convolution_convert_fusion.8.query, bf16[768,1536]{1,0:T(8,128)(2,1)} %convolution_convert_fusion.5.keys.values, bf16[768,1536]{1,0:T(8,128)(2,1)} %convolution_convert_fusion.5.keys.values, ...), custom_call_target="tpu_custom_call" | custom-call | flops 20000000000 | bytes 1048576 | tf_op jit(solution)/shard_map/pallas_call | solution.py:301
  294.3 17.6 %collective-permute-done.23.refs_1_ = bf16[256,1536]{1,0:T(8,128)(2,1)S(1)} collective-permute-done((bf16[256,1536]{1,0:T(8,128)(2,1)S(1)}, bf16[256,1536]{1,0:T(8,128)(2,1)S(1)}, u32[]{:S(2)}, u32[]{:S(2)}) %collective-permute-start.23) | collective-permute-done | bytes 786464 | tf_op jit(solution)/shard_map/ppermute | solution.py:430
  314.2 8.4 %collective-permute-done.25.refs_3_ = bf16[128,1536]{1,0:T(8,128)(2,1)S(1)} collective-permute-done((bf16[128,1536]{1,0:T(8,128)(2,1)S(1)}, bf16[128,1536]{1,0:T(8,128)(2,1)S(1)}, u32[]{:S(2)}, u32[]{:S(2)}) %collective-permute-start.25) | collective-permute-done | bytes 393248 | tf_op jit(solution)/shard_map/ppermute | solution.py:430
  332.1 7.8 %fusion.67 = f32[1024,1536]{1,0:T(8,128)S(1)} fusion(bf16[1024,1536]{1,0:T(8,128)(2,1)S(1)} %bitcast.281, bf16[1536,1536]{1,0:T(8,128)(2,1)} %bitcast.317), kind=kOutput, calls=%fused_computation.250 | convolution fusion | flops 4831838208 | bytes 14155776 | tf_op jit(solution)/shard_map/dot_general | solution.py:422
  366.3 7.8 %convolution_convert_fusion.3 = bf16[1024,1536]{1,0:T(8,128)(2,1)S(1)} fusion(bf16[1024,1536]{1,0:T(8,128)(2,1)S(1)} %pad_maximum_fusion.2, bf16[1536,1536]{1,0:T(8,128)(2,1)} %bitcast.318), kind=kOutput, calls=%fused_computation.15 | convolution fusion | flops 4833411072 | bytes 11010048 | tf_op jit(solution)/shard_map/dot_general | solution.py:422
  374.6 9.0 %convolution_convert_fusion.4 = bf16[1024,1536]{1,0:T(8,128)(2,1)} fusion(bf16[1024,1536]{1,0:T(8,128)(2,1)S(1)} %copy-done.82, bf16[1536,1536]{1,0:T(8,128)(2,1)} %bitcast.319), kind=kOutput, calls=%fused_computation.16 | convolution fusion | flops 4833411072 | bytes 11010048 | tf_op jit(solution)/shard_map/dot_general | solution.py:422
  435.3 11.0 %shard_map.266 = (bf16[256,1536]{1,0:T(8,128)(2,1)S(1)}, bf16[384,1536]{1,0:T(8,128)(2,1)S(1)}, bf16[384,1536]{1,0:T(8,128)(2,1)S(1)}) custom-call(bf16[256,1536]{1,0:T(8,128)(2,1)S(1)} %copy-done.51, bf16[768,1536]{1,0:T(8,128)(2,1)} %convolution_convert_fusion.5.keys.values, bf16[768,1536]{1,0:T(8,128)(2,1)} %convolution_convert_fusion.5.keys.values, ...), custom_call_target="tpu_custom_call" | custom-call | flops 120000004096 | bytes 1048576 | tf_op jit(solution)/shard_map/pallas_call | solution.py:327
  472.9 15.3 %shard_map.267 = (bf16[4,4,96,1536]{3,2,1,0:T(8,128)(2,1)}, bf16[4,4,96,1536]{3,2,1,0:T(8,128)(2,1)}) custom-call(s32[2]{0:T(128)S(1)} %pad_add_fusion.1.places, bf16[256,1536]{1,0:T(8,128)(2,1)} %get-tuple-element.243.refs_0_, bf16[256,1536]{1,0:T(8,128)(2,1)} %collective-permute-done.27.refs_1_, bf16[768,1536]{1,0:T(8,128)(2,1)} %pad_maximum_fusion.3.refs_2_, ...), custom_call_target="tpu_custom_call" | custom-call | flops 100000000 | bytes 1048576 | tf_op jit(solution)/shard_map/pallas_call | solution.py:642
  495.4 17.7 %all-to-all-done.3 = bf16[256,4,384]{2,0,1:T(8,128)(2,1)S(1)} async-done(((bf16[256,4,384]{2,0,1:T(8,128)(2,1)}), bf16[256,4,384]{2,0,1:T(8,128)(2,1)S(1)}, u32[]{:S(2)}, u32[]{:S(2)}) %all-to-all-start.3) | async-done | bytes 786464 | tf_op jit(solution)/shard_map/all_to_all | solution.py:418
  520.8 21.2 %shard_map.268 = bf16[1152,1152]{1,0:T(8,128)(2,1)} custom-call(bf16[1152,1152]{1,0:T(8,128)(2,1)} %get-tuple-element.209.low, bf16[1024,384]{1,0:T(8,128)(2,1)S(1)} %bitcast.248, f32[1024,384]{1,0:T(8,128)S(1)} %copy-done.26, f32[1024,384]{1,0:T(8,128)S(1)} %copy-done.28, f32[1152,128]{1,0:T(8,128)S(1)} %copy-done.20, f32[1152,128]{1,0:T(8,128)S(1)} %copy-done.18, ...), custom_call_target="tpu_custom_call" | custom-call | flops 2000000000 | bytes 1048576 | tf_op jit(solution)/shard_map/pallas_call | solution.py:272
  542.0 6.6 fusion.71
  591.2 20.7 %collective-permute-done.45 = bf16[4,96,1536]{2,1,0:T(8,128)(2,1)} collective-permute-done((bf16[4,96,1536]{2,1,0:T(8,128)(2,1)}, bf16[4,96,1536]{2,1,0:T(8,128)(2,1)}, u32[]{:S(2)}, u32[]{:S(2)}) %collective-permute-start.45) | collective-permute-done | bytes 1179680 | tf_op jit(solution)/shard_map/ppermute | solution.py:430
  628.5 10.7 %collective-permute-done.48 = bf16[2,48,1152]{2,1,0:T(8,128)(2,1)S(1)} collective-permute-done((bf16[2,48,1152]{2,1,0:T(8,128)(2,1)S(1)}, bf16[2,48,1152]{2,1,0:T(8,128)(2,1)S(1)}, u32[]{:S(2)}, u32[]{:S(2)}) %collective-permute-start.48) | collective-permute-done | bytes 221216 | tf_op jit(solution)/shard_map/ppermute | solution.py:430
  656.4 10.0 %all-to-all-done.5 = bf16[32,48,128]{2,1,0:T(8,128)(2,1)} async-done(((bf16[32,48,128]{2,1,0:T(8,128)(2,1)}), bf16[32,48,128]{2,1,0:T(8,128)(2,1)}, u32[]{:S(2)}, u32[]{:S(2)}) %all-to-all-start.5) | async-done | bytes 393248 | tf_op jit(solution)/shard_map/all_to_all | solution.py:1076
  (695 shorter events, 380.9 us)
Async XLA Ops:
  7.2 126.6 %all-gather.7.cloned.1.call-start = ((), (), s32[]{:S(2)}) async-start(), calls=%async_computation.15 | async-start | bytes 6881280 | tf_op jit(solution)/shard_map/all_gather | solution.py:774
  13.2 39.3 %all-to-all-start = ((bf16[4,64,1152]{2,1,0:T(8,128)(2,1)}), bf16[4,64,1152]{2,1,0:T(8,128)(2,1)S(1)}, u32[]{:S(2)}, u32[]{:S(2)}) async-start(bf16[4,64,1152]{2,1,0:T(8,128)(2,1)} %pad_maximum_fusion.16), calls=%async_computation | async-start | bytes 1179648 | tf_op jit(solution)/shard_map/all_to_all | solution.py:418
  52.5 39.2 %collective-permute-start.2 = (bf16[256,1536]{1,0:T(8,128)(2,1)S(1)}, bf16[256,1536]{1,0:T(8,128)(2,1)S(1)}, u32[]{:S(2)}, u32[]{:S(2)}) collective-permute-start(bf16[256,1536]{1,0:T(8,128)(2,1)S(1)} %bitcast.245), channel_id=1, source_target_pairs={{0,8},{4,12},{8,0},{12,4},{16,24},{20,28},{24,16},{28,20},{1,9},{5... | collective-permute-start | bytes 2359304 | tf_op jit(solution)/shard_map/ppermute | solution.py:430
  54.0 37.7 %collective-permute-start.3 = (bf16[256,1536]{1,0:T(8,128)(2,1)S(1)}, bf16[256,1536]{1,0:T(8,128)(2,1)}, u32[]{:S(2)}, u32[]{:S(2)}) collective-permute-start(bf16[256,1536]{1,0:T(8,128)(2,1)S(1)} %bitcast.246), channel_id=1, source_target_pairs={{0,16},{4,20},{8,24},{12,28},{16,0},{20,4},{24,8},{28,12},{1,17},{... | collective-permute-start | bytes 2359304 | tf_op jit(solution)/shard_map/ppermute | solution.py:430
  55.5 60.8 %all-to-all-start.1 = ((bf16[8,48,1536]{2,1,0:T(8,128)(2,1)}), bf16[8,48,1536]{2,1,0:T(8,128)(2,1)}, u32[]{:S(2)}, u32[]{:S(2)}) async-start(bf16[8,48,1536]{2,1,0:T(8,128)(2,1)} %reshape.519), calls=%async_computation.1 | async-start | bytes 2359296 | tf_op jit(solution)/shard_map/all_to_all | solution.py:786
  59.8 136.2 %all-gather.9.cloned.1.call-start = ((), (), s32[]{:S(2)}) async-start(), calls=%async_computation.16 | async-start | bytes 4423680 | tf_op jit(solution)/shard_map/all_gather | solution.py:822
  166.9 40.8 %collective-permute-start.14 = (bf16[4,96,1536]{2,1,0:T(8,128)(2,1)S(1)}, bf16[4,96,1536]{2,1,0:T(8,128)(2,1)S(1)}, u32[]{:S(2)}, u32[]{:S(2)}) collective-permute-start(bf16[4,96,1536]{2,1,0:T(8,128)(2,1)S(1)} %slice.346.refs_0_), channel_id=1, source_target_pairs={{0,8},{4,12},{8,0},{12,4},{16,24},{20,28},{24,16},{28,20},{1,9},{5... | collective-permute-start | bytes 3538952 | tf_op jit(solution)/shard_map/ppermute | solution.py:430
  168.2 39.6 %collective-permute-start.15 = (bf16[4,96,1536]{2,1,0:T(8,128)(2,1)S(1)}, bf16[4,96,1536]{2,1,0:T(8,128)(2,1)}, u32[]{:S(2)}, u32[]{:S(2)}) collective-permute-start(bf16[4,96,1536]{2,1,0:T(8,128)(2,1)S(1)} %slice.346.refs_0_), channel_id=1, source_target_pairs={{0,16},{4,20},{8,24},{12,28},{16,0},{20,4},{24,8},{28,12},{1,17},{... | collective-permute-start | bytes 3538952 | tf_op jit(solution)/shard_map/ppermute | solution.py:430
  169.9 37.9 %collective-permute-start.12 = (bf16[2,96,1536]{2,1,0:T(8,128)(2,1)}, bf16[2,96,1536]{2,1,0:T(8,128)(2,1)}, u32[]{:S(2)}, u32[]{:S(2)}) collective-permute-start(bf16[2,96,1536]{2,1,0:T(8,128)(2,1)} %slice.344), channel_id=1, source_target_pairs={{0,16},{4,20},{8,24},{12,28},{16,0},{20,4},{24,8},{28,12},{1,17},{... | collective-permute-start | bytes 1769480 | tf_op jit(solution)/shard_map/ppermute | solution.py:430
  172.0 35.8 %collective-permute-start.13 = (bf16[2,96,1536]{2,1,0:T(8,128)(2,1)}, bf16[2,96,1536]{2,1,0:T(8,128)(2,1)}, u32[]{:S(2)}, u32[]{:S(2)}) collective-permute-start(bf16[2,96,1536]{2,1,0:T(8,128)(2,1)} %slice.345), channel_id=1, source_target_pairs={{0,8},{4,12},{8,0},{12,4},{16,24},{20,28},{24,16},{28,20},{1,9},{5... | collective-permute-start | bytes 1769480 | tf_op jit(solution)/shard_map/ppermute | solution.py:430
  218.2 108.9 %all-gather.11.cloned.1.call-start = ((), (), s32[]{:S(2)}) async-start(), calls=%async_computation.17 | async-start | bytes 4423680 | tf_op jit(solution)/shard_map/all_gather | solution.py:856
  258.6 176.7 %reduce-scatter.5.cloned.1.call-start = ((), (), s32[]{:S(2)}) async-start(), calls=%async_computation.11 | async-start | bytes 2949120 | tf_op jit(solution)/shard_map/reduce_scatter | solution.py:933
  387.7 166.0 %reduce-scatter.7.cloned.1.call-start = ((), (), s32[]{:S(2)}) async-start(), calls=%async_computation.12 | async-start | bytes 5898240 | tf_op jit(solution)/shard_map/reduce_scatter | solution.py:950
  467.0 46.0 %all-to-all-start.3 = ((bf16[256,4,384]{2,0,1:T(8,128)(2,1)}), bf16[256,4,384]{2,0,1:T(8,128)(2,1)S(1)}, u32[]{:S(2)}, u32[]{:S(2)}) async-start(bf16[256,4,384]{2,0,1:T(8,128)(2,1)} %bitcast.283), calls=%async_computation.4 | async-start | bytes 1572864 | tf_op jit(solution)/shard_map/all_to_all | solution.py:418
  470.6 145.2 %reduce-scatter.9.cloned.1.call-start = ((), (), s32[]{:S(2)}) async-start(), calls=%async_computation.13 | async-start | bytes 3932160 | tf_op jit(solution)/shard_map/reduce_scatter | solution.py:1034
  515.5 38.1 %collective-permute-start.39 = (bf16[2,96,1536]{2,1,0:T(8,128)(2,1)}, bf16[2,96,1536]{2,1,0:T(8,128)(2,1)}, u32[]{:S(2)}, u32[]{:S(2)}) collective-permute-start(bf16[2,96,1536]{2,1,0:T(8,128)(2,1)} %get-tuple-element.402), channel_id=1, source_target_pairs={{0,8},{4,12},{8,0},{12,4},{16,24},{20,28},{24,16},{28,20},{1,9},{5... | collective-permute-start | bytes 1769480 | tf_op jit(solution)/shard_map/ppermute | solution.py:430
  516.9 36.8 %collective-permute-start.40 = (bf16[2,96,1536]{2,1,0:T(8,128)(2,1)}, bf16[2,96,1536]{2,1,0:T(8,128)(2,1)S(1)}, u32[]{:S(2)}, u32[]{:S(2)}) collective-permute-start(bf16[2,96,1536]{2,1,0:T(8,128)(2,1)} %get-tuple-element.401), channel_id=1, source_target_pairs={{0,16},{4,20},{8,24},{12,28},{16,0},{20,4},{24,8},{28,12},{1,17},{... | collective-permute-start | bytes 1769480 | tf_op jit(solution)/shard_map/ppermute | solution.py:430
  565.2 46.7 %collective-permute-start.45 = (bf16[4,96,1536]{2,1,0:T(8,128)(2,1)}, bf16[4,96,1536]{2,1,0:T(8,128)(2,1)}, u32[]{:S(2)}, u32[]{:S(2)}) collective-permute-start(bf16[4,96,1536]{2,1,0:T(8,128)(2,1)} %pad_maximum_fusion.8), channel_id=1, source_target_pairs={{0,16},{4,20},{8,24},{12,28},{16,0},{20,4},{24,8},{28,12},{1,17},{... | collective-permute-start | bytes 3538952 | tf_op jit(solution)/shard_map/ppermute | solution.py:430
  567.1 48.6 %collective-permute-start.44 = (bf16[4,96,1536]{2,1,0:T(8,128)(2,1)}, bf16[4,96,1536]{2,1,0:T(8,128)(2,1)}, u32[]{:S(2)}, u32[]{:S(2)}) collective-permute-start(bf16[4,96,1536]{2,1,0:T(8,128)(2,1)} %pad_maximum_fusion.7), channel_id=1, source_target_pairs={{0,8},{4,12},{8,0},{12,4},{16,24},{20,28},{24,16},{28,20},{1,9},{5... | collective-permute-start | bytes 3538952 | tf_op jit(solution)/shard_map/ppermute | solution.py:430
  576.1 39.6 %collective-permute-start.43 = (bf16[4,1,4,48,1152]{4,3,2,1,0:T(8,128)(2,1)}, bf16[4,1,4,48,1152]{4,3,2,1,0:T(8,128)(2,1)S(1)}, u32[]{:S(2)}, u32[]{:S(2)}) collective-permute-start(bf16[4,1,4,48,1152]{4,3,2,1,0:T(8,128)(2,1)} %constant_dynamic-slice_fusion.1), channel_id=1, source_target_pairs={{0,4},{4,0},{8,12},{12,8},{16,20},{20,16},{24,28},{28,24},{1,5},{5... | collective-permute-start | bytes 5308424 | tf_op jit(solution)/shard_map/ppermute | solution.py:430
  579.0 49.5 %all-to-all-start.4 = ((bf16[8,48,1536]{2,1,0:T(8,128)(2,1)}), bf16[8,48,1536]{2,1,0:T(8,128)(2,1)S(1)}, u32[]{:S(2)}, u32[]{:S(2)}) async-start(bf16[8,48,1536]{2,1,0:T(8,128)(2,1)} %bitcast.296), calls=%async_computation.7 | async-start | bytes 2359296 | tf_op jit(solution)/shard_map/all_to_all | solution.py:1068
  582.6 112.4 %reduce-scatter.11.cloned.1.call-start = ((), (), s32[]{:S(2)}) async-start(), calls=%async_computation.14 | async-start | bytes 2949120 | tf_op jit(solution)/shard_map/reduce_scatter | solution.py:1067
  586.6 80.9 %collective-permute-start.52 = (bf16[128,1536]{1,0:T(8,128)(2,1)}, bf16[128,1536]{1,0:T(8,128)(2,1)}, u32[]{:S(2)}, u32[]{:S(2)}) collective-permute-start(bf16[128,1536]{1,0:T(8,128)(2,1)} %get-tuple-element.404), channel_id=1, source_target_pairs={{0,8},{4,12},{8,0},{12,4},{16,24},{20,28},{24,16},{28,20},{1,9},{5... | collective-permute-start | bytes 1179656 | tf_op jit(solution)/shard_map/ppermute | solution.py:430
  590.4 77.1 %collective-permute-start.53 = (bf16[128,1536]{1,0:T(8,128)(2,1)}, bf16[128,1536]{1,0:T(8,128)(2,1)}, u32[]{:S(2)}, u32[]{:S(2)}) collective-permute-start(bf16[128,1536]{1,0:T(8,128)(2,1)} %get-tuple-element.403), channel_id=1, source_target_pairs={{0,16},{4,20},{8,24},{12,28},{16,0},{20,4},{24,8},{28,12},{1,17},{... | collective-permute-start | bytes 1179656 | tf_op jit(solution)/shard_map/ppermute | solution.py:430
  (212 other events, 2053.7 us)
Sparse Core Ops, SparseCore 0:
  10.8 113.7 all-gather.6
  126.8 69.1 all-gather.8
  258.7 68.2 all-gather.10
  387.8 46.7 reduce-scatter.4
  436.8 97.4 reduce-scatter.6
  553.8 61.1 reduce-scatter.8
  628.4 54.2 reduce-scatter.10

commit v7 on v6

--- a/solution.py
+++ b/solution.py
@@ -885,30 +885,43 @@
     norm_three, inverse_three = norm_forward(after_cross)
     normed_three = (norm_three * feed_gain).astype(bf16)
     crossed_other = flip(crossed, 1)
+    normed_three, ffn_early, cotangent_same, cotangent_other = tie(
+        normed_three, ffn_early, cotangent_same, cotangent_other
+    )
     frames_state = plane_relay(plane_open(normed_three))
+    half_frames = chips * frame_count
+    tangents = [cotangent_same.reshape(half_frames, D), cotangent_other.reshape(half_frames, D)]
+    shrink_own = ffn_early
+    if joined:
+        shrink_own = assemble(
+            [ffn_early],
+            [(seq_count, hidden_width // seq_count, D)],
+            [(0, at(slice(None), pl.ds(0, hidden_width // seq_count)), 0, everything)],
+            jnp.zeros((1,), jnp.int32),
+        )[0]
+    shrink_own = shrink_own.reshape(hidden_width, D)
+    hidden_grads = [dot(side, shrink_own.T) for side in tangents]
     frames_same = plane_chips(frames_state)
-    frames_same, expand_lined, crossed_other = tie(frames_same, expand_lined, crossed_other)
+    frames_same, expand_lined, crossed_other, hidden_grads = tie(
+        frames_same, expand_lined, crossed_other, hidden_grads
+    )
 
     if joined:
-        moves = [(0, at(slice(None), pl.ds(0, hidden_width // seq_count)), 1, everything)]
+        moves = []
         for line in range(seq_count):
             target = at(pl.ds(early_parts, dp_count - early_parts), line)
             moves.append((1, at(line), 0, target))
             for part in range(early_parts):
                 rows = pl.ds(hidden_width // seq_count + part * shard, shard)
                 moves.append((0, at(line, rows), 0, at(part, line)))
-        expand_own, shrink_own = assemble(
+        expand_own = assemble(
             [ffn_early, expand_lined],
-            [
-                (dp_count, seq_count, shard, 2 * hidden_width),
-                (seq_count, hidden_width // seq_count, D),
-            ],
+            [(dp_count, seq_count, shard, 2 * hidden_width)],
             moves,
             jnp.zeros((1,), jnp.int32),
-        )
+        )[0]
     else:
-        expand_own, shrink_own = expand_lined.transpose(1, 0, 2, 3), ffn_early
-    shrink_own = shrink_own.reshape(hidden_width, D)
+        expand_own = expand_lined.transpose(1, 0, 2, 3)
     expand_own = expand_own.reshape(D, 2 * hidden_width)
     half_frames = chips * frame_count
     frames_other = flip(frames_same, 1)
@@ -920,7 +933,7 @@
         gate_part = gate_up[:, :hidden_width]
         upward = gate_up[:, hidden_width:]
         hidden_low.append((jax.nn.silu(gate_part) * upward).astype(bf16))
-        hidden_grad = dot(tangents[side], shrink_own.T)
+        hidden_grad = hidden_grads[side]
         expand_low.append(gated_back(hidden_grad, gate_part, upward))
 
     def sides(array):

time: 719 us -> 713 us (level)
  waiting for transfers between devices: 209 us -> 197 us
    ppermute x56, waiting for transfers between devices: 144 us -> 132 us  [flip(): return lax.ppermute(values, 'dp', xor_pairs(lax.axis_size('dp'), bit))]
    unnamed x345 -> x351, local copies, waits for them, and re-layouts: 39.4 us -> 42.2 us
    pallas_call x9 -> x10, Pallas kernels: 35 us -> 34.9 us  [assemble(): pl.pallas_call(kernel, in_specs=[pl.BlockSpec(memory_space=pltpu.SMEM)] +...]
  transfers between devices with their start and end apart: 70 -> 70, of which waited for: 27 -> 28; matrix products, arithmetic and copies ran while one was open for 31% -> 32% of each run, Pallas kernels for 15% -> 15%
where the time goes in v7:
time: 713 us; the launch traced here: 704 us
  waiting for transfers between devices  197 us (28%)
  matrix products  117 us (16%)
  Pallas kernels  115 us (16%)
  local copies, waits for them, and re-layouts  97.4 us (14%)
  other arithmetic  81.6 us (11%)
  starting transfers between devices  79.6 us (11%)
  between operations  16.9 us (2%)
    ppermute x56, waiting for transfers between devices, flip(): return lax.ppermute(values, 'dp', xor_pairs(lax.axis_size('dp'), bit))  132 us
    dot_general x25, matrix products, dot(): return jnp.dot(left, right, preferred_element_type=jnp.float32)  115 us
    all_to_all x4, waiting for transfers between devices, line_swap(): return lax.all_to_all(blocks, 'seq', split, join, tiled=True)  53 us
    ppermute x56, starting transfers between devices, flip(): return lax.ppermute(values, 'dp', xor_pairs(lax.axis_size('dp'), bit))  49.6 us
    unnamed x351, local copies, waits for them, and re-layouts  42.2 us
    pallas_call x10, Pallas kernels, assemble(): pl.pallas_call(kernel, in_specs=[pl.BlockSpec(memory_space=pltpu.SMEM)] +...  34.9 us
    pallas_call x1, Pallas kernels, self_backward(): pl.pallas_call(self_backward_kernel, grid=(pairs,), in_specs=[lanes(total...  21.4 us
    pallas_call x1, Pallas kernels, self_forward(): pl.pallas_call(self_forward_kernel, grid=(pairs,), in_specs=[lanes(total,...  19.4 us
  transfers between devices with their start and end apart: 70, of which 28 were waited for; matrix products, arithmetic and copies ran while one was open for 32% of the time, Pallas kernels for 15%

profile of v7, /device:TPU:0, one launch (start us, length us, event | category | flops | bytes accessed | tf_op | source)
XLA Modules:
  0.0 704.1 jit_solution(11011368709615679443)
XLA Ops:
  33.4 19.1 %all-to-all-done.refs_0_ = bf16[4,64,1152]{2,1,0:T(8,128)(2,1)S(1)} async-done(((bf16[4,64,1152]{2,1,0:T(8,128)(2,1)}), bf16[4,64,1152]{2,1,0:T(8,128)(2,1)S(1)}, u32[]{:S(2)}, u32[]{:S(2)}) %all-to-all-start) | async-done | bytes 589856 | tf_op jit(solution)/shard_map/all_to_all | solution.py:418
  63.6 27.0 %collective-permute-done.refs_1_ = bf16[4,64,1152]{2,1,0:T(8,128)(2,1)S(1)} collective-permute-done((bf16[4,64,1152]{2,1,0:T(8,128)(2,1)S(1)}, bf16[4,64,1152]{2,1,0:T(8,128)(2,1)S(1)}, u32[]{:S(2)}, u32[]{:S(2)}) %collective-permute-start) | collective-permute-done | bytes 589856 | tf_op jit(solution)/shard_map/ppermute | solution.py:430
  98.6 8.3 %collective-permute-done.4.refs_3_ = bf16[2,64,1152]{2,1,0:T(8,128)(2,1)S(1)} collective-permute-done((bf16[2,64,1152]{2,1,0:T(8,128)(2,1)S(1)}, bf16[2,64,1152]{2,1,0:T(8,128)(2,1)S(1)}, u32[]{:S(2)}, u32[]{:S(2)}) %collective-permute-start.4) | collective-permute-done | bytes 294944 | tf_op jit(solution)/shard_map/ppermute | solution.py:430
  145.4 7.0 fusion.9.projected
  152.4 13.9 %collective-permute-done.10.refs_1_ = bf16[4,96,1536]{2,1,0:T(8,128)(2,1)S(1)} collective-permute-done((bf16[4,96,1536]{2,1,0:T(8,128)(2,1)S(1)}, bf16[4,96,1536]{2,1,0:T(8,128)(2,1)S(1)}, u32[]{:S(2)}, u32[]{:S(2)}) %collective-permute-start.10) | collective-permute-done | bytes 1179680 | tf_op jit(solution)/shard_map/ppermute | solution.py:430
  172.8 19.4 %shard_map.258 = (bf16[1024,384]{1,0:T(8,128)(2,1)S(1)}, f32[1024,384]{1,0:T(8,128)S(1)}, f32[1024,384]{1,0:T(8,128)S(1)}, bf16[1152,1152]{1,0:T(8,128)(2,1)}) custom-call(f32[1152,1152]{1,0:T(8,128)} %fusion.9.projected, f32[1152,128]{1,0:T(8,128)S(1)} %copy-done.21, f32[1152,128]{1,0:T(8,128)S(1)} %copy-done.19, f32[1152,1]{1,0:T(8,128)S(1)} %copy-done.23), custom_call_target="tpu_custom_call" | custom-call | flops 120000004096 | bytes 1048576 | tf_op jit(solution)/shard_map/pallas_call | solution.py:242
  196.0 11.8 %collective-permute-done.12.refs_3_ = bf16[2,96,1536]{2,1,0:T(8,128)(2,1)} collective-permute-done((bf16[2,96,1536]{2,1,0:T(8,128)(2,1)}, bf16[2,96,1536]{2,1,0:T(8,128)(2,1)}, u32[]{:S(2)}, u32[]{:S(2)}) %collective-permute-start.12) | collective-permute-done | bytes 589856 | tf_op jit(solution)/shard_map/ppermute | solution.py:430
  223.2 16.0 %all-to-all-done.2 = bf16[4,256,384]{2,1,0:T(8,128)(2,1)S(1)} async-done(((bf16[4,256,384]{2,1,0:T(8,128)(2,1)}), bf16[4,256,384]{2,1,0:T(8,128)(2,1)S(1)}, u32[]{:S(2)}, u32[]{:S(2)}) %all-to-all-start.2) | async-done | bytes 786464 | tf_op jit(solution)/shard_map/all_to_all | solution.py:418
  262.4 7.2 %shard_map.262 = (bf16[4,2,4,48,1536]{4,3,2,1,0:T(8,128)(2,1)S(1)}, bf16[4,2,4,48,1536]{4,3,2,1,0:T(8,128)(2,1)}) custom-call(s32[1]{0:T(128)} %bitcast.10.places_ref, bf16[4,4,96,1536]{3,2,1,0:T(8,128)(2,1)} %shard_map.261.refs_0_, bf16[4,4,96,1536]{3,2,1,0:T(8,128)(2,1)} %collective-permute-done.19.refs_1_), custom_call_target="tpu_custom_call" | custom-call | bytes 18874368 | tf_op jit(solution)/shard_map/pallas_call | solution.py:455
  269.6 7.0 convolution_convert_fusion.5.keys.values
  276.7 10.6 %shard_map.263 = (bf16[256,1536]{1,0:T(8,128)(2,1)}, f32[256,1536]{1,0:T(8,128)S(1)}, f32[256,1536]{1,0:T(8,128)S(1)}) custom-call(bf16[256,1536]{1,0:T(8,128)(2,1)S(1)} %convolution_convert_fusion.8.query, bf16[768,1536]{1,0:T(8,128)(2,1)} %convolution_convert_fusion.5.keys.values, bf16[768,1536]{1,0:T(8,128)(2,1)} %convolution_convert_fusion.5.keys.values, ...), custom_call_target="tpu_custom_call" | custom-call | flops 20000000000 | bytes 1048576 | tf_op jit(solution)/shard_map/pallas_call | solution.py:301
  294.1 7.1 %fusion.68 = f32[1024,768]{1,0:T(8,128)} fusion(bf16[1024,1536]{1,0:T(8,128)(2,1)} %bitcast.30, bf16[768,1536]{1,0:T(8,128)(2,1)S(1)} %bitcast.250), kind=kOutput, calls=%fused_computation.251 | convolution fusion | flops 2415919104 | bytes 8650752 | tf_op jit(solution)/shard_map/dot_general | solution.py:422
  301.2 10.3 %collective-permute-done.23.refs_1_ = bf16[256,1536]{1,0:T(8,128)(2,1)S(1)} collective-permute-done((bf16[256,1536]{1,0:T(8,128)(2,1)S(1)}, bf16[256,1536]{1,0:T(8,128)(2,1)S(1)}, u32[]{:S(2)}, u32[]{:S(2)}) %collective-permute-start.23) | collective-permute-done | bytes 786464 | tf_op jit(solution)/shard_map/ppermute | solution.py:430
  331.9 7.1 %fusion.69 = f32[1024,1536]{1,0:T(8,128)S(1)} fusion(bf16[1024,1536]{1,0:T(8,128)(2,1)S(1)} %bitcast.288, bf16[1536,1536]{1,0:T(8,128)(2,1)} %bitcast.276), kind=kOutput, calls=%fused_computation.252 | convolution fusion | flops 4831838208 | bytes 14155776 | tf_op jit(solution)/shard_map/dot_general | solution.py:422
  362.1 7.8 %convolution_convert_fusion.3 = bf16[1024,1536]{1,0:T(8,128)(2,1)S(1)} fusion(bf16[1024,1536]{1,0:T(8,128)(2,1)S(1)} %pad_maximum_fusion.2, bf16[1536,1536]{1,0:T(8,128)(2,1)} %bitcast.277), kind=kOutput, calls=%fused_computation.15 | convolution fusion | flops 4833411072 | bytes 11010048 | tf_op jit(solution)/shard_map/dot_general | solution.py:422
  370.4 9.0 %convolution_convert_fusion.4 = bf16[1024,1536]{1,0:T(8,128)(2,1)} fusion(bf16[1024,1536]{1,0:T(8,128)(2,1)S(1)} %copy-done.87, bf16[1536,1536]{1,0:T(8,128)(2,1)} %bitcast.278), kind=kOutput, calls=%fused_computation.16 | convolution fusion | flops 4833411072 | bytes 11010048 | tf_op jit(solution)/shard_map/dot_general | solution.py:422
  431.3 10.8 %shard_map.267 = (bf16[256,1536]{1,0:T(8,128)(2,1)S(1)}, bf16[384,1536]{1,0:T(8,128)(2,1)S(1)}, bf16[384,1536]{1,0:T(8,128)(2,1)S(1)}) custom-call(bf16[256,1536]{1,0:T(8,128)(2,1)S(1)} %copy-done.51, bf16[768,1536]{1,0:T(8,128)(2,1)} %convolution_convert_fusion.5.keys.values, bf16[768,1536]{1,0:T(8,128)(2,1)} %convolution_convert_fusion.5.keys.values, ...), custom_call_target="tpu_custom_call" | custom-call | flops 120000004096 | bytes 1048576 | tf_op jit(solution)/shard_map/pallas_call | solution.py:327
  468.7 15.3 %shard_map.268 = (bf16[4,4,96,1536]{3,2,1,0:T(8,128)(2,1)}, bf16[4,4,96,1536]{3,2,1,0:T(8,128)(2,1)}) custom-call(s32[2]{0:T(128)S(1)} %pad_add_fusion.1.places, bf16[256,1536]{1,0:T(8,128)(2,1)} %get-tuple-element.247.refs_0_, bf16[256,1536]{1,0:T(8,128)(2,1)} %collective-permute-done.27.refs_1_, bf16[768,1536]{1,0:T(8,128)(2,1)} %pad_maximum_fusion.3.refs_2_, ...), custom_call_target="tpu_custom_call" | custom-call | flops 100000000 | bytes 1048576 | tf_op jit(solution)/shard_map/pallas_call | solution.py:642
  491.1 17.7 %all-to-all-done.3 = bf16[256,4,384]{2,0,1:T(8,128)(2,1)S(1)} async-done(((bf16[256,4,384]{2,0,1:T(8,128)(2,1)}), bf16[256,4,384]{2,0,1:T(8,128)(2,1)S(1)}, u32[]{:S(2)}, u32[]{:S(2)}) %all-to-all-start.3) | async-done | bytes 786464 | tf_op jit(solution)/shard_map/all_to_all | solution.py:418
  516.6 21.4 %shard_map.269 = bf16[1152,1152]{1,0:T(8,128)(2,1)} custom-call(bf16[1152,1152]{1,0:T(8,128)(2,1)} %get-tuple-element.213.low, bf16[1024,384]{1,0:T(8,128)(2,1)S(1)} %bitcast.249, f32[1024,384]{1,0:T(8,128)S(1)} %copy-done.28, f32[1024,384]{1,0:T(8,128)S(1)} %copy-done.30, f32[1152,128]{1,0:T(8,128)S(1)} %copy-done.22, f32[1152,128]{1,0:T(8,128)S(1)} %copy-done.20, ...), custom_call_target="tpu_custom_call" | custom-call | flops 2000000000 | bytes 1048576 | tf_op jit(solution)/shard_map/pallas_call | solution.py:272
  537.9 6.6 fusion.73
  587.0 20.7 %collective-permute-done.45 = bf16[4,96,1536]{2,1,0:T(8,128)(2,1)} collective-permute-done((bf16[4,96,1536]{2,1,0:T(8,128)(2,1)}, bf16[4,96,1536]{2,1,0:T(8,128)(2,1)}, u32[]{:S(2)}, u32[]{:S(2)}) %collective-permute-start.45) | collective-permute-done | bytes 1179680 | tf_op jit(solution)/shard_map/ppermute | solution.py:430
  624.3 10.8 %collective-permute-done.48 = bf16[2,48,1152]{2,1,0:T(8,128)(2,1)S(1)} collective-permute-done((bf16[2,48,1152]{2,1,0:T(8,128)(2,1)S(1)}, bf16[2,48,1152]{2,1,0:T(8,128)(2,1)S(1)}, u32[]{:S(2)}, u32[]{:S(2)}) %collective-permute-start.48) | collective-permute-done | bytes 221216 | tf_op jit(solution)/shard_map/ppermute | solution.py:430
  652.2 9.1 %all-to-all-done.5 = bf16[32,48,128]{2,1,0:T(8,128)(2,1)} async-done(((bf16[32,48,128]{2,1,0:T(8,128)(2,1)}), bf16[32,48,128]{2,1,0:T(8,128)(2,1)}, u32[]{:S(2)}, u32[]{:S(2)}) %all-to-all-start.5) | async-done | bytes 393248 | tf_op jit(solution)/shard_map/all_to_all | solution.py:1089
  (704 shorter events, 386.1 us)
Async XLA Ops:
  7.2 126.6 %all-gather.7.cloned.1.call-start = ((), (), s32[]{:S(2)}) async-start(), calls=%async_computation.15 | async-start | bytes 6881280 | tf_op jit(solution)/shard_map/all_gather | solution.py:774
  13.2 39.3 %all-to-all-start = ((bf16[4,64,1152]{2,1,0:T(8,128)(2,1)}), bf16[4,64,1152]{2,1,0:T(8,128)(2,1)S(1)}, u32[]{:S(2)}, u32[]{:S(2)}) async-start(bf16[4,64,1152]{2,1,0:T(8,128)(2,1)} %pad_maximum_fusion.16), calls=%async_computation | async-start | bytes 1179648 | tf_op jit(solution)/shard_map/all_to_all | solution.py:418
  52.5 39.2 %collective-permute-start.2 = (bf16[256,1536]{1,0:T(8,128)(2,1)S(1)}, bf16[256,1536]{1,0:T(8,128)(2,1)S(1)}, u32[]{:S(2)}, u32[]{:S(2)}) collective-permute-start(bf16[256,1536]{1,0:T(8,128)(2,1)S(1)} %bitcast.246), channel_id=1, source_target_pairs={{0,8},{4,12},{8,0},{12,4},{16,24},{20,28},{24,16},{28,20},{1,9},{5... | collective-permute-start | bytes 2359304 | tf_op jit(solution)/shard_map/ppermute | solution.py:430
  54.0 37.7 %collective-permute-start.3 = (bf16[256,1536]{1,0:T(8,128)(2,1)S(1)}, bf16[256,1536]{1,0:T(8,128)(2,1)}, u32[]{:S(2)}, u32[]{:S(2)}) collective-permute-start(bf16[256,1536]{1,0:T(8,128)(2,1)S(1)} %bitcast.247), channel_id=1, source_target_pairs={{0,16},{4,20},{8,24},{12,28},{16,0},{20,4},{24,8},{28,12},{1,17},{... | collective-permute-start | bytes 2359304 | tf_op jit(solution)/shard_map/ppermute | solution.py:430
  55.5 60.8 %all-to-all-start.1 = ((bf16[8,48,1536]{2,1,0:T(8,128)(2,1)}), bf16[8,48,1536]{2,1,0:T(8,128)(2,1)}, u32[]{:S(2)}, u32[]{:S(2)}) async-start(bf16[8,48,1536]{2,1,0:T(8,128)(2,1)} %reshape.521), calls=%async_computation.1 | async-start | bytes 2359296 | tf_op jit(solution)/shard_map/all_to_all | solution.py:786
  59.8 136.2 %all-gather.9.cloned.1.call-start = ((), (), s32[]{:S(2)}) async-start(), calls=%async_computation.16 | async-start | bytes 4423680 | tf_op jit(solution)/shard_map/all_gather | solution.py:822
  167.0 40.8 %collective-permute-start.14 = (bf16[4,96,1536]{2,1,0:T(8,128)(2,1)S(1)}, bf16[4,96,1536]{2,1,0:T(8,128)(2,1)S(1)}, u32[]{:S(2)}, u32[]{:S(2)}) collective-permute-start(bf16[4,96,1536]{2,1,0:T(8,128)(2,1)S(1)} %slice.346.refs_0_), channel_id=1, source_target_pairs={{0,8},{4,12},{8,0},{12,4},{16,24},{20,28},{24,16},{28,20},{1,9},{5... | collective-permute-start | bytes 3538952 | tf_op jit(solution)/shard_map/ppermute | solution.py:430
  168.2 39.6 %collective-permute-start.15 = (bf16[4,96,1536]{2,1,0:T(8,128)(2,1)S(1)}, bf16[4,96,1536]{2,1,0:T(8,128)(2,1)}, u32[]{:S(2)}, u32[]{:S(2)}) collective-permute-start(bf16[4,96,1536]{2,1,0:T(8,128)(2,1)S(1)} %slice.346.refs_0_), channel_id=1, source_target_pairs={{0,16},{4,20},{8,24},{12,28},{16,0},{20,4},{24,8},{28,12},{1,17},{... | collective-permute-start | bytes 3538952 | tf_op jit(solution)/shard_map/ppermute | solution.py:430
  169.9 37.9 %collective-permute-start.12 = (bf16[2,96,1536]{2,1,0:T(8,128)(2,1)}, bf16[2,96,1536]{2,1,0:T(8,128)(2,1)}, u32[]{:S(2)}, u32[]{:S(2)}) collective-permute-start(bf16[2,96,1536]{2,1,0:T(8,128)(2,1)} %slice.344), channel_id=1, source_target_pairs={{0,16},{4,20},{8,24},{12,28},{16,0},{20,4},{24,8},{28,12},{1,17},{... | collective-permute-start | bytes 1769480 | tf_op jit(solution)/shard_map/ppermute | solution.py:430
  172.0 35.8 %collective-permute-start.13 = (bf16[2,96,1536]{2,1,0:T(8,128)(2,1)}, bf16[2,96,1536]{2,1,0:T(8,128)(2,1)}, u32[]{:S(2)}, u32[]{:S(2)}) collective-permute-start(bf16[2,96,1536]{2,1,0:T(8,128)(2,1)} %slice.345), channel_id=1, source_target_pairs={{0,8},{4,12},{8,0},{12,4},{16,24},{20,28},{24,16},{28,20},{1,9},{5... | collective-permute-start | bytes 1769480 | tf_op jit(solution)/shard_map/ppermute | solution.py:430
  218.2 108.9 %all-gather.11.cloned.1.call-start = ((), (), s32[]{:S(2)}) async-start(), calls=%async_computation.17 | async-start | bytes 4423680 | tf_op jit(solution)/shard_map/all_gather | solution.py:856
  258.6 172.7 %reduce-scatter.5.cloned.1.call-start = ((), (), s32[]{:S(2)}) async-start(), calls=%async_computation.11 | async-start | bytes 2949120 | tf_op jit(solution)/shard_map/reduce_scatter | solution.py:946
  383.5 166.0 %reduce-scatter.7.cloned.1.call-start = ((), (), s32[]{:S(2)}) async-start(), calls=%async_computation.12 | async-start | bytes 5898240 | tf_op jit(solution)/shard_map/reduce_scatter | solution.py:963
  462.8 46.0 %all-to-all-start.3 = ((bf16[256,4,384]{2,0,1:T(8,128)(2,1)}), bf16[256,4,384]{2,0,1:T(8,128)(2,1)S(1)}, u32[]{:S(2)}, u32[]{:S(2)}) async-start(bf16[256,4,384]{2,0,1:T(8,128)(2,1)} %bitcast.290), calls=%async_computation.4 | async-start | bytes 1572864 | tf_op jit(solution)/shard_map/all_to_all | solution.py:418
  466.3 145.4 %reduce-scatter.9.cloned.1.call-start = ((), (), s32[]{:S(2)}) async-start(), calls=%async_computation.13 | async-start | bytes 3932160 | tf_op jit(solution)/shard_map/reduce_scatter | solution.py:1047
  511.3 38.2 %collective-permute-start.39 = (bf16[2,96,1536]{2,1,0:T(8,128)(2,1)}, bf16[2,96,1536]{2,1,0:T(8,128)(2,1)}, u32[]{:S(2)}, u32[]{:S(2)}) collective-permute-start(bf16[2,96,1536]{2,1,0:T(8,128)(2,1)} %get-tuple-element.410), channel_id=1, source_target_pairs={{0,8},{4,12},{8,0},{12,4},{16,24},{20,28},{24,16},{28,20},{1,9},{5... | collective-permute-start | bytes 1769480 | tf_op jit(solution)/shard_map/ppermute | solution.py:430
  512.8 36.7 %collective-permute-start.40 = (bf16[2,96,1536]{2,1,0:T(8,128)(2,1)}, bf16[2,96,1536]{2,1,0:T(8,128)(2,1)S(1)}, u32[]{:S(2)}, u32[]{:S(2)}) collective-permute-start(bf16[2,96,1536]{2,1,0:T(8,128)(2,1)} %get-tuple-element.409), channel_id=1, source_target_pairs={{0,16},{4,20},{8,24},{12,28},{16,0},{20,4},{24,8},{28,12},{1,17},{... | collective-permute-start | bytes 1769480 | tf_op jit(solution)/shard_map/ppermute | solution.py:430
  561.2 46.5 %collective-permute-start.45 = (bf16[4,96,1536]{2,1,0:T(8,128)(2,1)}, bf16[4,96,1536]{2,1,0:T(8,128)(2,1)}, u32[]{:S(2)}, u32[]{:S(2)}) collective-permute-start(bf16[4,96,1536]{2,1,0:T(8,128)(2,1)} %pad_maximum_fusion.8), channel_id=1, source_target_pairs={{0,16},{4,20},{8,24},{12,28},{16,0},{20,4},{24,8},{28,12},{1,17},{... | collective-permute-start | bytes 3538952 | tf_op jit(solution)/shard_map/ppermute | solution.py:430
  563.0 48.7 %collective-permute-start.44 = (bf16[4,96,1536]{2,1,0:T(8,128)(2,1)}, bf16[4,96,1536]{2,1,0:T(8,128)(2,1)}, u32[]{:S(2)}, u32[]{:S(2)}) collective-permute-start(bf16[4,96,1536]{2,1,0:T(8,128)(2,1)} %pad_maximum_fusion.7), channel_id=1, source_target_pairs={{0,8},{4,12},{8,0},{12,4},{16,24},{20,28},{24,16},{28,20},{1,9},{5... | collective-permute-start | bytes 3538952 | tf_op jit(solution)/shard_map/ppermute | solution.py:430
  572.1 39.6 %collective-permute-start.43 = (bf16[4,1,4,48,1152]{4,3,2,1,0:T(8,128)(2,1)}, bf16[4,1,4,48,1152]{4,3,2,1,0:T(8,128)(2,1)S(1)}, u32[]{:S(2)}, u32[]{:S(2)}) collective-permute-start(bf16[4,1,4,48,1152]{4,3,2,1,0:T(8,128)(2,1)} %constant_dynamic-slice_fusion.1), channel_id=1, source_target_pairs={{0,4},{4,0},{8,12},{12,8},{16,20},{20,16},{24,28},{28,24},{1,5},{5... | collective-permute-start | bytes 5308424 | tf_op jit(solution)/shard_map/ppermute | solution.py:430
  575.0 49.2 %all-to-all-start.4 = ((bf16[8,48,1536]{2,1,0:T(8,128)(2,1)}), bf16[8,48,1536]{2,1,0:T(8,128)(2,1)S(1)}, u32[]{:S(2)}, u32[]{:S(2)}) async-start(bf16[8,48,1536]{2,1,0:T(8,128)(2,1)} %bitcast.303), calls=%async_computation.7 | async-start | bytes 2359296 | tf_op jit(solution)/shard_map/all_to_all | solution.py:1081
  578.6 111.3 %reduce-scatter.11.cloned.1.call-start = ((), (), s32[]{:S(2)}) async-start(), calls=%async_computation.14 | async-start | bytes 2949120 | tf_op jit(solution)/shard_map/reduce_scatter | solution.py:1080
  582.4 79.9 %collective-permute-start.52 = (bf16[128,1536]{1,0:T(8,128)(2,1)}, bf16[128,1536]{1,0:T(8,128)(2,1)}, u32[]{:S(2)}, u32[]{:S(2)}) collective-permute-start(bf16[128,1536]{1,0:T(8,128)(2,1)} %get-tuple-element.412), channel_id=1, source_target_pairs={{0,8},{4,12},{8,0},{12,4},{16,24},{20,28},{24,16},{28,20},{1,9},{5... | collective-permute-start | bytes 1179656 | tf_op jit(solution)/shard_map/ppermute | solution.py:430
  586.4 75.9 %collective-permute-start.53 = (bf16[128,1536]{1,0:T(8,128)(2,1)}, bf16[128,1536]{1,0:T(8,128)(2,1)}, u32[]{:S(2)}, u32[]{:S(2)}) collective-permute-start(bf16[128,1536]{1,0:T(8,128)(2,1)} %get-tuple-element.411), channel_id=1, source_target_pairs={{0,16},{4,20},{8,24},{12,28},{16,0},{20,4},{24,8},{28,12},{1,17},{... | collective-permute-start | bytes 1179656 | tf_op jit(solution)/shard_map/ppermute | solution.py:430
  (215 other events, 2039.2 us)
Sparse Core Ops, SparseCore 0:
  10.8 113.7 all-gather.6
  126.8 69.1 all-gather.8
  258.7 68.2 all-gather.10
  383.7 46.7 reduce-scatter.4
  432.6 97.3 reduce-scatter.6
  549.6 59.4 reduce-scatter.8
  624.0 53.5 reduce-scatter.10
